TPU v7x, 32 devices: a whole 2x2x4 slice. The times are simulated.
32 devices in a mesh: grp: 4 (over x, core), dev: 8 (over z, y).
Axes of the slice: x: 2, y: 2, z: 4, core: 2. Of those that a mesh axis runs over, the one named last changes fastest.
Arguments:
- hot_table: float32 [2048, 768], P('dev'), may hold values from -6 to 6
- cold_table: float32 [32768, 768], P(('grp', 'dev')), may hold values from -6 to 6
- hot_need: int32 [256, 32], P(('grp', 'dev')), may hold values from -1 to 255, as said below
- cold_need: int32 [1024, 4], P(('grp', 'dev')), may hold values from -1 to 1023, as said below
- self_index: int32 [65536], P(('grp', 'dev')), may hold values from 0 to 383, as said below
- neighbors: int32 [65536, 25], P(('grp', 'dev')), may hold values from 0 to 383, as said below
- w_self: bfloat16 [768, 1024], replicated, may hold values from -0.21875 to 0.21875
- w_neigh: bfloat16 [768, 1024], replicated, may hold values from -1 to 1
- cotangent: bfloat16 [65536, 1024], P(('grp', 'dev')), may hold values from -0.0234375 to 0.0234375
Outputs:
- hidden: bfloat16 [65536, 1024], P(('grp', 'dev'))
- grad_self: float32 [768, 1024], replicated
- grad_neigh: float32 [768, 1024], replicated
Inputs may be any that keep to these rules, and one draw needn't show every extreme that they name: `hot_need`: in each row the asked slots come first, 1 to 32 of them, then -1. In every draw some dev index is asked 32 slots by every device. `cold_need`: in each row the asked slots come first, 1 to 4 of them, then -1. In every draw some owner is asked 4 slots by every device. `self_index`: each entry names an asked slot of the device's own requests: p * 32 + k for the k-th hot slot asked of dev index p, or (devices along dev) * 32 + q * 4 + k for the k-th cold slot asked of owner q. `neighbors`: each entry names an asked slot of the device's own requests, numbered as for self_index.
All inputs are finite; a program needn't handle non-finite values.
Results may differ from a plain program's by a relative error of at most 0.0058.
Values sent between devices are 32-bit elements; how exact they have to be, the bound alone decides.
No kernel may reach another device: no remote copies, remote signals or barrier semaphores. Data moves between devices by JAX's collectives and lax.ppermute only.
A program may use at most 192 MiB of HBM per device.

v0:
```python
import jax
import jax.numpy as jnp
from jax import lax
from jax.sharding import PartitionSpec as P

FAN = 25


def look_up(feature_table, requests):
    picked = jnp.take(feature_table, jnp.maximum(requests, 0), axis=0)
    return picked * (requests >= 0)[..., None].astype(jnp.float32)


def body(
    hot_table, cold_table, hot_need, cold_need, self_index, neighbors, w_self, w_neigh, cotangent
):
    feat_width = hot_table.shape[1]
    hot_shard = hot_table.shape[0]
    dev_count = lax.axis_size("dev")
    whole_cache = lax.all_gather(hot_table, "dev", axis=0, tiled=True)
    offsets = (jnp.arange(dev_count, dtype=jnp.int32) * hot_shard)[:, None]
    hot_rows = jnp.take(whole_cache, jnp.maximum(hot_need, 0) + offsets, axis=0)
    hot_rows = hot_rows * (hot_need >= 0)[..., None].astype(jnp.float32)
    cold_rows = lax.all_to_all(
        look_up(
            cold_table,
            lax.all_to_all(cold_need, ("grp", "dev"), split_axis=0, concat_axis=0, tiled=True),
        ),
        ("grp", "dev"),
        split_axis=0,
        concat_axis=0,
        tiled=True,
    )
    sources = jnp.concatenate(
        [hot_rows.reshape(-1, feat_width), cold_rows.reshape(-1, feat_width)], axis=0
    )
    self_feat = jnp.take(sources, self_index, axis=0).astype(jnp.bfloat16)
    target_count = neighbors.shape[0]
    block_rows = min(target_count, 256)

    def mean_block(indices):
        return (jnp.sum(jnp.take(sources, indices, axis=0), axis=1) / FAN).astype(jnp.bfloat16)

    neigh_feat = lax.map(mean_block, neighbors.reshape(-1, block_rows, FAN)).reshape(
        target_count, feat_width
    )
    pre_act = jnp.dot(self_feat, w_self, preferred_element_type=jnp.float32) + jnp.dot(
        neigh_feat, w_neigh, preferred_element_type=jnp.float32
    )
    sigma = jax.nn.sigmoid(pre_act)
    hidden = (pre_act * sigma).astype(jnp.bfloat16)
    slope = sigma * (1.0 + pre_act * (1.0 - sigma))
    masked = (cotangent.astype(jnp.float32) * slope).astype(jnp.bfloat16)
    contract_rows = (((0,), (0,)), ((), ()))
    self_term = lax.dot_general(
        self_feat, masked, contract_rows, preferred_element_type=jnp.float32
    )
    neigh_term = lax.dot_general(
        neigh_feat, masked, contract_rows, preferred_element_type=jnp.float32
    )
    summed = lax.psum((self_term, neigh_term), ("grp", "dev"))
    return (hidden, summed[0], summed[1])


def solution(mesh):
    in_specs = (
        P("dev", None),
        P(("grp", "dev"), None),
        P(("grp", "dev"), None),
        P(("grp", "dev"), None),
        P(("grp", "dev")),
        P(("grp", "dev"), None),
        P(),
        P(),
        P(("grp", "dev"), None),
    )
    out_specs = (P(("grp", "dev"), None), P(), P())
    return jax.shard_map(body, mesh=mesh, in_specs=in_specs, out_specs=out_specs, check_vma=False)
```

profile of v0, /device:TPU:0, one launch (start us, length us, event | category | flops | bytes accessed | tf_op | source)
XLA Modules:
  0.0 797.6 jit_solution(16933404815865742860)
XLA Ops:
  7.9 1.6 copy.26
  9.5 7.3 all-to-all-start
  17.3 6.5 all-to-all-done
  25.0 0.8 gather_fusion.2
  25.9 1.6 select_multiply_fusion.1
  27.5 2.6 all-to-all-start.1
  31.2 1.3 copy.32
  33.1 21.4 %all-to-all-done.1 = f32[32,4,768]{2,1,0:T(4,128)S(1)} async-done(((f32[32,4,768]{2,1,0:T(4,128)}), f32[32,4,768]{2,1,0:T(4,128)S(1)}, u32[]{:S(2)}, u32[]{:S(2)}) %all-to-all-start.1) | async-done | bytes 393248 | tf_op jit(solution)/shard_map/all_to_all | solution.py:24
  54.6 65.7 %all-gather.2.cloned.1.call-done = f32[2048,768]{1,0:T(8,128)} async-done(((f32[256,768]{1,0:T(8,128)}), f32[2048,768]{1,0:T(8,128)}) %all-gather.2.cloned.1.call-update) | async-done | bytes 6291472 | tf_op jit(solution)/shard_map/all_gather | solution.py:20
  120.4 4.2 gather_fusion.1
  124.8 9.1 %gather_fusion.3 = bf16[2048,768]{1,0:T(8,128)(2,1)} fusion(f32[384,768]{1,0:T(8,128)S(1)} %pad_maximum_fusion, s32[2048]{0:T(1024)S(1)} %fusion.2), kind=kCustom, calls=%fused_computation.3 | custom fusion | bytes 6299648 | tf_op jit(solution)/shard_map/jit(_take)/gather | solution.py:37
  133.9 472.1 %while.10 = (s32[]{:T(128)}, bf16[8,256,768]{2,1,0:T(8,128)(2,1)}, s32[8,256,25]{2,1,0:T(8,128)S(1)}, f32[384,768]{1,0:T(8,128)S(1)}, s32[]{:T(128)}) while((s32[]{:T(128)}, bf16[8,256,768]{2,1,0:T(8,128)(2,1)}, s32[8,256,25]{2,1,0:T(8,128)S(1)}, f32[384,768]{1,0:T(8,128)S(1)}, s32[]{:T(128)}) %tuple.35), condition=%wide.region_2.3_spmd, body=%wide.region_0.0_spmd.sunk | while | flops 10091778 | bytes 100490832 | solution.py:44
  134.2 19.7 %gather_fusion = f32[6400,768]{1,0:T(8,128)} fusion(f32[384,768]{1,0:T(8,128)S(1)} %get-tuple-element.81, s32[7168]{0:T(1024)S(1)} %pad_clamp_fusion.4), kind=kCustom, calls=%fused_computation.clone.1 | custom fusion | bytes 39347200 | tf_op jit(solution)/shard_map/while/body/eval_jaxpr/jit(_take)/gather | solution.py:42
  153.9 20.3 %reshape.171 = f32[256,25,768]{2,1,0:T(8,128)} reshape(f32[6400,768]{1,0:T(8,128)} %gather_fusion) | data formatting | bytes 39321600 | tf_op jit(solution)/shard_map/while/body/eval_jaxpr/jit(_take)/gather | solution.py:42
  174.2 17.9 %select_reduce_fusion.2 = f32[256,768]{1,0:T(8,128)S(1)} fusion(f32[256,25,768]{2,1,0:T(8,128)} %reshape.171, pred[256,25]{1,0:T(8,128)(4,1)S(1)} %compare_and_fusion.4), kind=kLoop, calls=%fused_computation.4.clone.1 | loop fusion | flops 9633792 | bytes 20453632 | tf_op jit(solution)/shard_map/while/body/eval_jaxpr/reduce_sum | solution.py:42
  193.2 19.7 %gather_fusion = f32[6400,768]{1,0:T(8,128)} fusion(f32[384,768]{1,0:T(8,128)S(1)} %get-tuple-element.81, s32[7168]{0:T(1024)S(1)} %pad_clamp_fusion.4), kind=kCustom, calls=%fused_computation.clone.1 | custom fusion | bytes 39347200 | tf_op jit(solution)/shard_map/while/body/eval_jaxpr/jit(_take)/gather | solution.py:42
  212.9 20.3 %reshape.171 = f32[256,25,768]{2,1,0:T(8,128)} reshape(f32[6400,768]{1,0:T(8,128)} %gather_fusion) | data formatting | bytes 39321600 | tf_op jit(solution)/shard_map/while/body/eval_jaxpr/jit(_take)/gather | solution.py:42
  233.2 17.9 %select_reduce_fusion.2 = f32[256,768]{1,0:T(8,128)S(1)} fusion(f32[256,25,768]{2,1,0:T(8,128)} %reshape.171, pred[256,25]{1,0:T(8,128)(4,1)S(1)} %compare_and_fusion.4), kind=kLoop, calls=%fused_computation.4.clone.1 | loop fusion | flops 9633792 | bytes 20453632 | tf_op jit(solution)/shard_map/while/body/eval_jaxpr/reduce_sum | solution.py:42
  251.1 0.8 fusion.13
  252.2 19.7 %gather_fusion = f32[6400,768]{1,0:T(8,128)} fusion(f32[384,768]{1,0:T(8,128)S(1)} %get-tuple-element.81, s32[7168]{0:T(1024)S(1)} %pad_clamp_fusion.4), kind=kCustom, calls=%fused_computation.clone.1 | custom fusion | bytes 39347200 | tf_op jit(solution)/shard_map/while/body/eval_jaxpr/jit(_take)/gather | solution.py:42
  271.9 20.3 %reshape.171 = f32[256,25,768]{2,1,0:T(8,128)} reshape(f32[6400,768]{1,0:T(8,128)} %gather_fusion) | data formatting | bytes 39321600 | tf_op jit(solution)/shard_map/while/body/eval_jaxpr/jit(_take)/gather | solution.py:42
  292.2 17.9 %select_reduce_fusion.2 = f32[256,768]{1,0:T(8,128)S(1)} fusion(f32[256,25,768]{2,1,0:T(8,128)} %reshape.171, pred[256,25]{1,0:T(8,128)(4,1)S(1)} %compare_and_fusion.4), kind=kLoop, calls=%fused_computation.4.clone.1 | loop fusion | flops 9633792 | bytes 20453632 | tf_op jit(solution)/shard_map/while/body/eval_jaxpr/reduce_sum | solution.py:42
  310.1 0.8 fusion.13
  311.2 19.7 %gather_fusion = f32[6400,768]{1,0:T(8,128)} fusion(f32[384,768]{1,0:T(8,128)S(1)} %get-tuple-element.81, s32[7168]{0:T(1024)S(1)} %pad_clamp_fusion.4), kind=kCustom, calls=%fused_computation.clone.1 | custom fusion | bytes 39347200 | tf_op jit(solution)/shard_map/while/body/eval_jaxpr/jit(_take)/gather | solution.py:42
  330.9 20.3 %reshape.171 = f32[256,25,768]{2,1,0:T(8,128)} reshape(f32[6400,768]{1,0:T(8,128)} %gather_fusion) | data formatting | bytes 39321600 | tf_op jit(solution)/shard_map/while/body/eval_jaxpr/jit(_take)/gather | solution.py:42
  351.2 17.9 %select_reduce_fusion.2 = f32[256,768]{1,0:T(8,128)S(1)} fusion(f32[256,25,768]{2,1,0:T(8,128)} %reshape.171, pred[256,25]{1,0:T(8,128)(4,1)S(1)} %compare_and_fusion.4), kind=kLoop, calls=%fused_computation.4.clone.1 | loop fusion | flops 9633792 | bytes 20453632 | tf_op jit(solution)/shard_map/while/body/eval_jaxpr/reduce_sum | solution.py:42
  369.1 0.8 fusion.13
  370.2 19.7 %gather_fusion = f32[6400,768]{1,0:T(8,128)} fusion(f32[384,768]{1,0:T(8,128)S(1)} %get-tuple-element.81, s32[7168]{0:T(1024)S(1)} %pad_clamp_fusion.4), kind=kCustom, calls=%fused_computation.clone.1 | custom fusion | bytes 39347200 | tf_op jit(solution)/shard_map/while/body/eval_jaxpr/jit(_take)/gather | solution.py:42
  389.9 20.3 %reshape.171 = f32[256,25,768]{2,1,0:T(8,128)} reshape(f32[6400,768]{1,0:T(8,128)} %gather_fusion) | data formatting | bytes 39321600 | tf_op jit(solution)/shard_map/while/body/eval_jaxpr/jit(_take)/gather | solution.py:42
  410.2 17.9 %select_reduce_fusion.2 = f32[256,768]{1,0:T(8,128)S(1)} fusion(f32[256,25,768]{2,1,0:T(8,128)} %reshape.171, pred[256,25]{1,0:T(8,128)(4,1)S(1)} %compare_and_fusion.4), kind=kLoop, calls=%fused_computation.4.clone.1 | loop fusion | flops 9633792 | bytes 20453632 | tf_op jit(solution)/shard_map/while/body/eval_jaxpr/reduce_sum | solution.py:42
  428.1 0.8 fusion.13
  429.2 19.7 %gather_fusion = f32[6400,768]{1,0:T(8,128)} fusion(f32[384,768]{1,0:T(8,128)S(1)} %get-tuple-element.81, s32[7168]{0:T(1024)S(1)} %pad_clamp_fusion.4), kind=kCustom, calls=%fused_computation.clone.1 | custom fusion | bytes 39347200 | tf_op jit(solution)/shard_map/while/body/eval_jaxpr/jit(_take)/gather | solution.py:42
  449.0 20.3 %reshape.171 = f32[256,25,768]{2,1,0:T(8,128)} reshape(f32[6400,768]{1,0:T(8,128)} %gather_fusion) | data formatting | bytes 39321600 | tf_op jit(solution)/shard_map/while/body/eval_jaxpr/jit(_take)/gather | solution.py:42
  469.2 17.9 %select_reduce_fusion.2 = f32[256,768]{1,0:T(8,128)S(1)} fusion(f32[256,25,768]{2,1,0:T(8,128)} %reshape.171, pred[256,25]{1,0:T(8,128)(4,1)S(1)} %compare_and_fusion.4), kind=kLoop, calls=%fused_computation.4.clone.1 | loop fusion | flops 9633792 | bytes 20453632 | tf_op jit(solution)/shard_map/while/body/eval_jaxpr/reduce_sum | solution.py:42
  487.1 0.8 fusion.13
  488.2 19.7 %gather_fusion = f32[6400,768]{1,0:T(8,128)} fusion(f32[384,768]{1,0:T(8,128)S(1)} %get-tuple-element.81, s32[7168]{0:T(1024)S(1)} %pad_clamp_fusion.4), kind=kCustom, calls=%fused_computation.clone.1 | custom fusion | bytes 39347200 | tf_op jit(solution)/shard_map/while/body/eval_jaxpr/jit(_take)/gather | solution.py:42
  508.0 20.3 %reshape.171 = f32[256,25,768]{2,1,0:T(8,128)} reshape(f32[6400,768]{1,0:T(8,128)} %gather_fusion) | data formatting | bytes 39321600 | tf_op jit(solution)/shard_map/while/body/eval_jaxpr/jit(_take)/gather | solution.py:42
  528.3 17.9 %select_reduce_fusion.2 = f32[256,768]{1,0:T(8,128)S(1)} fusion(f32[256,25,768]{2,1,0:T(8,128)} %reshape.171, pred[256,25]{1,0:T(8,128)(4,1)S(1)} %compare_and_fusion.4), kind=kLoop, calls=%fused_computation.4.clone.1 | loop fusion | flops 9633792 | bytes 20453632 | tf_op jit(solution)/shard_map/while/body/eval_jaxpr/reduce_sum | solution.py:42
  547.2 19.7 %gather_fusion = f32[6400,768]{1,0:T(8,128)} fusion(f32[384,768]{1,0:T(8,128)S(1)} %get-tuple-element.81, s32[7168]{0:T(1024)S(1)} %pad_clamp_fusion.4), kind=kCustom, calls=%fused_computation.clone.1 | custom fusion | bytes 39347200 | tf_op jit(solution)/shard_map/while/body/eval_jaxpr/jit(_take)/gather | solution.py:42
  567.0 20.3 %reshape.171 = f32[256,25,768]{2,1,0:T(8,128)} reshape(f32[6400,768]{1,0:T(8,128)} %gather_fusion) | data formatting | bytes 39321600 | tf_op jit(solution)/shard_map/while/body/eval_jaxpr/jit(_take)/gather | solution.py:42
  587.3 17.9 %select_reduce_fusion.2 = f32[256,768]{1,0:T(8,128)S(1)} fusion(f32[256,25,768]{2,1,0:T(8,128)} %reshape.171, pred[256,25]{1,0:T(8,128)(4,1)S(1)} %compare_and_fusion.4), kind=kLoop, calls=%fused_computation.4.clone.1 | loop fusion | flops 9633792 | bytes 20453632 | tf_op jit(solution)/shard_map/while/body/eval_jaxpr/reduce_sum | solution.py:42
  606.0 6.0 fusion.4
  612.0 8.1 %multiply_convert_fusion.1 = (bf16[2048,1024]{1,0:T(8,128)(2,1)S(1)}, bf16[2048,1024]{1,0:T(8,128)(2,1)}) fusion(bf16[2048,1024]{1,0:T(8,128)(2,1)S(1)} %copy-done.6, f32[2048,1024]{1,0:T(8,128)S(1)} %fusion.4, bf16[2048,768]{1,0:T(8,128)(2,1)S(1)} %bitcast.35, bf16[768,1024]{1,0:T(8,128)(2,1)S(1)} %copy-done.8), kind=kOutput, calls=%fused_computation.12 | convolution fusion | flops 3248488448 | bytes 25690112 | tf_op jit(solution)/shard_map/dot_general | solution.py:47
  620.1 5.2 fusion.3
  625.3 5.1 fusion.5
  630.5 154.5 %all-reduce.3.cloned.1.call-done = (f32[768,1024]{1,0:T(8,128)}, f32[768,1024]{1,0:T(8,128)}) async-done(((f32[768,1024]{1,0:T(8,128)}, f32[768,1024]{1,0:T(8,128)}), (f32[768,1024]{1,0:T(8,128)}, f32[768,1024]{1,0:T(8,128)})) %all-reduce.3.cloned.1.call-update) | async-done | bytes 6291472 | tf_op jit(solution)/shard_map/psum | solution.py:61
  785.0 4.1 copy.44
  789.1 1.7 copy.45
  (78 shorter events, 9.2 us)
Async XLA Ops:
  7.2 17.8 %copy-start = (f32[1024,768]{1,0:T(8,128)S(1)}, f32[1024,768]{1,0:T(8,128)}, u32[]{:S(2)}) copy-start(f32[1024,768]{1,0:T(8,128)} %param.12) | copy-start | bytes 9437188
  7.2 113.2 %all-gather.2.cloned.1.call-start = ((), (), s32[]{:S(2)}) async-start(), calls=%async_computation.2 | async-start | bytes 7077888 | tf_op jit(solution)/shard_map/all_gather | solution.py:20
  9.5 14.3 %all-to-all-start = ((s32[32,1,4]{2,1,0:T(1,128)}), s32[32,1,4]{2,1,0:T(1,128)S(1)}, u32[]{:S(2)}, u32[]{:S(2)}) async-start(s32[32,1,4]{2,1,0:T(1,128)} %copy.26), calls=%async_computation | async-start | bytes 32768 | tf_op jit(solution)/shard_map/all_to_all | solution.py:27
  24.9 7.6 copy-start.4
  27.5 27.0 %all-to-all-start.1 = ((f32[32,4,768]{2,1,0:T(4,128)}), f32[32,4,768]{2,1,0:T(4,128)S(1)}, u32[]{:S(2)}, u32[]{:S(2)}) async-start(f32[32,4,768]{2,1,0:T(4,128)} %select_multiply_fusion.1), calls=%async_computation.1 | async-start | bytes 786432 | tf_op jit(solution)/shard_map/all_to_all | solution.py:24
  30.1 754.8 %all-reduce.3.cloned.1.call-start = ((), (), s32[]{:S(2)}) async-start(), calls=%async_computation.3 | async-start | bytes 12582912 | tf_op jit(solution)/shard_map/psum | solution.py:61
  133.9 472.1 %copy-start.5 = (pred[2048]{0:T(1024)(128)(4,1)S(1)}, pred[2048]{0:T(1024)(128)(4,1)}, u32[]{:S(2)}) copy-start(pred[2048]{0:T(1024)(128)(4,1)} %compare_and_fusion.1) | copy-start | bytes 6148
  606.0 6.0 copy-start.6
  606.0 6.0 copy-start.7
  606.0 6.0 copy-start.8
  612.0 8.1 %copy-start.3 = (bf16[2048,768]{1,0:T(8,128)(2,1)S(1)}, bf16[2048,768]{1,0:T(8,128)(2,1)}, u32[]{:S(2)}) copy-start(bf16[2048,768]{1,0:T(8,128)(2,1)} %gather_fusion.3) | copy-start | bytes 9437188
  785.0 4.1 copy-start.2
  785.0 5.8 copy-start.1
Sparse Core Ops, SparseCore 0:
  10.2 110.1 all-gather.1
  630.6 154.3 all-reduce.2
where the time goes:
time: 802 us; the launch traced here: 798 us
  local copies, waits for them, and re-layouts  346 us (43%)
  waiting for transfers between devices  249 us (31%)
  other arithmetic  154 us (19%)
  matrix products  24.4 us (3%)
  between operations  14.2 us (2%)
  starting transfers between devices  9.97 us (1%)
    gather x16, local copies, waits for them, and re-layouts, mean_block(): jnp.take(sources, indices, axis=0)  320 us
    psum x1, waiting for transfers between devices, body(): summed = lax.psum((self_term, neigh_term), ('grp', 'dev'))  154 us
    reduce_sum x8, other arithmetic, mean_block(): jnp.sum(jnp.take(sources, indices, axis=0), axis=1) / FAN  143 us
    all_gather x1, waiting for transfers between devices, body(): whole_cache = lax.all_gather(hot_table, 'dev', axis=0, tiled=True)  65.7 us
    all_to_all x1, waiting for transfers between devices, body(): lax.all_to_all(look_up(cold_table, lax.all_to_all(cold_need, ('grp', 'dev...  21.4 us
  transfers between devices with their start and end apart: 4, of which 4 were waited for; matrix products, arithmetic and copies ran while one was open for 1% of the time, Pallas kernels for 0%

commit v1 on v0

v1 whole, which is shorter than its diff:
```python
import functools

import jax
import jax.numpy as jnp
from jax import lax
from jax.experimental import pallas as pl
from jax.experimental.pallas import tpu as pltpu
from jax.sharding import PartitionSpec as P

FAN = 25
CORES = 2
CHUNKS = 4
VMEM_LIMIT = 48 * 1024 * 1024


def look_up(feature_table, requests):
    picked = jnp.take(feature_table, jnp.maximum(requests, 0), axis=0)
    return picked * (requests >= 0)[..., None].astype(jnp.float32)


def count_kernel(slots_ref, self_ref, x_ref, xt_ref):
    rows, n_src = x_ref.shape[0], x_ref.shape[1] // 2
    step = 64

    @pl.loop(0, rows // step)
    def _(i):
        here = pl.ds(pl.multiple_of(i * step, step), step)
        lanes = lax.broadcasted_iota(jnp.int32, (step, n_src), 1)
        slots = slots_ref[here, :]
        total = jnp.zeros((step, n_src), jnp.float32)
        for j in range(FAN):
            total += jnp.where(slots[:, j : j + 1] == lanes, 1.0, 0.0)
        x_ref[here, pl.ds(n_src, n_src)] = total.astype(jnp.bfloat16)
        own = jnp.where(self_ref[here, :] == lanes, 1.0, 0.0)
        x_ref[here, pl.ds(0, n_src)] = own.astype(jnp.bfloat16)

    xt_ref[...] = x_ref[...].astype(jnp.float32).T.astype(jnp.bfloat16)


def count_matrices(neighbors, self_index, n_src):
    targets = neighbors.shape[0]
    block = 256
    return pl.pallas_call(
        count_kernel,
        grid=(targets // block,),
        in_specs=[
            pl.BlockSpec((block, FAN), lambda i: (i, 0)),
            pl.BlockSpec((block, 1), lambda i: (i, 0)),
        ],
        out_specs=[
            pl.BlockSpec((block, 2 * n_src), lambda i: (i, 0)),
            pl.BlockSpec((2 * n_src, block), lambda i: (0, i)),
        ],
        out_shape=[
            jax.ShapeDtypeStruct((targets, 2 * n_src), jnp.bfloat16),
            jax.ShapeDtypeStruct((2 * n_src, targets), jnp.bfloat16),
        ],
        compiler_params=pltpu.CompilerParams(vmem_limit_bytes=VMEM_LIMIT),
        cost_estimate=pl.CostEstimate(
            flops=2 * targets * n_src * FAN, bytes_accessed=4 * targets * n_src * 2, transcendentals=0
        ),
        name="count_matrices",
    )(neighbors, self_index[:, None])


def layer_kernel(
    core_ref, x_ref, xt_ref, hot_ref, cold_ref, w_self_ref, w_neigh_ref, cot_ref, *rest
):
    hidden_ref, keep_ref, send_ref, src, src_t, prod, back = rest[-7:]
    n_hot, n_src = hot_ref.shape[0], src.shape[0]
    step = pl.program_id(0)

    @pl.when(step == 0)
    def _():
        src[:n_hot, :] = hot_ref[...].astype(jnp.bfloat16)
        src[n_hot:, :] = cold_ref[...].astype(jnp.bfloat16)
        src_t[...] = jnp.concatenate([hot_ref[...], cold_ref[...]], axis=0).T.astype(jnp.bfloat16)
        prod[:n_src, :] = jnp.dot(
            src[...], w_self_ref[...], preferred_element_type=jnp.float32
        ).astype(jnp.bfloat16)
        prod[n_src:, :] = (
            jnp.dot(src[...], w_neigh_ref[...], preferred_element_type=jnp.float32) * (1.0 / FAN)
        ).astype(jnp.bfloat16)
        back[...] = jnp.zeros_like(back)

    pre_act = jnp.dot(x_ref[...], prod[...], preferred_element_type=jnp.float32)
    sigma = jax.nn.sigmoid(pre_act)
    hidden_ref[...] = (pre_act * sigma).astype(jnp.bfloat16)
    slope = sigma * (1.0 + pre_act * (1.0 - sigma))
    masked = (cot_ref[...].astype(jnp.float32) * slope).astype(jnp.bfloat16)
    back[0] += jnp.dot(xt_ref[:n_src, :], masked, preferred_element_type=jnp.float32)
    back[1] += jnp.dot(xt_ref[n_src:, :], masked, preferred_element_type=jnp.float32)

    @pl.when(step == pl.num_programs(0) - 1)
    def _():
        core = core_ref[0]
        for which, out_ref in ((core, keep_ref), (1 - core, send_ref)):
            scale = jnp.where(which == 0, 1.0, 1.0 / FAN)
            term = (back[which] * scale).astype(jnp.bfloat16)
            out_ref[...] = jnp.dot(src_t[...], term, preferred_element_type=jnp.float32)


def layer_chunk(chunk, core, x, xt, hot_rows, cold_rows, w_self, w_neigh, cotangent, hidden):
    targets, hidden_units = cotangent.shape
    feat_width = w_self.shape[0]
    n_src = x.shape[1] // 2
    cols = hidden_units // CHUNKS
    block = 512
    whole = lambda i, c: (0, 0)
    column = lambda i, c: (0, chunk)
    tile = lambda i, c: (i, chunk)
    in_specs = [
        pl.BlockSpec((block, 2 * n_src), lambda i, c: (i, 0)),
        pl.BlockSpec((2 * n_src, block), lambda i, c: (0, i)),
        pl.BlockSpec(hot_rows.shape, whole),
        pl.BlockSpec(cold_rows.shape, whole),
        pl.BlockSpec((feat_width, cols), column),
        pl.BlockSpec((feat_width, cols), column),
        pl.BlockSpec((block, cols), tile),
    ]
    operands = [core, x, xt, hot_rows, cold_rows, w_self, w_neigh, cotangent]
    aliases = {}
    if hidden is not None:
        in_specs.append(pl.BlockSpec(memory_space=pl.ANY))
        operands.append(hidden)
        aliases = {8: 0}
    return pl.pallas_call(
        layer_kernel,
        grid_spec=pltpu.PrefetchScalarGridSpec(
            num_scalar_prefetch=1,
            grid=(targets // block,),
            in_specs=in_specs,
            out_specs=[
                pl.BlockSpec((block, cols), tile),
                pl.BlockSpec((feat_width, cols), whole),
                pl.BlockSpec((feat_width, cols), whole),
            ],
            scratch_shapes=[
                pltpu.VMEM((n_src, feat_width), jnp.bfloat16),
                pltpu.VMEM((feat_width, n_src), jnp.bfloat16),
                pltpu.VMEM((2 * n_src, cols), jnp.bfloat16),
                pltpu.VMEM((2, n_src, cols), jnp.float32),
            ],
        ),
        out_shape=[
            jax.ShapeDtypeStruct((targets, hidden_units), jnp.bfloat16),
            jax.ShapeDtypeStruct((feat_width, cols), jnp.float32),
            jax.ShapeDtypeStruct((feat_width, cols), jnp.float32),
        ],
        input_output_aliases=aliases,
        compiler_params=pltpu.CompilerParams(vmem_limit_bytes=VMEM_LIMIT),
        cost_estimate=pl.CostEstimate(
            flops=4 * n_src * cols * (2 * targets + 2 * feat_width),
            bytes_accessed=8 * targets * n_src + 4 * targets * cols,
            transcendentals=targets * cols,
        ),
        name=f"layer_chunk_{chunk}",
    )(*operands)


class Line:
    def __init__(self, name, size, inner):
        self.name, self.size, self.inner = name, size, inner
        self.total = lax.axis_size(name)
        self.me = lax.rem(lax.div(lax.axis_index(name), jnp.int32(inner)), jnp.int32(size))

    def other(self, shift):
        return lax.rem(self.me + shift, jnp.int32(self.size))

    def send(self, value, shift):
        pairs = []
        for i in range(self.total):
            low, mine, high = i % self.inner, i // self.inner % self.size, i // (self.inner * self.size)
            to = (high * self.size + (mine + shift) % self.size) * self.inner + low
            pairs.append((i, to))
        return lax.ppermute(value, self.name, pairs)


def part(value, index, rows):
    return lax.dynamic_slice_in_dim(value, index * rows, rows, axis=0)


def scatter_sum(terms, line):
    rows = terms[0].shape[0] // line.size
    mine = [part(t, line.me, rows) for t in terms]
    for shift in range(1, line.size):
        out = functools.reduce(jnp.add, [part(t, line.other(shift), rows) for t in terms])
        mine.append(line.send(out, shift))
    return mine


def gather(value, line):
    rows = value.shape[0]
    whole = jnp.zeros((line.size * rows,) + value.shape[1:], value.dtype)
    whole = lax.dynamic_update_slice_in_dim(whole, value, line.me * rows, axis=0)
    for shift in range(1, line.size):
        got = line.send(value, shift)
        origin = lax.rem(line.me + line.size - shift, jnp.int32(line.size))
        whole = lax.dynamic_update_slice_in_dim(whole, got, origin * rows, axis=0)
    return whole


def body(
    hot_table, cold_table, hot_need, cold_need, self_index, neighbors, w_self, w_neigh, cotangent
):
    feat_width = hot_table.shape[1]
    both = ("grp", "dev")
    n_src = hot_need.size + cold_need.size
    x, xt = count_matrices(neighbors, self_index, n_src)

    swap = functools.partial(lax.all_to_all, split_axis=0, concat_axis=0, tiled=True)
    hot_rows = swap(look_up(hot_table, swap(hot_need, "dev")), "dev").reshape(-1, feat_width)
    cold_rows = swap(look_up(cold_table, swap(cold_need, both)), both).reshape(-1, feat_width)

    grp_size, dev_size = lax.axis_size("grp"), lax.axis_size("dev")
    x_size = grp_size // CORES
    y_size = x_size if dev_size % x_size == 0 else 1
    core = Line("grp", CORES, 1)
    along_x = Line("grp", x_size, CORES)
    along_y = Line("dev", y_size, 1)
    along_z = Line("dev", dev_size // y_size, y_size)

    hidden = None
    grads = []
    for chunk in range(CHUNKS):
        hidden, keep, send = layer_chunk(
            chunk, core.me[None], x, xt, hot_rows, cold_rows, w_self, w_neigh, cotangent, hidden
        )
        order = (along_x, along_y, along_z) if chunk % 2 == 0 else (along_y, along_x, along_z)
        terms = [keep, core.send(send, 1)]
        for line in order:
            terms = scatter_sum(terms, line)
        value = functools.reduce(jnp.add, terms)
        for line in reversed(order):
            value = gather(value, line)
        grads.append((value, core.send(value, 1)))
    own = jnp.concatenate([g[0] for g in grads], axis=1)
    other = jnp.concatenate([g[1] for g in grads], axis=1)
    first = core.me == 0
    return (hidden, jnp.where(first, own, other), jnp.where(first, other, own))


def solution(mesh):
    in_specs = (
        P("dev", None),
        P(("grp", "dev"), None),
        P(("grp", "dev"), None),
        P(("grp", "dev"), None),
        P(("grp", "dev")),
        P(("grp", "dev"), None),
        P(),
        P(),
        P(("grp", "dev"), None),
    )
    out_specs = (P(("grp", "dev"), None), P(), P())
    return jax.shard_map(body, mesh=mesh, in_specs=in_specs, out_specs=out_specs, check_vma=False)
```

time: 802 us -> 226 us (0.28)
  local copies, waits for them, and re-layouts: 346 us -> 38.8 us
  waiting for transfers between devices: 249 us -> 26.2 us
  other arithmetic: 154 us -> 30.1 us
  starting transfers between devices: 9.97 us -> 67 us
  Pallas kernels: 0 us -> 47.2 us
  matrix products: 24.4 us -> 0 us
  blocking collectives: 0 us -> 14.2 us
  between operations: 14.2 us -> 1.09 us
    gather x18 -> x0, local copies, waits for them, and re-layouts: 333 us -> none  [the longest x16 320 us: mean_block(): jnp.take(sources, indices, axis=0)]
    psum x1 -> x0, waiting for transfers between devices: 154 us -> none  [body(): summed = lax.psum((self_term, neigh_term), ('grp', 'dev'))]
    reduce_sum x8 -> x0, other arithmetic: 143 us -> none  [mean_block(): jnp.sum(jnp.take(sources, indices, axis=0), axis=1) / FAN]
    all_gather x1 -> x0, waiting for transfers between devices: 65.7 us -> none  [body(): whole_cache = lax.all_gather(hot_table, 'dev', axis=0, tiled=True)]
    ppermute x0 -> x48, starting transfers between devices: none -> 56.7 us  [send(): return lax.ppermute(value, self.name, pairs)]
    pallas_call x0 -> x5, Pallas kernels: none -> 47.2 us  [the longest x4 34.3 us: layer_chunk(): pl.pallas_call(layer_kernel, grid_spec=pltpu.PrefetchScalarGridSpec(num_s...]
    dot_general x4 -> x0, matrix products: 24.4 us -> none  [the longest x1 8.06 us: body(): jnp.dot(neigh_feat, w_neigh, preferred_element_type=jnp.float32)]
    add x0 -> x12, other arithmetic: none -> 16.6 us  [scatter_sum(): functools.reduce(jnp.add, [part(t, line.other(shift), rows) for t in terms])]
  transfers between devices with their start and end apart: 4 -> 51, of which waited for: 4 -> 8; matrix products, arithmetic and copies ran while one was open for 1% -> 20% of each run, Pallas kernels for 0% -> 13%
where the time goes in v1:
time: 226 us; the launch traced here: 225 us
  starting transfers between devices  67 us (30%)
  Pallas kernels  47.2 us (21%)
  local copies, waits for them, and re-layouts  38.8 us (17%)
  other arithmetic  30.1 us (13%)
  waiting for transfers between devices  26.2 us (12%)
  blocking collectives  14.2 us (6%)
    ppermute x48, starting transfers between devices, send(): return lax.ppermute(value, self.name, pairs)  56.7 us
    pallas_call x4, Pallas kernels, layer_chunk(): pl.pallas_call(layer_kernel, grid_spec=pltpu.PrefetchScalarGridSpec(num_s...  34.3 us
    add x12, other arithmetic, scatter_sum(): functools.reduce(jnp.add, [part(t, line.other(shift), rows) for t in terms])  16.6 us
    unnamed x34, local copies, waits for them, and re-layouts  16.5 us
    all_to_all x1, blocking collectives, body(): swap(cold_need, both)  14.2 us
    ppermute x48, waiting for transfers between devices, send(): return lax.ppermute(value, self.name, pairs)  13.1 us
    pallas_call x1, Pallas kernels, count_matrices(): pl.pallas_call(count_kernel, grid=(targets // block,), in_specs=[pl.Block...  13 us
    all_to_all x1, waiting for transfers between devices, body(): swap(look_up(cold_table, swap(cold_need, both)), both)  7.82 us
  transfers between devices with their start and end apart: 51, of which 8 were waited for; matrix products, arithmetic and copies ran while one was open for 20% of the time, Pallas kernels for 13%

profile of v1, /device:TPU:0, one launch (start us, length us, event | category | flops | bytes accessed | tf_op | source)
XLA Modules:
  0.0 224.6 jit_solution(10783609773862587035)
XLA Ops:
  1.6 14.2 %all_to_all.28 = s32[32,1,4]{2,1,0:T(1,128)S(1)} all-to-all(s32[32,1,4]{2,1,0:T(1,128)S(1)} %copy.44), channel_id=1, replica_groups=mesh['grp'=4,'dev'=8] {'grp','dev'}, dimensions={0} | all-to-all | bytes 1024 | tf_op jit(solution)/shard_map/all_to_all | solution.py:213
  15.8 3.3 %all-to-all-start = ((s32[8,1,32]{2,1,0:T(1,128)}), s32[8,1,32]{2,1,0:T(1,128)S(1)}, u32[]{:S(2)}, u32[]{:S(2)}) async-start(s32[8,1,32]{2,1,0:T(1,128)} %bitcast.23), calls=%async_computation | async-start | bytes 8192 | tf_op jit(solution)/shard_map/all_to_all | solution.py:212
  20.2 5.3 %all-to-all-done = s32[8,1,32]{2,1,0:T(1,128)S(1)} async-done(((s32[8,1,32]{2,1,0:T(1,128)}), s32[8,1,32]{2,1,0:T(1,128)S(1)}, u32[]{:S(2)}, u32[]{:S(2)}) %all-to-all-start) | async-done | bytes 1056 | tf_op jit(solution)/shard_map/all_to_all | solution.py:212
  26.1 1.6 gather_fusion.1
  28.8 1.6 select_multiply_fusion.1
  30.4 2.6 %all-to-all-start.3 = ((f32[32,4,768]{2,1,0:T(4,128)}), f32[32,4,768]{2,1,0:T(4,128)S(1)}, u32[]{:S(2)}, u32[]{:S(2)}) async-start(f32[32,4,768]{2,1,0:T(4,128)} %select_multiply_fusion.1), calls=%async_computation.3 | async-start | bytes 786432 | tf_op jit(solution)/shard_map/all_to_all | solution.py:213
  33.0 3.5 %gather_fusion = f32[256,768]{1,0:T(8,128)} fusion(f32[256,768]{1,0:T(8,128)} %param.9, s32[1024]{0:T(1024)} %get-tuple-element.58), kind=kCustom, calls=%fused_computation | custom fusion | bytes 1573888 | tf_op jit(solution)/shard_map/jit(_take)/gather | solution.py:17
  36.5 2.2 select_multiply_fusion
  38.7 7.8 %all-to-all-done.3 = f32[32,4,768]{2,1,0:T(4,128)S(1)} async-done(((f32[32,4,768]{2,1,0:T(4,128)}), f32[32,4,768]{2,1,0:T(4,128)S(1)}, u32[]{:S(2)}, u32[]{:S(2)}) %all-to-all-start.3) | async-done | bytes 393248 | tf_op jit(solution)/shard_map/all_to_all | solution.py:213
  46.5 4.4 %all-to-all-start.1 = ((f32[8,32,768]{2,1,0:T(8,128)}), f32[8,32,768]{2,1,0:T(8,128)}, u32[]{:S(2)}, u32[]{:S(2)}) async-start(f32[8,32,768]{2,1,0:T(8,128)} %select_multiply_fusion), calls=%async_computation.1 | async-start | bytes 1572864 | tf_op jit(solution)/shard_map/all_to_all | solution.py:212
  50.9 2.3 %copy.40.slots_ref = s32[2048,25]{1,0:T(8,128)} copy(s32[2048,25]{0,1:T(8,128)} %param.14) | data formatting | bytes 409600 | tf_op args[5]
  57.0 13.0 %count_matrices.1 = (bf16[2048,768]{1,0:T(8,128)(2,1)S(1)}, bf16[768,2048]{1,0:T(8,128)(2,1)}) custom-call(s32[2048,25]{1,0:T(8,128)S(1)} %copy-done.4, s32[2048,1]{1,0:T(8,128)S(1)} %copy-done.5), custom_call_target="tpu_custom_call" | custom-call | flops 39321600 | bytes 6291456 | tf_op jit(solution)/shard_map/count_matrices/pallas_call | solution.py:43
  70.0 1.7 copy-done.1
  72.8 1.4 copy-done.2
  74.2 1.4 copy-done.3
  75.6 8.5 %layer_chunk_0.1 = (bf16[2048,1024]{1,0:T(8,128)(2,1)}, f32[768,256]{1,0:T(8,128)S(1)}, f32[768,256]{1,0:T(8,128)}) custom-call(s32[1]{0:T(128)} %bitcast.core_ref, bf16[2048,768]{1,0:T(8,128)(2,1)} %copy-done.1, bf16[768,2048]{1,0:T(8,128)(2,1)} %get-tuple-element.18.xt_ref, f32[256,768]{1,0:T(8,128)} %bitcast.7.hot_ref, f32[128,768]{1,0:T(8,128)S(1)} %reshape.83.cold_ref, ...), custom_call_target="tpu_custom_call" | custom-call | flops 2214592512 | bytes 8388608 | tf_op jit(solution)/shard_map/layer_chunk_0/pallas_call | solution.py:127
  85.0 8.6 %layer_chunk_1.1 = (bf16[2048,1024]{1,0:T(8,128)(2,1)}, f32[768,256]{1,0:T(8,128)S(1)}, f32[768,256]{1,0:T(8,128)}) custom-call(s32[1]{0:T(128)} %bitcast.core_ref, bf16[2048,768]{1,0:T(8,128)(2,1)} %copy-done.1, bf16[768,2048]{1,0:T(8,128)(2,1)} %get-tuple-element.18.xt_ref, f32[256,768]{1,0:T(8,128)} %bitcast.7.hot_ref, ...), custom_call_target="tpu_custom_call", output_to_operand_aliasing={{0}: (8, {})} | custom-call | flops 2214592512 | bytes 8388608 | tf_op jit(solution)/shard_map/layer_chunk_1/pallas_call | solution.py:127
  95.0 8.6 %layer_chunk_2.1 = (bf16[2048,1024]{1,0:T(8,128)(2,1)}, f32[768,256]{1,0:T(8,128)S(1)}, f32[768,256]{1,0:T(8,128)}) custom-call(s32[1]{0:T(128)} %bitcast.core_ref, bf16[2048,768]{1,0:T(8,128)(2,1)} %copy-done.1, bf16[768,2048]{1,0:T(8,128)(2,1)} %get-tuple-element.18.xt_ref, f32[256,768]{1,0:T(8,128)} %bitcast.7.hot_ref, ...), custom_call_target="tpu_custom_call", output_to_operand_aliasing={{0}: (8, {})} | custom-call | flops 2214592512 | bytes 8388608 | tf_op jit(solution)/shard_map/layer_chunk_2/pallas_call | solution.py:127
  104.5 8.5 %layer_chunk_3.1 = (bf16[2048,1024]{1,0:T(8,128)(2,1)}, f32[768,256]{1,0:T(8,128)S(1)}, f32[768,256]{1,0:T(8,128)}) custom-call(s32[1]{0:T(128)} %bitcast.core_ref, bf16[2048,768]{1,0:T(8,128)(2,1)} %copy-done.1, bf16[768,2048]{1,0:T(8,128)(2,1)} %get-tuple-element.18.xt_ref, f32[256,768]{1,0:T(8,128)} %bitcast.7.hot_ref, ...), custom_call_target="tpu_custom_call", output_to_operand_aliasing={{0}: (8, {})} | custom-call | flops 2214592512 | bytes 8388608 | tf_op jit(solution)/shard_map/layer_chunk_3/pallas_call | solution.py:127
  114.5 2.0 dynamic-slice_add_fusion.3
  117.0 2.0 dynamic-slice_add_fusion.2
  119.0 1.7 collective-permute-start.12
  120.7 2.0 dynamic-slice_add_fusion.1
  122.6 1.5 collective-permute-start.23
  124.1 1.8 dynamic-slice_add_fusion
  126.3 2.5 %collective-permute-done.1 = f32[384,256]{1,0:T(8,128)} collective-permute-done((f32[384,256]{1,0:T(8,128)}, f32[384,256]{1,0:T(8,128)}, u32[]{:S(2)}, u32[]{:S(2)}) %collective-permute-start.1) | collective-permute-done | bytes 393248 | tf_op jit(solution)/shard_map/ppermute | solution.py:176
  129.9 1.8 collective-permute-start.2
  134.0 3.2 %collective-permute-done.23 = f32[384,256]{1,0:T(8,128)} collective-permute-done((f32[384,256]{1,0:T(8,128)}, f32[384,256]{1,0:T(8,128)}, u32[]{:S(2)}, u32[]{:S(2)}) %collective-permute-start.23) | collective-permute-done | bytes 393248 | tf_op jit(solution)/shard_map/ppermute | solution.py:176
  138.3 1.8 collective-permute-start.24
  142.2 1.5 collective-permute-done.2
  144.9 3.6 %collective-permute-start.5 = (f32[48,256]{1,0:T(8,128)S(1)}, f32[48,256]{1,0:T(8,128)S(1)}, u32[]{:S(2)}, u32[]{:S(2)}) collective-permute-start(f32[48,256]{1,0:T(8,128)S(1)} %get-tuple-element.51), channel_id=1, source_target_pairs={{0,6},{1,7},{2,0},{3,1},{4,2},{5,3},{6,4},{7,5},{8,14},{9,15},{10,... | collective-permute-start | bytes 147464 | tf_op jit(solution)/shard_map/ppermute | solution.py:176
  150.8 2.8 %collective-permute-start.16 = (f32[48,256]{1,0:T(8,128)S(1)}, f32[48,256]{1,0:T(8,128)S(1)}, u32[]{:S(2)}, u32[]{:S(2)}) collective-permute-start(f32[48,256]{1,0:T(8,128)S(1)} %get-tuple-element.48), channel_id=1, source_target_pairs={{0,6},{1,7},{2,0},{3,1},{4,2},{5,3},{6,4},{7,5},{8,14},{9,15},{10,... | collective-permute-start | bytes 147464 | tf_op jit(solution)/shard_map/ppermute | solution.py:176
  158.8 1.9 collective-permute-start.25
  163.4 2.2 collective-permute-start.38
  168.1 2.0 collective-permute-start.6
  174.4 1.7 collective-permute-start.18
  177.0 1.9 collective-permute-start.19
  179.3 1.4 collective-permute-start.29
  180.8 2.9 %collective-permute-start.30 = (f32[48,256]{1,0:T(8,128)S(1)}, f32[48,256]{1,0:T(8,128)S(1)}, u32[]{:S(2)}, u32[]{:S(2)}) collective-permute-start(f32[48,256]{1,0:T(8,128)S(1)} %get-tuple-element.34), channel_id=1, source_target_pairs={{0,6},{1,7},{2,0},{3,1},{4,2},{5,3},{6,4},{7,5},{8,14},{9,15},{10,... | collective-permute-start | bytes 147464 | tf_op jit(solution)/shard_map/ppermute | solution.py:176
  183.9 1.5 collective-permute-start.40
  185.4 2.9 %collective-permute-start.41 = (f32[48,256]{1,0:T(8,128)S(1)}, f32[48,256]{1,0:T(8,128)S(1)}, u32[]{:S(2)}, u32[]{:S(2)}) collective-permute-start(f32[48,256]{1,0:T(8,128)S(1)} %get-tuple-element.32), channel_id=1, source_target_pairs={{0,6},{1,7},{2,0},{3,1},{4,2},{5,3},{6,4},{7,5},{8,14},{9,15},{10,... | collective-permute-start | bytes 147464 | tf_op jit(solution)/shard_map/ppermute | solution.py:176
  188.4 1.5 collective-permute-start.9
  190.0 1.8 collective-permute-start.20
  192.9 3.4 %collective-permute-done.9 = f32[192,256]{1,0:T(8,128)S(1)} collective-permute-done((f32[192,256]{1,0:T(8,128)S(1)}, f32[192,256]{1,0:T(8,128)S(1)}, u32[]{:S(2)}, u32[]{:S(2)}) %collective-permute-start.9) | collective-permute-done | bytes 196640 | tf_op jit(solution)/shard_map/ppermute | solution.py:176
  202.3 1.4 collective-permute-start.32
  203.7 1.5 collective-permute-start.43
  209.0 1.4 collective-permute-done.32
  219.2 5.4 %fusion = (f32[768,1024]{1,0:T(8,128)}, f32[768,1024]{1,0:T(8,128)}) fusion(f32[768,1024]{1,0:T(8,128)S(1)} %constant_dynamic-update-slice_fusion.32, f32[768,256]{1,0:T(8,128)} %constant_dynamic-update-slice_fusion.7, f32[768,256]{1,0:T(8,128)} %constant_dynamic-update-slice_fusion.10, f32[768,256]{1,0:T(8,128)} %constant_dynamic-update-slice_fusion.30, ...), kind=kLoop, calls=%fused_computation.3 | loop fusion | flops 3932160 | bytes 12582913 | tf_op jit(solution)/shard_map/jit(_where)/select_n | solution.py:240
  (171 shorter events, 60.2 us)
Async XLA Ops:
  15.8 9.6 %all-to-all-start = ((s32[8,1,32]{2,1,0:T(1,128)}), s32[8,1,32]{2,1,0:T(1,128)S(1)}, u32[]{:S(2)}, u32[]{:S(2)}) async-start(s32[8,1,32]{2,1,0:T(1,128)} %bitcast.23), calls=%async_computation | async-start | bytes 8192 | tf_op jit(solution)/shard_map/all_to_all | solution.py:212
  30.4 16.1 %all-to-all-start.3 = ((f32[32,4,768]{2,1,0:T(4,128)}), f32[32,4,768]{2,1,0:T(4,128)S(1)}, u32[]{:S(2)}, u32[]{:S(2)}) async-start(f32[32,4,768]{2,1,0:T(4,128)} %select_multiply_fusion.1), calls=%async_computation.3 | async-start | bytes 786432 | tf_op jit(solution)/shard_map/all_to_all | solution.py:213
  46.5 26.3 %all-to-all-start.1 = ((f32[8,32,768]{2,1,0:T(8,128)}), f32[8,32,768]{2,1,0:T(8,128)}, u32[]{:S(2)}, u32[]{:S(2)}) async-start(f32[8,32,768]{2,1,0:T(8,128)} %select_multiply_fusion), calls=%async_computation.1 | async-start | bytes 1572864 | tf_op jit(solution)/shard_map/all_to_all | solution.py:212
  94.5 19.9 %collective-permute-start = (f32[768,256]{1,0:T(8,128)}, f32[768,256]{1,0:T(8,128)}, u32[]{:S(2)}, u32[]{:S(2)}) collective-permute-start(f32[768,256]{1,0:T(8,128)} %get-tuple-element.24), channel_id=1, source_target_pairs={{0,8},{8,0},{16,24},{24,16},{1,9},{9,1},{17,25},{25,17},{2,10},{10... | collective-permute-start | bytes 2359304 | tf_op jit(solution)/shard_map/ppermute | solution.py:176
  94.5 22.5 %collective-permute-start.11 = (f32[768,256]{1,0:T(8,128)}, f32[768,256]{1,0:T(8,128)}, u32[]{:S(2)}, u32[]{:S(2)}) collective-permute-start(f32[768,256]{1,0:T(8,128)} %get-tuple-element.26), channel_id=1, source_target_pairs={{0,8},{8,0},{16,24},{24,16},{1,9},{9,1},{17,25},{25,17},{2,10},{10... | collective-permute-start | bytes 2359304 | tf_op jit(solution)/shard_map/ppermute | solution.py:176
  104.5 16.1 %collective-permute-start.22 = (f32[768,256]{1,0:T(8,128)}, f32[768,256]{1,0:T(8,128)}, u32[]{:S(2)}, u32[]{:S(2)}) collective-permute-start(f32[768,256]{1,0:T(8,128)} %get-tuple-element.28), channel_id=1, source_target_pairs={{0,8},{8,0},{16,24},{24,16},{1,9},{9,1},{17,25},{25,17},{2,10},{10... | collective-permute-start | bytes 2359304 | tf_op jit(solution)/shard_map/ppermute | solution.py:176
  114.0 10.1 %collective-permute-start.33 = (f32[768,256]{1,0:T(8,128)}, f32[768,256]{1,0:T(8,128)}, u32[]{:S(2)}, u32[]{:S(2)}) collective-permute-start(f32[768,256]{1,0:T(8,128)} %get-tuple-element.30), channel_id=1, source_target_pairs={{0,8},{8,0},{16,24},{24,16},{1,9},{9,1},{17,25},{25,17},{2,10},{10... | collective-permute-start | bytes 2359304 | tf_op jit(solution)/shard_map/ppermute | solution.py:176
  116.5 12.3 %collective-permute-start.1 = (f32[384,256]{1,0:T(8,128)}, f32[384,256]{1,0:T(8,128)}, u32[]{:S(2)}, u32[]{:S(2)}) collective-permute-start(f32[384,256]{1,0:T(8,128)} %dynamic-slice_add_fusion.3), channel_id=1, source_target_pairs={{0,16},{8,24},{16,0},{24,8},{1,17},{9,25},{17,1},{25,9},{2,18},{10... | collective-permute-start | bytes 1179656 | tf_op jit(solution)/shard_map/ppermute | solution.py:176
  119.0 12.7 %collective-permute-start.12 = (f32[384,256]{1,0:T(8,128)}, f32[384,256]{1,0:T(8,128)}, u32[]{:S(2)}, u32[]{:S(2)}) collective-permute-start(f32[384,256]{1,0:T(8,128)} %dynamic-slice_add_fusion.2), channel_id=1, source_target_pairs={{0,1},{1,0},{2,3},{3,2},{4,5},{5,4},{6,7},{7,6},{8,9},{9,8},{10,11... | collective-permute-start | bytes 1179656 | tf_op jit(solution)/shard_map/ppermute | solution.py:176
  122.6 14.5 %collective-permute-start.23 = (f32[384,256]{1,0:T(8,128)}, f32[384,256]{1,0:T(8,128)}, u32[]{:S(2)}, u32[]{:S(2)}) collective-permute-start(f32[384,256]{1,0:T(8,128)} %dynamic-slice_add_fusion.1), channel_id=1, source_target_pairs={{0,16},{8,24},{16,0},{24,8},{1,17},{9,25},{17,1},{25,9},{2,18},{10... | collective-permute-start | bytes 1179656 | tf_op jit(solution)/shard_map/ppermute | solution.py:176
  126.0 14.1 %collective-permute-start.34 = (f32[384,256]{1,0:T(8,128)}, f32[384,256]{1,0:T(8,128)S(1)}, u32[]{:S(2)}, u32[]{:S(2)}) collective-permute-start(f32[384,256]{1,0:T(8,128)} %dynamic-slice_add_fusion), channel_id=1, source_target_pairs={{0,1},{1,0},{2,3},{3,2},{4,5},{5,4},{6,7},{7,6},{8,9},{9,8},{10,11... | collective-permute-start | bytes 1179656 | tf_op jit(solution)/shard_map/ppermute | solution.py:176
  129.9 13.9 %collective-permute-start.2 = (f32[192,256]{1,0:T(8,128)S(1)}, f32[192,256]{1,0:T(8,128)S(1)}, u32[]{:S(2)}, u32[]{:S(2)}) collective-permute-start(f32[192,256]{1,0:T(8,128)S(1)} %dynamic-slice_add_fusion.7), channel_id=1, source_target_pairs={{0,1},{1,0},{2,3},{3,2},{4,5},{5,4},{6,7},{7,6},{8,9},{9,8},{10,11... | collective-permute-start | bytes 589832 | tf_op jit(solution)/shard_map/ppermute | solution.py:176
  132.9 15.7 %collective-permute-start.13 = (f32[192,256]{1,0:T(8,128)S(1)}, f32[192,256]{1,0:T(8,128)S(1)}, u32[]{:S(2)}, u32[]{:S(2)}) collective-permute-start(f32[192,256]{1,0:T(8,128)S(1)} %dynamic-slice_add_fusion.6), channel_id=1, source_target_pairs={{0,16},{8,24},{16,0},{24,8},{1,17},{9,25},{17,1},{25,9},{2,18},{10... | collective-permute-start | bytes 589832 | tf_op jit(solution)/shard_map/ppermute | solution.py:176
  138.3 12.4 %collective-permute-start.24 = (f32[192,256]{1,0:T(8,128)S(1)}, f32[192,256]{1,0:T(8,128)S(1)}, u32[]{:S(2)}, u32[]{:S(2)}) collective-permute-start(f32[192,256]{1,0:T(8,128)S(1)} %dynamic-slice_add_fusion.5), channel_id=1, source_target_pairs={{0,1},{1,0},{2,3},{3,2},{4,5},{5,4},{6,7},{7,6},{8,9},{9,8},{10,11... | collective-permute-start | bytes 589832 | tf_op jit(solution)/shard_map/ppermute | solution.py:176
  141.2 13.4 %collective-permute-start.35 = (f32[192,256]{1,0:T(8,128)S(1)}, f32[192,256]{1,0:T(8,128)S(1)}, u32[]{:S(2)}, u32[]{:S(2)}) collective-permute-start(f32[192,256]{1,0:T(8,128)S(1)} %dynamic-slice_add_fusion.4), channel_id=1, source_target_pairs={{0,16},{8,24},{16,0},{24,8},{1,17},{9,25},{17,1},{25,9},{2,18},{10... | collective-permute-start | bytes 589832 | tf_op jit(solution)/shard_map/ppermute | solution.py:176
  144.9 11.9 %collective-permute-start.5 = (f32[48,256]{1,0:T(8,128)S(1)}, f32[48,256]{1,0:T(8,128)S(1)}, u32[]{:S(2)}, u32[]{:S(2)}) collective-permute-start(f32[48,256]{1,0:T(8,128)S(1)} %get-tuple-element.51), channel_id=1, source_target_pairs={{0,6},{1,7},{2,0},{3,1},{4,2},{5,3},{6,4},{7,5},{8,14},{9,15},{10,... | collective-permute-start | bytes 147464 | tf_op jit(solution)/shard_map/ppermute | solution.py:176
  148.5 9.3 %collective-permute-start.4 = (f32[48,256]{1,0:T(8,128)S(1)}, f32[48,256]{1,0:T(8,128)S(1)}, u32[]{:S(2)}, u32[]{:S(2)}) collective-permute-start(f32[48,256]{1,0:T(8,128)S(1)} %get-tuple-element.52), channel_id=1, source_target_pairs={{0,4},{1,5},{2,6},{3,7},{4,0},{5,1},{6,2},{7,3},{8,12},{9,13},{10,... | collective-permute-start | bytes 147464 | tf_op jit(solution)/shard_map/ppermute | solution.py:176
  148.5 10.3 %collective-permute-start.3 = (f32[48,256]{1,0:T(8,128)S(1)}, f32[48,256]{1,0:T(8,128)S(1)}, u32[]{:S(2)}, u32[]{:S(2)}) collective-permute-start(f32[48,256]{1,0:T(8,128)S(1)} %get-tuple-element.50), channel_id=1, source_target_pairs={{0,2},{1,3},{2,4},{3,5},{4,6},{5,7},{6,0},{7,1},{8,10},{9,11},{10,... | collective-permute-start | bytes 147464 | tf_op jit(solution)/shard_map/ppermute | solution.py:176
  150.8 16.1 %collective-permute-start.16 = (f32[48,256]{1,0:T(8,128)S(1)}, f32[48,256]{1,0:T(8,128)S(1)}, u32[]{:S(2)}, u32[]{:S(2)}) collective-permute-start(f32[48,256]{1,0:T(8,128)S(1)} %get-tuple-element.48), channel_id=1, source_target_pairs={{0,6},{1,7},{2,0},{3,1},{4,2},{5,3},{6,4},{7,5},{8,14},{9,15},{10,... | collective-permute-start | bytes 147464 | tf_op jit(solution)/shard_map/ppermute | solution.py:176
  154.6 13.4 %collective-permute-start.15 = (f32[48,256]{1,0:T(8,128)S(1)}, f32[48,256]{1,0:T(8,128)S(1)}, u32[]{:S(2)}, u32[]{:S(2)}) collective-permute-start(f32[48,256]{1,0:T(8,128)S(1)} %get-tuple-element.49), channel_id=1, source_target_pairs={{0,4},{1,5},{2,6},{3,7},{4,0},{5,1},{6,2},{7,3},{8,12},{9,13},{10,... | collective-permute-start | bytes 147464 | tf_op jit(solution)/shard_map/ppermute | solution.py:176
  157.8 5.5 %collective-permute-start.26 = (f32[48,256]{1,0:T(8,128)S(1)}, f32[48,256]{1,0:T(8,128)S(1)}, u32[]{:S(2)}, u32[]{:S(2)}) collective-permute-start(f32[48,256]{1,0:T(8,128)S(1)} %get-tuple-element.46), channel_id=1, source_target_pairs={{0,4},{1,5},{2,6},{3,7},{4,0},{5,1},{6,2},{7,3},{8,12},{9,13},{10,... | collective-permute-start | bytes 147464 | tf_op jit(solution)/shard_map/ppermute | solution.py:176
  158.8 6.8 %collective-permute-start.25 = (f32[48,256]{1,0:T(8,128)S(1)}, f32[48,256]{1,0:T(8,128)S(1)}, u32[]{:S(2)}, u32[]{:S(2)}) collective-permute-start(f32[48,256]{1,0:T(8,128)S(1)} %get-tuple-element.44), channel_id=1, source_target_pairs={{0,2},{1,3},{2,4},{3,5},{4,6},{5,7},{6,0},{7,1},{8,10},{9,11},{10,... | collective-permute-start | bytes 147464 | tf_op jit(solution)/shard_map/ppermute | solution.py:176
  161.7 8.4 %collective-permute-start.14 = (f32[48,256]{1,0:T(8,128)S(1)}, f32[48,256]{1,0:T(8,128)S(1)}, u32[]{:S(2)}, u32[]{:S(2)}) collective-permute-start(f32[48,256]{1,0:T(8,128)S(1)} %get-tuple-element.47), channel_id=1, source_target_pairs={{0,2},{1,3},{2,4},{3,5},{4,6},{5,7},{6,0},{7,1},{8,10},{9,11},{10,... | collective-permute-start | bytes 147464 | tf_op jit(solution)/shard_map/ppermute | solution.py:176
  163.4 8.9 %collective-permute-start.38 = (f32[48,256]{1,0:T(8,128)S(1)}, f32[48,256]{1,0:T(8,128)S(1)}, u32[]{:S(2)}, u32[]{:S(2)}) collective-permute-start(f32[48,256]{1,0:T(8,128)S(1)} %get-tuple-element.42), channel_id=1, source_target_pairs={{0,6},{1,7},{2,0},{3,1},{4,2},{5,3},{6,4},{7,5},{8,14},{9,15},{10,... | collective-permute-start | bytes 147464 | tf_op jit(solution)/shard_map/ppermute | solution.py:176
  165.6 7.9 %collective-permute-start.37 = (f32[48,256]{1,0:T(8,128)S(1)}, f32[48,256]{1,0:T(8,128)S(1)}, u32[]{:S(2)}, u32[]{:S(2)}) collective-permute-start(f32[48,256]{1,0:T(8,128)S(1)} %get-tuple-element.43), channel_id=1, source_target_pairs={{0,4},{1,5},{2,6},{3,7},{4,0},{5,1},{6,2},{7,3},{8,12},{9,13},{10,... | collective-permute-start | bytes 147464 | tf_op jit(solution)/shard_map/ppermute | solution.py:176
  166.9 7.5 %collective-permute-start.36 = (f32[48,256]{1,0:T(8,128)S(1)}, f32[48,256]{1,0:T(8,128)S(1)}, u32[]{:S(2)}, u32[]{:S(2)}) collective-permute-start(f32[48,256]{1,0:T(8,128)S(1)} %get-tuple-element.41), channel_id=1, source_target_pairs={{0,2},{1,3},{2,4},{3,5},{4,6},{5,7},{6,0},{7,1},{8,10},{9,11},{10,... | collective-permute-start | bytes 147464 | tf_op jit(solution)/shard_map/ppermute | solution.py:176
  168.1 8.9 %collective-permute-start.6 = (f32[48,256]{1,0:T(8,128)S(1)}, f32[48,256]{1,0:T(8,128)S(1)}, u32[]{:S(2)}, u32[]{:S(2)}) collective-permute-start(f32[48,256]{1,0:T(8,128)S(1)} %get-tuple-element.38), channel_id=1, source_target_pairs={{0,2},{1,3},{2,4},{3,5},{4,6},{5,7},{6,0},{7,1},{8,10},{9,11},{10,... | collective-permute-start | bytes 147464 | tf_op jit(solution)/shard_map/ppermute | solution.py:176
  170.1 8.8 %collective-permute-start.7 = (f32[48,256]{1,0:T(8,128)S(1)}, f32[48,256]{1,0:T(8,128)S(1)}, u32[]{:S(2)}, u32[]{:S(2)}) collective-permute-start(f32[48,256]{1,0:T(8,128)S(1)} %get-tuple-element.38), channel_id=1, source_target_pairs={{0,4},{1,5},{2,6},{3,7},{4,0},{5,1},{6,2},{7,3},{8,12},{9,13},{10,... | collective-permute-start | bytes 147464 | tf_op jit(solution)/shard_map/ppermute | solution.py:176
  172.3 7.1 %collective-permute-start.8 = (f32[48,256]{1,0:T(8,128)S(1)}, f32[48,256]{1,0:T(8,128)S(1)}, u32[]{:S(2)}, u32[]{:S(2)}) collective-permute-start(f32[48,256]{1,0:T(8,128)S(1)} %get-tuple-element.38), channel_id=1, source_target_pairs={{0,6},{1,7},{2,0},{3,1},{4,2},{5,3},{6,4},{7,5},{8,14},{9,15},{10,... | collective-permute-start | bytes 147464 | tf_op jit(solution)/shard_map/ppermute | solution.py:176
  173.5 7.3 %collective-permute-start.17 = (f32[48,256]{1,0:T(8,128)S(1)}, f32[48,256]{1,0:T(8,128)S(1)}, u32[]{:S(2)}, u32[]{:S(2)}) collective-permute-start(f32[48,256]{1,0:T(8,128)S(1)} %get-tuple-element.36), channel_id=1, source_target_pairs={{0,2},{1,3},{2,4},{3,5},{4,6},{5,7},{6,0},{7,1},{8,10},{9,11},{10,... | collective-permute-start | bytes 147464 | tf_op jit(solution)/shard_map/ppermute | solution.py:176
  174.4 9.4 %collective-permute-start.18 = (f32[48,256]{1,0:T(8,128)S(1)}, f32[48,256]{1,0:T(8,128)S(1)}, u32[]{:S(2)}, u32[]{:S(2)}) collective-permute-start(f32[48,256]{1,0:T(8,128)S(1)} %get-tuple-element.36), channel_id=1, source_target_pairs={{0,4},{1,5},{2,6},{3,7},{4,0},{5,1},{6,2},{7,3},{8,12},{9,13},{10,... | collective-permute-start | bytes 147464 | tf_op jit(solution)/shard_map/ppermute | solution.py:176
  177.0 6.9 %collective-permute-start.19 = (f32[48,256]{1,0:T(8,128)S(1)}, f32[48,256]{1,0:T(8,128)S(1)}, u32[]{:S(2)}, u32[]{:S(2)}) collective-permute-start(f32[48,256]{1,0:T(8,128)S(1)} %get-tuple-element.36), channel_id=1, source_target_pairs={{0,6},{1,7},{2,0},{3,1},{4,2},{5,3},{6,4},{7,5},{8,14},{9,15},{10,... | collective-permute-start | bytes 147464 | tf_op jit(solution)/shard_map/ppermute | solution.py:176
  178.9 6.6 %collective-permute-start.28 = (f32[48,256]{1,0:T(8,128)S(1)}, f32[48,256]{1,0:T(8,128)S(1)}, u32[]{:S(2)}, u32[]{:S(2)}) collective-permute-start(f32[48,256]{1,0:T(8,128)S(1)} %get-tuple-element.34), channel_id=1, source_target_pairs={{0,2},{1,3},{2,4},{3,5},{4,6},{5,7},{6,0},{7,1},{8,10},{9,11},{10,... | collective-permute-start | bytes 147464 | tf_op jit(solution)/shard_map/ppermute | solution.py:176
  179.3 9.0 %collective-permute-start.29 = (f32[48,256]{1,0:T(8,128)S(1)}, f32[48,256]{1,0:T(8,128)S(1)}, u32[]{:S(2)}, u32[]{:S(2)}) collective-permute-start(f32[48,256]{1,0:T(8,128)S(1)} %get-tuple-element.34), channel_id=1, source_target_pairs={{0,4},{1,5},{2,6},{3,7},{4,0},{5,1},{6,2},{7,3},{8,12},{9,13},{10,... | collective-permute-start | bytes 147464 | tf_op jit(solution)/shard_map/ppermute | solution.py:176
  180.8 9.1 %collective-permute-start.30 = (f32[48,256]{1,0:T(8,128)S(1)}, f32[48,256]{1,0:T(8,128)S(1)}, u32[]{:S(2)}, u32[]{:S(2)}) collective-permute-start(f32[48,256]{1,0:T(8,128)S(1)} %get-tuple-element.34), channel_id=1, source_target_pairs={{0,6},{1,7},{2,0},{3,1},{4,2},{5,3},{6,4},{7,5},{8,14},{9,15},{10,... | collective-permute-start | bytes 147464 | tf_op jit(solution)/shard_map/ppermute | solution.py:176
  183.8 8.0 %collective-permute-start.39 = (f32[48,256]{1,0:T(8,128)S(1)}, f32[48,256]{1,0:T(8,128)S(1)}, u32[]{:S(2)}, u32[]{:S(2)}) collective-permute-start(f32[48,256]{1,0:T(8,128)S(1)} %get-tuple-element.32), channel_id=1, source_target_pairs={{0,2},{1,3},{2,4},{3,5},{4,6},{5,7},{6,0},{7,1},{8,10},{9,11},{10,... | collective-permute-start | bytes 147464 | tf_op jit(solution)/shard_map/ppermute | solution.py:176
  183.9 8.5 %collective-permute-start.40 = (f32[48,256]{1,0:T(8,128)S(1)}, f32[48,256]{1,0:T(8,128)S(1)}, u32[]{:S(2)}, u32[]{:S(2)}) collective-permute-start(f32[48,256]{1,0:T(8,128)S(1)} %get-tuple-element.32), channel_id=1, source_target_pairs={{0,4},{1,5},{2,6},{3,7},{4,0},{5,1},{6,2},{7,3},{8,12},{9,13},{10,... | collective-permute-start | bytes 147464 | tf_op jit(solution)/shard_map/ppermute | solution.py:176
  185.4 6.9 %collective-permute-start.41 = (f32[48,256]{1,0:T(8,128)S(1)}, f32[48,256]{1,0:T(8,128)S(1)}, u32[]{:S(2)}, u32[]{:S(2)}) collective-permute-start(f32[48,256]{1,0:T(8,128)S(1)} %get-tuple-element.32), channel_id=1, source_target_pairs={{0,6},{1,7},{2,0},{3,1},{4,2},{5,3},{6,4},{7,5},{8,14},{9,15},{10,... | collective-permute-start | bytes 147464 | tf_op jit(solution)/shard_map/ppermute | solution.py:176
  188.4 7.9 %collective-permute-start.9 = (f32[192,256]{1,0:T(8,128)S(1)}, f32[192,256]{1,0:T(8,128)S(1)}, u32[]{:S(2)}, u32[]{:S(2)}) collective-permute-start(f32[192,256]{1,0:T(8,128)S(1)} %constant_dynamic-update-slice_fusion.18), channel_id=1, source_target_pairs={{0,1},{1,0},{2,3},{3,2},{4,5},{5,4},{6,7},{7,6},{8,9},{9,8},{10,11... | collective-permute-start | bytes 589832 | tf_op jit(solution)/shard_map/ppermute | solution.py:176
  190.0 7.7 %collective-permute-start.20 = (f32[192,256]{1,0:T(8,128)S(1)}, f32[192,256]{1,0:T(8,128)S(1)}, u32[]{:S(2)}, u32[]{:S(2)}) collective-permute-start(f32[192,256]{1,0:T(8,128)S(1)} %constant_dynamic-update-slice_fusion.2), channel_id=1, source_target_pairs={{0,16},{8,24},{16,0},{24,8},{1,17},{9,25},{17,1},{25,9},{2,18},{10... | collective-permute-start | bytes 589832 | tf_op jit(solution)/shard_map/ppermute | solution.py:176
  191.8 10.5 %collective-permute-start.31 = (f32[192,256]{1,0:T(8,128)S(1)}, f32[192,256]{1,0:T(8,128)S(1)}, u32[]{:S(2)}, u32[]{:S(2)}) collective-permute-start(f32[192,256]{1,0:T(8,128)S(1)} %constant_dynamic-update-slice_fusion.25), channel_id=1, source_target_pairs={{0,1},{1,0},{2,3},{3,2},{4,5},{5,4},{6,7},{7,6},{8,9},{9,8},{10,11... | collective-permute-start | bytes 589832 | tf_op jit(solution)/shard_map/ppermute | solution.py:176
  192.4 11.3 %collective-permute-start.42 = (f32[192,256]{1,0:T(8,128)S(1)}, f32[192,256]{1,0:T(8,128)S(1)}, u32[]{:S(2)}, u32[]{:S(2)}) collective-permute-start(f32[192,256]{1,0:T(8,128)S(1)} %constant_dynamic-update-slice_fusion.8), channel_id=1, source_target_pairs={{0,16},{8,24},{16,0},{24,8},{1,17},{9,25},{17,1},{25,9},{2,18},{10... | collective-permute-start | bytes 589832 | tf_op jit(solution)/shard_map/ppermute | solution.py:176
  196.3 10.6 %collective-permute-start.10 = (f32[384,256]{1,0:T(8,128)S(1)}, f32[384,256]{1,0:T(8,128)S(1)}, u32[]{:S(2)}, u32[]{:S(2)}) collective-permute-start(f32[384,256]{1,0:T(8,128)S(1)} %constant_dynamic-update-slice_fusion.16), channel_id=1, source_target_pairs={{0,16},{8,24},{16,0},{24,8},{1,17},{9,25},{17,1},{25,9},{2,18},{10... | collective-permute-start | bytes 1179656 | tf_op jit(solution)/shard_map/ppermute | solution.py:176
  197.7 10.1 %collective-permute-start.21 = (f32[384,256]{1,0:T(8,128)S(1)}, f32[384,256]{1,0:T(8,128)S(1)}, u32[]{:S(2)}, u32[]{:S(2)}) collective-permute-start(f32[384,256]{1,0:T(8,128)S(1)} %constant_dynamic-update-slice_fusion), channel_id=1, source_target_pairs={{0,1},{1,0},{2,3},{3,2},{4,5},{5,4},{6,7},{7,6},{8,9},{9,8},{10,11... | collective-permute-start | bytes 1179656 | tf_op jit(solution)/shard_map/ppermute | solution.py:176
  202.3 8.1 %collective-permute-start.32 = (f32[384,256]{1,0:T(8,128)S(1)}, f32[384,256]{1,0:T(8,128)S(1)}, u32[]{:S(2)}, u32[]{:S(2)}) collective-permute-start(f32[384,256]{1,0:T(8,128)S(1)} %constant_dynamic-update-slice_fusion.13), channel_id=1, source_target_pairs={{0,16},{8,24},{16,0},{24,8},{1,17},{9,25},{17,1},{25,9},{2,18},{10... | collective-permute-start | bytes 1179656 | tf_op jit(solution)/shard_map/ppermute | solution.py:176
  203.7 9.2 %collective-permute-start.43 = (f32[384,256]{1,0:T(8,128)S(1)}, f32[384,256]{1,0:T(8,128)S(1)}, u32[]{:S(2)}, u32[]{:S(2)}) collective-permute-start(f32[384,256]{1,0:T(8,128)S(1)} %constant_dynamic-update-slice_fusion.11), channel_id=1, source_target_pairs={{0,1},{1,0},{2,3},{3,2},{4,5},{5,4},{6,7},{7,6},{8,9},{9,8},{10,11... | collective-permute-start | bytes 1179656 | tf_op jit(solution)/shard_map/ppermute | solution.py:176
  207.8 6.5 %collective-permute-start.44 = (f32[768,256]{1,0:T(8,128)}, f32[768,256]{1,0:T(8,128)}, u32[]{:S(2)}, u32[]{:S(2)}) collective-permute-start(f32[768,256]{1,0:T(8,128)} %constant_dynamic-update-slice_fusion.14), channel_id=1, source_target_pairs={{0,8},{8,0},{16,24},{24,16},{1,9},{9,1},{17,25},{25,17},{2,10},{10... | collective-permute-start | bytes 2359304 | tf_op jit(solution)/shard_map/ppermute | solution.py:176
  208.5 6.9 %collective-permute-start.45 = (f32[768,256]{1,0:T(8,128)}, f32[768,256]{1,0:T(8,128)}, u32[]{:S(2)}, u32[]{:S(2)}) collective-permute-start(f32[768,256]{1,0:T(8,128)} %constant_dynamic-update-slice_fusion.30), channel_id=1, source_target_pairs={{0,8},{8,0},{16,24},{24,16},{1,9},{9,1},{17,25},{25,17},{2,10},{10... | collective-permute-start | bytes 2359304 | tf_op jit(solution)/shard_map/ppermute | solution.py:176
  (18 other events, 89.2 us)

commit v2 on v0

v2 whole, which is shorter than its diff:
```python
import functools

import jax
import jax.numpy as jnp
from jax import lax
from jax.experimental import pallas as pl
from jax.experimental.pallas import tpu as pltpu
from jax.sharding import PartitionSpec as P

FAN = 25
CORES = 2
CHUNKS = 4
CALLS = 2
VMEM_LIMIT = 48 * 1024 * 1024


def look_up(feature_table, requests):
    picked = jnp.take(feature_table, jnp.maximum(requests, 0), axis=0)
    return picked * (requests >= 0)[..., None].astype(jnp.float32)


def split(value):
    high = value.astype(jnp.bfloat16)
    return high, (value - high.astype(jnp.float32)).astype(jnp.bfloat16)


def dot(left, right):
    return jnp.dot(left, right, preferred_element_type=jnp.float32)


def dot_rows(left, right):
    return lax.dot_general(
        left, right, (((0,), (0,)), ((), ())), preferred_element_type=jnp.float32
    )


def count_kernel(slots_ref, self_ref, counts_ref):
    n_src, targets = counts_ref.shape[0] // 2, counts_ref.shape[1]
    step = 32
    slots = slots_ref[...].astype(jnp.int16)
    own = self_ref[...].astype(jnp.int16)

    @pl.loop(0, n_src // step)
    def _(i):
        base = pl.multiple_of(i * step, step)
        ids = (lax.broadcasted_iota(jnp.int32, (step, targets), 0) + base).astype(jnp.int16)
        one = jnp.ones((step, targets), jnp.bfloat16)
        zero = jnp.zeros((step, targets), jnp.bfloat16)
        total = zero
        for j in range(FAN):
            total += jnp.where(slots[j : j + 1, :] == ids, one, zero)
        counts_ref[pl.ds(n_src + base, step), :] = total
        counts_ref[pl.ds(base, step), :] = jnp.where(own == ids, one, zero)


def count_matrices(neighbors, self_index, n_src):
    targets = neighbors.shape[0]
    block = 512
    return pl.pallas_call(
        count_kernel,
        grid=(targets // block,),
        in_specs=[
            pl.BlockSpec((FAN, block), lambda i: (0, i)),
            pl.BlockSpec((1, block), lambda i: (0, i)),
        ],
        out_specs=pl.BlockSpec((2 * n_src, block), lambda i: (0, i)),
        out_shape=jax.ShapeDtypeStruct((2 * n_src, targets), jnp.bfloat16),
        compiler_params=pltpu.CompilerParams(vmem_limit_bytes=VMEM_LIMIT),
        cost_estimate=pl.CostEstimate(
            flops=2 * targets * n_src * FAN, bytes_accessed=4 * targets * n_src, transcendentals=0
        ),
        name="count_matrices",
    )(neighbors.T, self_index[None, :])


def layer_kernel(
    chunks, core_ref, counts_ref, hot_ref, cold_ref, w_self_ref, w_neigh_ref, cot_ref, *rest
):
    src, prod, back = rest[-3:]
    grad_refs = rest[-3 - 2 * chunks : -3]
    hidden_ref = rest[-4 - 2 * chunks]
    n_hot, n_src = hot_ref.shape[0], src.shape[1]
    step = pl.program_id(0)

    @pl.when(step == 0)
    def _():
        src[0, :n_hot, :], src[1, :n_hot, :] = split(hot_ref[...])
        src[0, n_hot:, :], src[1, n_hot:, :] = split(cold_ref[...])
        prod[:n_src, :] = dot(src[0], w_self_ref[...]).astype(jnp.bfloat16)
        both = dot(src[0], w_neigh_ref[...]) + dot(src[1], w_neigh_ref[...])
        prod[n_src:, :] = (both * (1.0 / FAN)).astype(jnp.bfloat16)
        back[...] = jnp.zeros_like(back)

    pre_act = dot_rows(counts_ref[...], prod[...])
    sigma = 0.5 * jnp.tanh(0.5 * pre_act) + 0.5
    hidden_ref[...] = (pre_act * sigma).astype(jnp.bfloat16)
    slope = sigma * (1.0 + pre_act * (1.0 - sigma))
    masked = (cot_ref[...].astype(jnp.float32) * slope).astype(jnp.bfloat16)
    back[...] += dot(counts_ref[...], masked)

    @pl.when(step == pl.num_programs(0) - 1)
    def _():
        cols = back.shape[1] // chunks

        def self_term(part):
            high, low = split(back[:n_src, pl.ds(part * cols, cols)])
            return dot_rows(src[0], high) + dot_rows(src[0], low)

        def neigh_term(part):
            high, low = split(back[n_src:, pl.ds(part * cols, cols)] * (1.0 / FAN))
            return dot_rows(src[0], high) + dot_rows(src[0], low) + dot_rows(src[1], high)

        @pl.when(core_ref[0] == 0)
        def _():
            for part in range(chunks):
                grad_refs[2 * part][...] = self_term(part)
                grad_refs[2 * part + 1][...] = neigh_term(part)

        @pl.when(core_ref[0] != 0)
        def _():
            for part in range(chunks):
                grad_refs[2 * part][...] = neigh_term(part)
                grad_refs[2 * part + 1][...] = self_term(part)


def layer(call, chunks, core, counts, hot_rows, cold_rows, w_self, w_neigh, cotangent, hidden):
    targets, hidden_units = cotangent.shape
    feat_width = w_self.shape[0]
    n_src = counts.shape[0] // 2
    wide = hidden_units // CALLS
    cols = wide // chunks
    block = 512
    whole = lambda i, c: (0, 0)
    column = lambda i, c: (0, call)
    tile = lambda i, c: (i, call)
    in_specs = [
        pl.BlockSpec((2 * n_src, block), lambda i, c: (0, i)),
        pl.BlockSpec(hot_rows.shape, whole),
        pl.BlockSpec(cold_rows.shape, whole),
        pl.BlockSpec((feat_width, wide), column),
        pl.BlockSpec((feat_width, wide), column),
        pl.BlockSpec((block, wide), tile),
    ]
    operands = [core, counts, hot_rows, cold_rows, w_self, w_neigh, cotangent]
    aliases = {}
    if hidden is not None:
        in_specs.append(pl.BlockSpec(memory_space=pl.ANY))
        operands.append(hidden)
        aliases = {7: 0}
    return pl.pallas_call(
        functools.partial(layer_kernel, chunks),
        grid_spec=pltpu.PrefetchScalarGridSpec(
            num_scalar_prefetch=1,
            grid=(targets // block,),
            in_specs=in_specs,
            out_specs=[pl.BlockSpec((block, wide), tile)]
            + [pl.BlockSpec((feat_width, cols), whole)] * (2 * chunks),
            scratch_shapes=[
                pltpu.VMEM((2, n_src, feat_width), jnp.bfloat16),
                pltpu.VMEM((2 * n_src, wide), jnp.bfloat16),
                pltpu.VMEM((2 * n_src, wide), jnp.float32),
            ],
        ),
        out_shape=[jax.ShapeDtypeStruct((targets, hidden_units), jnp.bfloat16)]
        + [jax.ShapeDtypeStruct((feat_width, cols), jnp.float32)] * (2 * chunks),
        input_output_aliases=aliases,
        compiler_params=pltpu.CompilerParams(vmem_limit_bytes=VMEM_LIMIT),
        cost_estimate=pl.CostEstimate(
            flops=4 * n_src * wide * (2 * targets + 2 * feat_width),
            bytes_accessed=4 * targets * n_src + 4 * targets * wide,
            transcendentals=targets * wide,
        ),
        name=f"layer_{call}",
    )(*operands)


def place_kernel(where_ref, mine, got, other_mine, other_got, *rest):
    out_self, out_neigh = rest[-2:]
    mine_here = pl.program_id(0) == where_ref[1]
    first_core = where_ref[0] == 0
    for here, own, other in ((mine_here, mine, other_mine), (~mine_here, got, other_got)):

        @pl.when(here & first_core)
        def _(own=own, other=other):
            out_self[...] = own[...]
            out_neigh[...] = other[...]

        @pl.when(here & ~first_core)
        def _(own=own, other=other):
            out_self[...] = other[...]
            out_neigh[...] = own[...]


def place(chunk, where, pieces, outs):
    rows, cols = pieces[0].shape
    shape = jax.ShapeDtypeStruct((2 * rows, CHUNKS * cols), jnp.float32)
    return pl.pallas_call(
        place_kernel,
        grid_spec=pltpu.PrefetchScalarGridSpec(
            num_scalar_prefetch=1,
            grid=(2,),
            in_specs=[pl.BlockSpec((rows, cols), lambda i, w: (0, 0))] * 4
            + [pl.BlockSpec(memory_space=pl.ANY)] * len(outs),
            out_specs=[pl.BlockSpec((rows, cols), lambda i, w: (i, chunk))] * 2,
        ),
        out_shape=[shape, shape],
        input_output_aliases={5: 0, 6: 1} if outs else {},
        compiler_params=pltpu.CompilerParams(vmem_limit_bytes=VMEM_LIMIT),
        cost_estimate=pl.CostEstimate(flops=0, bytes_accessed=32 * rows * cols, transcendentals=0),
        name=f"place_chunk_{chunk}",
    )(where, *pieces, *outs)


class Swap:
    def __init__(self, name, mask, bit):
        self.name, self.mask, self.bit = name, mask, bit
        self.pairs = [(i, i ^ mask) for i in range(lax.axis_size(name))]

    def send(self, value):
        return lax.ppermute(value, self.name, self.pairs)


def swaps(name, stride, size):
    index = lax.axis_index(name)
    found = []
    step = 1
    while step < size:
        low = lax.rem(lax.div(index, jnp.int32(stride * step)), jnp.int32(2))
        high = lax.rem(lax.div(index, jnp.int32(stride * step * 2)), jnp.int32(2)) if 2 * step < size else 0
        found.append(Swap(name, stride * (2 * step - 1), lax.rem(low + high, jnp.int32(2))))
        step *= 2
    return found


def halve(terms, swap):
    rows = terms[0].shape[0] // 2
    low = functools.reduce(jnp.add, [t[:rows] for t in terms])
    high = functools.reduce(jnp.add, [t[rows:] for t in terms])
    out = jnp.where(swap.bit == 0, high, low)
    return [jnp.where(swap.bit == 0, low, high), swap.send(out)]


def double(value, swap):
    got = swap.send(value)
    first = swap.bit == 0
    return jnp.concatenate([jnp.where(first, value, got), jnp.where(first, got, value)], axis=0)


def sum_over_devices(terms, core):
    groups, dev_size = lax.axis_size("grp"), lax.axis_size("dev")
    x_size = groups // CORES
    y_size = x_size if dev_size % x_size == 0 else 1
    along_x = swaps("grp", CORES, x_size)
    along_y = swaps("dev", 1, y_size)
    along_z = swaps("dev", y_size, dev_size // y_size)
    near_z, far_z = along_z[:1], along_z[1:]
    orders = [
        along_x + along_y + near_z + far_z,
        along_y + along_x + near_z + far_z,
        near_z + along_x + along_y + far_z,
        along_y + along_x + near_z + far_z,
    ]
    grads = []
    for chunk, (keep, send) in enumerate(terms):
        order = orders[chunk]
        parts = [keep, core.send(send)]
        for swap in order[:-1]:
            parts = halve(parts, swap)
        value = parts[0] + parts[1]
        value = value + order[-1].send(value)
        for swap in order[-2:0:-1]:
            value = double(value, swap)
        got = order[0].send(value)
        where = jnp.stack([core.bit, order[0].bit]).astype(jnp.int32)
        grads = place(chunk, where, [value, got, core.send(value), core.send(got)], grads)
    return grads


def body(
    hot_table, cold_table, hot_need, cold_need, self_index, neighbors, w_self, w_neigh, cotangent
):
    feat_width = hot_table.shape[1]
    both = ("grp", "dev")
    n_src = hot_need.size + cold_need.size
    counts = count_matrices(neighbors, self_index, n_src)

    exchange = functools.partial(
        lax.all_to_all, axis_name=both, split_axis=0, concat_axis=0, tiled=True
    )
    groups, dev_size = lax.axis_size("grp"), lax.axis_size("dev")
    cold_slots = cold_need.shape[1]
    asked = exchange(jnp.concatenate([cold_need, jnp.tile(hot_need, (groups, 1))], axis=1))
    cold_asked = asked[:, :cold_slots]
    hot_asked = lax.dynamic_slice_in_dim(
        asked[:, cold_slots:], lax.axis_index("grp") * dev_size, dev_size, axis=0
    )
    cold_rows = exchange(look_up(cold_table, cold_asked)).reshape(-1, feat_width)
    hot_rows = lax.all_to_all(
        look_up(hot_table, hot_asked), "dev", split_axis=0, concat_axis=0, tiled=True
    ).reshape(-1, feat_width)

    core = swaps("grp", 1, CORES)[0]
    hidden = None
    terms = []
    for call in range(CALLS):
        hidden, *grads = layer(
            call, CHUNKS // CALLS, core.bit[None], counts, hot_rows, cold_rows, w_self, w_neigh, cotangent, hidden
        )
        terms += list(zip(grads[::2], grads[1::2]))
    grad_self, grad_neigh = sum_over_devices(terms, core)
    return (hidden, grad_self, grad_neigh)


def solution(mesh):
    in_specs = (
        P("dev", None),
        P(("grp", "dev"), None),
        P(("grp", "dev"), None),
        P(("grp", "dev"), None),
        P(("grp", "dev")),
        P(("grp", "dev"), None),
        P(),
        P(),
        P(("grp", "dev"), None),
    )
    out_specs = (P(("grp", "dev"), None), P(), P())
    return jax.shard_map(body, mesh=mesh, in_specs=in_specs, out_specs=out_specs, check_vma=False)
```

time: 802 us -> 182 us (0.23)
  local copies, waits for them, and re-layouts: 346 us -> 16.7 us
  waiting for transfers between devices: 249 us -> 52.9 us
  other arithmetic: 154 us -> 9.93 us
  starting transfers between devices: 9.97 us -> 49.2 us
  Pallas kernels: 0 us -> 36.9 us
  matrix products: 24.4 us -> 0 us
  blocking collectives: 0 us -> 14.2 us
  between operations: 14.2 us -> 0.99 us
    gather x18 -> x0, local copies, waits for them, and re-layouts: 333 us -> none  [the longest x16 320 us: mean_block(): jnp.take(sources, indices, axis=0)]
    psum x1 -> x0, waiting for transfers between devices: 154 us -> none  [body(): summed = lax.psum((self_term, neigh_term), ('grp', 'dev'))]
    reduce_sum x8 -> x0, other arithmetic: 143 us -> none  [mean_block(): jnp.sum(jnp.take(sources, indices, axis=0), axis=1) / FAN]
    all_gather x1 -> x0, waiting for transfers between devices: 65.7 us -> none  [body(): whole_cache = lax.all_gather(hot_table, 'dev', axis=0, tiled=True)]
    ppermute x0 -> x40, starting transfers between devices: none -> 41.5 us  [send(): return lax.ppermute(value, self.name, self.pairs)]
    pallas_call x0 -> x7, Pallas kernels: none -> 36.9 us  [the longest x2 23.8 us: layer(): pl.pallas_call(functools.partial(layer_kernel, chunks), grid_spec=pltpu.P...]
    ppermute x0 -> x40, waiting for transfers between devices: none -> 33.9 us  [send(): return lax.ppermute(value, self.name, self.pairs)]
    dot_general x4 -> x0, matrix products: 24.4 us -> none  [the longest x1 8.06 us: body(): jnp.dot(neigh_feat, w_neigh, preferred_element_type=jnp.float32)]
  transfers between devices with their start and end apart: 4 -> 42, of which waited for: 4 -> 17; matrix products, arithmetic and copies ran while one was open for 1% -> 7% of each run, Pallas kernels for 0% -> 6%
where the time goes in v2:
time: 182 us; the launch traced here: 181 us
  waiting for transfers between devices  52.9 us (29%)
  starting transfers between devices  49.2 us (27%)
  Pallas kernels  36.9 us (20%)
  local copies, waits for them, and re-layouts  16.7 us (9%)
  blocking collectives  14.2 us (8%)
  other arithmetic  9.93 us (5%)
    ppermute x40, starting transfers between devices, send(): return lax.ppermute(value, self.name, self.pairs)  41.5 us
    ppermute x40, waiting for transfers between devices, send(): return lax.ppermute(value, self.name, self.pairs)  33.9 us
    pallas_call x2, Pallas kernels, layer(): pl.pallas_call(functools.partial(layer_kernel, chunks), grid_spec=pltpu.P...  23.8 us
    all_to_all x1, blocking collectives, body(): exchange(jnp.concatenate([cold_need, jnp.tile(hot_need, (groups, 1))], ax...  14.2 us
    all_to_all x1, waiting for transfers between devices, body(): lax.all_to_all(look_up(hot_table, hot_asked), 'dev', split_axis=0, concat...  11.3 us
    unnamed x25, local copies, waits for them, and re-layouts  8.47 us
    all_to_all x1, waiting for transfers between devices, body(): exchange(look_up(cold_table, cold_asked)).reshape(-1, feat_width)  7.76 us
    pallas_call x4, Pallas kernels, place(): pl.pallas_call(place_kernel, grid_spec=pltpu.PrefetchScalarGridSpec(num_s...  7.12 us
  transfers between devices with their start and end apart: 42, of which 17 were waited for; matrix products, arithmetic and copies ran while one was open for 7% of the time, Pallas kernels for 6%

profile of v2, /device:TPU:0, one launch (start us, length us, event | category | flops | bytes accessed | tf_op | source)
XLA Modules:
  0.0 180.9 jit_solution(10739464461538448078)
XLA Ops:
  2.4 14.2 %all_to_all.22 = s32[32,1,36]{2,1,0:T(1,128)S(1)} all-to-all(s32[32,1,36]{2,1,0:T(1,128)S(1)} %bitcast.18), channel_id=1, replica_groups=mesh['grp'=4,'dev'=8] {'grp','dev'}, dimensions={0} | all-to-all | bytes 9216 | tf_op jit(solution)/shard_map/all_to_all | solution.py:292
  17.4 1.6 gather_fusion.1
  20.1 1.6 select_multiply_fusion.1
  21.7 3.3 %all-to-all-start.2 = ((f32[32,4,768]{2,1,0:T(4,128)}), f32[32,4,768]{2,1,0:T(4,128)}, u32[]{:S(2)}, u32[]{:S(2)}) async-start(f32[32,4,768]{2,1,0:T(4,128)} %select_multiply_fusion.1), calls=%async_computation.2 | async-start | bytes 786432 | tf_op jit(solution)/shard_map/all_to_all | solution.py:297
  25.2 3.4 %gather_fusion = f32[256,768]{1,0:T(8,128)} fusion(f32[256,768]{1,0:T(8,128)} %param.9, s32[1024]{0:T(1024)S(1)} %pad_clamp_fusion.1), kind=kCustom, calls=%fused_computation | custom fusion | bytes 1573888 | tf_op jit(solution)/shard_map/jit(_take)/gather | solution.py:18
  28.6 2.2 %select_multiply_fusion = f32[8,32,768]{2,1,0:T(8,128)} fusion(f32[8,32,768]{2,1,0:T(8,128)} %bitcast.14, f32[8,32]{1,0:T(8,128)S(1)} %get-tuple-element.75, pred[8,32]{1,0:T(8,128)(4,1)S(1)} %get-tuple-element.39), kind=kLoop, calls=%fused_computation.2 | loop fusion | flops 393216 | bytes 1574144 | tf_op jit(solution)/shard_map/mul | solution.py:19
  30.8 7.8 %all-to-all-done.2 = f32[32,4,768]{2,1,0:T(4,128)} async-done(((f32[32,4,768]{2,1,0:T(4,128)}), f32[32,4,768]{2,1,0:T(4,128)}, u32[]{:S(2)}, u32[]{:S(2)}) %all-to-all-start.2) | async-done | bytes 393248 | tf_op jit(solution)/shard_map/all_to_all | solution.py:297
  38.5 4.4 %all-to-all-start.1 = ((f32[8,32,768]{2,1,0:T(8,128)}), f32[8,32,768]{2,1,0:T(8,128)}, u32[]{:S(2)}, u32[]{:S(2)}) async-start(f32[8,32,768]{2,1,0:T(8,128)} %select_multiply_fusion), calls=%async_computation.1 | async-start | bytes 1572864 | tf_op jit(solution)/shard_map/all_to_all | solution.py:298
  43.0 6.0 %count_matrices.1.counts_ref = bf16[768,2048]{1,0:T(8,128)(2,1)S(1)} custom-call(s32[25,2048]{1,0:T(8,128)S(1)} %bitcast.12, s32[1,2048]{1,0:T(1,128)S(1)} %bitcast.13), custom_call_target="tpu_custom_call" | custom-call | flops 39321600 | bytes 3145728 | tf_op jit(solution)/shard_map/count_matrices/pallas_call | solution.py:59
  48.9 1.7 copy-done.1
  51.7 11.3 %all-to-all-done.1 = f32[8,32,768]{2,1,0:T(8,128)} async-done(((f32[8,32,768]{2,1,0:T(8,128)}), f32[8,32,768]{2,1,0:T(8,128)}, u32[]{:S(2)}, u32[]{:S(2)}) %all-to-all-start.1) | async-done | bytes 786464 | tf_op jit(solution)/shard_map/all_to_all | solution.py:298
  63.0 1.4 copy-done.10
  64.4 11.8 %layer_0.1 = (bf16[2048,1024]{1,0:T(8,128)(2,1)}, f32[768,256]{1,0:T(8,128)S(1)}, f32[768,256]{1,0:T(8,128)S(1)}, f32[768,256]{1,0:T(8,128)S(1)}, f32[768,256]{1,0:T(8,128)}) custom-call(s32[1]{0:T(128)} %bitcast.core_ref, bf16[768,2048]{1,0:T(8,128)(2,1)} %copy-done.1, f32[256,768]{1,0:T(8,128)} %bitcast.7.hot_ref, f32[128,768]{1,0:T(8,128)S(1)} %reshape.33.cold_ref, ...), custom_call_target="tpu_custom_call" | custom-call | flops 4429185024 | bytes 7340032 | tf_op jit(solution)/shard_map/layer_0/pallas_call | solution.py:150
  78.9 12.1 %layer_1.1 = (bf16[2048,1024]{1,0:T(8,128)(2,1)}, f32[768,256]{1,0:T(8,128)S(1)}, f32[768,256]{1,0:T(8,128)}, f32[768,256]{1,0:T(8,128)S(1)}, f32[768,256]{1,0:T(8,128)}) custom-call(s32[1]{0:T(128)} %bitcast.core_ref, bf16[768,2048]{1,0:T(8,128)(2,1)} %copy-done.1, f32[256,768]{1,0:T(8,128)} %bitcast.7.hot_ref, ...), custom_call_target="tpu_custom_call", output_to_operand_aliasing={{0}: (7, {})} | custom-call | flops 4429185024 | bytes 7340032 | tf_op jit(solution)/shard_map/layer_1/pallas_call | solution.py:150
  93.8 1.6 collective-permute-done
  95.4 1.5 broadcast_select_fusion.7
  97.0 1.5 collective-permute-start.1
  98.4 1.5 broadcast_select_fusion.3
  100.0 1.2 broadcast_select_fusion.5
  103.3 5.7 %collective-permute-done.1 = f32[384,256]{1,0:T(8,128)S(1)} collective-permute-done((f32[384,256]{1,0:T(8,128)S(1)}, f32[384,256]{1,0:T(8,128)S(1)}, u32[]{:S(2)}, u32[]{:S(2)}) %collective-permute-start.1) | collective-permute-done | bytes 393248 | tf_op jit(solution)/shard_map/ppermute | solution.py:220
  109.0 1.2 collective-permute-start.2
  110.9 1.2 collective-permute-start.12
  112.1 4.5 %collective-permute-done.21 = f32[384,256]{1,0:T(8,128)S(1)} collective-permute-done((f32[384,256]{1,0:T(8,128)S(1)}, f32[384,256]{1,0:T(8,128)S(1)}, u32[]{:S(2)}, u32[]{:S(2)}) %collective-permute-start.21) | collective-permute-done | bytes 393248 | tf_op jit(solution)/shard_map/ppermute | solution.py:220
  116.7 1.2 collective-permute-start.22
  118.0 1.5 collective-permute-start.32
  120.5 2.4 %collective-permute-done.12 = f32[192,256]{1,0:T(8,128)S(1)} collective-permute-done((f32[192,256]{1,0:T(8,128)S(1)}, f32[192,256]{1,0:T(8,128)S(1)}, u32[]{:S(2)}, u32[]{:S(2)}) %collective-permute-start.12) | collective-permute-done | bytes 196640 | tf_op jit(solution)/shard_map/ppermute | solution.py:220
  122.9 1.2 collective-permute-start.13
  124.1 1.6 collective-permute-done.22
  125.7 1.8 collective-permute-start.23
  127.9 1.5 collective-permute-start.4
  129.4 2.5 %collective-permute-start.14 = (f32[96,256]{1,0:T(8,128)S(1)}, f32[96,256]{1,0:T(8,128)S(1)}, u32[]{:S(2)}, u32[]{:S(2)}) collective-permute-start(f32[96,256]{1,0:T(8,128)S(1)} %select_add_fusion.2), channel_id=1, source_target_pairs={{0,6},{1,7},{2,4},{3,5},{4,2},{5,3},{6,0},{7,1},{8,14},{9,15},{10,... | collective-permute-start | bytes 294920 | tf_op jit(solution)/shard_map/ppermute | solution.py:220
  131.9 1.5 collective-permute-start.24
  133.5 2.5 %collective-permute-start.34 = (f32[96,256]{1,0:T(8,128)S(1)}, f32[96,256]{1,0:T(8,128)S(1)}, u32[]{:S(2)}, u32[]{:S(2)}) collective-permute-start(f32[96,256]{1,0:T(8,128)S(1)} %select_add_fusion), channel_id=1, source_target_pairs={{0,6},{1,7},{2,4},{3,5},{4,2},{5,3},{6,0},{7,1},{8,14},{9,15},{10,... | collective-permute-start | bytes 294920 | tf_op jit(solution)/shard_map/ppermute | solution.py:220
  136.9 5.9 %collective-permute-start.5 = (f32[96,256]{1,0:T(8,128)S(1)}, f32[96,256]{1,0:T(8,128)S(1)}, u32[]{:S(2)}, u32[]{:S(2)}) collective-permute-start(f32[96,256]{1,0:T(8,128)S(1)} %add.119), channel_id=1, source_target_pairs={{0,2},{1,3},{2,0},{3,1},{4,6},{5,7},{6,4},{7,5},{8,10},{9,11},{10,... | collective-permute-start | bytes 294920 | tf_op jit(solution)/shard_map/ppermute | solution.py:220
  142.8 1.2 collective-permute-start.15
  144.0 2.2 %collective-permute-start.25 = (f32[96,256]{1,0:T(8,128)S(1)}, f32[96,256]{1,0:T(8,128)S(1)}, u32[]{:S(2)}, u32[]{:S(2)}) collective-permute-start(f32[96,256]{1,0:T(8,128)S(1)} %add.135), channel_id=1, source_target_pairs={{0,2},{1,3},{2,0},{3,1},{4,6},{5,7},{6,4},{7,5},{8,10},{9,11},{10,... | collective-permute-start | bytes 294920 | tf_op jit(solution)/shard_map/ppermute | solution.py:220
  147.4 1.2 collective-permute-start.6
  149.6 1.2 collective-permute-start.26
  151.9 3.4 %collective-permute-done.6 = f32[192,256]{1,0:T(8,128)S(1)} collective-permute-done((f32[192,256]{1,0:T(8,128)S(1)}, f32[192,256]{1,0:T(8,128)S(1)}, u32[]{:S(2)}, u32[]{:S(2)}) %collective-permute-start.6) | collective-permute-done | bytes 196640 | tf_op jit(solution)/shard_map/ppermute | solution.py:220
  156.2 2.7 %collective-permute-done.36 = f32[192,256]{1,0:T(8,128)S(1)} collective-permute-done((f32[192,256]{1,0:T(8,128)S(1)}, f32[192,256]{1,0:T(8,128)S(1)}, u32[]{:S(2)}, u32[]{:S(2)}) %collective-permute-start.36) | collective-permute-done | bytes 196640 | tf_op jit(solution)/shard_map/ppermute | solution.py:220
  159.0 1.2 collective-permute-start.37
  160.2 3.5 %collective-permute-done.26 = f32[192,256]{1,0:T(8,128)S(1)} collective-permute-done((f32[192,256]{1,0:T(8,128)S(1)}, f32[192,256]{1,0:T(8,128)S(1)}, u32[]{:S(2)}, u32[]{:S(2)}) %collective-permute-start.26) | collective-permute-done | bytes 196640 | tf_op jit(solution)/shard_map/ppermute | solution.py:220
  166.5 2.6 %collective-permute-done.37.got = f32[384,256]{1,0:T(8,128)S(1)} collective-permute-done((f32[384,256]{1,0:T(8,128)S(1)}, f32[384,256]{1,0:T(8,128)S(1)}, u32[]{:S(2)}, u32[]{:S(2)}) %collective-permute-start.37) | collective-permute-done | bytes 393248 | tf_op jit(solution)/shard_map/ppermute | solution.py:220
  169.1 2.8 %collective-permute-done.27.got = f32[384,256]{1,0:T(8,128)S(1)} collective-permute-done((f32[384,256]{1,0:T(8,128)S(1)}, f32[384,256]{1,0:T(8,128)S(1)}, u32[]{:S(2)}, u32[]{:S(2)}) %collective-permute-start.27) | collective-permute-done | bytes 393248 | tf_op jit(solution)/shard_map/ppermute | solution.py:220
  173.8 1.8 place_chunk_0.1
  175.6 1.8 place_chunk_1.1
  177.4 1.8 place_chunk_2.1
  179.2 1.8 place_chunk_3.1
  (124 shorter events, 24.7 us)
Async XLA Ops:
  0.6 16.8 %copy-start = (f32[1024,768]{1,0:T(8,128)S(1)}, f32[1024,768]{1,0:T(8,128)}, u32[]{:S(2)}) copy-start(f32[1024,768]{1,0:T(8,128)} %param.10) | copy-start | bytes 9437188
  21.7 16.8 %all-to-all-start.2 = ((f32[32,4,768]{2,1,0:T(4,128)}), f32[32,4,768]{2,1,0:T(4,128)}, u32[]{:S(2)}, u32[]{:S(2)}) async-start(f32[32,4,768]{2,1,0:T(4,128)} %select_multiply_fusion.1), calls=%async_computation.2 | async-start | bytes 786432 | tf_op jit(solution)/shard_map/all_to_all | solution.py:297
  28.6 14.4 %copy-start.8 = (s32[2048,25]{0,1:T(8,128)S(1)}, s32[2048,25]{0,1:T(8,128)}, u32[]{:S(2)}) copy-start(s32[2048,25]{0,1:T(8,128)} %param.14) | copy-start | bytes 614404
  28.6 14.4 %copy-start.9 = (s32[2048]{0:T(1024)S(1)}, s32[2048]{0:T(1024)}, u32[]{:S(2)}) copy-start(s32[2048]{0:T(1024)} %param.13) | copy-start | bytes 24580
  38.5 24.5 %all-to-all-start.1 = ((f32[8,32,768]{2,1,0:T(8,128)}), f32[8,32,768]{2,1,0:T(8,128)}, u32[]{:S(2)}, u32[]{:S(2)}) async-start(f32[8,32,768]{2,1,0:T(8,128)} %select_multiply_fusion), calls=%async_computation.1 | async-start | bytes 1572864 | tf_op jit(solution)/shard_map/all_to_all | solution.py:298
  48.9 1.7 copy-start.1
  92.8 2.6 %collective-permute-start = (f32[768,256]{1,0:T(8,128)}, f32[768,256]{1,0:T(8,128)}, u32[]{:S(2)}, u32[]{:S(2)}) collective-permute-start(f32[768,256]{1,0:T(8,128)} %get-tuple-element.24), channel_id=1, source_target_pairs={{0,8},{8,0},{16,24},{24,16},{1,9},{9,1},{17,25},{25,17},{2,10},{10... | collective-permute-start | bytes 2359304 | tf_op jit(solution)/shard_map/ppermute | solution.py:220
  92.8 5.7 %collective-permute-start.10 = (f32[768,256]{1,0:T(8,128)}, f32[768,256]{1,0:T(8,128)}, u32[]{:S(2)}, u32[]{:S(2)}) collective-permute-start(f32[768,256]{1,0:T(8,128)} %get-tuple-element.26), channel_id=1, source_target_pairs={{0,8},{8,0},{16,24},{24,16},{1,9},{9,1},{17,25},{25,17},{2,10},{10... | collective-permute-start | bytes 2359304 | tf_op jit(solution)/shard_map/ppermute | solution.py:220
  93.3 6.7 %collective-permute-start.20 = (f32[768,256]{1,0:T(8,128)}, f32[768,256]{1,0:T(8,128)}, u32[]{:S(2)}, u32[]{:S(2)}) collective-permute-start(f32[768,256]{1,0:T(8,128)} %get-tuple-element.28), channel_id=1, source_target_pairs={{0,8},{8,0},{16,24},{24,16},{1,9},{9,1},{17,25},{25,17},{2,10},{10... | collective-permute-start | bytes 2359304 | tf_op jit(solution)/shard_map/ppermute | solution.py:220
  93.3 6.7 %copy-start.5 = (f32[768,256]{1,0:T(8,128)S(1)}, f32[768,256]{1,0:T(8,128)}, u32[]{:S(2)}) copy-start(f32[768,256]{1,0:T(8,128)} %copy-done.4) | copy-start | bytes 2359300
  93.3 8.9 %collective-permute-start.30 = (f32[768,256]{1,0:T(8,128)}, f32[768,256]{1,0:T(8,128)S(1)}, u32[]{:S(2)}, u32[]{:S(2)}) collective-permute-start(f32[768,256]{1,0:T(8,128)} %copy-done.11), channel_id=1, source_target_pairs={{0,8},{8,0},{16,24},{24,16},{1,9},{9,1},{17,25},{25,17},{2,10},{10... | collective-permute-start | bytes 2359304 | tf_op jit(solution)/shard_map/ppermute | solution.py:220
  95.4 6.8 %copy-start.3 = (f32[768,256]{1,0:T(8,128)S(1)}, f32[768,256]{1,0:T(8,128)}, u32[]{:S(2)}) copy-start(f32[768,256]{1,0:T(8,128)} %copy-done.2) | copy-start | bytes 2359300
  97.0 12.0 %collective-permute-start.1 = (f32[384,256]{1,0:T(8,128)S(1)}, f32[384,256]{1,0:T(8,128)S(1)}, u32[]{:S(2)}, u32[]{:S(2)}) collective-permute-start(f32[384,256]{1,0:T(8,128)S(1)} %get-tuple-element.48), channel_id=1, source_target_pairs={{0,1},{1,0},{2,3},{3,2},{4,5},{5,4},{6,7},{7,6},{8,9},{9,8},{10,11... | collective-permute-start | bytes 1179656 | tf_op jit(solution)/shard_map/ppermute | solution.py:220
  99.9 10.9 %collective-permute-start.11 = (f32[384,256]{1,0:T(8,128)S(1)}, f32[384,256]{1,0:T(8,128)S(1)}, u32[]{:S(2)}, u32[]{:S(2)}) collective-permute-start(f32[384,256]{1,0:T(8,128)S(1)} %get-tuple-element.46), channel_id=1, source_target_pairs={{0,2},{1,3},{2,0},{3,1},{4,6},{5,7},{6,4},{7,5},{8,10},{9,11},{10,... | collective-permute-start | bytes 1179656 | tf_op jit(solution)/shard_map/ppermute | solution.py:220
  101.2 15.4 %collective-permute-start.21 = (f32[384,256]{1,0:T(8,128)S(1)}, f32[384,256]{1,0:T(8,128)S(1)}, u32[]{:S(2)}, u32[]{:S(2)}) collective-permute-start(f32[384,256]{1,0:T(8,128)S(1)} %get-tuple-element.44), channel_id=1, source_target_pairs={{0,1},{1,0},{2,3},{3,2},{4,5},{5,4},{6,7},{7,6},{8,9},{9,8},{10,11... | collective-permute-start | bytes 1179656 | tf_op jit(solution)/shard_map/ppermute | solution.py:220
  102.4 15.5 %collective-permute-start.31 = (f32[384,256]{1,0:T(8,128)S(1)}, f32[384,256]{1,0:T(8,128)S(1)}, u32[]{:S(2)}, u32[]{:S(2)}) collective-permute-start(f32[384,256]{1,0:T(8,128)S(1)} %get-tuple-element.42), channel_id=1, source_target_pairs={{0,16},{8,24},{16,0},{24,8},{1,17},{9,25},{17,1},{25,9},{2,18},{10... | collective-permute-start | bytes 1179656 | tf_op jit(solution)/shard_map/ppermute | solution.py:220
  109.0 10.4 %collective-permute-start.2 = (f32[192,256]{1,0:T(8,128)S(1)}, f32[192,256]{1,0:T(8,128)S(1)}, u32[]{:S(2)}, u32[]{:S(2)}) collective-permute-start(f32[192,256]{1,0:T(8,128)S(1)} %get-tuple-element.56), channel_id=1, source_target_pairs={{0,16},{8,24},{16,0},{24,8},{1,17},{9,25},{17,1},{25,9},{2,18},{10... | collective-permute-start | bytes 589832 | tf_op jit(solution)/shard_map/ppermute | solution.py:220
  110.9 12.0 %collective-permute-start.12 = (f32[192,256]{1,0:T(8,128)S(1)}, f32[192,256]{1,0:T(8,128)S(1)}, u32[]{:S(2)}, u32[]{:S(2)}) collective-permute-start(f32[192,256]{1,0:T(8,128)S(1)} %get-tuple-element.54), channel_id=1, source_target_pairs={{0,16},{8,24},{16,0},{24,8},{1,17},{9,25},{17,1},{25,9},{2,18},{10... | collective-permute-start | bytes 589832 | tf_op jit(solution)/shard_map/ppermute | solution.py:220
  116.7 9.0 %collective-permute-start.22 = (f32[192,256]{1,0:T(8,128)S(1)}, f32[192,256]{1,0:T(8,128)S(1)}, u32[]{:S(2)}, u32[]{:S(2)}) collective-permute-start(f32[192,256]{1,0:T(8,128)S(1)} %get-tuple-element.52), channel_id=1, source_target_pairs={{0,16},{8,24},{16,0},{24,8},{1,17},{9,25},{17,1},{25,9},{2,18},{10... | collective-permute-start | bytes 589832 | tf_op jit(solution)/shard_map/ppermute | solution.py:220
  118.0 9.5 %collective-permute-start.32 = (f32[192,256]{1,0:T(8,128)S(1)}, f32[192,256]{1,0:T(8,128)S(1)}, u32[]{:S(2)}, u32[]{:S(2)}) collective-permute-start(f32[192,256]{1,0:T(8,128)S(1)} %get-tuple-element.50), channel_id=1, source_target_pairs={{0,1},{1,0},{2,3},{3,2},{4,5},{5,4},{6,7},{7,6},{8,9},{9,8},{10,11... | collective-permute-start | bytes 589832 | tf_op jit(solution)/shard_map/ppermute | solution.py:220
  119.5 8.4 %collective-permute-start.3 = (f32[96,256]{1,0:T(8,128)S(1)}, f32[96,256]{1,0:T(8,128)S(1)}, u32[]{:S(2)}, u32[]{:S(2)}) collective-permute-start(f32[96,256]{1,0:T(8,128)S(1)} %broadcast_select_fusion.35), channel_id=1, source_target_pairs={{0,2},{1,3},{2,0},{3,1},{4,6},{5,7},{6,4},{7,5},{8,10},{9,11},{10,... | collective-permute-start | bytes 294920 | tf_op jit(solution)/shard_map/ppermute | solution.py:220
  122.9 6.5 %collective-permute-start.13 = (f32[96,256]{1,0:T(8,128)S(1)}, f32[96,256]{1,0:T(8,128)S(1)}, u32[]{:S(2)}, u32[]{:S(2)}) collective-permute-start(f32[96,256]{1,0:T(8,128)S(1)} %broadcast_select_fusion.26), channel_id=1, source_target_pairs={{0,1},{1,0},{2,3},{3,2},{4,5},{5,4},{6,7},{7,6},{8,9},{9,8},{10,11... | collective-permute-start | bytes 294920 | tf_op jit(solution)/shard_map/ppermute | solution.py:220
  125.7 6.2 %collective-permute-start.23 = (f32[96,256]{1,0:T(8,128)S(1)}, f32[96,256]{1,0:T(8,128)S(1)}, u32[]{:S(2)}, u32[]{:S(2)}) collective-permute-start(f32[96,256]{1,0:T(8,128)S(1)} %broadcast_select_fusion.32), channel_id=1, source_target_pairs={{0,2},{1,3},{2,0},{3,1},{4,6},{5,7},{6,4},{7,5},{8,10},{9,11},{10,... | collective-permute-start | bytes 294920 | tf_op jit(solution)/shard_map/ppermute | solution.py:220
  127.5 6.0 %collective-permute-start.33 = (f32[96,256]{1,0:T(8,128)S(1)}, f32[96,256]{1,0:T(8,128)S(1)}, u32[]{:S(2)}, u32[]{:S(2)}) collective-permute-start(f32[96,256]{1,0:T(8,128)S(1)} %broadcast_select_fusion.29), channel_id=1, source_target_pairs={{0,2},{1,3},{2,0},{3,1},{4,6},{5,7},{6,4},{7,5},{8,10},{9,11},{10,... | collective-permute-start | bytes 294920 | tf_op jit(solution)/shard_map/ppermute | solution.py:220
  127.9 9.0 %collective-permute-start.4 = (f32[96,256]{1,0:T(8,128)S(1)}, f32[96,256]{1,0:T(8,128)S(1)}, u32[]{:S(2)}, u32[]{:S(2)}) collective-permute-start(f32[96,256]{1,0:T(8,128)S(1)} %select_add_fusion.3), channel_id=1, source_target_pairs={{0,6},{1,7},{2,4},{3,5},{4,2},{5,3},{6,0},{7,1},{8,14},{9,15},{10,... | collective-permute-start | bytes 294920 | tf_op jit(solution)/shard_map/ppermute | solution.py:220
  129.4 13.4 %collective-permute-start.14 = (f32[96,256]{1,0:T(8,128)S(1)}, f32[96,256]{1,0:T(8,128)S(1)}, u32[]{:S(2)}, u32[]{:S(2)}) collective-permute-start(f32[96,256]{1,0:T(8,128)S(1)} %select_add_fusion.2), channel_id=1, source_target_pairs={{0,6},{1,7},{2,4},{3,5},{4,2},{5,3},{6,0},{7,1},{8,14},{9,15},{10,... | collective-permute-start | bytes 294920 | tf_op jit(solution)/shard_map/ppermute | solution.py:220
  131.9 12.1 %collective-permute-start.24 = (f32[96,256]{1,0:T(8,128)S(1)}, f32[96,256]{1,0:T(8,128)S(1)}, u32[]{:S(2)}, u32[]{:S(2)}) collective-permute-start(f32[96,256]{1,0:T(8,128)S(1)} %select_add_fusion.1), channel_id=1, source_target_pairs={{0,6},{1,7},{2,4},{3,5},{4,2},{5,3},{6,0},{7,1},{8,14},{9,15},{10,... | collective-permute-start | bytes 294920 | tf_op jit(solution)/shard_map/ppermute | solution.py:220
  133.5 12.8 %collective-permute-start.34 = (f32[96,256]{1,0:T(8,128)S(1)}, f32[96,256]{1,0:T(8,128)S(1)}, u32[]{:S(2)}, u32[]{:S(2)}) collective-permute-start(f32[96,256]{1,0:T(8,128)S(1)} %select_add_fusion), channel_id=1, source_target_pairs={{0,6},{1,7},{2,4},{3,5},{4,2},{5,3},{6,0},{7,1},{8,14},{9,15},{10,... | collective-permute-start | bytes 294920 | tf_op jit(solution)/shard_map/ppermute | solution.py:220
  136.9 10.4 %collective-permute-start.5 = (f32[96,256]{1,0:T(8,128)S(1)}, f32[96,256]{1,0:T(8,128)S(1)}, u32[]{:S(2)}, u32[]{:S(2)}) collective-permute-start(f32[96,256]{1,0:T(8,128)S(1)} %add.119), channel_id=1, source_target_pairs={{0,2},{1,3},{2,0},{3,1},{4,6},{5,7},{6,4},{7,5},{8,10},{9,11},{10,... | collective-permute-start | bytes 294920 | tf_op jit(solution)/shard_map/ppermute | solution.py:220
  142.8 5.8 %collective-permute-start.15 = (f32[96,256]{1,0:T(8,128)S(1)}, f32[96,256]{1,0:T(8,128)S(1)}, u32[]{:S(2)}, u32[]{:S(2)}) collective-permute-start(f32[96,256]{1,0:T(8,128)S(1)} %add.127), channel_id=1, source_target_pairs={{0,1},{1,0},{2,3},{3,2},{4,5},{5,4},{6,7},{7,6},{8,9},{9,8},{10,11... | collective-permute-start | bytes 294920 | tf_op jit(solution)/shard_map/ppermute | solution.py:220
  144.0 5.5 %collective-permute-start.25 = (f32[96,256]{1,0:T(8,128)S(1)}, f32[96,256]{1,0:T(8,128)S(1)}, u32[]{:S(2)}, u32[]{:S(2)}) collective-permute-start(f32[96,256]{1,0:T(8,128)S(1)} %add.135), channel_id=1, source_target_pairs={{0,2},{1,3},{2,0},{3,1},{4,6},{5,7},{6,4},{7,5},{8,10},{9,11},{10,... | collective-permute-start | bytes 294920 | tf_op jit(solution)/shard_map/ppermute | solution.py:220
  146.3 4.7 %collective-permute-start.35 = (f32[96,256]{1,0:T(8,128)S(1)}, f32[96,256]{1,0:T(8,128)S(1)}, u32[]{:S(2)}, u32[]{:S(2)}) collective-permute-start(f32[96,256]{1,0:T(8,128)S(1)} %add.143), channel_id=1, source_target_pairs={{0,2},{1,3},{2,0},{3,1},{4,6},{5,7},{6,4},{7,5},{8,10},{9,11},{10,... | collective-permute-start | bytes 294920 | tf_op jit(solution)/shard_map/ppermute | solution.py:220
  147.4 7.9 %collective-permute-start.6 = (f32[192,256]{1,0:T(8,128)S(1)}, f32[192,256]{1,0:T(8,128)S(1)}, u32[]{:S(2)}, u32[]{:S(2)}) collective-permute-start(f32[192,256]{1,0:T(8,128)S(1)} %pad_maximum_fusion.4), channel_id=1, source_target_pairs={{0,16},{8,24},{16,0},{24,8},{1,17},{9,25},{17,1},{25,9},{2,18},{10... | collective-permute-start | bytes 589832 | tf_op jit(solution)/shard_map/ppermute | solution.py:220
  148.6 16.0 %collective-permute-start.16 = (f32[192,256]{1,0:T(8,128)S(1)}, f32[192,256]{1,0:T(8,128)S(1)}, u32[]{:S(2)}, u32[]{:S(2)}) collective-permute-start(f32[192,256]{1,0:T(8,128)S(1)} %pad_maximum_fusion.5), channel_id=1, source_target_pairs={{0,16},{8,24},{16,0},{24,8},{1,17},{9,25},{17,1},{25,9},{2,18},{10... | collective-permute-start | bytes 589832 | tf_op jit(solution)/shard_map/ppermute | solution.py:220
  149.6 14.1 %collective-permute-start.26 = (f32[192,256]{1,0:T(8,128)S(1)}, f32[192,256]{1,0:T(8,128)S(1)}, u32[]{:S(2)}, u32[]{:S(2)}) collective-permute-start(f32[192,256]{1,0:T(8,128)S(1)} %pad_maximum_fusion.6), channel_id=1, source_target_pairs={{0,16},{8,24},{16,0},{24,8},{1,17},{9,25},{17,1},{25,9},{2,18},{10... | collective-permute-start | bytes 589832 | tf_op jit(solution)/shard_map/ppermute | solution.py:220
  151.0 7.9 %collective-permute-start.36 = (f32[192,256]{1,0:T(8,128)S(1)}, f32[192,256]{1,0:T(8,128)S(1)}, u32[]{:S(2)}, u32[]{:S(2)}) collective-permute-start(f32[192,256]{1,0:T(8,128)S(1)} %pad_maximum_fusion.7), channel_id=1, source_target_pairs={{0,1},{1,0},{2,3},{3,2},{4,5},{5,4},{6,7},{7,6},{8,9},{9,8},{10,11... | collective-permute-start | bytes 589832 | tf_op jit(solution)/shard_map/ppermute | solution.py:220
  155.3 11.1 %collective-permute-start.7 = (f32[384,256]{1,0:T(8,128)S(1)}, f32[384,256]{1,0:T(8,128)S(1)}, u32[]{:S(2)}, u32[]{:S(2)}) collective-permute-start(f32[384,256]{1,0:T(8,128)S(1)} %pad_maximum_fusion.mine), channel_id=1, source_target_pairs={{0,1},{1,0},{2,3},{3,2},{4,5},{5,4},{6,7},{7,6},{8,9},{9,8},{10,11... | collective-permute-start | bytes 1179656 | tf_op jit(solution)/shard_map/ppermute | solution.py:220
  159.0 10.1 %collective-permute-start.37 = (f32[384,256]{1,0:T(8,128)S(1)}, f32[384,256]{1,0:T(8,128)S(1)}, u32[]{:S(2)}, u32[]{:S(2)}) collective-permute-start(f32[384,256]{1,0:T(8,128)S(1)} %pad_maximum_fusion.3.mine), channel_id=1, source_target_pairs={{0,16},{8,24},{16,0},{24,8},{1,17},{9,25},{17,1},{25,9},{2,18},{10... | collective-permute-start | bytes 1179656 | tf_op jit(solution)/shard_map/ppermute | solution.py:220
  163.8 8.2 %collective-permute-start.27 = (f32[384,256]{1,0:T(8,128)S(1)}, f32[384,256]{1,0:T(8,128)S(1)}, u32[]{:S(2)}, u32[]{:S(2)}) collective-permute-start(f32[384,256]{1,0:T(8,128)S(1)} %pad_maximum_fusion.2.mine), channel_id=1, source_target_pairs={{0,1},{1,0},{2,3},{3,2},{4,5},{5,4},{6,7},{7,6},{8,9},{9,8},{10,11... | collective-permute-start | bytes 1179656 | tf_op jit(solution)/shard_map/ppermute | solution.py:220
  164.7 7.8 %collective-permute-start.17 = (f32[384,256]{1,0:T(8,128)S(1)}, f32[384,256]{1,0:T(8,128)S(1)}, u32[]{:S(2)}, u32[]{:S(2)}) collective-permute-start(f32[384,256]{1,0:T(8,128)S(1)} %pad_maximum_fusion.1.mine), channel_id=1, source_target_pairs={{0,2},{1,3},{2,0},{3,1},{4,6},{5,7},{6,4},{7,5},{8,10},{9,11},{10,... | collective-permute-start | bytes 1179656 | tf_op jit(solution)/shard_map/ppermute | solution.py:220
  165.6 6.9 %collective-permute-start.28 = (f32[384,256]{1,0:T(8,128)S(1)}, f32[384,256]{1,0:T(8,128)S(1)}, u32[]{:S(2)}, u32[]{:S(2)}) collective-permute-start(f32[384,256]{1,0:T(8,128)S(1)} %pad_maximum_fusion.2.mine), channel_id=1, source_target_pairs={{0,8},{8,0},{16,24},{24,16},{1,9},{9,1},{17,25},{25,17},{2,10},{10... | collective-permute-start | bytes 1179656 | tf_op jit(solution)/shard_map/ppermute | solution.py:220
  166.5 6.6 %collective-permute-start.38 = (f32[384,256]{1,0:T(8,128)S(1)}, f32[384,256]{1,0:T(8,128)S(1)}, u32[]{:S(2)}, u32[]{:S(2)}) collective-permute-start(f32[384,256]{1,0:T(8,128)S(1)} %pad_maximum_fusion.3.mine), channel_id=1, source_target_pairs={{0,8},{8,0},{16,24},{24,16},{1,9},{9,1},{17,25},{25,17},{2,10},{10... | collective-permute-start | bytes 1179656 | tf_op jit(solution)/shard_map/ppermute | solution.py:220
  169.1 4.0 %collective-permute-start.39 = (f32[384,256]{1,0:T(8,128)S(1)}, f32[384,256]{1,0:T(8,128)S(1)}, u32[]{:S(2)}, u32[]{:S(2)}) collective-permute-start(f32[384,256]{1,0:T(8,128)S(1)} %collective-permute-done.37.got), channel_id=1, source_target_pairs={{0,8},{8,0},{16,24},{24,16},{1,9},{9,1},{17,25},{25,17},{2,10},{10... | collective-permute-start | bytes 1179656 | tf_op jit(solution)/shard_map/ppermute | solution.py:220
  171.9 3.6 %collective-permute-start.29 = (f32[384,256]{1,0:T(8,128)S(1)}, f32[384,256]{1,0:T(8,128)S(1)}, u32[]{:S(2)}, u32[]{:S(2)}) collective-permute-start(f32[384,256]{1,0:T(8,128)S(1)} %collective-permute-done.27.got), channel_id=1, source_target_pairs={{0,8},{8,0},{16,24},{24,16},{1,9},{9,1},{17,25},{25,17},{2,10},{10... | collective-permute-start | bytes 1179656 | tf_op jit(solution)/shard_map/ppermute | solution.py:220
  172.5 4.8 %collective-permute-start.18 = (f32[384,256]{1,0:T(8,128)S(1)}, f32[384,256]{1,0:T(8,128)S(1)}, u32[]{:S(2)}, u32[]{:S(2)}) collective-permute-start(f32[384,256]{1,0:T(8,128)S(1)} %pad_maximum_fusion.1.mine), channel_id=1, source_target_pairs={{0,8},{8,0},{16,24},{24,16},{1,9},{9,1},{17,25},{25,17},{2,10},{10... | collective-permute-start | bytes 1179656 | tf_op jit(solution)/shard_map/ppermute | solution.py:220
  172.5 4.8 %collective-permute-start.19 = (f32[384,256]{1,0:T(8,128)S(1)}, f32[384,256]{1,0:T(8,128)S(1)}, u32[]{:S(2)}, u32[]{:S(2)}) collective-permute-start(f32[384,256]{1,0:T(8,128)S(1)} %collective-permute-done.17.got), channel_id=1, source_target_pairs={{0,8},{8,0},{16,24},{24,16},{1,9},{9,1},{17,25},{25,17},{2,10},{10... | collective-permute-start | bytes 1179656 | tf_op jit(solution)/shard_map/ppermute | solution.py:220
  173.1 6.1 %collective-permute-start.8 = (f32[384,256]{1,0:T(8,128)S(1)}, f32[384,256]{1,0:T(8,128)S(1)}, u32[]{:S(2)}, u32[]{:S(2)}) collective-permute-start(f32[384,256]{1,0:T(8,128)S(1)} %pad_maximum_fusion.mine), channel_id=1, source_target_pairs={{0,8},{8,0},{16,24},{24,16},{1,9},{9,1},{17,25},{25,17},{2,10},{10... | collective-permute-start | bytes 1179656 | tf_op jit(solution)/shard_map/ppermute | solution.py:220
  173.1 6.0 %collective-permute-start.9 = (f32[384,256]{1,0:T(8,128)S(1)}, f32[384,256]{1,0:T(8,128)S(1)}, u32[]{:S(2)}, u32[]{:S(2)}) collective-permute-start(f32[384,256]{1,0:T(8,128)S(1)} %collective-permute-done.7.got), channel_id=1, source_target_pairs={{0,8},{8,0},{16,24},{24,16},{1,9},{9,1},{17,25},{25,17},{2,10},{10... | collective-permute-start | bytes 1179656 | tf_op jit(solution)/shard_map/ppermute | solution.py:220
  (6 other events, 5.9 us)

commit v3 on v2

--- a/solution.py
+++ b/solution.py
@@ -12,11 +12,6 @@
 CHUNKS = 4
 CALLS = 2
 VMEM_LIMIT = 48 * 1024 * 1024
-
-
-def look_up(feature_table, requests):
-    picked = jnp.take(feature_table, jnp.maximum(requests, 0), axis=0)
-    return picked * (requests >= 0)[..., None].astype(jnp.float32)
 
 
 def split(value):
@@ -73,18 +68,82 @@
     )(neighbors.T, self_index[None, :])
 
 
+def pick(rows_named, table):
+    ids = lax.broadcasted_iota(jnp.int32, (table.shape[0], rows_named.shape[1]), 0)
+    chosen = jnp.where(ids == rows_named, 1.0, 0.0).astype(jnp.bfloat16)
+    high, low = split(table)
+    return dot_rows(chosen, high) + dot_rows(chosen, low)
+
+
+def cold_kernel(asked_ref, table_ref, out_ref):
+    out_ref[...] = pick(asked_ref[...], table_ref[...])
+
+
+def cold_look_up(asked, table):
+    count, width = asked.shape[1], table.shape[1]
+    return pl.pallas_call(
+        cold_kernel,
+        out_shape=jax.ShapeDtypeStruct((count, width), jnp.float32),
+        compiler_params=pltpu.CompilerParams(vmem_limit_bytes=VMEM_LIMIT),
+        cost_estimate=pl.CostEstimate(
+            flops=4 * count * table.size, bytes_accessed=4 * table.size, transcendentals=0
+        ),
+        name="cold_look_up",
+    )(asked, table)
+
+
+def hot_kernel(half, device_ref, asked_ref, own_ref, far_ref, *out_refs):
+    slots = asked_ref.shape[1] // 2
+    rows = own_ref.shape[0]
+    at = device_ref[1] % half
+    table = jnp.concatenate([own_ref[...], far_ref[...]], axis=0)
+    high, low = split(table)
+    lanes = lax.broadcasted_iota(jnp.int32, (1, 2 * slots), 1)
+    ids = lax.broadcasted_iota(jnp.int32, (2 * rows, 2 * slots), 0)
+    for away in range(half):
+        asked = asked_ref[pl.ds(at ^ away, 1), :]
+        asked = jnp.where((lanes >= slots) & (asked >= 0), asked + rows, asked)
+        chosen = jnp.where(ids == asked, 1.0, 0.0).astype(jnp.bfloat16)
+        out_refs[away][...] = dot_rows(chosen, high) + dot_rows(chosen, low)
+
+
+def hot_look_up(half, device, asked, own, far):
+    slots, width = asked.shape[1], own.shape[1]
+    vmem = pl.BlockSpec(memory_space=pltpu.VMEM)
+    return pl.pallas_call(
+        functools.partial(hot_kernel, half),
+        in_specs=[pl.BlockSpec(memory_space=pltpu.SMEM)] + [vmem] * 3,
+        out_specs=[vmem] * half,
+        out_shape=[jax.ShapeDtypeStruct((slots, width), jnp.float32)] * half,
+        compiler_params=pltpu.CompilerParams(vmem_limit_bytes=VMEM_LIMIT),
+        cost_estimate=pl.CostEstimate(
+            flops=8 * half * slots * own.size, bytes_accessed=12 * own.size, transcendentals=0
+        ),
+        name="hot_look_up",
+    )(device, asked, own, far)
+
+
 def layer_kernel(
-    chunks, core_ref, counts_ref, hot_ref, cold_ref, w_self_ref, w_neigh_ref, cot_ref, *rest
+    chunks, half, far_mask, device_ref, counts_ref, cold_ref, w_self_ref, w_neigh_ref, cot_ref, *rest
 ):
+    hot_refs = rest[:half]
     src, prod, back = rest[-3:]
     grad_refs = rest[-3 - 2 * chunks : -3]
     hidden_ref = rest[-4 - 2 * chunks]
-    n_hot, n_src = hot_ref.shape[0], src.shape[1]
+    n_src = src.shape[1]
+    n_hot = n_src - cold_ref.shape[0]
+    slots = hot_refs[0].shape[0] // 2
     step = pl.program_id(0)
 
     @pl.when(step == 0)
     def _():
-        src[0, :n_hot, :], src[1, :n_hot, :] = split(hot_ref[...])
+        for away in range(half):
+            owner = device_ref[1] ^ away
+            high, low = split(hot_refs[away][...])
+            for peer, first in ((owner, 0), (owner ^ far_mask, slots)):
+                rows = pl.ds(pl.multiple_of(peer * slots, slots), slots)
+                src[0, rows, :] = high[first : first + slots, :]
+                src[1, rows, :] = low[first : first + slots, :]
         src[0, n_hot:, :], src[1, n_hot:, :] = split(cold_ref[...])
         prod[:n_src, :] = dot(src[0], w_self_ref[...]).astype(jnp.bfloat16)
         both = dot(src[0], w_neigh_ref[...]) + dot(src[1], w_neigh_ref[...])
@@ -110,20 +169,20 @@
             high, low = split(back[n_src:, pl.ds(part * cols, cols)] * (1.0 / FAN))
             return dot_rows(src[0], high) + dot_rows(src[0], low) + dot_rows(src[1], high)
 
-        @pl.when(core_ref[0] == 0)
+        @pl.when(device_ref[0] == 0)
         def _():
             for part in range(chunks):
                 grad_refs[2 * part][...] = self_term(part)
                 grad_refs[2 * part + 1][...] = neigh_term(part)
 
-        @pl.when(core_ref[0] != 0)
+        @pl.when(device_ref[0] != 0)
         def _():
             for part in range(chunks):
                 grad_refs[2 * part][...] = neigh_term(part)
                 grad_refs[2 * part + 1][...] = self_term(part)
 
 
-def layer(call, chunks, core, counts, hot_rows, cold_rows, w_self, w_neigh, cotangent, hidden):
+def layer(call, chunks, far_mask, device, counts, hot_rows, cold_rows, w_self, w_neigh, cotangent, hidden):
     targets, hidden_units = cotangent.shape
     feat_width = w_self.shape[0]
     n_src = counts.shape[0] // 2
@@ -135,20 +194,19 @@
     tile = lambda i, c: (i, call)
     in_specs = [
         pl.BlockSpec((2 * n_src, block), lambda i, c: (0, i)),
-        pl.BlockSpec(hot_rows.shape, whole),
         pl.BlockSpec(cold_rows.shape, whole),
         pl.BlockSpec((feat_width, wide), column),
         pl.BlockSpec((feat_width, wide), column),
         pl.BlockSpec((block, wide), tile),
-    ]
-    operands = [core, counts, hot_rows, cold_rows, w_self, w_neigh, cotangent]
+    ] + [pl.BlockSpec(rows.shape, whole) for rows in hot_rows]
+    operands = [device, counts, cold_rows, w_self, w_neigh, cotangent, *hot_rows]
     aliases = {}
     if hidden is not None:
         in_specs.append(pl.BlockSpec(memory_space=pl.ANY))
         operands.append(hidden)
-        aliases = {7: 0}
+        aliases = {len(operands) - 1: 0}
     return pl.pallas_call(
-        functools.partial(layer_kernel, chunks),
+        functools.partial(layer_kernel, chunks, len(hot_rows), far_mask),
         grid_spec=pltpu.PrefetchScalarGridSpec(
             num_scalar_prefetch=1,
             grid=(targets // block,),
@@ -220,14 +278,15 @@
         return lax.ppermute(value, self.name, self.pairs)
 
 
-def swaps(name, stride, size):
+def swaps(name, stride, size, plain=False):
     index = lax.axis_index(name)
     found = []
     step = 1
     while step < size:
-        low = lax.rem(lax.div(index, jnp.int32(stride * step)), jnp.int32(2))
-        high = lax.rem(lax.div(index, jnp.int32(stride * step * 2)), jnp.int32(2)) if 2 * step < size else 0
-        found.append(Swap(name, stride * (2 * step - 1), lax.rem(low + high, jnp.int32(2))))
+        bit = lax.rem(lax.div(index, jnp.int32(stride * step)), jnp.int32(2))
+        if 2 * step < size and not plain:
+            bit = bit ^ lax.rem(lax.div(index, jnp.int32(stride * step * 2)), jnp.int32(2))
+        found.append(Swap(name, stride * (2 * step - 1), bit))
         step *= 2
     return found
 
@@ -246,13 +305,63 @@
     return jnp.concatenate([jnp.where(first, value, got), jnp.where(first, got, value)], axis=0)
 
 
-def sum_over_devices(terms, core):
+def axis_swaps(plain=False):
     groups, dev_size = lax.axis_size("grp"), lax.axis_size("dev")
     x_size = groups // CORES
     y_size = x_size if dev_size % x_size == 0 else 1
-    along_x = swaps("grp", CORES, x_size)
-    along_y = swaps("dev", 1, y_size)
-    along_z = swaps("dev", y_size, dev_size // y_size)
+    return (
+        swaps("grp", 1, CORES, plain),
+        swaps("grp", CORES, x_size, plain),
+        swaps("dev", 1, y_size, plain),
+        swaps("dev", y_size, dev_size // y_size, plain),
+    )
+
+
+def fetch_rows(hot_table, cold_table, hot_need, cold_need, device):
+    core, along_x, along_y, along_z = axis_swaps(plain=True)
+    far = along_z[-1]
+    half = lax.axis_size("dev") // 2
+    me = lax.axis_index("dev")
+    slots = hot_need.shape[1]
+
+    spread = along_x + core
+    share = hot_table.shape[0] // lax.axis_size("grp")
+    which = functools.reduce(jnp.add, [s.bit * (1 << k) for k, s in enumerate(spread)])
+    far_table = far.send(lax.dynamic_slice_in_dim(hot_table, which * share, share, axis=0))
+    for swap in spread:
+        far_table = double(far_table, swap)
+
+    needs = jnp.concatenate([hot_need.reshape(1, -1), cold_need.reshape(1, -1)], axis=1)
+    for swap in along_y + along_z[:-1]:
+        needs = double(needs, swap)
+    hot_asked = jnp.concatenate(
+        [
+            lax.dynamic_slice_in_dim(needs, peer * slots, slots, axis=1)
+            for peer in (me, me ^ far.mask)
+        ],
+        axis=1,
+    )
+    for swap in [far] + core + along_x:
+        needs = double(needs, swap)
+    first = hot_need.size + (lax.axis_index("grp") * 2 * half + me) * cold_need.shape[1]
+    cold_asked = lax.dynamic_slice_in_dim(needs, first, cold_need.shape[1], axis=1)
+    cold_rows = lax.all_to_all(
+        cold_look_up(cold_asked.reshape(1, -1), cold_table),
+        ("grp", "dev"),
+        split_axis=0,
+        concat_axis=0,
+        tiled=True,
+    )
+    served = hot_look_up(half, device, hot_asked, hot_table, far_table)
+    pairs = lambda away: [(i, i ^ away) for i in range(2 * half)]
+    hot_rows = [served[0]] + [
+        lax.ppermute(served[away], "dev", pairs(away)) for away in range(1, half)
+    ]
+    return hot_rows, cold_rows, far.mask
+
+
+def sum_over_devices(terms):
+    (core,), along_x, along_y, along_z = axis_swaps()
     near_z, far_z = along_z[:1], along_z[1:]
     orders = [
         along_x + along_y + near_z + far_z,
@@ -279,35 +388,28 @@
 def body(
     hot_table, cold_table, hot_need, cold_need, self_index, neighbors, w_self, w_neigh, cotangent
 ):
-    feat_width = hot_table.shape[1]
-    both = ("grp", "dev")
     n_src = hot_need.size + cold_need.size
     counts = count_matrices(neighbors, self_index, n_src)
-
-    exchange = functools.partial(
-        lax.all_to_all, axis_name=both, split_axis=0, concat_axis=0, tiled=True
-    )
-    groups, dev_size = lax.axis_size("grp"), lax.axis_size("dev")
-    cold_slots = cold_need.shape[1]
-    asked = exchange(jnp.concatenate([cold_need, jnp.tile(hot_need, (groups, 1))], axis=1))
-    cold_asked = asked[:, :cold_slots]
-    hot_asked = lax.dynamic_slice_in_dim(
-        asked[:, cold_slots:], lax.axis_index("grp") * dev_size, dev_size, axis=0
-    )
-    cold_rows = exchange(look_up(cold_table, cold_asked)).reshape(-1, feat_width)
-    hot_rows = lax.all_to_all(
-        look_up(hot_table, hot_asked), "dev", split_axis=0, concat_axis=0, tiled=True
-    ).reshape(-1, feat_width)
-
-    core = swaps("grp", 1, CORES)[0]
+    device = jnp.stack([lax.rem(lax.axis_index("grp"), jnp.int32(CORES)), lax.axis_index("dev")])
+    hot_rows, cold_rows, far_mask = fetch_rows(hot_table, cold_table, hot_need, cold_need, device)
     hidden = None
     terms = []
     for call in range(CALLS):
         hidden, *grads = layer(
-            call, CHUNKS // CALLS, core.bit[None], counts, hot_rows, cold_rows, w_self, w_neigh, cotangent, hidden
+            call,
+            CHUNKS // CALLS,
+            far_mask,
+            device,
+            counts,
+            hot_rows,
+            cold_rows,
+            w_self,
+            w_neigh,
+            cotangent,
+            hidden,
         )
         terms += list(zip(grads[::2], grads[1::2]))
-    grad_self, grad_neigh = sum_over_devices(terms, core)
+    grad_self, grad_neigh = sum_over_devices(terms)
     return (hidden, grad_self, grad_neigh)
 
 

time: 182 us -> 174 us (0.956)
  blocking collectives: 14.2 us -> 0 us
  starting transfers between devices: 49.2 us -> 61.4 us
  other arithmetic: 9.93 us -> 5.39 us
  Pallas kernels: 36.9 us -> 41.3 us
  waiting for transfers between devices: 52.9 us -> 49 us
    all_to_all x2 -> x1, waiting for transfers between devices: 19 us -> 0.01 us  [fetch_rows(): lax.all_to_all(cold_look_up(cold_asked.reshape(1, -1), cold_table), ('grp...]
    all_to_all x1 -> x0, blocking collectives: 14.2 us -> none  [body(): exchange(jnp.concatenate([cold_need, jnp.tile(hot_need, (groups, 1))], ax...]
    ppermute x40 -> x48, starting transfers between devices: 41.5 us -> 54.6 us  [send(): return lax.ppermute(value, self.name, self.pairs)]
    ppermute x40 -> x48, waiting for transfers between devices: 33.9 us -> 46.8 us  [send(): return lax.ppermute(value, self.name, self.pairs)]
    gather x3 -> x0, local copies, waits for them, and re-layouts: 6.06 us -> none  [look_up(): picked = jnp.take(feature_table, jnp.maximum(requests, 0), axis=0)]
    pallas_call x2 -> x4, Pallas kernels: 23.8 us -> 28.2 us  [the longest x2 24.9 us: layer(): pl.pallas_call(functools.partial(layer_kernel, chunks, len(hot_rows), far...]
    all_to_all x2 -> x1, starting transfers between devices: 7.7 us -> 3.34 us  [fetch_rows(): lax.all_to_all(cold_look_up(cold_asked.reshape(1, -1), cold_table), ('grp...]
    mul x2 -> x0, other arithmetic: 3.83 us -> none  [look_up(): return picked * (requests >= 0)[..., None].astype(jnp.float32)]
  transfers between devices with their start and end apart: 42 -> 52, of which waited for: 17 -> 20; matrix products, arithmetic and copies ran while one was open for 7% -> 4% of each run, Pallas kernels for 6% -> 8%
where the time goes in v3:
time: 174 us; the launch traced here: 173 us
  starting transfers between devices  61.4 us (35%)
  waiting for transfers between devices  49 us (28%)
  Pallas kernels  41.3 us (24%)
  local copies, waits for them, and re-layouts  14.9 us (9%)
  other arithmetic  5.39 us (3%)
    ppermute x48, starting transfers between devices, send(): return lax.ppermute(value, self.name, self.pairs)  54.6 us
    ppermute x48, waiting for transfers between devices, send(): return lax.ppermute(value, self.name, self.pairs)  46.8 us
    pallas_call x2, Pallas kernels, layer(): pl.pallas_call(functools.partial(layer_kernel, chunks, len(hot_rows), far...  24.9 us
    unnamed x34, local copies, waits for them, and re-layouts  11 us
    pallas_call x4, Pallas kernels, place(): pl.pallas_call(place_kernel, grid_spec=pltpu.PrefetchScalarGridSpec(num_s...  7.12 us
    pallas_call x1, Pallas kernels, count_matrices(): pl.pallas_call(count_kernel, grid=(targets // block,), in_specs=[pl.Block...  5.94 us
    select_n x8, other arithmetic, halve(): return [jnp.where(swap.bit == 0, low, high), swap.send(out)]  3.98 us
    ppermute x3, starting transfers between devices, fetch_rows(): lax.ppermute(served[away], 'dev', pairs(away))  3.49 us
  transfers between devices with their start and end apart: 52, of which 20 were waited for; matrix products, arithmetic and copies ran while one was open for 4% of the time, Pallas kernels for 8%

profile of v3, /device:TPU:0, one launch (start us, length us, event | category | flops | bytes accessed | tf_op | source)
XLA Modules:
  0.0 173.1 jit_solution(1137875589725182346)
XLA Ops:
  2.3 3.0 %collective-permute-start = (s32[1,384]{1,0:T(1,128)S(1)}, s32[1,384]{1,0:T(1,128)S(1)}, u32[]{:S(2)}, u32[]{:S(2)}) collective-permute-start(s32[1,384]{1,0:T(1,128)S(1)} %constant_dynamic-update-slice_fusion), channel_id=1, source_target_pairs={{0,1},{1,0},{2,3},{3,2},{4,5},{5,4},{6,7},{7,6},{8,9},{9,8},{10,11... | collective-permute-start | bytes 4616 | tf_op jit(solution)/shard_map/ppermute | solution.py:278
  5.3 1.6 collective-permute-done
  6.9 2.1 %collective-permute-start.1 = (s32[2,384]{1,0:T(2,128)S(1)}, s32[2,384]{1,0:T(2,128)S(1)}, u32[]{:S(2)}, u32[]{:S(2)}) collective-permute-start(s32[2,384]{1,0:T(2,128)S(1)} %pad_add_fusion.3), channel_id=1, source_target_pairs={{0,2},{1,3},{2,0},{3,1},{4,6},{5,7},{6,4},{7,5},{8,10},{9,11},{10,... | collective-permute-start | bytes 9224 | tf_op jit(solution)/shard_map/ppermute | solution.py:278
  9.0 1.6 collective-permute-done.1
  10.6 4.1 %collective-permute-start.2 = (s32[4,384]{1,0:T(4,128)S(1)}, s32[4,384]{1,0:T(4,128)S(1)}, u32[]{:S(2)}, u32[]{:S(2)}) collective-permute-start(s32[4,384]{1,0:T(4,128)S(1)} %pad_add_fusion.2), channel_id=1, source_target_pairs={{0,6},{1,7},{2,4},{3,5},{4,2},{5,3},{6,0},{7,1},{8,14},{9,15},{10,... | collective-permute-start | bytes 18440 | tf_op jit(solution)/shard_map/ppermute | solution.py:278
  16.6 6.7 %collective-permute-done.5 = f32[64,768]{1,0:T(8,128)S(1)} collective-permute-done((f32[64,768]{1,0:T(8,128)S(1)}, f32[64,768]{1,0:T(8,128)S(1)}, u32[]{:S(2)}, u32[]{:S(2)}) %collective-permute-start.5) | collective-permute-done | bytes 196640 | tf_op jit(solution)/shard_map/ppermute | solution.py:278
  23.3 1.5 collective-permute-start.6
  25.4 3.6 %collective-permute-done.6 = f32[64,768]{1,0:T(8,128)S(1)} collective-permute-done((f32[64,768]{1,0:T(8,128)S(1)}, f32[64,768]{1,0:T(8,128)S(1)}, u32[]{:S(2)}, u32[]{:S(2)}) %collective-permute-start.6) | collective-permute-done | bytes 196640 | tf_op jit(solution)/shard_map/ppermute | solution.py:278
  29.5 1.9 %copy-done.1 = f32[1024,768]{1,0:T(8,128)S(1)} copy-done((f32[1024,768]{1,0:T(8,128)S(1)}, f32[1024,768]{1,0:T(8,128)}, u32[]{:S(2)}) %copy-start.1) | copy-done | bytes 3145752
  33.0 3.3 %all-to-all-start = ((f32[32,4,768]{2,1,0:T(4,128)}), f32[32,4,768]{2,1,0:T(4,128)}, u32[]{:S(2)}, u32[]{:S(2)}) async-start(f32[32,4,768]{2,1,0:T(4,128)} %all_to_all.7), calls=%async_computation | async-start | bytes 786432 | tf_op jit(solution)/shard_map/all_to_all | solution.py:348
  36.7 2.5 %hot_look_up.1 = (f32[64,768]{1,0:T(8,128)S(1)}, f32[64,768]{1,0:T(8,128)}, f32[64,768]{1,0:T(8,128)}, f32[64,768]{1,0:T(8,128)}) custom-call(s32[2]{0:T(128)S(1)} %pad_add_fusion.5.device_ref, s32[4,64]{1,0:T(4,128)S(1)} %pad_add_fusion.4.asked_ref, f32[256,768]{1,0:T(8,128)S(1)} %copy-done.2, f32[256,768]{1,0:T(8,128)S(1)} %pad_maximum_fusion.far_ref), custom_call_target="tpu_custom_call" | custom-call | flops 402653184 | bytes 2359296 | tf_op jit(solution)/shard_map/hot_look_up/pallas_call | solution.py:113
  39.2 1.7 collective-permute-start.8
  40.9 1.5 collective-permute-start.9
  42.7 5.9 %count_matrices.1.counts_ref = bf16[768,2048]{1,0:T(8,128)(2,1)S(1)} custom-call(s32[25,2048]{1,0:T(8,128)S(1)} %bitcast.7, s32[1,2048]{1,0:T(1,128)S(1)} %bitcast.8), custom_call_target="tpu_custom_call" | custom-call | flops 39321600 | bytes 3145728 | tf_op jit(solution)/shard_map/count_matrices/pallas_call | solution.py:54
  48.7 1.7 copy-done
  52.8 2.2 %collective-permute-done.10.rest_3_ = f32[64,768]{1,0:T(8,128)S(1)} collective-permute-done((f32[64,768]{1,0:T(8,128)}, f32[64,768]{1,0:T(8,128)S(1)}, u32[]{:S(2)}, u32[]{:S(2)}) %collective-permute-start.10) | collective-permute-done | bytes 196640 | tf_op jit(solution)/shard_map/ppermute | solution.py:358
  59.4 12.3 %layer_0.1 = (bf16[2048,1024]{1,0:T(8,128)(2,1)}, f32[768,256]{1,0:T(8,128)S(1)}, f32[768,256]{1,0:T(8,128)S(1)}, f32[768,256]{1,0:T(8,128)S(1)}, f32[768,256]{1,0:T(8,128)}) custom-call(s32[2]{0:T(128)S(1)} %pad_add_fusion.5.device_ref, bf16[768,2048]{1,0:T(8,128)(2,1)} %copy-done, f32[128,768]{1,0:T(8,128)S(1)} %all_to_all.9.cold_ref, ...), custom_call_target="tpu_custom_call" | custom-call | flops 4429185024 | bytes 7340032 | tf_op jit(solution)/shard_map/layer_0/pallas_call | solution.py:208
  72.6 12.7 %layer_1.1 = (bf16[2048,1024]{1,0:T(8,128)(2,1)}, f32[768,256]{1,0:T(8,128)S(1)}, f32[768,256]{1,0:T(8,128)}, f32[768,256]{1,0:T(8,128)S(1)}, f32[768,256]{1,0:T(8,128)}) custom-call(s32[2]{0:T(128)S(1)} %pad_add_fusion.5.device_ref, bf16[768,2048]{1,0:T(8,128)(2,1)} %copy-done, ...), custom_call_target="tpu_custom_call", output_to_operand_aliasing={{0}: (10, {})} | custom-call | flops 4429185024 | bytes 7340032 | tf_op jit(solution)/shard_map/layer_1/pallas_call | solution.py:208
  86.3 1.6 collective-permute-done.11
  87.9 1.2 broadcast_select_fusion.7
  90.3 1.2 broadcast_select_fusion.3
  92.6 1.2 broadcast_select_fusion.5
  95.8 5.4 %collective-permute-done.12 = f32[384,256]{1,0:T(8,128)S(1)} collective-permute-done((f32[384,256]{1,0:T(8,128)S(1)}, f32[384,256]{1,0:T(8,128)S(1)}, u32[]{:S(2)}, u32[]{:S(2)}) %collective-permute-start.12) | collective-permute-done | bytes 393248 | tf_op jit(solution)/shard_map/ppermute | solution.py:278
  101.2 1.6 collective-permute-start.13
  102.9 1.4 collective-permute-start.23
  104.3 4.5 %collective-permute-done.32 = f32[384,256]{1,0:T(8,128)S(1)} collective-permute-done((f32[384,256]{1,0:T(8,128)S(1)}, f32[384,256]{1,0:T(8,128)S(1)}, u32[]{:S(2)}, u32[]{:S(2)}) %collective-permute-start.32) | collective-permute-done | bytes 393248 | tf_op jit(solution)/shard_map/ppermute | solution.py:278
  108.9 1.6 collective-permute-start.33
  112.4 3.1 %collective-permute-done.23 = f32[192,256]{1,0:T(8,128)S(1)} collective-permute-done((f32[192,256]{1,0:T(8,128)S(1)}, f32[192,256]{1,0:T(8,128)S(1)}, u32[]{:S(2)}, u32[]{:S(2)}) %collective-permute-start.23) | collective-permute-done | bytes 196640 | tf_op jit(solution)/shard_map/ppermute | solution.py:278
  116.7 1.6 collective-permute-done.33
  120.5 2.4 %collective-permute-start.15 = (f32[96,256]{1,0:T(8,128)S(1)}, f32[96,256]{1,0:T(8,128)S(1)}, u32[]{:S(2)}, u32[]{:S(2)}) collective-permute-start(f32[96,256]{1,0:T(8,128)S(1)} %select_add_fusion.3), channel_id=1, source_target_pairs={{0,6},{1,7},{2,4},{3,5},{4,2},{5,3},{6,0},{7,1},{8,14},{9,15},{10,... | collective-permute-start | bytes 294920 | tf_op jit(solution)/shard_map/ppermute | solution.py:278
  123.0 1.6 collective-permute-start.25
  124.6 2.4 %collective-permute-start.35 = (f32[96,256]{1,0:T(8,128)S(1)}, f32[96,256]{1,0:T(8,128)S(1)}, u32[]{:S(2)}, u32[]{:S(2)}) collective-permute-start(f32[96,256]{1,0:T(8,128)S(1)} %select_add_fusion.1), channel_id=1, source_target_pairs={{0,6},{1,7},{2,4},{3,5},{4,2},{5,3},{6,0},{7,1},{8,14},{9,15},{10,... | collective-permute-start | bytes 294920 | tf_op jit(solution)/shard_map/ppermute | solution.py:278
  127.0 1.6 collective-permute-start.45
  129.2 4.9 %collective-permute-start.16 = (f32[96,256]{1,0:T(8,128)S(1)}, f32[96,256]{1,0:T(8,128)S(1)}, u32[]{:S(2)}, u32[]{:S(2)}) collective-permute-start(f32[96,256]{1,0:T(8,128)S(1)} %add.133), channel_id=1, source_target_pairs={{0,2},{1,3},{2,0},{3,1},{4,6},{5,7},{6,4},{7,5},{8,10},{9,11},{10,... | collective-permute-start | bytes 294920 | tf_op jit(solution)/shard_map/ppermute | solution.py:278
  135.2 3.0 %collective-permute-start.36 = (f32[96,256]{1,0:T(8,128)S(1)}, f32[96,256]{1,0:T(8,128)S(1)}, u32[]{:S(2)}, u32[]{:S(2)}) collective-permute-start(f32[96,256]{1,0:T(8,128)S(1)} %add.149), channel_id=1, source_target_pairs={{0,2},{1,3},{2,0},{3,1},{4,6},{5,7},{6,4},{7,5},{8,10},{9,11},{10,... | collective-permute-start | bytes 294920 | tf_op jit(solution)/shard_map/ppermute | solution.py:278
  139.2 1.5 collective-permute-start.17
  141.5 1.5 collective-permute-start.37
  144.2 3.0 %collective-permute-done.17 = f32[192,256]{1,0:T(8,128)S(1)} collective-permute-done((f32[192,256]{1,0:T(8,128)S(1)}, f32[192,256]{1,0:T(8,128)S(1)}, u32[]{:S(2)}, u32[]{:S(2)}) %collective-permute-start.17) | collective-permute-done | bytes 196640 | tf_op jit(solution)/shard_map/ppermute | solution.py:278
  148.4 2.6 %collective-permute-done.47 = f32[192,256]{1,0:T(8,128)S(1)} collective-permute-done((f32[192,256]{1,0:T(8,128)S(1)}, f32[192,256]{1,0:T(8,128)S(1)}, u32[]{:S(2)}, u32[]{:S(2)}) %collective-permute-start.47) | collective-permute-done | bytes 196640 | tf_op jit(solution)/shard_map/ppermute | solution.py:278
  151.0 1.3 collective-permute-start.48
  152.3 3.3 %collective-permute-done.37 = f32[192,256]{1,0:T(8,128)S(1)} collective-permute-done((f32[192,256]{1,0:T(8,128)S(1)}, f32[192,256]{1,0:T(8,128)S(1)}, u32[]{:S(2)}, u32[]{:S(2)}) %collective-permute-start.37) | collective-permute-done | bytes 196640 | tf_op jit(solution)/shard_map/ppermute | solution.py:278
  157.8 1.2 collective-permute-done.18.got
  159.1 1.5 collective-permute-done.48.got
  160.6 3.2 %collective-permute-done.38.got = f32[384,256]{1,0:T(8,128)S(1)} collective-permute-done((f32[384,256]{1,0:T(8,128)S(1)}, f32[384,256]{1,0:T(8,128)S(1)}, u32[]{:S(2)}, u32[]{:S(2)}) %collective-permute-start.38) | collective-permute-done | bytes 393248 | tf_op jit(solution)/shard_map/ppermute | solution.py:278
  166.0 1.8 %place_chunk_0.1 = (f32[768,1024]{1,0:T(8,128)}, f32[768,1024]{1,0:T(8,128)}) custom-call(s32[2]{0:T(128)S(1)} %pad_add_fusion.8.where_ref, f32[384,256]{1,0:T(8,128)S(1)} %pad_maximum_fusion.5.mine, f32[384,256]{1,0:T(8,128)S(1)} %collective-permute-done.48.got, f32[384,256]{1,0:T(8,128)S(1)} %collective-permute-done.49.other_mine, ...), custom_call_target="tpu_custom_call" | custom-call | bytes 3145728 | tf_op jit(solution)/shard_map/place_chunk_0/pallas_call | solution.py:255
  167.7 1.8 %place_chunk_1.1 = (f32[768,1024]{1,0:T(8,128)}, f32[768,1024]{1,0:T(8,128)}) custom-call(s32[2]{0:T(128)S(1)} %pad_add_fusion.6.where_ref, f32[384,256]{1,0:T(8,128)S(1)} %pad_maximum_fusion.4.mine, f32[384,256]{1,0:T(8,128)S(1)} %collective-permute-done.38.got, ...), custom_call_target="tpu_custom_call", output_to_operand_aliasing={{0}: (5, {}), {1}: (6, {})} | custom-call | bytes 3145728 | tf_op jit(solution)/shard_map/place_chunk_1/pallas_call | solution.py:255
  169.5 1.8 %place_chunk_2.1 = (f32[768,1024]{1,0:T(8,128)}, f32[768,1024]{1,0:T(8,128)}) custom-call(s32[2]{0:T(128)S(1)} %pad_add_fusion.7.where_ref, f32[384,256]{1,0:T(8,128)S(1)} %pad_maximum_fusion.3.mine, f32[384,256]{1,0:T(8,128)S(1)} %collective-permute-done.28.got, ...), custom_call_target="tpu_custom_call", output_to_operand_aliasing={{0}: (5, {}), {1}: (6, {})} | custom-call | bytes 3145728 | tf_op jit(solution)/shard_map/place_chunk_2/pallas_call | solution.py:255
  171.3 1.8 %place_chunk_3.1 = (f32[768,1024]{1,0:T(8,128)}, f32[768,1024]{1,0:T(8,128)}) custom-call(s32[2]{0:T(128)S(1)} %pad_add_fusion.6.where_ref, f32[384,256]{1,0:T(8,128)S(1)} %pad_maximum_fusion.2.mine, f32[384,256]{1,0:T(8,128)S(1)} %collective-permute-done.18.got, ...), custom_call_target="tpu_custom_call", output_to_operand_aliasing={{0}: (5, {}), {1}: (6, {})} | custom-call | bytes 3145728 | tf_op jit(solution)/shard_map/place_chunk_3/pallas_call | solution.py:255
  (162 shorter events, 35.8 us)
Async XLA Ops:
  2.3 4.6 %collective-permute-start = (s32[1,384]{1,0:T(1,128)S(1)}, s32[1,384]{1,0:T(1,128)S(1)}, u32[]{:S(2)}, u32[]{:S(2)}) collective-permute-start(s32[1,384]{1,0:T(1,128)S(1)} %constant_dynamic-update-slice_fusion), channel_id=1, source_target_pairs={{0,1},{1,0},{2,3},{3,2},{4,5},{5,4},{6,7},{7,6},{8,9},{9,8},{10,11... | collective-permute-start | bytes 4616 | tf_op jit(solution)/shard_map/ppermute | solution.py:278
  10.6 5.8 %collective-permute-start.2 = (s32[4,384]{1,0:T(4,128)S(1)}, s32[4,384]{1,0:T(4,128)S(1)}, u32[]{:S(2)}, u32[]{:S(2)}) collective-permute-start(s32[4,384]{1,0:T(4,128)S(1)} %pad_add_fusion.2), channel_id=1, source_target_pairs={{0,6},{1,7},{2,4},{3,5},{4,2},{5,3},{6,0},{7,1},{8,14},{9,15},{10,... | collective-permute-start | bytes 18440 | tf_op jit(solution)/shard_map/ppermute | solution.py:278
  15.7 7.6 %collective-permute-start.5 = (f32[64,768]{1,0:T(8,128)S(1)}, f32[64,768]{1,0:T(8,128)S(1)}, u32[]{:S(2)}, u32[]{:S(2)}) collective-permute-start(f32[64,768]{1,0:T(8,128)S(1)} %constant_dynamic-slice_fusion), channel_id=1, source_target_pairs={{0,6},{1,7},{2,4},{3,5},{4,2},{5,3},{6,0},{7,1},{8,14},{9,15},{10,... | collective-permute-start | bytes 589832 | tf_op jit(solution)/shard_map/ppermute | solution.py:278
  16.5 8.3 %collective-permute-start.3 = (s32[8,384]{1,0:T(8,128)S(1)}, s32[8,384]{1,0:T(8,128)S(1)}, u32[]{:S(2)}, u32[]{:S(2)}) collective-permute-start(s32[8,384]{1,0:T(8,128)S(1)} %pad_add_fusion.1), channel_id=1, source_target_pairs={{0,8},{8,0},{16,24},{24,16},{1,9},{9,1},{17,25},{25,17},{2,10},{10... | collective-permute-start | bytes 36872 | tf_op jit(solution)/shard_map/ppermute | solution.py:278
  23.3 5.7 %collective-permute-start.6 = (f32[64,768]{1,0:T(8,128)S(1)}, f32[64,768]{1,0:T(8,128)S(1)}, u32[]{:S(2)}, u32[]{:S(2)}) collective-permute-start(f32[64,768]{1,0:T(8,128)S(1)} %collective-permute-done.5), channel_id=1, source_target_pairs={{0,16},{8,24},{16,0},{24,8},{1,17},{9,25},{17,1},{25,9},{2,18},{10... | collective-permute-start | bytes 589832 | tf_op jit(solution)/shard_map/ppermute | solution.py:278
  29.1 7.5 %collective-permute-start.7 = (f32[128,768]{1,0:T(8,128)S(1)}, f32[128,768]{1,0:T(8,128)S(1)}, u32[]{:S(2)}, u32[]{:S(2)}) collective-permute-start(f32[128,768]{1,0:T(8,128)S(1)} %pad_maximum_fusion.1), channel_id=1, source_target_pairs={{0,8},{8,0},{16,24},{24,16},{1,9},{9,1},{17,25},{25,17},{2,10},{10... | collective-permute-start | bytes 1179656 | tf_op jit(solution)/shard_map/ppermute | solution.py:278
  33.0 17.3 %all-to-all-start = ((f32[32,4,768]{2,1,0:T(4,128)}), f32[32,4,768]{2,1,0:T(4,128)}, u32[]{:S(2)}, u32[]{:S(2)}) async-start(f32[32,4,768]{2,1,0:T(4,128)} %all_to_all.7), calls=%async_computation | async-start | bytes 786432 | tf_op jit(solution)/shard_map/all_to_all | solution.py:348
  39.2 12.3 %collective-permute-start.8 = (f32[64,768]{1,0:T(8,128)}, f32[64,768]{1,0:T(8,128)S(1)}, u32[]{:S(2)}, u32[]{:S(2)}) collective-permute-start(f32[64,768]{1,0:T(8,128)} %get-tuple-element.26), channel_id=1, source_target_pairs={{0,1},{1,0},{2,3},{3,2},{4,5},{5,4},{6,7},{7,6},{8,9},{9,8},{10,11... | collective-permute-start | bytes 589832 | tf_op jit(solution)/shard_map/ppermute | solution.py:358
  40.9 11.2 %collective-permute-start.9 = (f32[64,768]{1,0:T(8,128)}, f32[64,768]{1,0:T(8,128)S(1)}, u32[]{:S(2)}, u32[]{:S(2)}) collective-permute-start(f32[64,768]{1,0:T(8,128)} %get-tuple-element.27), channel_id=1, source_target_pairs={{0,2},{1,3},{2,0},{3,1},{4,6},{5,7},{6,4},{7,5},{8,10},{9,11},{10,... | collective-permute-start | bytes 589832 | tf_op jit(solution)/shard_map/ppermute | solution.py:358
  42.4 12.7 %collective-permute-start.10 = (f32[64,768]{1,0:T(8,128)}, f32[64,768]{1,0:T(8,128)S(1)}, u32[]{:S(2)}, u32[]{:S(2)}) collective-permute-start(f32[64,768]{1,0:T(8,128)} %get-tuple-element.28), channel_id=1, source_target_pairs={{0,3},{1,2},{2,1},{3,0},{4,7},{5,6},{6,5},{7,4},{8,11},{9,10},{10,... | collective-permute-start | bytes 589832 | tf_op jit(solution)/shard_map/ppermute | solution.py:358
  85.3 5.0 %collective-permute-start.21 = (f32[768,256]{1,0:T(8,128)}, f32[768,256]{1,0:T(8,128)}, u32[]{:S(2)}, u32[]{:S(2)}) collective-permute-start(f32[768,256]{1,0:T(8,128)} %get-tuple-element.34), channel_id=1, source_target_pairs={{0,8},{8,0},{16,24},{24,16},{1,9},{9,1},{17,25},{25,17},{2,10},{10... | collective-permute-start | bytes 2359304 | tf_op jit(solution)/shard_map/ppermute | solution.py:278
  85.8 6.8 %collective-permute-start.31 = (f32[768,256]{1,0:T(8,128)}, f32[768,256]{1,0:T(8,128)}, u32[]{:S(2)}, u32[]{:S(2)}) collective-permute-start(f32[768,256]{1,0:T(8,128)} %get-tuple-element.36), channel_id=1, source_target_pairs={{0,8},{8,0},{16,24},{24,16},{1,9},{9,1},{17,25},{25,17},{2,10},{10... | collective-permute-start | bytes 2359304 | tf_op jit(solution)/shard_map/ppermute | solution.py:278
  85.9 9.0 %collective-permute-start.41 = (f32[768,256]{1,0:T(8,128)}, f32[768,256]{1,0:T(8,128)S(1)}, u32[]{:S(2)}, u32[]{:S(2)}) collective-permute-start(f32[768,256]{1,0:T(8,128)} %copy-done.7), channel_id=1, source_target_pairs={{0,8},{8,0},{16,24},{24,16},{1,9},{9,1},{17,25},{25,17},{2,10},{10... | collective-permute-start | bytes 2359304 | tf_op jit(solution)/shard_map/ppermute | solution.py:278
  89.2 12.0 %collective-permute-start.12 = (f32[384,256]{1,0:T(8,128)S(1)}, f32[384,256]{1,0:T(8,128)S(1)}, u32[]{:S(2)}, u32[]{:S(2)}) collective-permute-start(f32[384,256]{1,0:T(8,128)S(1)} %get-tuple-element.54), channel_id=1, source_target_pairs={{0,1},{1,0},{2,3},{3,2},{4,5},{5,4},{6,7},{7,6},{8,9},{9,8},{10,11... | collective-permute-start | bytes 1179656 | tf_op jit(solution)/shard_map/ppermute | solution.py:278
  91.5 11.3 %collective-permute-start.22 = (f32[384,256]{1,0:T(8,128)S(1)}, f32[384,256]{1,0:T(8,128)S(1)}, u32[]{:S(2)}, u32[]{:S(2)}) collective-permute-start(f32[384,256]{1,0:T(8,128)S(1)} %get-tuple-element.52), channel_id=1, source_target_pairs={{0,2},{1,3},{2,0},{3,1},{4,6},{5,7},{6,4},{7,5},{8,10},{9,11},{10,... | collective-permute-start | bytes 1179656 | tf_op jit(solution)/shard_map/ppermute | solution.py:278
  93.8 14.9 %collective-permute-start.32 = (f32[384,256]{1,0:T(8,128)S(1)}, f32[384,256]{1,0:T(8,128)S(1)}, u32[]{:S(2)}, u32[]{:S(2)}) collective-permute-start(f32[384,256]{1,0:T(8,128)S(1)} %get-tuple-element.50), channel_id=1, source_target_pairs={{0,1},{1,0},{2,3},{3,2},{4,5},{5,4},{6,7},{7,6},{8,9},{9,8},{10,11... | collective-permute-start | bytes 1179656 | tf_op jit(solution)/shard_map/ppermute | solution.py:278
  95.0 15.5 %collective-permute-start.42 = (f32[384,256]{1,0:T(8,128)S(1)}, f32[384,256]{1,0:T(8,128)S(1)}, u32[]{:S(2)}, u32[]{:S(2)}) collective-permute-start(f32[384,256]{1,0:T(8,128)S(1)} %get-tuple-element.48), channel_id=1, source_target_pairs={{0,16},{8,24},{16,0},{24,8},{1,17},{9,25},{17,1},{25,9},{2,18},{10... | collective-permute-start | bytes 1179656 | tf_op jit(solution)/shard_map/ppermute | solution.py:278
  101.2 10.3 %collective-permute-start.13 = (f32[192,256]{1,0:T(8,128)S(1)}, f32[192,256]{1,0:T(8,128)S(1)}, u32[]{:S(2)}, u32[]{:S(2)}) collective-permute-start(f32[192,256]{1,0:T(8,128)S(1)} %get-tuple-element.62), channel_id=1, source_target_pairs={{0,16},{8,24},{16,0},{24,8},{1,17},{9,25},{17,1},{25,9},{2,18},{10... | collective-permute-start | bytes 589832 | tf_op jit(solution)/shard_map/ppermute | solution.py:278
  102.9 12.7 %collective-permute-start.23 = (f32[192,256]{1,0:T(8,128)S(1)}, f32[192,256]{1,0:T(8,128)S(1)}, u32[]{:S(2)}, u32[]{:S(2)}) collective-permute-start(f32[192,256]{1,0:T(8,128)S(1)} %get-tuple-element.60), channel_id=1, source_target_pairs={{0,16},{8,24},{16,0},{24,8},{1,17},{9,25},{17,1},{25,9},{2,18},{10... | collective-permute-start | bytes 589832 | tf_op jit(solution)/shard_map/ppermute | solution.py:278
  108.9 9.4 %collective-permute-start.33 = (f32[192,256]{1,0:T(8,128)S(1)}, f32[192,256]{1,0:T(8,128)S(1)}, u32[]{:S(2)}, u32[]{:S(2)}) collective-permute-start(f32[192,256]{1,0:T(8,128)S(1)} %get-tuple-element.58), channel_id=1, source_target_pairs={{0,16},{8,24},{16,0},{24,8},{1,17},{9,25},{17,1},{25,9},{2,18},{10... | collective-permute-start | bytes 589832 | tf_op jit(solution)/shard_map/ppermute | solution.py:278
  110.5 8.9 %collective-permute-start.43 = (f32[192,256]{1,0:T(8,128)S(1)}, f32[192,256]{1,0:T(8,128)S(1)}, u32[]{:S(2)}, u32[]{:S(2)}) collective-permute-start(f32[192,256]{1,0:T(8,128)S(1)} %get-tuple-element.56), channel_id=1, source_target_pairs={{0,1},{1,0},{2,3},{3,2},{4,5},{5,4},{6,7},{7,6},{8,9},{9,8},{10,11... | collective-permute-start | bytes 589832 | tf_op jit(solution)/shard_map/ppermute | solution.py:278
  111.6 8.9 %collective-permute-start.14 = (f32[96,256]{1,0:T(8,128)S(1)}, f32[96,256]{1,0:T(8,128)S(1)}, u32[]{:S(2)}, u32[]{:S(2)}) collective-permute-start(f32[96,256]{1,0:T(8,128)S(1)} %broadcast_select_fusion.39), channel_id=1, source_target_pairs={{0,2},{1,3},{2,0},{3,1},{4,6},{5,7},{6,4},{7,5},{8,10},{9,11},{10,... | collective-permute-start | bytes 294920 | tf_op jit(solution)/shard_map/ppermute | solution.py:278
  115.5 7.4 %collective-permute-start.24 = (f32[96,256]{1,0:T(8,128)S(1)}, f32[96,256]{1,0:T(8,128)S(1)}, u32[]{:S(2)}, u32[]{:S(2)}) collective-permute-start(f32[96,256]{1,0:T(8,128)S(1)} %broadcast_select_fusion.30), channel_id=1, source_target_pairs={{0,1},{1,0},{2,3},{3,2},{4,5},{5,4},{6,7},{7,6},{8,9},{9,8},{10,11... | collective-permute-start | bytes 294920 | tf_op jit(solution)/shard_map/ppermute | solution.py:278
  118.3 6.2 %collective-permute-start.34 = (f32[96,256]{1,0:T(8,128)S(1)}, f32[96,256]{1,0:T(8,128)S(1)}, u32[]{:S(2)}, u32[]{:S(2)}) collective-permute-start(f32[96,256]{1,0:T(8,128)S(1)} %broadcast_select_fusion.36), channel_id=1, source_target_pairs={{0,2},{1,3},{2,0},{3,1},{4,6},{5,7},{6,4},{7,5},{8,10},{9,11},{10,... | collective-permute-start | bytes 294920 | tf_op jit(solution)/shard_map/ppermute | solution.py:278
  119.4 7.6 %collective-permute-start.44 = (f32[96,256]{1,0:T(8,128)S(1)}, f32[96,256]{1,0:T(8,128)S(1)}, u32[]{:S(2)}, u32[]{:S(2)}) collective-permute-start(f32[96,256]{1,0:T(8,128)S(1)} %broadcast_select_fusion.33), channel_id=1, source_target_pairs={{0,2},{1,3},{2,0},{3,1},{4,6},{5,7},{6,4},{7,5},{8,10},{9,11},{10,... | collective-permute-start | bytes 294920 | tf_op jit(solution)/shard_map/ppermute | solution.py:278
  120.5 8.7 %collective-permute-start.15 = (f32[96,256]{1,0:T(8,128)S(1)}, f32[96,256]{1,0:T(8,128)S(1)}, u32[]{:S(2)}, u32[]{:S(2)}) collective-permute-start(f32[96,256]{1,0:T(8,128)S(1)} %select_add_fusion.3), channel_id=1, source_target_pairs={{0,6},{1,7},{2,4},{3,5},{4,2},{5,3},{6,0},{7,1},{8,14},{9,15},{10,... | collective-permute-start | bytes 294920 | tf_op jit(solution)/shard_map/ppermute | solution.py:278
  123.0 11.1 %collective-permute-start.25 = (f32[96,256]{1,0:T(8,128)S(1)}, f32[96,256]{1,0:T(8,128)S(1)}, u32[]{:S(2)}, u32[]{:S(2)}) collective-permute-start(f32[96,256]{1,0:T(8,128)S(1)} %select_add_fusion.2), channel_id=1, source_target_pairs={{0,6},{1,7},{2,4},{3,5},{4,2},{5,3},{6,0},{7,1},{8,14},{9,15},{10,... | collective-permute-start | bytes 294920 | tf_op jit(solution)/shard_map/ppermute | solution.py:278
  124.6 10.6 %collective-permute-start.35 = (f32[96,256]{1,0:T(8,128)S(1)}, f32[96,256]{1,0:T(8,128)S(1)}, u32[]{:S(2)}, u32[]{:S(2)}) collective-permute-start(f32[96,256]{1,0:T(8,128)S(1)} %select_add_fusion.1), channel_id=1, source_target_pairs={{0,6},{1,7},{2,4},{3,5},{4,2},{5,3},{6,0},{7,1},{8,14},{9,15},{10,... | collective-permute-start | bytes 294920 | tf_op jit(solution)/shard_map/ppermute | solution.py:278
  127.0 11.2 %collective-permute-start.45 = (f32[96,256]{1,0:T(8,128)S(1)}, f32[96,256]{1,0:T(8,128)S(1)}, u32[]{:S(2)}, u32[]{:S(2)}) collective-permute-start(f32[96,256]{1,0:T(8,128)S(1)} %select_add_fusion), channel_id=1, source_target_pairs={{0,6},{1,7},{2,4},{3,5},{4,2},{5,3},{6,0},{7,1},{8,14},{9,15},{10,... | collective-permute-start | bytes 294920 | tf_op jit(solution)/shard_map/ppermute | solution.py:278
  129.2 10.0 %collective-permute-start.16 = (f32[96,256]{1,0:T(8,128)S(1)}, f32[96,256]{1,0:T(8,128)S(1)}, u32[]{:S(2)}, u32[]{:S(2)}) collective-permute-start(f32[96,256]{1,0:T(8,128)S(1)} %add.133), channel_id=1, source_target_pairs={{0,2},{1,3},{2,0},{3,1},{4,6},{5,7},{6,4},{7,5},{8,10},{9,11},{10,... | collective-permute-start | bytes 294920 | tf_op jit(solution)/shard_map/ppermute | solution.py:278
  134.1 6.6 %collective-permute-start.26 = (f32[96,256]{1,0:T(8,128)S(1)}, f32[96,256]{1,0:T(8,128)S(1)}, u32[]{:S(2)}, u32[]{:S(2)}) collective-permute-start(f32[96,256]{1,0:T(8,128)S(1)} %add.141), channel_id=1, source_target_pairs={{0,1},{1,0},{2,3},{3,2},{4,5},{5,4},{6,7},{7,6},{8,9},{9,8},{10,11... | collective-permute-start | bytes 294920 | tf_op jit(solution)/shard_map/ppermute | solution.py:278
  135.2 6.3 %collective-permute-start.36 = (f32[96,256]{1,0:T(8,128)S(1)}, f32[96,256]{1,0:T(8,128)S(1)}, u32[]{:S(2)}, u32[]{:S(2)}) collective-permute-start(f32[96,256]{1,0:T(8,128)S(1)} %add.149), channel_id=1, source_target_pairs={{0,2},{1,3},{2,0},{3,1},{4,6},{5,7},{6,4},{7,5},{8,10},{9,11},{10,... | collective-permute-start | bytes 294920 | tf_op jit(solution)/shard_map/ppermute | solution.py:278
  138.2 4.7 %collective-permute-start.46 = (f32[96,256]{1,0:T(8,128)S(1)}, f32[96,256]{1,0:T(8,128)S(1)}, u32[]{:S(2)}, u32[]{:S(2)}) collective-permute-start(f32[96,256]{1,0:T(8,128)S(1)} %add.157), channel_id=1, source_target_pairs={{0,2},{1,3},{2,0},{3,1},{4,6},{5,7},{6,4},{7,5},{8,10},{9,11},{10,... | collective-permute-start | bytes 294920 | tf_op jit(solution)/shard_map/ppermute | solution.py:278
  139.2 7.9 %collective-permute-start.17 = (f32[192,256]{1,0:T(8,128)S(1)}, f32[192,256]{1,0:T(8,128)S(1)}, u32[]{:S(2)}, u32[]{:S(2)}) collective-permute-start(f32[192,256]{1,0:T(8,128)S(1)} %pad_maximum_fusion.6), channel_id=1, source_target_pairs={{0,16},{8,24},{16,0},{24,8},{1,17},{9,25},{17,1},{25,9},{2,18},{10... | collective-permute-start | bytes 589832 | tf_op jit(solution)/shard_map/ppermute | solution.py:278
  140.8 16.0 %collective-permute-start.27 = (f32[192,256]{1,0:T(8,128)S(1)}, f32[192,256]{1,0:T(8,128)S(1)}, u32[]{:S(2)}, u32[]{:S(2)}) collective-permute-start(f32[192,256]{1,0:T(8,128)S(1)} %pad_maximum_fusion.7), channel_id=1, source_target_pairs={{0,16},{8,24},{16,0},{24,8},{1,17},{9,25},{17,1},{25,9},{2,18},{10... | collective-permute-start | bytes 589832 | tf_op jit(solution)/shard_map/ppermute | solution.py:278
  141.5 14.1 %collective-permute-start.37 = (f32[192,256]{1,0:T(8,128)S(1)}, f32[192,256]{1,0:T(8,128)S(1)}, u32[]{:S(2)}, u32[]{:S(2)}) collective-permute-start(f32[192,256]{1,0:T(8,128)S(1)} %pad_maximum_fusion.8), channel_id=1, source_target_pairs={{0,16},{8,24},{16,0},{24,8},{1,17},{9,25},{17,1},{25,9},{2,18},{10... | collective-permute-start | bytes 589832 | tf_op jit(solution)/shard_map/ppermute | solution.py:278
  143.0 7.9 %collective-permute-start.47 = (f32[192,256]{1,0:T(8,128)S(1)}, f32[192,256]{1,0:T(8,128)S(1)}, u32[]{:S(2)}, u32[]{:S(2)}) collective-permute-start(f32[192,256]{1,0:T(8,128)S(1)} %pad_maximum_fusion.9), channel_id=1, source_target_pairs={{0,1},{1,0},{2,3},{3,2},{4,5},{5,4},{6,7},{7,6},{8,9},{9,8},{10,11... | collective-permute-start | bytes 589832 | tf_op jit(solution)/shard_map/ppermute | solution.py:278
  147.2 11.8 %collective-permute-start.18 = (f32[384,256]{1,0:T(8,128)S(1)}, f32[384,256]{1,0:T(8,128)S(1)}, u32[]{:S(2)}, u32[]{:S(2)}) collective-permute-start(f32[384,256]{1,0:T(8,128)S(1)} %pad_maximum_fusion.2.mine), channel_id=1, source_target_pairs={{0,1},{1,0},{2,3},{3,2},{4,5},{5,4},{6,7},{7,6},{8,9},{9,8},{10,11... | collective-permute-start | bytes 1179656 | tf_op jit(solution)/shard_map/ppermute | solution.py:278
  151.0 9.6 %collective-permute-start.48 = (f32[384,256]{1,0:T(8,128)S(1)}, f32[384,256]{1,0:T(8,128)S(1)}, u32[]{:S(2)}, u32[]{:S(2)}) collective-permute-start(f32[384,256]{1,0:T(8,128)S(1)} %pad_maximum_fusion.5.mine), channel_id=1, source_target_pairs={{0,16},{8,24},{16,0},{24,8},{1,17},{9,25},{17,1},{25,9},{2,18},{10... | collective-permute-start | bytes 1179656 | tf_op jit(solution)/shard_map/ppermute | solution.py:278
  155.6 8.1 %collective-permute-start.38 = (f32[384,256]{1,0:T(8,128)S(1)}, f32[384,256]{1,0:T(8,128)S(1)}, u32[]{:S(2)}, u32[]{:S(2)}) collective-permute-start(f32[384,256]{1,0:T(8,128)S(1)} %pad_maximum_fusion.4.mine), channel_id=1, source_target_pairs={{0,1},{1,0},{2,3},{3,2},{4,5},{5,4},{6,7},{7,6},{8,9},{9,8},{10,11... | collective-permute-start | bytes 1179656 | tf_op jit(solution)/shard_map/ppermute | solution.py:278
  156.8 7.8 %collective-permute-start.28 = (f32[384,256]{1,0:T(8,128)S(1)}, f32[384,256]{1,0:T(8,128)S(1)}, u32[]{:S(2)}, u32[]{:S(2)}) collective-permute-start(f32[384,256]{1,0:T(8,128)S(1)} %pad_maximum_fusion.3.mine), channel_id=1, source_target_pairs={{0,2},{1,3},{2,0},{3,1},{4,6},{5,7},{6,4},{7,5},{8,10},{9,11},{10,... | collective-permute-start | bytes 1179656 | tf_op jit(solution)/shard_map/ppermute | solution.py:278
  157.8 6.9 %collective-permute-start.39 = (f32[384,256]{1,0:T(8,128)S(1)}, f32[384,256]{1,0:T(8,128)S(1)}, u32[]{:S(2)}, u32[]{:S(2)}) collective-permute-start(f32[384,256]{1,0:T(8,128)S(1)} %pad_maximum_fusion.4.mine), channel_id=1, source_target_pairs={{0,8},{8,0},{16,24},{24,16},{1,9},{9,1},{17,25},{25,17},{2,10},{10... | collective-permute-start | bytes 1179656 | tf_op jit(solution)/shard_map/ppermute | solution.py:278
  159.0 6.2 %collective-permute-start.49 = (f32[384,256]{1,0:T(8,128)S(1)}, f32[384,256]{1,0:T(8,128)S(1)}, u32[]{:S(2)}, u32[]{:S(2)}) collective-permute-start(f32[384,256]{1,0:T(8,128)S(1)} %pad_maximum_fusion.5.mine), channel_id=1, source_target_pairs={{0,8},{8,0},{16,24},{24,16},{1,9},{9,1},{17,25},{25,17},{2,10},{10... | collective-permute-start | bytes 1179656 | tf_op jit(solution)/shard_map/ppermute | solution.py:278
  160.6 4.7 %collective-permute-start.50 = (f32[384,256]{1,0:T(8,128)S(1)}, f32[384,256]{1,0:T(8,128)S(1)}, u32[]{:S(2)}, u32[]{:S(2)}) collective-permute-start(f32[384,256]{1,0:T(8,128)S(1)} %collective-permute-done.48.got), channel_id=1, source_target_pairs={{0,8},{8,0},{16,24},{24,16},{1,9},{9,1},{17,25},{25,17},{2,10},{10... | collective-permute-start | bytes 1179656 | tf_op jit(solution)/shard_map/ppermute | solution.py:278
  164.7 4.8 %collective-permute-start.29 = (f32[384,256]{1,0:T(8,128)S(1)}, f32[384,256]{1,0:T(8,128)S(1)}, u32[]{:S(2)}, u32[]{:S(2)}) collective-permute-start(f32[384,256]{1,0:T(8,128)S(1)} %pad_maximum_fusion.3.mine), channel_id=1, source_target_pairs={{0,8},{8,0},{16,24},{24,16},{1,9},{9,1},{17,25},{25,17},{2,10},{10... | collective-permute-start | bytes 1179656 | tf_op jit(solution)/shard_map/ppermute | solution.py:278
  164.7 4.8 %collective-permute-start.30 = (f32[384,256]{1,0:T(8,128)S(1)}, f32[384,256]{1,0:T(8,128)S(1)}, u32[]{:S(2)}, u32[]{:S(2)}) collective-permute-start(f32[384,256]{1,0:T(8,128)S(1)} %collective-permute-done.28.got), channel_id=1, source_target_pairs={{0,8},{8,0},{16,24},{24,16},{1,9},{9,1},{17,25},{25,17},{2,10},{10... | collective-permute-start | bytes 1179656 | tf_op jit(solution)/shard_map/ppermute | solution.py:278
  165.2 6.1 %collective-permute-start.19 = (f32[384,256]{1,0:T(8,128)S(1)}, f32[384,256]{1,0:T(8,128)S(1)}, u32[]{:S(2)}, u32[]{:S(2)}) collective-permute-start(f32[384,256]{1,0:T(8,128)S(1)} %pad_maximum_fusion.2.mine), channel_id=1, source_target_pairs={{0,8},{8,0},{16,24},{24,16},{1,9},{9,1},{17,25},{25,17},{2,10},{10... | collective-permute-start | bytes 1179656 | tf_op jit(solution)/shard_map/ppermute | solution.py:278
  165.3 6.0 %collective-permute-start.20 = (f32[384,256]{1,0:T(8,128)S(1)}, f32[384,256]{1,0:T(8,128)S(1)}, u32[]{:S(2)}, u32[]{:S(2)}) collective-permute-start(f32[384,256]{1,0:T(8,128)S(1)} %collective-permute-done.18.got), channel_id=1, source_target_pairs={{0,8},{8,0},{16,24},{24,16},{1,9},{9,1},{17,25},{25,17},{2,10},{10... | collective-permute-start | bytes 1179656 | tf_op jit(solution)/shard_map/ppermute | solution.py:278
  (20 other events, 98.6 us)

commit v4 on v3

--- a/solution.py
+++ b/solution.py
@@ -10,8 +10,8 @@
 FAN = 25
 CORES = 2
 CHUNKS = 4
-CALLS = 2
-VMEM_LIMIT = 48 * 1024 * 1024
+CALLS = 1
+MIB = 1024 * 1024
 
 
 def split(value):
@@ -60,7 +60,7 @@
         ],
         out_specs=pl.BlockSpec((2 * n_src, block), lambda i: (0, i)),
         out_shape=jax.ShapeDtypeStruct((2 * n_src, targets), jnp.bfloat16),
-        compiler_params=pltpu.CompilerParams(vmem_limit_bytes=VMEM_LIMIT),
+        compiler_params=pltpu.CompilerParams(vmem_limit_bytes=60 * MIB),
         cost_estimate=pl.CostEstimate(
             flops=2 * targets * n_src * FAN, bytes_accessed=4 * targets * n_src, transcendentals=0
         ),
@@ -84,7 +84,7 @@
     return pl.pallas_call(
         cold_kernel,
         out_shape=jax.ShapeDtypeStruct((count, width), jnp.float32),
-        compiler_params=pltpu.CompilerParams(vmem_limit_bytes=VMEM_LIMIT),
+        compiler_params=pltpu.CompilerParams(vmem_limit_bytes=60 * MIB),
         cost_estimate=pl.CostEstimate(
             flops=4 * count * table.size, bytes_accessed=4 * table.size, transcendentals=0
         ),
@@ -115,7 +115,7 @@
         in_specs=[pl.BlockSpec(memory_space=pltpu.SMEM)] + [vmem] * 3,
         out_specs=[vmem] * half,
         out_shape=[jax.ShapeDtypeStruct((slots, width), jnp.float32)] * half,
-        compiler_params=pltpu.CompilerParams(vmem_limit_bytes=VMEM_LIMIT),
+        compiler_params=pltpu.CompilerParams(vmem_limit_bytes=60 * MIB),
         cost_estimate=pl.CostEstimate(
             flops=8 * half * slots * own.size, bytes_accessed=12 * own.size, transcendentals=0
         ),
@@ -202,9 +202,9 @@
     operands = [device, counts, cold_rows, w_self, w_neigh, cotangent, *hot_rows]
     aliases = {}
     if hidden is not None:
+        aliases = {len(operands): 0}
         in_specs.append(pl.BlockSpec(memory_space=pl.ANY))
         operands.append(hidden)
-        aliases = {len(operands) - 1: 0}
     return pl.pallas_call(
         functools.partial(layer_kernel, chunks, len(hot_rows), far_mask),
         grid_spec=pltpu.PrefetchScalarGridSpec(
@@ -222,7 +222,7 @@
         out_shape=[jax.ShapeDtypeStruct((targets, hidden_units), jnp.bfloat16)]
         + [jax.ShapeDtypeStruct((feat_width, cols), jnp.float32)] * (2 * chunks),
         input_output_aliases=aliases,
-        compiler_params=pltpu.CompilerParams(vmem_limit_bytes=VMEM_LIMIT),
+        compiler_params=pltpu.CompilerParams(vmem_limit_bytes=60 * MIB),
         cost_estimate=pl.CostEstimate(
             flops=4 * n_src * wide * (2 * targets + 2 * feat_width),
             bytes_accessed=4 * targets * n_src + 4 * targets * wide,
@@ -232,41 +232,51 @@
     )(*operands)
 
 
-def place_kernel(where_ref, mine, got, other_mine, other_got, *rest):
-    out_self, out_neigh = rest[-2:]
-    mine_here = pl.program_id(0) == where_ref[1]
-    first_core = where_ref[0] == 0
-    for here, own, other in ((mine_here, mine, other_mine), (~mine_here, got, other_got)):
-
-        @pl.when(here & first_core)
-        def _(own=own, other=other):
-            out_self[...] = own[...]
-            out_neigh[...] = other[...]
-
-        @pl.when(here & ~first_core)
-        def _(own=own, other=other):
-            out_self[...] = other[...]
-            out_neigh[...] = own[...]
-
-
-def place(chunk, where, pieces, outs):
+def place_kernel(where_ref, *rest):
+    out_self, out_neigh, sems = rest[-3:]
+    pieces = rest[:-3]
     rows, cols = pieces[0].shape
-    shape = jax.ShapeDtypeStruct((2 * rows, CHUNKS * cols), jnp.float32)
+
+    def put(own, other):
+        copies = []
+        for chunk in range(len(pieces) // 4):
+            first = where_ref[chunk + 1] * rows
+            for k, (out, start) in enumerate(
+                ((own, first), (own, rows - first), (other, first), (other, rows - first))
+            ):
+                there = out.at[pl.ds(pl.multiple_of(start, 8), rows), pl.ds(chunk * cols, cols)]
+                at = 4 * chunk + k
+                copies.append(pltpu.make_async_copy(pieces[at], there, sems.at[at]))
+        for copy in copies:
+            copy.start()
+        for copy in copies:
+            copy.wait()
+
+    @pl.when(where_ref[0] == 0)
+    def _():
+        put(out_self, out_neigh)
+
+    @pl.when(where_ref[0] != 0)
+    def _():
+        put(out_neigh, out_self)
+
+
+def place(where, pieces):
+    rows, cols = pieces[0].shape
+    shape = jax.ShapeDtypeStruct((2 * rows, len(pieces) // 4 * cols), jnp.float32)
     return pl.pallas_call(
         place_kernel,
-        grid_spec=pltpu.PrefetchScalarGridSpec(
-            num_scalar_prefetch=1,
-            grid=(2,),
-            in_specs=[pl.BlockSpec((rows, cols), lambda i, w: (0, 0))] * 4
-            + [pl.BlockSpec(memory_space=pl.ANY)] * len(outs),
-            out_specs=[pl.BlockSpec((rows, cols), lambda i, w: (i, chunk))] * 2,
-        ),
+        in_specs=[pl.BlockSpec(memory_space=pltpu.SMEM)]
+        + [pl.BlockSpec(memory_space=pltpu.VMEM)] * len(pieces),
+        out_specs=[pl.BlockSpec(memory_space=pl.ANY)] * 2,
         out_shape=[shape, shape],
-        input_output_aliases={5: 0, 6: 1} if outs else {},
-        compiler_params=pltpu.CompilerParams(vmem_limit_bytes=VMEM_LIMIT),
-        cost_estimate=pl.CostEstimate(flops=0, bytes_accessed=32 * rows * cols, transcendentals=0),
-        name=f"place_chunk_{chunk}",
-    )(where, *pieces, *outs)
+        scratch_shapes=[pltpu.SemaphoreType.DMA((len(pieces),))],
+        compiler_params=pltpu.CompilerParams(vmem_limit_bytes=16 * MIB),
+        cost_estimate=pl.CostEstimate(
+            flops=0, bytes_accessed=8 * len(pieces) * rows * cols, transcendentals=0
+        ),
+        name="place",
+    )(where, *pieces)
 
 
 class Swap:
@@ -291,12 +301,12 @@
     return found
 
 
-def halve(terms, swap):
+def cut(terms, swap):
     rows = terms[0].shape[0] // 2
     low = functools.reduce(jnp.add, [t[:rows] for t in terms])
     high = functools.reduce(jnp.add, [t[rows:] for t in terms])
-    out = jnp.where(swap.bit == 0, high, low)
-    return [jnp.where(swap.bit == 0, low, high), swap.send(out)]
+    first = swap.bit == 0
+    return jnp.where(first, low, high), jnp.where(first, high, low)
 
 
 def double(value, swap):
@@ -328,30 +338,30 @@
     share = hot_table.shape[0] // lax.axis_size("grp")
     which = functools.reduce(jnp.add, [s.bit * (1 << k) for k, s in enumerate(spread)])
     far_table = far.send(lax.dynamic_slice_in_dim(hot_table, which * share, share, axis=0))
-    for swap in spread:
-        far_table = double(far_table, swap)
-
-    needs = jnp.concatenate([hot_need.reshape(1, -1), cold_need.reshape(1, -1)], axis=1)
-    for swap in along_y + along_z[:-1]:
-        needs = double(needs, swap)
+
+    both = ("grp", "dev")
+    exchange = functools.partial(
+        lax.all_to_all, axis_name=both, split_axis=0, concat_axis=0, tiled=True
+    )
+    devices, cold_slots = cold_need.shape
+    hot_list = jnp.broadcast_to(hot_need.reshape(1, -1), (devices, hot_need.size))
+    asked = exchange(jnp.concatenate([cold_need, hot_list], axis=1))
+    far_table, asked = lax.optimization_barrier((far_table, asked))
+    cold_asked = asked[:, :cold_slots]
+    first = lax.axis_index("grp") * 2 * half + me - lax.rem(me, jnp.int32(half))
     hot_asked = jnp.concatenate(
         [
-            lax.dynamic_slice_in_dim(needs, peer * slots, slots, axis=1)
+            lax.dynamic_slice(asked, (first, cold_slots + peer * slots), (half, slots))
             for peer in (me, me ^ far.mask)
         ],
         axis=1,
     )
-    for swap in [far] + core + along_x:
-        needs = double(needs, swap)
-    first = hot_need.size + (lax.axis_index("grp") * 2 * half + me) * cold_need.shape[1]
-    cold_asked = lax.dynamic_slice_in_dim(needs, first, cold_need.shape[1], axis=1)
-    cold_rows = lax.all_to_all(
-        cold_look_up(cold_asked.reshape(1, -1), cold_table),
-        ("grp", "dev"),
-        split_axis=0,
-        concat_axis=0,
-        tiled=True,
-    )
+    cold_served = cold_look_up(cold_asked.reshape(1, -1), cold_table)
+    for swap in spread[:-1]:
+        far_table = double(far_table, swap)
+    far_table, cold_served = lax.optimization_barrier((far_table, cold_served))
+    far_table = double(far_table, spread[-1])
+    cold_rows = exchange(cold_served)
     served = hot_look_up(half, device, hot_asked, hot_table, far_table)
     pairs = lambda away: [(i, i ^ away) for i in range(2 * half)]
     hot_rows = [served[0]] + [
@@ -360,29 +370,27 @@
     return hot_rows, cold_rows, far.mask
 
 
-def sum_over_devices(terms):
-    (core,), along_x, along_y, along_z = axis_swaps()
+def orders_of_sums():
+    _, along_x, along_y, along_z = axis_swaps()
     near_z, far_z = along_z[:1], along_z[1:]
-    orders = [
+    return [
         along_x + along_y + near_z + far_z,
         along_y + along_x + near_z + far_z,
         near_z + along_x + along_y + far_z,
         along_y + along_x + near_z + far_z,
     ]
-    grads = []
-    for chunk, (keep, send) in enumerate(terms):
-        order = orders[chunk]
-        parts = [keep, core.send(send)]
-        for swap in order[:-1]:
-            parts = halve(parts, swap)
-        value = parts[0] + parts[1]
-        value = value + order[-1].send(value)
-        for swap in order[-2:0:-1]:
-            value = double(value, swap)
-        got = order[0].send(value)
-        where = jnp.stack([core.bit, order[0].bit]).astype(jnp.int32)
-        grads = place(chunk, where, [value, got, core.send(value), core.send(got)], grads)
-    return grads
+
+
+def sum_chunk(parts, core, order):
+    for swap in order[:-1]:
+        own, out = cut(parts, swap)
+        parts = [own, swap.send(out)]
+    value = parts[0] + parts[1]
+    value = value + order[-1].send(value)
+    for swap in order[-2:0:-1]:
+        value = double(value, swap)
+    got = order[0].send(value)
+    return [value, got, core.send(value), core.send(got)]
 
 
 def body(
@@ -392,12 +400,14 @@
     counts = count_matrices(neighbors, self_index, n_src)
     device = jnp.stack([lax.rem(lax.axis_index("grp"), jnp.int32(CORES)), lax.axis_index("dev")])
     hot_rows, cold_rows, far_mask = fetch_rows(hot_table, cold_table, hot_need, cold_need, device)
-    hidden = None
-    terms = []
+    core = axis_swaps()[0][0]
+    orders = orders_of_sums()
+    chunks = CHUNKS // CALLS
+    hidden, sums = None, []
     for call in range(CALLS):
         hidden, *grads = layer(
             call,
-            CHUNKS // CALLS,
+            chunks,
             far_mask,
             device,
             counts,
@@ -408,8 +418,13 @@
             cotangent,
             hidden,
         )
-        terms += list(zip(grads[::2], grads[1::2]))
-    grad_self, grad_neigh = sum_over_devices(terms)
+        for keep, send in zip(grads[::2], grads[1::2]):
+            sums.append([keep, core.send(send)])
+    pieces = []
+    for parts, order in zip(sums, orders):
+        pieces += sum_chunk(parts, core, order)
+    where = jnp.stack([core.bit] + [order[0].bit for order in orders]).astype(jnp.int32)
+    grad_self, grad_neigh = place(where, pieces)
     return (hidden, grad_self, grad_neigh)
 
 

time: 174 us -> 165 us (0.948)
  starting transfers between devices: 61.4 us -> 50.6 us
  blocking collectives: 0 us -> 9.85 us
  local copies, waits for them, and re-layouts: 14.9 us -> 6.81 us
    ppermute x48 -> x43, starting transfers between devices: 54.6 us -> 44.6 us  [send(): return lax.ppermute(value, self.name, self.pairs)]
    all_to_all x0 -> x1, blocking collectives: none -> 9.85 us  [fetch_rows(): asked = exchange(jnp.concatenate([cold_need, hot_list], axis=1))]
    unnamed x34 -> x12, local copies, waits for them, and re-layouts: 11 us -> 1.45 us
    pallas_call x2 -> x1, Pallas kernels: 24.9 us -> 21.5 us  [layer(): pl.pallas_call(functools.partial(layer_kernel, chunks, len(hot_rows), far...]
    pallas_call x1, Pallas kernels: 0.77 us -> 3.42 us  [cold_look_up(): pl.pallas_call(cold_kernel, out_shape=jax.ShapeDtypeStruct((count, width)...]
    pallas_call x4 -> x1, Pallas kernels: 7.12 us -> 4.5 us  [place(): pl.pallas_call(place_kernel, in_specs=[pl.BlockSpec(memory_space=pltpu.SM...]
    select_n x13 -> x12, other arithmetic: 4.09 us -> 3.03 us  [cut(): return (jnp.where(first, low, high), jnp.where(first, high, low))]
    ppermute x48 -> x43, waiting for transfers between devices: 46.8 us -> 47 us  [send(): return lax.ppermute(value, self.name, self.pairs)]
  transfers between devices with their start and end apart: 52 -> 47, of which waited for: 20 -> 18; matrix products, arithmetic and copies ran while one was open for 4% -> 5% of each run, Pallas kernels for 8% -> 9%
where the time goes in v4:
time: 165 us; the launch traced here: 164 us
  starting transfers between devices  50.6 us (31%)
  waiting for transfers between devices  49.9 us (30%)
  Pallas kernels  40.2 us (24%)
  blocking collectives  9.85 us (6%)
  local copies, waits for them, and re-layouts  6.81 us (4%)
  other arithmetic  5.87 us (4%)
    ppermute x43, waiting for transfers between devices, send(): return lax.ppermute(value, self.name, self.pairs)  47 us
    ppermute x43, starting transfers between devices, send(): return lax.ppermute(value, self.name, self.pairs)  44.6 us
    pallas_call x1, Pallas kernels, layer(): pl.pallas_call(functools.partial(layer_kernel, chunks, len(hot_rows), far...  21.5 us
    all_to_all x1, blocking collectives, fetch_rows(): asked = exchange(jnp.concatenate([cold_need, hot_list], axis=1))  9.85 us
    pallas_call x1, Pallas kernels, count_matrices(): pl.pallas_call(count_kernel, grid=(targets // block,), in_specs=[pl.Block...  7.39 us
    pallas_call x1, Pallas kernels, place(): pl.pallas_call(place_kernel, in_specs=[pl.BlockSpec(memory_space=pltpu.SM...  4.5 us
    ppermute x3, starting transfers between devices, fetch_rows(): lax.ppermute(served[away], 'dev', pairs(away))  3.49 us
    pallas_call x1, Pallas kernels, cold_look_up(): pl.pallas_call(cold_kernel, out_shape=jax.ShapeDtypeStruct((count, width)...  3.42 us
  transfers between devices with their start and end apart: 47, of which 18 were waited for; matrix products, arithmetic and copies ran while one was open for 5% of the time, Pallas kernels for 9%

profile of v4, /device:TPU:0, one launch (start us, length us, event | category | flops | bytes accessed | tf_op | source)
XLA Modules:
  0.0 164.5 jit_solution(14373017833140306694)
XLA Ops:
  1.6 5.1 %collective-permute-start = (f32[64,768]{1,0:T(8,128)S(1)}, f32[64,768]{1,0:T(8,128)S(1)}, u32[]{:S(2)}, u32[]{:S(2)}) collective-permute-start(f32[64,768]{1,0:T(8,128)S(1)} %constant_dynamic-slice_fusion), channel_id=1, source_target_pairs={{0,6},{1,7},{2,4},{3,5},{4,2},{5,3},{6,0},{7,1},{8,14},{9,15},{10,... | collective-permute-start | bytes 589832 | tf_op jit(solution)/shard_map/ppermute | solution.py:288
  8.4 9.9 %all_to_all.23 = s32[32,1,260]{2,1,0:T(1,128)S(1)} all-to-all(s32[32,1,260]{2,1,0:T(1,128)S(1)} %all_to_all.15), channel_id=1, replica_groups=mesh['grp'=4,'dev'=8] {'grp','dev'}, dimensions={0} | all-to-all | bytes 66560 | tf_op jit(solution)/shard_map/all_to_all | solution.py:348
  19.6 3.4 %cold_look_up.1 = f32[128,768]{1,0:T(8,128)} custom-call(s32[1,128]{1,0:T(1,128)} %reshape.15.asked_ref, f32[1024,768]{1,0:T(8,128)} %table_ref.1), custom_call_target="tpu_custom_call" | custom-call | flops 402653184 | bytes 3145728 | tf_op jit(solution)/shard_map/cold_look_up/pallas_call | solution.py:84
  23.0 2.2 %collective-permute-done.1 = f32[64,768]{1,0:T(8,128)S(1)} collective-permute-done((f32[64,768]{1,0:T(8,128)S(1)}, f32[64,768]{1,0:T(8,128)S(1)}, u32[]{:S(2)}, u32[]{:S(2)}) %collective-permute-start.1) | collective-permute-done | bytes 196640 | tf_op jit(solution)/shard_map/ppermute | solution.py:288
  26.0 1.9 %all_to_all.18 = f32[32,4,768]{2,1,0:T(4,128)} reshape(f32[128,768]{1,0:T(8,128)} %cold_look_up.1) | data formatting | bytes 786432 | tf_op jit(solution)/shard_map/all_to_all | solution.py:364
  27.9 2.6 %all-to-all-start.1 = ((f32[32,4,768]{2,1,0:T(4,128)}), f32[32,4,768]{2,1,0:T(4,128)S(1)}, u32[]{:S(2)}, u32[]{:S(2)}) async-start(f32[32,4,768]{2,1,0:T(4,128)} %all_to_all.18), calls=%async_computation.1 | async-start | bytes 786432 | tf_op jit(solution)/shard_map/all_to_all | solution.py:364
  32.2 3.4 %hot_look_up.1 = (f32[64,768]{1,0:T(8,128)}, f32[64,768]{1,0:T(8,128)}, f32[64,768]{1,0:T(8,128)}, f32[64,768]{1,0:T(8,128)}) custom-call(s32[2]{0:T(128)} %pad_add_fusion.2.device_ref, s32[4,64]{1,0:T(4,128)} %pad_add_fusion.1.asked_ref, f32[256,768]{1,0:T(8,128)} %own_ref.1, f32[256,768]{1,0:T(8,128)} %pad_maximum_fusion.far_ref), custom_call_target="tpu_custom_call" | custom-call | flops 402653184 | bytes 2359296 | tf_op jit(solution)/shard_map/hot_look_up/pallas_call | solution.py:113
  35.6 1.7 %collective-permute-start.3 = (f32[64,768]{1,0:T(8,128)}, f32[64,768]{1,0:T(8,128)S(1)}, u32[]{:S(2)}, u32[]{:S(2)}) collective-permute-start(f32[64,768]{1,0:T(8,128)} %get-tuple-element.27), channel_id=1, source_target_pairs={{0,1},{1,0},{2,3},{3,2},{4,5},{5,4},{6,7},{7,6},{8,9},{9,8},{10,11... | collective-permute-start | bytes 589832 | tf_op jit(solution)/shard_map/ppermute | solution.py:368
  37.3 1.5 collective-permute-start.4
  39.0 7.4 %count_matrices.1.counts_ref = bf16[768,2048]{1,0:T(8,128)(2,1)} custom-call(s32[25,2048]{1,0:T(8,128)} %bitcast.10, s32[1,2048]{1,0:T(1,128)} %bitcast.13), custom_call_target="tpu_custom_call" | custom-call | flops 39321600 | bytes 3145728 | tf_op jit(solution)/shard_map/count_matrices/pallas_call | solution.py:54
  47.4 2.9 %collective-permute-done.5.rest_3_ = f32[64,768]{1,0:T(8,128)S(1)} collective-permute-done((f32[64,768]{1,0:T(8,128)}, f32[64,768]{1,0:T(8,128)S(1)}, u32[]{:S(2)}, u32[]{:S(2)}) %collective-permute-start.5) | collective-permute-done | bytes 196640 | tf_op jit(solution)/shard_map/ppermute | solution.py:368
  50.9 21.5 %layer_0.1 = (bf16[2048,1024]{1,0:T(8,128)(2,1)}, f32[768,256]{1,0:T(8,128)}, f32[768,256]{1,0:T(8,128)}, f32[768,256]{1,0:T(8,128)}, f32[768,256]{1,0:T(8,128)}...) custom-call(s32[2]{0:T(128)} %pad_add_fusion.2.device_ref, ...), custom_call_target="tpu_custom_call" | custom-call | flops 8858370048 | bytes 11534336 | tf_op jit(solution)/shard_map/layer_0/pallas_call | solution.py:208
  73.5 1.5 collective-permute-done.6
  75.0 1.3 broadcast_select_fusion.7
  76.3 1.7 %collective-permute-start.7 = (f32[384,256]{1,0:T(8,128)S(1)}, f32[384,256]{1,0:T(8,128)S(1)}, u32[]{:S(2)}, u32[]{:S(2)}) collective-permute-start(f32[384,256]{1,0:T(8,128)S(1)} %get-tuple-element.48), channel_id=1, source_target_pairs={{0,16},{8,24},{16,0},{24,8},{1,17},{9,25},{17,1},{25,9},{2,18},{10... | collective-permute-start | bytes 1179656 | tf_op jit(solution)/shard_map/ppermute | solution.py:288
  77.9 1.2 broadcast_select_fusion.5
  79.2 1.0 collective-permute-start.17
  80.5 1.1 collective-permute-start.37
  81.6 5.9 %collective-permute-done.7 = f32[384,256]{1,0:T(8,128)S(1)} collective-permute-done((f32[384,256]{1,0:T(8,128)S(1)}, f32[384,256]{1,0:T(8,128)S(1)}, u32[]{:S(2)}, u32[]{:S(2)}) %collective-permute-start.7) | collective-permute-done | bytes 393248 | tf_op jit(solution)/shard_map/ppermute | solution.py:288
  87.6 1.1 collective-permute-start.8
  88.7 2.5 %collective-permute-done.17 = f32[384,256]{1,0:T(8,128)S(1)} collective-permute-done((f32[384,256]{1,0:T(8,128)S(1)}, f32[384,256]{1,0:T(8,128)S(1)}, u32[]{:S(2)}, u32[]{:S(2)}) %collective-permute-start.17) | collective-permute-done | bytes 393248 | tf_op jit(solution)/shard_map/ppermute | solution.py:288
  91.8 1.7 %collective-permute-start.28 = (f32[192,256]{1,0:T(8,128)S(1)}, f32[192,256]{1,0:T(8,128)S(1)}, u32[]{:S(2)}, u32[]{:S(2)}) collective-permute-start(f32[192,256]{1,0:T(8,128)S(1)} %get-tuple-element.52), channel_id=1, source_target_pairs={{0,16},{8,24},{16,0},{24,8},{1,17},{9,25},{17,1},{25,9},{2,18},{10... | collective-permute-start | bytes 589832 | tf_op jit(solution)/shard_map/ppermute | solution.py:288
  93.5 6.2 %collective-permute-done.37 = f32[384,256]{1,0:T(8,128)S(1)} collective-permute-done((f32[384,256]{1,0:T(8,128)S(1)}, f32[384,256]{1,0:T(8,128)S(1)}, u32[]{:S(2)}, u32[]{:S(2)}) %collective-permute-start.37) | collective-permute-done | bytes 393248 | tf_op jit(solution)/shard_map/ppermute | solution.py:288
  100.2 2.5 %collective-permute-done.8 = f32[192,256]{1,0:T(8,128)S(1)} collective-permute-done((f32[192,256]{1,0:T(8,128)S(1)}, f32[192,256]{1,0:T(8,128)S(1)}, u32[]{:S(2)}, u32[]{:S(2)}) %collective-permute-start.8) | collective-permute-done | bytes 196640 | tf_op jit(solution)/shard_map/ppermute | solution.py:288
  102.9 2.1 %collective-permute-start.19 = (f32[96,256]{1,0:T(8,128)S(1)}, f32[96,256]{1,0:T(8,128)S(1)}, u32[]{:S(2)}, u32[]{:S(2)}) collective-permute-start(f32[96,256]{1,0:T(8,128)S(1)} %broadcast_select_fusion.36), channel_id=1, source_target_pairs={{0,2},{1,3},{2,0},{3,1},{4,6},{5,7},{6,4},{7,5},{8,10},{9,11},{10,... | collective-permute-start | bytes 294920 | tf_op jit(solution)/shard_map/ppermute | solution.py:288
  105.0 1.0 collective-permute-start.29
  106.1 2.1 %collective-permute-done.9 = f32[96,256]{1,0:T(8,128)S(1)} collective-permute-done((f32[96,256]{1,0:T(8,128)S(1)}, f32[96,256]{1,0:T(8,128)S(1)}, u32[]{:S(2)}, u32[]{:S(2)}) %collective-permute-start.9) | collective-permute-done | bytes 98336 | tf_op jit(solution)/shard_map/ppermute | solution.py:288
  108.3 1.8 %collective-permute-start.10 = (f32[96,256]{1,0:T(8,128)S(1)}, f32[96,256]{1,0:T(8,128)S(1)}, u32[]{:S(2)}, u32[]{:S(2)}) collective-permute-start(f32[96,256]{1,0:T(8,128)S(1)} %select_add_fusion.3), channel_id=1, source_target_pairs={{0,6},{1,7},{2,4},{3,5},{4,2},{5,3},{6,0},{7,1},{8,14},{9,15},{10,... | collective-permute-start | bytes 294920 | tf_op jit(solution)/shard_map/ppermute | solution.py:288
  110.2 2.1 %collective-permute-start.20 = (f32[96,256]{1,0:T(8,128)S(1)}, f32[96,256]{1,0:T(8,128)S(1)}, u32[]{:S(2)}, u32[]{:S(2)}) collective-permute-start(f32[96,256]{1,0:T(8,128)S(1)} %select_add_fusion.2), channel_id=1, source_target_pairs={{0,6},{1,7},{2,4},{3,5},{4,2},{5,3},{6,0},{7,1},{8,14},{9,15},{10,... | collective-permute-start | bytes 294920 | tf_op jit(solution)/shard_map/ppermute | solution.py:288
  112.4 1.8 %collective-permute-start.30 = (f32[96,256]{1,0:T(8,128)S(1)}, f32[96,256]{1,0:T(8,128)S(1)}, u32[]{:S(2)}, u32[]{:S(2)}) collective-permute-start(f32[96,256]{1,0:T(8,128)S(1)} %select_add_fusion.1), channel_id=1, source_target_pairs={{0,6},{1,7},{2,4},{3,5},{4,2},{5,3},{6,0},{7,1},{8,14},{9,15},{10,... | collective-permute-start | bytes 294920 | tf_op jit(solution)/shard_map/ppermute | solution.py:288
  114.2 2.1 %collective-permute-start.40 = (f32[96,256]{1,0:T(8,128)S(1)}, f32[96,256]{1,0:T(8,128)S(1)}, u32[]{:S(2)}, u32[]{:S(2)}) collective-permute-start(f32[96,256]{1,0:T(8,128)S(1)} %select_add_fusion), channel_id=1, source_target_pairs={{0,6},{1,7},{2,4},{3,5},{4,2},{5,3},{6,0},{7,1},{8,14},{9,15},{10,... | collective-permute-start | bytes 294920 | tf_op jit(solution)/shard_map/ppermute | solution.py:288
  116.4 4.8 %collective-permute-start.11 = (f32[96,256]{1,0:T(8,128)S(1)}, f32[96,256]{1,0:T(8,128)S(1)}, u32[]{:S(2)}, u32[]{:S(2)}) collective-permute-start(f32[96,256]{1,0:T(8,128)S(1)} %add.140), channel_id=1, source_target_pairs={{0,2},{1,3},{2,0},{3,1},{4,6},{5,7},{6,4},{7,5},{8,10},{9,11},{10,... | collective-permute-start | bytes 294920 | tf_op jit(solution)/shard_map/ppermute | solution.py:288
  121.2 3.0 %collective-permute-start.21 = (f32[96,256]{1,0:T(8,128)S(1)}, f32[96,256]{1,0:T(8,128)S(1)}, u32[]{:S(2)}, u32[]{:S(2)}) collective-permute-start(f32[96,256]{1,0:T(8,128)S(1)} %add.148), channel_id=1, source_target_pairs={{0,2},{1,3},{2,0},{3,1},{4,6},{5,7},{6,4},{7,5},{8,10},{9,11},{10,... | collective-permute-start | bytes 294920 | tf_op jit(solution)/shard_map/ppermute | solution.py:288
  124.2 1.2 collective-permute-start.31
  125.4 1.5 collective-permute-start.41
  126.9 1.0 collective-permute-start.12
  128.5 1.5 collective-permute-done.31
  130.5 1.6 %collective-permute-start.42 = (f32[192,256]{1,0:T(8,128)S(1)}, f32[192,256]{1,0:T(8,128)S(1)}, u32[]{:S(2)}, u32[]{:S(2)}) collective-permute-start(f32[192,256]{1,0:T(8,128)S(1)} %pad_maximum_fusion.9), channel_id=1, source_target_pairs={{0,16},{8,24},{16,0},{24,8},{1,17},{9,25},{17,1},{25,9},{2,18},{10... | collective-permute-start | bytes 589832 | tf_op jit(solution)/shard_map/ppermute | solution.py:288
  133.6 2.4 %collective-permute-done.22 = f32[192,256]{1,0:T(8,128)S(1)} collective-permute-done((f32[192,256]{1,0:T(8,128)S(1)}, f32[192,256]{1,0:T(8,128)S(1)}, u32[]{:S(2)}, u32[]{:S(2)}) %collective-permute-start.22) | collective-permute-done | bytes 196640 | tf_op jit(solution)/shard_map/ppermute | solution.py:288
  136.1 4.1 %collective-permute-done.32 = f32[192,256]{1,0:T(8,128)S(1)} collective-permute-done((f32[192,256]{1,0:T(8,128)S(1)}, f32[192,256]{1,0:T(8,128)S(1)}, u32[]{:S(2)}, u32[]{:S(2)}) %collective-permute-start.32) | collective-permute-done | bytes 196640 | tf_op jit(solution)/shard_map/ppermute | solution.py:288
  140.1 1.1 collective-permute-start.23
  141.3 3.1 %collective-permute-done.42 = f32[192,256]{1,0:T(8,128)S(1)} collective-permute-done((f32[192,256]{1,0:T(8,128)S(1)}, f32[192,256]{1,0:T(8,128)S(1)}, u32[]{:S(2)}, u32[]{:S(2)}) %collective-permute-start.42) | collective-permute-done | bytes 196640 | tf_op jit(solution)/shard_map/ppermute | solution.py:288
  144.4 1.5 collective-permute-start.33
  145.9 3.8 %collective-permute-done.13.rest_1_ = f32[384,256]{1,0:T(8,128)S(1)} collective-permute-done((f32[384,256]{1,0:T(8,128)S(1)}, f32[384,256]{1,0:T(8,128)S(1)}, u32[]{:S(2)}, u32[]{:S(2)}) %collective-permute-start.13) | collective-permute-done | bytes 393248 | tf_op jit(solution)/shard_map/ppermute | solution.py:288
  151.2 5.0 %collective-permute-done.33.rest_9_ = f32[384,256]{1,0:T(8,128)} collective-permute-done((f32[384,256]{1,0:T(8,128)S(1)}, f32[384,256]{1,0:T(8,128)}, u32[]{:S(2)}, u32[]{:S(2)}) %collective-permute-start.33) | collective-permute-done | bytes 393248 | tf_op jit(solution)/shard_map/ppermute | solution.py:288
  156.1 1.6 collective-permute-done.43.rest_13_
  158.2 1.6 collective-permute-done.45.rest_15_
  159.8 4.5 %place.1 = (f32[768,1024]{1,0:T(8,128)}, f32[768,1024]{1,0:T(8,128)}) custom-call(s32[5]{0:T(128)S(1)} %stack.29.where_ref, f32[384,256]{1,0:T(8,128)S(1)} %pad_maximum_fusion.2.rest_0_, f32[384,256]{1,0:T(8,128)S(1)} %collective-permute-done.13.rest_1_, f32[384,256]{1,0:T(8,128)S(1)} %collective-permute-done.14.rest_2_, ...), custom_call_target="tpu_custom_call" | custom-call | bytes 12582912 | tf_op jit(solution)/shard_map/place/pallas_call | solution.py:267
  (117 shorter events, 16.0 us)
Async XLA Ops:
  1.6 16.6 %collective-permute-start = (f32[64,768]{1,0:T(8,128)S(1)}, f32[64,768]{1,0:T(8,128)S(1)}, u32[]{:S(2)}, u32[]{:S(2)}) collective-permute-start(f32[64,768]{1,0:T(8,128)S(1)} %constant_dynamic-slice_fusion), channel_id=1, source_target_pairs={{0,6},{1,7},{2,4},{3,5},{4,2},{5,3},{6,0},{7,1},{8,14},{9,15},{10,... | collective-permute-start | bytes 589832 | tf_op jit(solution)/shard_map/ppermute | solution.py:288
  18.2 7.0 %collective-permute-start.1 = (f32[64,768]{1,0:T(8,128)S(1)}, f32[64,768]{1,0:T(8,128)S(1)}, u32[]{:S(2)}, u32[]{:S(2)}) collective-permute-start(f32[64,768]{1,0:T(8,128)S(1)} %collective-permute-done), channel_id=1, source_target_pairs={{0,16},{8,24},{16,0},{24,8},{1,17},{9,25},{17,1},{25,9},{2,18},{10... | collective-permute-start | bytes 589832 | tf_op jit(solution)/shard_map/ppermute | solution.py:288
  25.3 5.9 %collective-permute-start.2 = (f32[128,768]{1,0:T(8,128)S(1)}, f32[128,768]{1,0:T(8,128)S(1)}, u32[]{:S(2)}, u32[]{:S(2)}) collective-permute-start(f32[128,768]{1,0:T(8,128)S(1)} %pad_maximum_fusion.1), channel_id=1, source_target_pairs={{0,8},{8,0},{16,24},{24,16},{1,9},{9,1},{17,25},{25,17},{2,10},{10... | collective-permute-start | bytes 1179656 | tf_op jit(solution)/shard_map/ppermute | solution.py:288
  27.9 18.6 %all-to-all-start.1 = ((f32[32,4,768]{2,1,0:T(4,128)}), f32[32,4,768]{2,1,0:T(4,128)S(1)}, u32[]{:S(2)}, u32[]{:S(2)}) async-start(f32[32,4,768]{2,1,0:T(4,128)} %all_to_all.18), calls=%async_computation.1 | async-start | bytes 786432 | tf_op jit(solution)/shard_map/all_to_all | solution.py:364
  35.6 11.8 %collective-permute-start.3 = (f32[64,768]{1,0:T(8,128)}, f32[64,768]{1,0:T(8,128)S(1)}, u32[]{:S(2)}, u32[]{:S(2)}) collective-permute-start(f32[64,768]{1,0:T(8,128)} %get-tuple-element.27), channel_id=1, source_target_pairs={{0,1},{1,0},{2,3},{3,2},{4,5},{5,4},{6,7},{7,6},{8,9},{9,8},{10,11... | collective-permute-start | bytes 589832 | tf_op jit(solution)/shard_map/ppermute | solution.py:368
  37.3 10.1 %collective-permute-start.4 = (f32[64,768]{1,0:T(8,128)}, f32[64,768]{1,0:T(8,128)S(1)}, u32[]{:S(2)}, u32[]{:S(2)}) collective-permute-start(f32[64,768]{1,0:T(8,128)} %get-tuple-element.28), channel_id=1, source_target_pairs={{0,2},{1,3},{2,0},{3,1},{4,6},{5,7},{6,4},{7,5},{8,10},{9,11},{10,... | collective-permute-start | bytes 589832 | tf_op jit(solution)/shard_map/ppermute | solution.py:368
  38.7 11.5 %collective-permute-start.5 = (f32[64,768]{1,0:T(8,128)}, f32[64,768]{1,0:T(8,128)S(1)}, u32[]{:S(2)}, u32[]{:S(2)}) collective-permute-start(f32[64,768]{1,0:T(8,128)} %get-tuple-element.29), channel_id=1, source_target_pairs={{0,3},{1,2},{2,1},{3,0},{4,7},{5,6},{6,5},{7,4},{8,11},{9,10},{10,... | collective-permute-start | bytes 589832 | tf_op jit(solution)/shard_map/ppermute | solution.py:368
  72.4 7.8 %copy-start.1 = (f32[768,256]{1,0:T(8,128)S(1)}, f32[768,256]{1,0:T(8,128)}, u32[]{:S(2)}) copy-start(f32[768,256]{1,0:T(8,128)} %get-tuple-element.35) | copy-start | bytes 2359300
  72.4 2.6 %collective-permute-start.6 = (f32[768,256]{1,0:T(8,128)}, f32[768,256]{1,0:T(8,128)S(1)}, u32[]{:S(2)}, u32[]{:S(2)}) collective-permute-start(f32[768,256]{1,0:T(8,128)} %get-tuple-element.32), channel_id=1, source_target_pairs={{0,8},{8,0},{16,24},{24,16},{1,9},{9,1},{17,25},{25,17},{2,10},{10... | collective-permute-start | bytes 2359304 | tf_op jit(solution)/shard_map/ppermute | solution.py:288
  72.5 5.4 %collective-permute-start.16 = (f32[768,256]{1,0:T(8,128)}, f32[768,256]{1,0:T(8,128)S(1)}, u32[]{:S(2)}, u32[]{:S(2)}) collective-permute-start(f32[768,256]{1,0:T(8,128)} %get-tuple-element.34), channel_id=1, source_target_pairs={{0,8},{8,0},{16,24},{24,16},{1,9},{9,1},{17,25},{25,17},{2,10},{10... | collective-permute-start | bytes 2359304 | tf_op jit(solution)/shard_map/ppermute | solution.py:288
  73.0 7.2 %collective-permute-start.26 = (f32[768,256]{1,0:T(8,128)}, f32[768,256]{1,0:T(8,128)S(1)}, u32[]{:S(2)}, u32[]{:S(2)}) collective-permute-start(f32[768,256]{1,0:T(8,128)} %get-tuple-element.36), channel_id=1, source_target_pairs={{0,8},{8,0},{16,24},{24,16},{1,9},{9,1},{17,25},{25,17},{2,10},{10... | collective-permute-start | bytes 2359304 | tf_op jit(solution)/shard_map/ppermute | solution.py:288
  73.1 7.3 %collective-permute-start.36 = (f32[768,256]{1,0:T(8,128)}, f32[768,256]{1,0:T(8,128)S(1)}, u32[]{:S(2)}, u32[]{:S(2)}) collective-permute-start(f32[768,256]{1,0:T(8,128)} %get-tuple-element.38), channel_id=1, source_target_pairs={{0,8},{8,0},{16,24},{24,16},{1,9},{9,1},{17,25},{25,17},{2,10},{10... | collective-permute-start | bytes 2359304 | tf_op jit(solution)/shard_map/ppermute | solution.py:288
  76.3 11.2 %collective-permute-start.7 = (f32[384,256]{1,0:T(8,128)S(1)}, f32[384,256]{1,0:T(8,128)S(1)}, u32[]{:S(2)}, u32[]{:S(2)}) collective-permute-start(f32[384,256]{1,0:T(8,128)S(1)} %get-tuple-element.48), channel_id=1, source_target_pairs={{0,16},{8,24},{16,0},{24,8},{1,17},{9,25},{17,1},{25,9},{2,18},{10... | collective-permute-start | bytes 1179656 | tf_op jit(solution)/shard_map/ppermute | solution.py:288
  79.2 12.1 %collective-permute-start.17 = (f32[384,256]{1,0:T(8,128)S(1)}, f32[384,256]{1,0:T(8,128)S(1)}, u32[]{:S(2)}, u32[]{:S(2)}) collective-permute-start(f32[384,256]{1,0:T(8,128)S(1)} %get-tuple-element.46), channel_id=1, source_target_pairs={{0,1},{1,0},{2,3},{3,2},{4,5},{5,4},{6,7},{7,6},{8,9},{9,8},{10,11... | collective-permute-start | bytes 1179656 | tf_op jit(solution)/shard_map/ppermute | solution.py:288
  80.3 11.5 %collective-permute-start.27 = (f32[384,256]{1,0:T(8,128)S(1)}, f32[384,256]{1,0:T(8,128)S(1)}, u32[]{:S(2)}, u32[]{:S(2)}) collective-permute-start(f32[384,256]{1,0:T(8,128)S(1)} %get-tuple-element.44), channel_id=1, source_target_pairs={{0,2},{1,3},{2,0},{3,1},{4,6},{5,7},{6,4},{7,5},{8,10},{9,11},{10,... | collective-permute-start | bytes 1179656 | tf_op jit(solution)/shard_map/ppermute | solution.py:288
  80.5 19.1 %collective-permute-start.37 = (f32[384,256]{1,0:T(8,128)S(1)}, f32[384,256]{1,0:T(8,128)S(1)}, u32[]{:S(2)}, u32[]{:S(2)}) collective-permute-start(f32[384,256]{1,0:T(8,128)S(1)} %get-tuple-element.42), channel_id=1, source_target_pairs={{0,1},{1,0},{2,3},{3,2},{4,5},{5,4},{6,7},{7,6},{8,9},{9,8},{10,11... | collective-permute-start | bytes 1179656 | tf_op jit(solution)/shard_map/ppermute | solution.py:288
  87.6 15.2 %collective-permute-start.8 = (f32[192,256]{1,0:T(8,128)S(1)}, f32[192,256]{1,0:T(8,128)S(1)}, u32[]{:S(2)}, u32[]{:S(2)}) collective-permute-start(f32[192,256]{1,0:T(8,128)S(1)} %get-tuple-element.56), channel_id=1, source_target_pairs={{0,1},{1,0},{2,3},{3,2},{4,5},{5,4},{6,7},{7,6},{8,9},{9,8},{10,11... | collective-permute-start | bytes 589832 | tf_op jit(solution)/shard_map/ppermute | solution.py:288
  91.3 11.6 %collective-permute-start.18 = (f32[192,256]{1,0:T(8,128)S(1)}, f32[192,256]{1,0:T(8,128)S(1)}, u32[]{:S(2)}, u32[]{:S(2)}) collective-permute-start(f32[192,256]{1,0:T(8,128)S(1)} %get-tuple-element.54), channel_id=1, source_target_pairs={{0,16},{8,24},{16,0},{24,8},{1,17},{9,25},{17,1},{25,9},{2,18},{10... | collective-permute-start | bytes 589832 | tf_op jit(solution)/shard_map/ppermute | solution.py:288
  91.8 13.1 %collective-permute-start.28 = (f32[192,256]{1,0:T(8,128)S(1)}, f32[192,256]{1,0:T(8,128)S(1)}, u32[]{:S(2)}, u32[]{:S(2)}) collective-permute-start(f32[192,256]{1,0:T(8,128)S(1)} %get-tuple-element.52), channel_id=1, source_target_pairs={{0,16},{8,24},{16,0},{24,8},{1,17},{9,25},{17,1},{25,9},{2,18},{10... | collective-permute-start | bytes 589832 | tf_op jit(solution)/shard_map/ppermute | solution.py:288
  99.7 6.3 %collective-permute-start.38 = (f32[192,256]{1,0:T(8,128)S(1)}, f32[192,256]{1,0:T(8,128)S(1)}, u32[]{:S(2)}, u32[]{:S(2)}) collective-permute-start(f32[192,256]{1,0:T(8,128)S(1)} %get-tuple-element.50), channel_id=1, source_target_pairs={{0,16},{8,24},{16,0},{24,8},{1,17},{9,25},{17,1},{25,9},{2,18},{10... | collective-permute-start | bytes 589832 | tf_op jit(solution)/shard_map/ppermute | solution.py:288
  102.8 5.5 %collective-permute-start.9 = (f32[96,256]{1,0:T(8,128)S(1)}, f32[96,256]{1,0:T(8,128)S(1)}, u32[]{:S(2)}, u32[]{:S(2)}) collective-permute-start(f32[96,256]{1,0:T(8,128)S(1)} %broadcast_select_fusion.39), channel_id=1, source_target_pairs={{0,2},{1,3},{2,0},{3,1},{4,6},{5,7},{6,4},{7,5},{8,10},{9,11},{10,... | collective-permute-start | bytes 294920 | tf_op jit(solution)/shard_map/ppermute | solution.py:288
  102.9 7.3 %collective-permute-start.19 = (f32[96,256]{1,0:T(8,128)S(1)}, f32[96,256]{1,0:T(8,128)S(1)}, u32[]{:S(2)}, u32[]{:S(2)}) collective-permute-start(f32[96,256]{1,0:T(8,128)S(1)} %broadcast_select_fusion.36), channel_id=1, source_target_pairs={{0,2},{1,3},{2,0},{3,1},{4,6},{5,7},{6,4},{7,5},{8,10},{9,11},{10,... | collective-permute-start | bytes 294920 | tf_op jit(solution)/shard_map/ppermute | solution.py:288
  105.0 7.3 %collective-permute-start.29 = (f32[96,256]{1,0:T(8,128)S(1)}, f32[96,256]{1,0:T(8,128)S(1)}, u32[]{:S(2)}, u32[]{:S(2)}) collective-permute-start(f32[96,256]{1,0:T(8,128)S(1)} %broadcast_select_fusion.30), channel_id=1, source_target_pairs={{0,1},{1,0},{2,3},{3,2},{4,5},{5,4},{6,7},{7,6},{8,9},{9,8},{10,11... | collective-permute-start | bytes 294920 | tf_op jit(solution)/shard_map/ppermute | solution.py:288
  106.1 8.1 %collective-permute-start.39 = (f32[96,256]{1,0:T(8,128)S(1)}, f32[96,256]{1,0:T(8,128)S(1)}, u32[]{:S(2)}, u32[]{:S(2)}) collective-permute-start(f32[96,256]{1,0:T(8,128)S(1)} %broadcast_select_fusion.33), channel_id=1, source_target_pairs={{0,2},{1,3},{2,0},{3,1},{4,6},{5,7},{6,4},{7,5},{8,10},{9,11},{10,... | collective-permute-start | bytes 294920 | tf_op jit(solution)/shard_map/ppermute | solution.py:288
  108.3 8.0 %collective-permute-start.10 = (f32[96,256]{1,0:T(8,128)S(1)}, f32[96,256]{1,0:T(8,128)S(1)}, u32[]{:S(2)}, u32[]{:S(2)}) collective-permute-start(f32[96,256]{1,0:T(8,128)S(1)} %select_add_fusion.3), channel_id=1, source_target_pairs={{0,6},{1,7},{2,4},{3,5},{4,2},{5,3},{6,0},{7,1},{8,14},{9,15},{10,... | collective-permute-start | bytes 294920 | tf_op jit(solution)/shard_map/ppermute | solution.py:288
  110.2 11.0 %collective-permute-start.20 = (f32[96,256]{1,0:T(8,128)S(1)}, f32[96,256]{1,0:T(8,128)S(1)}, u32[]{:S(2)}, u32[]{:S(2)}) collective-permute-start(f32[96,256]{1,0:T(8,128)S(1)} %select_add_fusion.2), channel_id=1, source_target_pairs={{0,6},{1,7},{2,4},{3,5},{4,2},{5,3},{6,0},{7,1},{8,14},{9,15},{10,... | collective-permute-start | bytes 294920 | tf_op jit(solution)/shard_map/ppermute | solution.py:288
  112.4 11.8 %collective-permute-start.30 = (f32[96,256]{1,0:T(8,128)S(1)}, f32[96,256]{1,0:T(8,128)S(1)}, u32[]{:S(2)}, u32[]{:S(2)}) collective-permute-start(f32[96,256]{1,0:T(8,128)S(1)} %select_add_fusion.1), channel_id=1, source_target_pairs={{0,6},{1,7},{2,4},{3,5},{4,2},{5,3},{6,0},{7,1},{8,14},{9,15},{10,... | collective-permute-start | bytes 294920 | tf_op jit(solution)/shard_map/ppermute | solution.py:288
  114.2 11.1 %collective-permute-start.40 = (f32[96,256]{1,0:T(8,128)S(1)}, f32[96,256]{1,0:T(8,128)S(1)}, u32[]{:S(2)}, u32[]{:S(2)}) collective-permute-start(f32[96,256]{1,0:T(8,128)S(1)} %select_add_fusion), channel_id=1, source_target_pairs={{0,6},{1,7},{2,4},{3,5},{4,2},{5,3},{6,0},{7,1},{8,14},{9,15},{10,... | collective-permute-start | bytes 294920 | tf_op jit(solution)/shard_map/ppermute | solution.py:288
  116.4 10.5 %collective-permute-start.11 = (f32[96,256]{1,0:T(8,128)S(1)}, f32[96,256]{1,0:T(8,128)S(1)}, u32[]{:S(2)}, u32[]{:S(2)}) collective-permute-start(f32[96,256]{1,0:T(8,128)S(1)} %add.140), channel_id=1, source_target_pairs={{0,2},{1,3},{2,0},{3,1},{4,6},{5,7},{6,4},{7,5},{8,10},{9,11},{10,... | collective-permute-start | bytes 294920 | tf_op jit(solution)/shard_map/ppermute | solution.py:288
  121.2 6.8 %collective-permute-start.21 = (f32[96,256]{1,0:T(8,128)S(1)}, f32[96,256]{1,0:T(8,128)S(1)}, u32[]{:S(2)}, u32[]{:S(2)}) collective-permute-start(f32[96,256]{1,0:T(8,128)S(1)} %add.148), channel_id=1, source_target_pairs={{0,2},{1,3},{2,0},{3,1},{4,6},{5,7},{6,4},{7,5},{8,10},{9,11},{10,... | collective-permute-start | bytes 294920 | tf_op jit(solution)/shard_map/ppermute | solution.py:288
  124.2 5.7 %collective-permute-start.31 = (f32[96,256]{1,0:T(8,128)S(1)}, f32[96,256]{1,0:T(8,128)S(1)}, u32[]{:S(2)}, u32[]{:S(2)}) collective-permute-start(f32[96,256]{1,0:T(8,128)S(1)} %add.156), channel_id=1, source_target_pairs={{0,1},{1,0},{2,3},{3,2},{4,5},{5,4},{6,7},{7,6},{8,9},{9,8},{10,11... | collective-permute-start | bytes 294920 | tf_op jit(solution)/shard_map/ppermute | solution.py:288
  125.4 5.1 %collective-permute-start.41 = (f32[96,256]{1,0:T(8,128)S(1)}, f32[96,256]{1,0:T(8,128)S(1)}, u32[]{:S(2)}, u32[]{:S(2)}) collective-permute-start(f32[96,256]{1,0:T(8,128)S(1)} %add.164), channel_id=1, source_target_pairs={{0,2},{1,3},{2,0},{3,1},{4,6},{5,7},{6,4},{7,5},{8,10},{9,11},{10,... | collective-permute-start | bytes 294920 | tf_op jit(solution)/shard_map/ppermute | solution.py:288
  126.9 6.0 %collective-permute-start.12 = (f32[192,256]{1,0:T(8,128)S(1)}, f32[192,256]{1,0:T(8,128)S(1)}, u32[]{:S(2)}, u32[]{:S(2)}) collective-permute-start(f32[192,256]{1,0:T(8,128)S(1)} %pad_maximum_fusion.6), channel_id=1, source_target_pairs={{0,1},{1,0},{2,3},{3,2},{4,5},{5,4},{6,7},{7,6},{8,9},{9,8},{10,11... | collective-permute-start | bytes 589832 | tf_op jit(solution)/shard_map/ppermute | solution.py:288
  128.0 7.9 %collective-permute-start.22 = (f32[192,256]{1,0:T(8,128)S(1)}, f32[192,256]{1,0:T(8,128)S(1)}, u32[]{:S(2)}, u32[]{:S(2)}) collective-permute-start(f32[192,256]{1,0:T(8,128)S(1)} %pad_maximum_fusion.7), channel_id=1, source_target_pairs={{0,16},{8,24},{16,0},{24,8},{1,17},{9,25},{17,1},{25,9},{2,18},{10... | collective-permute-start | bytes 589832 | tf_op jit(solution)/shard_map/ppermute | solution.py:288
  130.0 10.2 %collective-permute-start.32 = (f32[192,256]{1,0:T(8,128)S(1)}, f32[192,256]{1,0:T(8,128)S(1)}, u32[]{:S(2)}, u32[]{:S(2)}) collective-permute-start(f32[192,256]{1,0:T(8,128)S(1)} %pad_maximum_fusion.8), channel_id=1, source_target_pairs={{0,16},{8,24},{16,0},{24,8},{1,17},{9,25},{17,1},{25,9},{2,18},{10... | collective-permute-start | bytes 589832 | tf_op jit(solution)/shard_map/ppermute | solution.py:288
  130.5 13.8 %collective-permute-start.42 = (f32[192,256]{1,0:T(8,128)S(1)}, f32[192,256]{1,0:T(8,128)S(1)}, u32[]{:S(2)}, u32[]{:S(2)}) collective-permute-start(f32[192,256]{1,0:T(8,128)S(1)} %pad_maximum_fusion.9), channel_id=1, source_target_pairs={{0,16},{8,24},{16,0},{24,8},{1,17},{9,25},{17,1},{25,9},{2,18},{10... | collective-permute-start | bytes 589832 | tf_op jit(solution)/shard_map/ppermute | solution.py:288
  133.0 11.4 %collective-permute-start.14 = (f32[384,256]{1,0:T(8,128)S(1)}, f32[384,256]{1,0:T(8,128)S(1)}, u32[]{:S(2)}, u32[]{:S(2)}) collective-permute-start(f32[384,256]{1,0:T(8,128)S(1)} %pad_maximum_fusion.2.rest_0_), channel_id=1, source_target_pairs={{0,8},{8,0},{16,24},{24,16},{1,9},{9,1},{17,25},{25,17},{2,10},{10... | collective-permute-start | bytes 1179656 | tf_op jit(solution)/shard_map/ppermute | solution.py:288
  133.0 16.6 %collective-permute-start.13 = (f32[384,256]{1,0:T(8,128)S(1)}, f32[384,256]{1,0:T(8,128)S(1)}, u32[]{:S(2)}, u32[]{:S(2)}) collective-permute-start(f32[384,256]{1,0:T(8,128)S(1)} %pad_maximum_fusion.2.rest_0_), channel_id=1, source_target_pairs={{0,16},{8,24},{16,0},{24,8},{1,17},{9,25},{17,1},{25,9},{2,18},{10... | collective-permute-start | bytes 1179656 | tf_op jit(solution)/shard_map/ppermute | solution.py:288
  136.0 14.6 %collective-permute-start.24 = (f32[384,256]{1,0:T(8,128)S(1)}, f32[384,256]{1,0:T(8,128)S(1)}, u32[]{:S(2)}, u32[]{:S(2)}) collective-permute-start(f32[384,256]{1,0:T(8,128)S(1)} %pad_maximum_fusion.3.rest_4_), channel_id=1, source_target_pairs={{0,8},{8,0},{16,24},{24,16},{1,9},{9,1},{17,25},{25,17},{2,10},{10... | collective-permute-start | bytes 1179656 | tf_op jit(solution)/shard_map/ppermute | solution.py:288
  140.1 10.4 %collective-permute-start.23 = (f32[384,256]{1,0:T(8,128)S(1)}, f32[384,256]{1,0:T(8,128)S(1)}, u32[]{:S(2)}, u32[]{:S(2)}) collective-permute-start(f32[384,256]{1,0:T(8,128)S(1)} %pad_maximum_fusion.3.rest_4_), channel_id=1, source_target_pairs={{0,1},{1,0},{2,3},{3,2},{4,5},{5,4},{6,7},{7,6},{8,9},{9,8},{10,11... | collective-permute-start | bytes 1179656 | tf_op jit(solution)/shard_map/ppermute | solution.py:288
  144.3 6.7 %collective-permute-start.34 = (f32[384,256]{1,0:T(8,128)S(1)}, f32[384,256]{1,0:T(8,128)S(1)}, u32[]{:S(2)}, u32[]{:S(2)}) collective-permute-start(f32[384,256]{1,0:T(8,128)S(1)} %pad_maximum_fusion.4.rest_8_), channel_id=1, source_target_pairs={{0,8},{8,0},{16,24},{24,16},{1,9},{9,1},{17,25},{25,17},{2,10},{10... | collective-permute-start | bytes 1179656 | tf_op jit(solution)/shard_map/ppermute | solution.py:288
  144.4 11.7 %collective-permute-start.33 = (f32[384,256]{1,0:T(8,128)S(1)}, f32[384,256]{1,0:T(8,128)}, u32[]{:S(2)}, u32[]{:S(2)}) collective-permute-start(f32[384,256]{1,0:T(8,128)S(1)} %pad_maximum_fusion.4.rest_8_), channel_id=1, source_target_pairs={{0,2},{1,3},{2,0},{3,1},{4,6},{5,7},{6,4},{7,5},{8,10},{9,11},{10,... | collective-permute-start | bytes 1179656 | tf_op jit(solution)/shard_map/ppermute | solution.py:288
  149.6 8.1 %collective-permute-start.43 = (f32[384,256]{1,0:T(8,128)S(1)}, f32[384,256]{1,0:T(8,128)}, u32[]{:S(2)}, u32[]{:S(2)}) collective-permute-start(f32[384,256]{1,0:T(8,128)S(1)} %pad_maximum_fusion.5.rest_12_), channel_id=1, source_target_pairs={{0,1},{1,0},{2,3},{3,2},{4,5},{5,4},{6,7},{7,6},{8,9},{9,8},{10,11... | collective-permute-start | bytes 1179656 | tf_op jit(solution)/shard_map/ppermute | solution.py:288
  150.6 7.3 %collective-permute-start.44 = (f32[384,256]{1,0:T(8,128)S(1)}, f32[384,256]{1,0:T(8,128)}, u32[]{:S(2)}, u32[]{:S(2)}) collective-permute-start(f32[384,256]{1,0:T(8,128)S(1)} %pad_maximum_fusion.5.rest_12_), channel_id=1, source_target_pairs={{0,8},{8,0},{16,24},{24,16},{1,9},{9,1},{17,25},{25,17},{2,10},{10... | collective-permute-start | bytes 1179656 | tf_op jit(solution)/shard_map/ppermute | solution.py:288
  150.6 7.3 %collective-permute-start.15 = (f32[384,256]{1,0:T(8,128)S(1)}, f32[384,256]{1,0:T(8,128)}, u32[]{:S(2)}, u32[]{:S(2)}) collective-permute-start(f32[384,256]{1,0:T(8,128)S(1)} %collective-permute-done.13.rest_1_), channel_id=1, source_target_pairs={{0,8},{8,0},{16,24},{24,16},{1,9},{9,1},{17,25},{25,17},{2,10},{10... | collective-permute-start | bytes 1179656 | tf_op jit(solution)/shard_map/ppermute | solution.py:288
  151.1 6.8 %collective-permute-start.25 = (f32[384,256]{1,0:T(8,128)S(1)}, f32[384,256]{1,0:T(8,128)}, u32[]{:S(2)}, u32[]{:S(2)}) collective-permute-start(f32[384,256]{1,0:T(8,128)S(1)} %collective-permute-done.23.rest_5_), channel_id=1, source_target_pairs={{0,8},{8,0},{16,24},{24,16},{1,9},{9,1},{17,25},{25,17},{2,10},{10... | collective-permute-start | bytes 1179656 | tf_op jit(solution)/shard_map/ppermute | solution.py:288
  156.1 2.1 %collective-permute-start.35 = (f32[384,256]{1,0:T(8,128)}, f32[384,256]{1,0:T(8,128)}, u32[]{:S(2)}, u32[]{:S(2)}) collective-permute-start(f32[384,256]{1,0:T(8,128)} %collective-permute-done.33.rest_9_), channel_id=1, source_target_pairs={{0,8},{8,0},{16,24},{24,16},{1,9},{9,1},{17,25},{25,17},{2,10},{10... | collective-permute-start | bytes 1179656 | tf_op jit(solution)/shard_map/ppermute | solution.py:288
  157.8 2.1 %collective-permute-start.45 = (f32[384,256]{1,0:T(8,128)}, f32[384,256]{1,0:T(8,128)}, u32[]{:S(2)}, u32[]{:S(2)}) collective-permute-start(f32[384,256]{1,0:T(8,128)} %collective-permute-done.43.rest_13_), channel_id=1, source_target_pairs={{0,8},{8,0},{16,24},{24,16},{1,9},{9,1},{17,25},{25,17},{2,10},{10... | collective-permute-start | bytes 1179656 | tf_op jit(solution)/shard_map/ppermute | solution.py:288
  (4 other events, 11.9 us)

commit v5 on v4

--- a/solution.py
+++ b/solution.py
@@ -161,25 +161,31 @@
     def _():
         cols = back.shape[1] // chunks
 
-        def self_term(part):
-            high, low = split(back[:n_src, pl.ds(part * cols, cols)])
-            return dot_rows(src[0], high) + dot_rows(src[0], low)
-
-        def neigh_term(part):
-            high, low = split(back[n_src:, pl.ds(part * cols, cols)] * (1.0 / FAN))
-            return dot_rows(src[0], high) + dot_rows(src[0], low) + dot_rows(src[1], high)
+        half_rows = src.shape[2] // 2
+
+        def put(out_ref, part, neigh):
+            first = n_src if neigh else 0
+            term = back[first : first + n_src, pl.ds(part * cols, cols)]
+            high, low = split(term * (1.0 / FAN) if neigh else term)
+            bit = device_ref[2 + part]
+            for k, at in enumerate((bit, 1 - bit)):
+                here = pl.ds(pl.multiple_of(at * half_rows, half_rows), half_rows)
+                total = dot_rows(src[0, :, here], high) + dot_rows(src[0, :, here], low)
+                if neigh:
+                    total += dot_rows(src[1, :, here], high)
+                out_ref[k * half_rows : (k + 1) * half_rows, :] = total
 
         @pl.when(device_ref[0] == 0)
         def _():
             for part in range(chunks):
-                grad_refs[2 * part][...] = self_term(part)
-                grad_refs[2 * part + 1][...] = neigh_term(part)
+                put(grad_refs[2 * part], part, False)
+                put(grad_refs[2 * part + 1], part, True)
 
         @pl.when(device_ref[0] != 0)
         def _():
             for part in range(chunks):
-                grad_refs[2 * part][...] = neigh_term(part)
-                grad_refs[2 * part + 1][...] = self_term(part)
+                put(grad_refs[2 * part], part, True)
+                put(grad_refs[2 * part + 1], part, False)
 
 
 def layer(call, chunks, far_mask, device, counts, hot_rows, cold_rows, w_self, w_neigh, cotangent, hidden):
@@ -328,7 +334,7 @@
 
 
 def fetch_rows(hot_table, cold_table, hot_need, cold_need, device):
-    core, along_x, along_y, along_z = axis_swaps(plain=True)
+    core, along_x, _, along_z = axis_swaps(plain=True)
     far = along_z[-1]
     half = lax.axis_size("dev") // 2
     me = lax.axis_index("dev")
@@ -375,14 +381,17 @@
     near_z, far_z = along_z[:1], along_z[1:]
     return [
         along_x + along_y + near_z + far_z,
-        along_y + along_x + near_z + far_z,
-        near_z + along_x + along_y + far_z,
-        along_y + along_x + near_z + far_z,
+        along_y + near_z + along_x + far_z,
+        near_z + far_z + along_x + along_y,
+        along_x + along_y + near_z + far_z,
     ]
 
 
 def sum_chunk(parts, core, order):
-    for swap in order[:-1]:
+    rows = parts[0].shape[0] // 2
+    own, out = (parts[0][k : k + rows] + parts[1][k : k + rows] for k in (0, rows))
+    parts = [own, order[0].send(out)]
+    for swap in order[1:-1]:
         own, out = cut(parts, swap)
         parts = [own, swap.send(out)]
     value = parts[0] + parts[1]
@@ -398,10 +407,10 @@
 ):
     n_src = hot_need.size + cold_need.size
     counts = count_matrices(neighbors, self_index, n_src)
-    device = jnp.stack([lax.rem(lax.axis_index("grp"), jnp.int32(CORES)), lax.axis_index("dev")])
-    hot_rows, cold_rows, far_mask = fetch_rows(hot_table, cold_table, hot_need, cold_need, device)
     core = axis_swaps()[0][0]
     orders = orders_of_sums()
+    device = jnp.stack([core.bit, lax.axis_index("dev")] + [order[0].bit for order in orders])
+    hot_rows, cold_rows, far_mask = fetch_rows(hot_table, cold_table, hot_need, cold_need, device)
     chunks = CHUNKS // CALLS
     hidden, sums = None, []
     for call in range(CALLS):

time: 165 us -> 156 us (0.945)
  waiting for transfers between devices: 49.9 us -> 43.2 us
  starting transfers between devices: 50.6 us -> 48.2 us
    ppermute x43, waiting for transfers between devices: 47 us -> 40.2 us  [send(): return lax.ppermute(value, self.name, self.pairs)]
    select_n x12 -> x8, other arithmetic: 3.03 us -> 0.31 us  [cut(): return (jnp.where(first, low, high), jnp.where(first, high, low))]
    add x0 -> x4, other arithmetic: none -> 2.71 us  [sum_chunk(): own, out = (parts[0][k:k + rows] + parts[1][k:k + rows] for k in (0, rows))]
    ppermute x43, starting transfers between devices: 44.6 us -> 42.1 us  [send(): return lax.ppermute(value, self.name, self.pairs)]
  transfers between devices with their start and end apart: 47 -> 47, of which waited for: 18 -> 20; matrix products, arithmetic and copies ran while one was open for 5% -> 5% of each run, Pallas kernels for 9% -> 9%
where the time goes in v5:
time: 156 us
  starting transfers between devices  48.2 us (31%)
  waiting for transfers between devices  43.2 us (28%)
  Pallas kernels  40.4 us (26%)
  blocking collectives  9.85 us (6%)
  local copies, waits for them, and re-layouts  7.47 us (5%)
  other arithmetic  5.25 us (3%)
    ppermute x43, starting transfers between devices, send(): return lax.ppermute(value, self.name, self.pairs)  42.1 us
    ppermute x43, waiting for transfers between devices, send(): return lax.ppermute(value, self.name, self.pairs)  40.2 us
    pallas_call x1, Pallas kernels, layer(): pl.pallas_call(functools.partial(layer_kernel, chunks, len(hot_rows), far...  21.7 us
    all_to_all x1, blocking collectives, fetch_rows(): asked = exchange(jnp.concatenate([cold_need, hot_list], axis=1))  9.85 us
    pallas_call x1, Pallas kernels, count_matrices(): pl.pallas_call(count_kernel, grid=(targets // block,), in_specs=[pl.Block...  7.39 us
    pallas_call x1, Pallas kernels, place(): pl.pallas_call(place_kernel, in_specs=[pl.BlockSpec(memory_space=pltpu.SM...  4.5 us
    ppermute x3, starting transfers between devices, fetch_rows(): lax.ppermute(served[away], 'dev', pairs(away))  3.49 us
    pallas_call x1, Pallas kernels, cold_look_up(): pl.pallas_call(cold_kernel, out_shape=jax.ShapeDtypeStruct((count, width)...  3.42 us
  transfers between devices with their start and end apart: 47, of which 20 were waited for; matrix products, arithmetic and copies ran while one was open for 5% of the time, Pallas kernels for 9%

profile of v5, /device:TPU:0, one launch (start us, length us, event | category | flops | bytes accessed | tf_op | source)
XLA Modules:
  0.0 155.6 jit_solution(1154353196171397653)
XLA Ops:
  0.7 0.9 constant_dynamic-slice_fusion
  1.6 5.1 %collective-permute-start = (f32[64,768]{1,0:T(8,128)S(1)}, f32[64,768]{1,0:T(8,128)S(1)}, u32[]{:S(2)}, u32[]{:S(2)}) collective-permute-start(f32[64,768]{1,0:T(8,128)S(1)} %constant_dynamic-slice_fusion), channel_id=1, source_target_pairs={{0,6},{1,7},{2,4},{3,5},{4,2},{5,3},{6,0},{7,1},{8,14},{9,15},{10,... | collective-permute-start | bytes 589832 | tf_op jit(solution)/shard_map/ppermute | solution.py:294
  8.4 9.9 %all_to_all.23 = s32[32,1,260]{2,1,0:T(1,128)S(1)} all-to-all(s32[32,1,260]{2,1,0:T(1,128)S(1)} %all_to_all.15), channel_id=1, replica_groups=mesh['grp'=4,'dev'=8] {'grp','dev'}, dimensions={0} | all-to-all | bytes 66560 | tf_op jit(solution)/shard_map/all_to_all | solution.py:354
  19.6 3.4 %cold_look_up.1 = f32[128,768]{1,0:T(8,128)} custom-call(s32[1,128]{1,0:T(1,128)} %reshape.15.asked_ref, f32[1024,768]{1,0:T(8,128)} %table_ref.1), custom_call_target="tpu_custom_call" | custom-call | flops 402653184 | bytes 3145728 | tf_op jit(solution)/shard_map/cold_look_up/pallas_call | solution.py:84
  23.0 2.2 %collective-permute-done.1 = f32[64,768]{1,0:T(8,128)S(1)} collective-permute-done((f32[64,768]{1,0:T(8,128)S(1)}, f32[64,768]{1,0:T(8,128)S(1)}, u32[]{:S(2)}, u32[]{:S(2)}) %collective-permute-start.1) | collective-permute-done | bytes 196640 | tf_op jit(solution)/shard_map/ppermute | solution.py:294
  26.1 1.9 %all_to_all.18 = f32[32,4,768]{2,1,0:T(4,128)} reshape(f32[128,768]{1,0:T(8,128)} %cold_look_up.1) | data formatting | bytes 786432 | tf_op jit(solution)/shard_map/all_to_all | solution.py:370
  27.9 2.6 %all-to-all-start.1 = ((f32[32,4,768]{2,1,0:T(4,128)}), f32[32,4,768]{2,1,0:T(4,128)S(1)}, u32[]{:S(2)}, u32[]{:S(2)}) async-start(f32[32,4,768]{2,1,0:T(4,128)} %all_to_all.18), calls=%async_computation.1 | async-start | bytes 786432 | tf_op jit(solution)/shard_map/all_to_all | solution.py:370
  31.3 0.9 pad_maximum_fusion.far_ref
  32.3 3.4 %hot_look_up.1 = (f32[64,768]{1,0:T(8,128)}, f32[64,768]{1,0:T(8,128)}, f32[64,768]{1,0:T(8,128)}, f32[64,768]{1,0:T(8,128)}) custom-call(s32[6]{0:T(128)} %stack.32.device_ref, s32[4,64]{1,0:T(4,128)} %pad_add_fusion.1.asked_ref, f32[256,768]{1,0:T(8,128)} %own_ref.1, f32[256,768]{1,0:T(8,128)} %pad_maximum_fusion.far_ref), custom_call_target="tpu_custom_call" | custom-call | flops 402653184 | bytes 2359296 | tf_op jit(solution)/shard_map/hot_look_up/pallas_call | solution.py:113
  35.6 1.7 %collective-permute-start.3 = (f32[64,768]{1,0:T(8,128)}, f32[64,768]{1,0:T(8,128)S(1)}, u32[]{:S(2)}, u32[]{:S(2)}) collective-permute-start(f32[64,768]{1,0:T(8,128)} %get-tuple-element.27), channel_id=1, source_target_pairs={{0,1},{1,0},{2,3},{3,2},{4,5},{5,4},{6,7},{7,6},{8,9},{9,8},{10,11... | collective-permute-start | bytes 589832 | tf_op jit(solution)/shard_map/ppermute | solution.py:374
  37.3 1.5 collective-permute-start.4
  39.1 7.4 %count_matrices.1.counts_ref = bf16[768,2048]{1,0:T(8,128)(2,1)} custom-call(s32[25,2048]{1,0:T(8,128)} %bitcast.10, s32[1,2048]{1,0:T(1,128)} %bitcast.13), custom_call_target="tpu_custom_call" | custom-call | flops 39321600 | bytes 3145728 | tf_op jit(solution)/shard_map/count_matrices/pallas_call | solution.py:54
  46.5 0.9 all_to_all.20.cold_ref
  47.4 2.9 %collective-permute-done.5.rest_3_ = f32[64,768]{1,0:T(8,128)S(1)} collective-permute-done((f32[64,768]{1,0:T(8,128)}, f32[64,768]{1,0:T(8,128)S(1)}, u32[]{:S(2)}, u32[]{:S(2)}) %collective-permute-start.5) | collective-permute-done | bytes 196640 | tf_op jit(solution)/shard_map/ppermute | solution.py:374
  51.0 21.7 %layer_0.1 = (bf16[2048,1024]{1,0:T(8,128)(2,1)}, f32[768,256]{1,0:T(8,128)}, f32[768,256]{1,0:T(8,128)}, f32[768,256]{1,0:T(8,128)}, f32[768,256]{1,0:T(8,128)}...) custom-call(s32[6]{0:T(128)} %stack.32.device_ref, ...), custom_call_target="tpu_custom_call" | custom-call | flops 8858370048 | bytes 11534336 | tf_op jit(solution)/shard_map/layer_0/pallas_call | solution.py:214
  73.8 1.5 collective-permute-done.6
  75.3 1.3 slice_add_fusion.7
  76.6 1.6 %collective-permute-start.7 = (f32[384,256]{1,0:T(8,128)S(1)}, f32[384,256]{1,0:T(8,128)S(1)}, u32[]{:S(2)}, u32[]{:S(2)}) collective-permute-start(f32[384,256]{1,0:T(8,128)S(1)} %get-tuple-element.48), channel_id=1, source_target_pairs={{0,16},{8,24},{16,0},{24,8},{1,17},{9,25},{17,1},{25,9},{2,18},{10... | collective-permute-start | bytes 1179656 | tf_op jit(solution)/shard_map/ppermute | solution.py:294
  78.3 1.2 slice_add_fusion.5
  79.5 1.0 collective-permute-start.17
  81.7 7.0 %collective-permute-done.7 = f32[384,256]{1,0:T(8,128)S(1)} collective-permute-done((f32[384,256]{1,0:T(8,128)S(1)}, f32[384,256]{1,0:T(8,128)S(1)}, u32[]{:S(2)}, u32[]{:S(2)}) %collective-permute-start.7) | collective-permute-done | bytes 393248 | tf_op jit(solution)/shard_map/ppermute | solution.py:294
  88.7 1.1 collective-permute-start.8
  89.8 1.1 collective-permute-done.17
  91.4 2.3 %collective-permute-start.28 = (f32[192,256]{1,0:T(8,128)S(1)}, f32[192,256]{1,0:T(8,128)S(1)}, u32[]{:S(2)}, u32[]{:S(2)}) collective-permute-start(f32[192,256]{1,0:T(8,128)S(1)} %get-tuple-element.52), channel_id=1, source_target_pairs={{0,6},{1,7},{2,4},{3,5},{4,2},{5,3},{6,0},{7,1},{8,14},{9,15},{10,... | collective-permute-start | bytes 589832 | tf_op jit(solution)/shard_map/ppermute | solution.py:294
  93.6 2.7 %collective-permute-done.37 = f32[384,256]{1,0:T(8,128)S(1)} collective-permute-done((f32[384,256]{1,0:T(8,128)S(1)}, f32[384,256]{1,0:T(8,128)S(1)}, u32[]{:S(2)}, u32[]{:S(2)}) %collective-permute-start.37) | collective-permute-done | bytes 393248 | tf_op jit(solution)/shard_map/ppermute | solution.py:294
  96.3 1.1 collective-permute-start.38
  97.8 1.0 collective-permute-done.18
  99.3 2.9 %collective-permute-done.28 = f32[192,256]{1,0:T(8,128)S(1)} collective-permute-done((f32[192,256]{1,0:T(8,128)S(1)}, f32[192,256]{1,0:T(8,128)S(1)}, u32[]{:S(2)}, u32[]{:S(2)}) %collective-permute-start.28) | collective-permute-done | bytes 196640 | tf_op jit(solution)/shard_map/ppermute | solution.py:294
  103.2 2.1 %collective-permute-start.10 = (f32[96,256]{1,0:T(8,128)S(1)}, f32[96,256]{1,0:T(8,128)S(1)}, u32[]{:S(2)}, u32[]{:S(2)}) collective-permute-start(f32[96,256]{1,0:T(8,128)S(1)} %select_add_fusion.3), channel_id=1, source_target_pairs={{0,6},{1,7},{2,4},{3,5},{4,2},{5,3},{6,0},{7,1},{8,14},{9,15},{10,... | collective-permute-start | bytes 294920 | tf_op jit(solution)/shard_map/ppermute | solution.py:294
  105.3 1.9 %collective-permute-start.20 = (f32[96,256]{1,0:T(8,128)S(1)}, f32[96,256]{1,0:T(8,128)S(1)}, u32[]{:S(2)}, u32[]{:S(2)}) collective-permute-start(f32[96,256]{1,0:T(8,128)S(1)} %select_add_fusion.2), channel_id=1, source_target_pairs={{0,6},{1,7},{2,4},{3,5},{4,2},{5,3},{6,0},{7,1},{8,14},{9,15},{10,... | collective-permute-start | bytes 294920 | tf_op jit(solution)/shard_map/ppermute | solution.py:294
  107.2 1.0 collective-permute-start.30
  108.3 2.1 %collective-permute-start.40 = (f32[96,256]{1,0:T(8,128)S(1)}, f32[96,256]{1,0:T(8,128)S(1)}, u32[]{:S(2)}, u32[]{:S(2)}) collective-permute-start(f32[96,256]{1,0:T(8,128)S(1)} %select_add_fusion), channel_id=1, source_target_pairs={{0,6},{1,7},{2,4},{3,5},{4,2},{5,3},{6,0},{7,1},{8,14},{9,15},{10,... | collective-permute-start | bytes 294920 | tf_op jit(solution)/shard_map/ppermute | solution.py:294
  110.9 5.4 %collective-permute-start.11 = (f32[96,256]{1,0:T(8,128)S(1)}, f32[96,256]{1,0:T(8,128)S(1)}, u32[]{:S(2)}, u32[]{:S(2)}) collective-permute-start(f32[96,256]{1,0:T(8,128)S(1)} %add.140), channel_id=1, source_target_pairs={{0,2},{1,3},{2,0},{3,1},{4,6},{5,7},{6,4},{7,5},{8,10},{9,11},{10,... | collective-permute-start | bytes 294920 | tf_op jit(solution)/shard_map/ppermute | solution.py:294
  116.4 2.0 %collective-permute-start.31 = (f32[96,256]{1,0:T(8,128)S(1)}, f32[96,256]{1,0:T(8,128)S(1)}, u32[]{:S(2)}, u32[]{:S(2)}) collective-permute-start(f32[96,256]{1,0:T(8,128)S(1)} %add.156), channel_id=1, source_target_pairs={{0,16},{8,24},{16,0},{24,8},{1,17},{9,25},{17,1},{25,9},{2,18},{10... | collective-permute-start | bytes 294920 | tf_op jit(solution)/shard_map/ppermute | solution.py:294
  118.5 1.0 collective-permute-start.41
  119.6 1.0 collective-permute-start.12
  121.0 2.1 %collective-permute-start.22 = (f32[192,256]{1,0:T(8,128)S(1)}, f32[192,256]{1,0:T(8,128)S(1)}, u32[]{:S(2)}, u32[]{:S(2)}) collective-permute-start(f32[192,256]{1,0:T(8,128)S(1)} %pad_maximum_fusion.7), channel_id=1, source_target_pairs={{0,2},{1,3},{2,0},{3,1},{4,6},{5,7},{6,4},{7,5},{8,10},{9,11},{10,... | collective-permute-start | bytes 589832 | tf_op jit(solution)/shard_map/ppermute | solution.py:294
  123.2 1.9 %collective-permute-start.32 = (f32[192,256]{1,0:T(8,128)S(1)}, f32[192,256]{1,0:T(8,128)S(1)}, u32[]{:S(2)}, u32[]{:S(2)}) collective-permute-start(f32[192,256]{1,0:T(8,128)S(1)} %pad_maximum_fusion.8), channel_id=1, source_target_pairs={{0,6},{1,7},{2,4},{3,5},{4,2},{5,3},{6,0},{7,1},{8,14},{9,15},{10,... | collective-permute-start | bytes 589832 | tf_op jit(solution)/shard_map/ppermute | solution.py:294
  125.1 1.2 collective-permute-start.42
  126.4 1.0 collective-permute-start.13
  128.1 2.6 %collective-permute-done.32 = f32[192,256]{1,0:T(8,128)S(1)} collective-permute-done((f32[192,256]{1,0:T(8,128)S(1)}, f32[192,256]{1,0:T(8,128)S(1)}, u32[]{:S(2)}, u32[]{:S(2)}) %collective-permute-start.32) | collective-permute-done | bytes 196640 | tf_op jit(solution)/shard_map/ppermute | solution.py:294
  130.7 1.1 collective-permute-start.23
  132.1 5.8 %collective-permute-done.13.rest_1_ = f32[384,256]{1,0:T(8,128)S(1)} collective-permute-done((f32[384,256]{1,0:T(8,128)S(1)}, f32[384,256]{1,0:T(8,128)S(1)}, u32[]{:S(2)}, u32[]{:S(2)}) %collective-permute-start.13) | collective-permute-done | bytes 393248 | tf_op jit(solution)/shard_map/ppermute | solution.py:294
  138.0 0.9 collective-permute-start.43
  140.1 3.6 %collective-permute-done.33.rest_9_ = f32[384,256]{1,0:T(8,128)} collective-permute-done((f32[384,256]{1,0:T(8,128)S(1)}, f32[384,256]{1,0:T(8,128)}, u32[]{:S(2)}, u32[]{:S(2)}) %collective-permute-start.33) | collective-permute-done | bytes 393248 | tf_op jit(solution)/shard_map/ppermute | solution.py:294
  143.7 5.1 %collective-permute-done.43.rest_13_ = f32[384,256]{1,0:T(8,128)} collective-permute-done((f32[384,256]{1,0:T(8,128)S(1)}, f32[384,256]{1,0:T(8,128)}, u32[]{:S(2)}, u32[]{:S(2)}) %collective-permute-start.43) | collective-permute-done | bytes 393248 | tf_op jit(solution)/shard_map/ppermute | solution.py:294
  149.0 2.0 %collective-permute-done.45.rest_15_ = f32[384,256]{1,0:T(8,128)} collective-permute-done((f32[384,256]{1,0:T(8,128)}, f32[384,256]{1,0:T(8,128)}, u32[]{:S(2)}, u32[]{:S(2)}) %collective-permute-start.45) | collective-permute-done | bytes 393248 | tf_op jit(solution)/shard_map/ppermute | solution.py:294
  150.9 4.5 %place.1 = (f32[768,1024]{1,0:T(8,128)}, f32[768,1024]{1,0:T(8,128)}) custom-call(s32[5]{0:T(128)S(1)} %stack.33.where_ref, f32[384,256]{1,0:T(8,128)S(1)} %pad_maximum_fusion.2.rest_0_, f32[384,256]{1,0:T(8,128)S(1)} %collective-permute-done.13.rest_1_, f32[384,256]{1,0:T(8,128)S(1)} %collective-permute-done.14.rest_2_, ...), custom_call_target="tpu_custom_call" | custom-call | bytes 12582912 | tf_op jit(solution)/shard_map/place/pallas_call | solution.py:273
  (117 shorter events, 13.9 us)
Async XLA Ops:
  1.6 16.6 %collective-permute-start = (f32[64,768]{1,0:T(8,128)S(1)}, f32[64,768]{1,0:T(8,128)S(1)}, u32[]{:S(2)}, u32[]{:S(2)}) collective-permute-start(f32[64,768]{1,0:T(8,128)S(1)} %constant_dynamic-slice_fusion), channel_id=1, source_target_pairs={{0,6},{1,7},{2,4},{3,5},{4,2},{5,3},{6,0},{7,1},{8,14},{9,15},{10,... | collective-permute-start | bytes 589832 | tf_op jit(solution)/shard_map/ppermute | solution.py:294
  18.2 7.0 %collective-permute-start.1 = (f32[64,768]{1,0:T(8,128)S(1)}, f32[64,768]{1,0:T(8,128)S(1)}, u32[]{:S(2)}, u32[]{:S(2)}) collective-permute-start(f32[64,768]{1,0:T(8,128)S(1)} %collective-permute-done), channel_id=1, source_target_pairs={{0,16},{8,24},{16,0},{24,8},{1,17},{9,25},{17,1},{25,9},{2,18},{10... | collective-permute-start | bytes 589832 | tf_op jit(solution)/shard_map/ppermute | solution.py:294
  25.3 6.0 %collective-permute-start.2 = (f32[128,768]{1,0:T(8,128)S(1)}, f32[128,768]{1,0:T(8,128)S(1)}, u32[]{:S(2)}, u32[]{:S(2)}) collective-permute-start(f32[128,768]{1,0:T(8,128)S(1)} %pad_maximum_fusion.1), channel_id=1, source_target_pairs={{0,8},{8,0},{16,24},{24,16},{1,9},{9,1},{17,25},{25,17},{2,10},{10... | collective-permute-start | bytes 1179656 | tf_op jit(solution)/shard_map/ppermute | solution.py:294
  27.9 18.6 %all-to-all-start.1 = ((f32[32,4,768]{2,1,0:T(4,128)}), f32[32,4,768]{2,1,0:T(4,128)S(1)}, u32[]{:S(2)}, u32[]{:S(2)}) async-start(f32[32,4,768]{2,1,0:T(4,128)} %all_to_all.18), calls=%async_computation.1 | async-start | bytes 786432 | tf_op jit(solution)/shard_map/all_to_all | solution.py:370
  35.6 11.8 %collective-permute-start.3 = (f32[64,768]{1,0:T(8,128)}, f32[64,768]{1,0:T(8,128)S(1)}, u32[]{:S(2)}, u32[]{:S(2)}) collective-permute-start(f32[64,768]{1,0:T(8,128)} %get-tuple-element.27), channel_id=1, source_target_pairs={{0,1},{1,0},{2,3},{3,2},{4,5},{5,4},{6,7},{7,6},{8,9},{9,8},{10,11... | collective-permute-start | bytes 589832 | tf_op jit(solution)/shard_map/ppermute | solution.py:374
  37.3 10.1 %collective-permute-start.4 = (f32[64,768]{1,0:T(8,128)}, f32[64,768]{1,0:T(8,128)S(1)}, u32[]{:S(2)}, u32[]{:S(2)}) collective-permute-start(f32[64,768]{1,0:T(8,128)} %get-tuple-element.28), channel_id=1, source_target_pairs={{0,2},{1,3},{2,0},{3,1},{4,6},{5,7},{6,4},{7,5},{8,10},{9,11},{10,... | collective-permute-start | bytes 589832 | tf_op jit(solution)/shard_map/ppermute | solution.py:374
  38.8 11.5 %collective-permute-start.5 = (f32[64,768]{1,0:T(8,128)}, f32[64,768]{1,0:T(8,128)S(1)}, u32[]{:S(2)}, u32[]{:S(2)}) collective-permute-start(f32[64,768]{1,0:T(8,128)} %get-tuple-element.29), channel_id=1, source_target_pairs={{0,3},{1,2},{2,1},{3,0},{4,7},{5,6},{6,5},{7,4},{8,11},{9,10},{10,... | collective-permute-start | bytes 589832 | tf_op jit(solution)/shard_map/ppermute | solution.py:374
  72.8 7.8 %copy-start.1 = (f32[768,256]{1,0:T(8,128)S(1)}, f32[768,256]{1,0:T(8,128)}, u32[]{:S(2)}) copy-start(f32[768,256]{1,0:T(8,128)} %get-tuple-element.35) | copy-start | bytes 2359300
  72.8 2.6 %collective-permute-start.6 = (f32[768,256]{1,0:T(8,128)}, f32[768,256]{1,0:T(8,128)S(1)}, u32[]{:S(2)}, u32[]{:S(2)}) collective-permute-start(f32[768,256]{1,0:T(8,128)} %get-tuple-element.32), channel_id=1, source_target_pairs={{0,8},{8,0},{16,24},{24,16},{1,9},{9,1},{17,25},{25,17},{2,10},{10... | collective-permute-start | bytes 2359304 | tf_op jit(solution)/shard_map/ppermute | solution.py:294
  72.8 5.4 %collective-permute-start.16 = (f32[768,256]{1,0:T(8,128)}, f32[768,256]{1,0:T(8,128)S(1)}, u32[]{:S(2)}, u32[]{:S(2)}) collective-permute-start(f32[768,256]{1,0:T(8,128)} %get-tuple-element.34), channel_id=1, source_target_pairs={{0,8},{8,0},{16,24},{24,16},{1,9},{9,1},{17,25},{25,17},{2,10},{10... | collective-permute-start | bytes 2359304 | tf_op jit(solution)/shard_map/ppermute | solution.py:294
  73.3 7.2 %collective-permute-start.26 = (f32[768,256]{1,0:T(8,128)}, f32[768,256]{1,0:T(8,128)S(1)}, u32[]{:S(2)}, u32[]{:S(2)}) collective-permute-start(f32[768,256]{1,0:T(8,128)} %get-tuple-element.36), channel_id=1, source_target_pairs={{0,8},{8,0},{16,24},{24,16},{1,9},{9,1},{17,25},{25,17},{2,10},{10... | collective-permute-start | bytes 2359304 | tf_op jit(solution)/shard_map/ppermute | solution.py:294
  73.4 7.3 %collective-permute-start.36 = (f32[768,256]{1,0:T(8,128)}, f32[768,256]{1,0:T(8,128)S(1)}, u32[]{:S(2)}, u32[]{:S(2)}) collective-permute-start(f32[768,256]{1,0:T(8,128)} %get-tuple-element.38), channel_id=1, source_target_pairs={{0,8},{8,0},{16,24},{24,16},{1,9},{9,1},{17,25},{25,17},{2,10},{10... | collective-permute-start | bytes 2359304 | tf_op jit(solution)/shard_map/ppermute | solution.py:294
  76.6 12.0 %collective-permute-start.7 = (f32[384,256]{1,0:T(8,128)S(1)}, f32[384,256]{1,0:T(8,128)S(1)}, u32[]{:S(2)}, u32[]{:S(2)}) collective-permute-start(f32[384,256]{1,0:T(8,128)S(1)} %get-tuple-element.48), channel_id=1, source_target_pairs={{0,16},{8,24},{16,0},{24,8},{1,17},{9,25},{17,1},{25,9},{2,18},{10... | collective-permute-start | bytes 1179656 | tf_op jit(solution)/shard_map/ppermute | solution.py:294
  79.5 11.4 %collective-permute-start.17 = (f32[384,256]{1,0:T(8,128)S(1)}, f32[384,256]{1,0:T(8,128)S(1)}, u32[]{:S(2)}, u32[]{:S(2)}) collective-permute-start(f32[384,256]{1,0:T(8,128)S(1)} %get-tuple-element.46), channel_id=1, source_target_pairs={{0,1},{1,0},{2,3},{3,2},{4,5},{5,4},{6,7},{7,6},{8,9},{9,8},{10,11... | collective-permute-start | bytes 1179656 | tf_op jit(solution)/shard_map/ppermute | solution.py:294
  80.6 10.7 %collective-permute-start.27 = (f32[384,256]{1,0:T(8,128)S(1)}, f32[384,256]{1,0:T(8,128)S(1)}, u32[]{:S(2)}, u32[]{:S(2)}) collective-permute-start(f32[384,256]{1,0:T(8,128)S(1)} %get-tuple-element.44), channel_id=1, source_target_pairs={{0,2},{1,3},{2,0},{3,1},{4,6},{5,7},{6,4},{7,5},{8,10},{9,11},{10,... | collective-permute-start | bytes 1179656 | tf_op jit(solution)/shard_map/ppermute | solution.py:294
  80.8 15.4 %collective-permute-start.37 = (f32[384,256]{1,0:T(8,128)S(1)}, f32[384,256]{1,0:T(8,128)S(1)}, u32[]{:S(2)}, u32[]{:S(2)}) collective-permute-start(f32[384,256]{1,0:T(8,128)S(1)} %get-tuple-element.42), channel_id=1, source_target_pairs={{0,16},{8,24},{16,0},{24,8},{1,17},{9,25},{17,1},{25,9},{2,18},{10... | collective-permute-start | bytes 1179656 | tf_op jit(solution)/shard_map/ppermute | solution.py:294
  88.7 8.7 %collective-permute-start.8 = (f32[192,256]{1,0:T(8,128)S(1)}, f32[192,256]{1,0:T(8,128)S(1)}, u32[]{:S(2)}, u32[]{:S(2)}) collective-permute-start(f32[192,256]{1,0:T(8,128)S(1)} %get-tuple-element.56), channel_id=1, source_target_pairs={{0,1},{1,0},{2,3},{3,2},{4,5},{5,4},{6,7},{7,6},{8,9},{9,8},{10,11... | collective-permute-start | bytes 589832 | tf_op jit(solution)/shard_map/ppermute | solution.py:294
  91.0 7.8 %collective-permute-start.18 = (f32[192,256]{1,0:T(8,128)S(1)}, f32[192,256]{1,0:T(8,128)S(1)}, u32[]{:S(2)}, u32[]{:S(2)}) collective-permute-start(f32[192,256]{1,0:T(8,128)S(1)} %get-tuple-element.54), channel_id=1, source_target_pairs={{0,2},{1,3},{2,0},{3,1},{4,6},{5,7},{6,4},{7,5},{8,10},{9,11},{10,... | collective-permute-start | bytes 589832 | tf_op jit(solution)/shard_map/ppermute | solution.py:294
  91.4 10.8 %collective-permute-start.28 = (f32[192,256]{1,0:T(8,128)S(1)}, f32[192,256]{1,0:T(8,128)S(1)}, u32[]{:S(2)}, u32[]{:S(2)}) collective-permute-start(f32[192,256]{1,0:T(8,128)S(1)} %get-tuple-element.52), channel_id=1, source_target_pairs={{0,6},{1,7},{2,4},{3,5},{4,2},{5,3},{6,0},{7,1},{8,14},{9,15},{10,... | collective-permute-start | bytes 589832 | tf_op jit(solution)/shard_map/ppermute | solution.py:294
  96.3 6.2 %collective-permute-start.38 = (f32[192,256]{1,0:T(8,128)S(1)}, f32[192,256]{1,0:T(8,128)S(1)}, u32[]{:S(2)}, u32[]{:S(2)}) collective-permute-start(f32[192,256]{1,0:T(8,128)S(1)} %get-tuple-element.50), channel_id=1, source_target_pairs={{0,1},{1,0},{2,3},{3,2},{4,5},{5,4},{6,7},{7,6},{8,9},{9,8},{10,11... | collective-permute-start | bytes 589832 | tf_op jit(solution)/shard_map/ppermute | solution.py:294
  97.5 5.7 %collective-permute-start.9 = (f32[96,256]{1,0:T(8,128)S(1)}, f32[96,256]{1,0:T(8,128)S(1)}, u32[]{:S(2)}, u32[]{:S(2)}) collective-permute-start(f32[96,256]{1,0:T(8,128)S(1)} %broadcast_select_fusion.31), channel_id=1, source_target_pairs={{0,2},{1,3},{2,0},{3,1},{4,6},{5,7},{6,4},{7,5},{8,10},{9,11},{10,... | collective-permute-start | bytes 294920 | tf_op jit(solution)/shard_map/ppermute | solution.py:294
  98.8 6.4 %collective-permute-start.19 = (f32[96,256]{1,0:T(8,128)S(1)}, f32[96,256]{1,0:T(8,128)S(1)}, u32[]{:S(2)}, u32[]{:S(2)}) collective-permute-start(f32[96,256]{1,0:T(8,128)S(1)} %broadcast_select_fusion.25), channel_id=1, source_target_pairs={{0,16},{8,24},{16,0},{24,8},{1,17},{9,25},{17,1},{25,9},{2,18},{10... | collective-permute-start | bytes 294920 | tf_op jit(solution)/shard_map/ppermute | solution.py:294
  102.2 5.0 %collective-permute-start.29 = (f32[96,256]{1,0:T(8,128)S(1)}, f32[96,256]{1,0:T(8,128)S(1)}, u32[]{:S(2)}, u32[]{:S(2)}) collective-permute-start(f32[96,256]{1,0:T(8,128)S(1)} %broadcast_select_fusion.22), channel_id=1, source_target_pairs={{0,16},{8,24},{16,0},{24,8},{1,17},{9,25},{17,1},{25,9},{2,18},{10... | collective-permute-start | bytes 294920 | tf_op jit(solution)/shard_map/ppermute | solution.py:294
  102.5 5.7 %collective-permute-start.39 = (f32[96,256]{1,0:T(8,128)S(1)}, f32[96,256]{1,0:T(8,128)S(1)}, u32[]{:S(2)}, u32[]{:S(2)}) collective-permute-start(f32[96,256]{1,0:T(8,128)S(1)} %broadcast_select_fusion.28), channel_id=1, source_target_pairs={{0,2},{1,3},{2,0},{3,1},{4,6},{5,7},{6,4},{7,5},{8,10},{9,11},{10,... | collective-permute-start | bytes 294920 | tf_op jit(solution)/shard_map/ppermute | solution.py:294
  103.2 7.7 %collective-permute-start.10 = (f32[96,256]{1,0:T(8,128)S(1)}, f32[96,256]{1,0:T(8,128)S(1)}, u32[]{:S(2)}, u32[]{:S(2)}) collective-permute-start(f32[96,256]{1,0:T(8,128)S(1)} %select_add_fusion.3), channel_id=1, source_target_pairs={{0,6},{1,7},{2,4},{3,5},{4,2},{5,3},{6,0},{7,1},{8,14},{9,15},{10,... | collective-permute-start | bytes 294920 | tf_op jit(solution)/shard_map/ppermute | solution.py:294
  105.3 10.9 %collective-permute-start.20 = (f32[96,256]{1,0:T(8,128)S(1)}, f32[96,256]{1,0:T(8,128)S(1)}, u32[]{:S(2)}, u32[]{:S(2)}) collective-permute-start(f32[96,256]{1,0:T(8,128)S(1)} %select_add_fusion.2), channel_id=1, source_target_pairs={{0,6},{1,7},{2,4},{3,5},{4,2},{5,3},{6,0},{7,1},{8,14},{9,15},{10,... | collective-permute-start | bytes 294920 | tf_op jit(solution)/shard_map/ppermute | solution.py:294
  107.2 9.2 %collective-permute-start.30 = (f32[96,256]{1,0:T(8,128)S(1)}, f32[96,256]{1,0:T(8,128)S(1)}, u32[]{:S(2)}, u32[]{:S(2)}) collective-permute-start(f32[96,256]{1,0:T(8,128)S(1)} %select_add_fusion.1), channel_id=1, source_target_pairs={{0,1},{1,0},{2,3},{3,2},{4,5},{5,4},{6,7},{7,6},{8,9},{9,8},{10,11... | collective-permute-start | bytes 294920 | tf_op jit(solution)/shard_map/ppermute | solution.py:294
  108.3 10.2 %collective-permute-start.40 = (f32[96,256]{1,0:T(8,128)S(1)}, f32[96,256]{1,0:T(8,128)S(1)}, u32[]{:S(2)}, u32[]{:S(2)}) collective-permute-start(f32[96,256]{1,0:T(8,128)S(1)} %select_add_fusion), channel_id=1, source_target_pairs={{0,6},{1,7},{2,4},{3,5},{4,2},{5,3},{6,0},{7,1},{8,14},{9,15},{10,... | collective-permute-start | bytes 294920 | tf_op jit(solution)/shard_map/ppermute | solution.py:294
  110.9 8.6 %collective-permute-start.11 = (f32[96,256]{1,0:T(8,128)S(1)}, f32[96,256]{1,0:T(8,128)S(1)}, u32[]{:S(2)}, u32[]{:S(2)}) collective-permute-start(f32[96,256]{1,0:T(8,128)S(1)} %add.140), channel_id=1, source_target_pairs={{0,2},{1,3},{2,0},{3,1},{4,6},{5,7},{6,4},{7,5},{8,10},{9,11},{10,... | collective-permute-start | bytes 294920 | tf_op jit(solution)/shard_map/ppermute | solution.py:294
  116.3 4.7 %collective-permute-start.21 = (f32[96,256]{1,0:T(8,128)S(1)}, f32[96,256]{1,0:T(8,128)S(1)}, u32[]{:S(2)}, u32[]{:S(2)}) collective-permute-start(f32[96,256]{1,0:T(8,128)S(1)} %add.148), channel_id=1, source_target_pairs={{0,16},{8,24},{16,0},{24,8},{1,17},{9,25},{17,1},{25,9},{2,18},{10... | collective-permute-start | bytes 294920 | tf_op jit(solution)/shard_map/ppermute | solution.py:294
  116.4 6.7 %collective-permute-start.31 = (f32[96,256]{1,0:T(8,128)S(1)}, f32[96,256]{1,0:T(8,128)S(1)}, u32[]{:S(2)}, u32[]{:S(2)}) collective-permute-start(f32[96,256]{1,0:T(8,128)S(1)} %add.156), channel_id=1, source_target_pairs={{0,16},{8,24},{16,0},{24,8},{1,17},{9,25},{17,1},{25,9},{2,18},{10... | collective-permute-start | bytes 294920 | tf_op jit(solution)/shard_map/ppermute | solution.py:294
  118.5 6.6 %collective-permute-start.41 = (f32[96,256]{1,0:T(8,128)S(1)}, f32[96,256]{1,0:T(8,128)S(1)}, u32[]{:S(2)}, u32[]{:S(2)}) collective-permute-start(f32[96,256]{1,0:T(8,128)S(1)} %add.164), channel_id=1, source_target_pairs={{0,2},{1,3},{2,0},{3,1},{4,6},{5,7},{6,4},{7,5},{8,10},{9,11},{10,... | collective-permute-start | bytes 294920 | tf_op jit(solution)/shard_map/ppermute | solution.py:294
  119.6 6.7 %collective-permute-start.12 = (f32[192,256]{1,0:T(8,128)S(1)}, f32[192,256]{1,0:T(8,128)S(1)}, u32[]{:S(2)}, u32[]{:S(2)}) collective-permute-start(f32[192,256]{1,0:T(8,128)S(1)} %pad_maximum_fusion.6), channel_id=1, source_target_pairs={{0,1},{1,0},{2,3},{3,2},{4,5},{5,4},{6,7},{7,6},{8,9},{9,8},{10,11... | collective-permute-start | bytes 589832 | tf_op jit(solution)/shard_map/ppermute | solution.py:294
  121.0 6.9 %collective-permute-start.22 = (f32[192,256]{1,0:T(8,128)S(1)}, f32[192,256]{1,0:T(8,128)S(1)}, u32[]{:S(2)}, u32[]{:S(2)}) collective-permute-start(f32[192,256]{1,0:T(8,128)S(1)} %pad_maximum_fusion.7), channel_id=1, source_target_pairs={{0,2},{1,3},{2,0},{3,1},{4,6},{5,7},{6,4},{7,5},{8,10},{9,11},{10,... | collective-permute-start | bytes 589832 | tf_op jit(solution)/shard_map/ppermute | solution.py:294
  123.2 7.5 %collective-permute-start.32 = (f32[192,256]{1,0:T(8,128)S(1)}, f32[192,256]{1,0:T(8,128)S(1)}, u32[]{:S(2)}, u32[]{:S(2)}) collective-permute-start(f32[192,256]{1,0:T(8,128)S(1)} %pad_maximum_fusion.8), channel_id=1, source_target_pairs={{0,6},{1,7},{2,4},{3,5},{4,2},{5,3},{6,0},{7,1},{8,14},{9,15},{10,... | collective-permute-start | bytes 589832 | tf_op jit(solution)/shard_map/ppermute | solution.py:294
  125.1 6.8 %collective-permute-start.42 = (f32[192,256]{1,0:T(8,128)S(1)}, f32[192,256]{1,0:T(8,128)S(1)}, u32[]{:S(2)}, u32[]{:S(2)}) collective-permute-start(f32[192,256]{1,0:T(8,128)S(1)} %pad_maximum_fusion.9), channel_id=1, source_target_pairs={{0,1},{1,0},{2,3},{3,2},{4,5},{5,4},{6,7},{7,6},{8,9},{9,8},{10,11... | collective-permute-start | bytes 589832 | tf_op jit(solution)/shard_map/ppermute | solution.py:294
  126.3 5.7 %collective-permute-start.14 = (f32[384,256]{1,0:T(8,128)S(1)}, f32[384,256]{1,0:T(8,128)S(1)}, u32[]{:S(2)}, u32[]{:S(2)}) collective-permute-start(f32[384,256]{1,0:T(8,128)S(1)} %pad_maximum_fusion.2.rest_0_), channel_id=1, source_target_pairs={{0,8},{8,0},{16,24},{24,16},{1,9},{9,1},{17,25},{25,17},{2,10},{10... | collective-permute-start | bytes 1179656 | tf_op jit(solution)/shard_map/ppermute | solution.py:294
  126.4 11.5 %collective-permute-start.13 = (f32[384,256]{1,0:T(8,128)S(1)}, f32[384,256]{1,0:T(8,128)S(1)}, u32[]{:S(2)}, u32[]{:S(2)}) collective-permute-start(f32[384,256]{1,0:T(8,128)S(1)} %pad_maximum_fusion.2.rest_0_), channel_id=1, source_target_pairs={{0,16},{8,24},{16,0},{24,8},{1,17},{9,25},{17,1},{25,9},{2,18},{10... | collective-permute-start | bytes 1179656 | tf_op jit(solution)/shard_map/ppermute | solution.py:294
  128.0 10.8 %collective-permute-start.24 = (f32[384,256]{1,0:T(8,128)S(1)}, f32[384,256]{1,0:T(8,128)S(1)}, u32[]{:S(2)}, u32[]{:S(2)}) collective-permute-start(f32[384,256]{1,0:T(8,128)S(1)} %pad_maximum_fusion.3.rest_4_), channel_id=1, source_target_pairs={{0,8},{8,0},{16,24},{24,16},{1,9},{9,1},{17,25},{25,17},{2,10},{10... | collective-permute-start | bytes 1179656 | tf_op jit(solution)/shard_map/ppermute | solution.py:294
  130.7 8.9 %collective-permute-start.23 = (f32[384,256]{1,0:T(8,128)S(1)}, f32[384,256]{1,0:T(8,128)S(1)}, u32[]{:S(2)}, u32[]{:S(2)}) collective-permute-start(f32[384,256]{1,0:T(8,128)S(1)} %pad_maximum_fusion.3.rest_4_), channel_id=1, source_target_pairs={{0,1},{1,0},{2,3},{3,2},{4,5},{5,4},{6,7},{7,6},{8,9},{9,8},{10,11... | collective-permute-start | bytes 1179656 | tf_op jit(solution)/shard_map/ppermute | solution.py:294
  131.9 7.8 %collective-permute-start.34 = (f32[384,256]{1,0:T(8,128)S(1)}, f32[384,256]{1,0:T(8,128)S(1)}, u32[]{:S(2)}, u32[]{:S(2)}) collective-permute-start(f32[384,256]{1,0:T(8,128)S(1)} %pad_maximum_fusion.4.rest_8_), channel_id=1, source_target_pairs={{0,8},{8,0},{16,24},{24,16},{1,9},{9,1},{17,25},{25,17},{2,10},{10... | collective-permute-start | bytes 1179656 | tf_op jit(solution)/shard_map/ppermute | solution.py:294
  132.0 11.7 %collective-permute-start.33 = (f32[384,256]{1,0:T(8,128)S(1)}, f32[384,256]{1,0:T(8,128)}, u32[]{:S(2)}, u32[]{:S(2)}) collective-permute-start(f32[384,256]{1,0:T(8,128)S(1)} %pad_maximum_fusion.4.rest_8_), channel_id=1, source_target_pairs={{0,2},{1,3},{2,0},{3,1},{4,6},{5,7},{6,4},{7,5},{8,10},{9,11},{10,... | collective-permute-start | bytes 1179656 | tf_op jit(solution)/shard_map/ppermute | solution.py:294
  138.0 10.9 %collective-permute-start.43 = (f32[384,256]{1,0:T(8,128)S(1)}, f32[384,256]{1,0:T(8,128)}, u32[]{:S(2)}, u32[]{:S(2)}) collective-permute-start(f32[384,256]{1,0:T(8,128)S(1)} %pad_maximum_fusion.5.rest_12_), channel_id=1, source_target_pairs={{0,16},{8,24},{16,0},{24,8},{1,17},{9,25},{17,1},{25,9},{2,18},{10... | collective-permute-start | bytes 1179656 | tf_op jit(solution)/shard_map/ppermute | solution.py:294
  138.8 10.1 %collective-permute-start.44 = (f32[384,256]{1,0:T(8,128)S(1)}, f32[384,256]{1,0:T(8,128)}, u32[]{:S(2)}, u32[]{:S(2)}) collective-permute-start(f32[384,256]{1,0:T(8,128)S(1)} %pad_maximum_fusion.5.rest_12_), channel_id=1, source_target_pairs={{0,8},{8,0},{16,24},{24,16},{1,9},{9,1},{17,25},{25,17},{2,10},{10... | collective-permute-start | bytes 1179656 | tf_op jit(solution)/shard_map/ppermute | solution.py:294
  139.6 9.3 %collective-permute-start.15 = (f32[384,256]{1,0:T(8,128)S(1)}, f32[384,256]{1,0:T(8,128)}, u32[]{:S(2)}, u32[]{:S(2)}) collective-permute-start(f32[384,256]{1,0:T(8,128)S(1)} %collective-permute-done.13.rest_1_), channel_id=1, source_target_pairs={{0,8},{8,0},{16,24},{24,16},{1,9},{9,1},{17,25},{25,17},{2,10},{10... | collective-permute-start | bytes 1179656 | tf_op jit(solution)/shard_map/ppermute | solution.py:294
  139.6 9.3 %collective-permute-start.25 = (f32[384,256]{1,0:T(8,128)S(1)}, f32[384,256]{1,0:T(8,128)}, u32[]{:S(2)}, u32[]{:S(2)}) collective-permute-start(f32[384,256]{1,0:T(8,128)S(1)} %collective-permute-done.23.rest_5_), channel_id=1, source_target_pairs={{0,8},{8,0},{16,24},{24,16},{1,9},{9,1},{17,25},{25,17},{2,10},{10... | collective-permute-start | bytes 1179656 | tf_op jit(solution)/shard_map/ppermute | solution.py:294
  143.7 5.2 %collective-permute-start.35 = (f32[384,256]{1,0:T(8,128)}, f32[384,256]{1,0:T(8,128)}, u32[]{:S(2)}, u32[]{:S(2)}) collective-permute-start(f32[384,256]{1,0:T(8,128)} %collective-permute-done.33.rest_9_), channel_id=1, source_target_pairs={{0,8},{8,0},{16,24},{24,16},{1,9},{9,1},{17,25},{25,17},{2,10},{10... | collective-permute-start | bytes 1179656 | tf_op jit(solution)/shard_map/ppermute | solution.py:294
  148.8 2.1 %collective-permute-start.45 = (f32[384,256]{1,0:T(8,128)}, f32[384,256]{1,0:T(8,128)}, u32[]{:S(2)}, u32[]{:S(2)}) collective-permute-start(f32[384,256]{1,0:T(8,128)} %collective-permute-done.43.rest_13_), channel_id=1, source_target_pairs={{0,8},{8,0},{16,24},{24,16},{1,9},{9,1},{17,25},{25,17},{2,10},{10... | collective-permute-start | bytes 1179656 | tf_op jit(solution)/shard_map/ppermute | solution.py:294
  (4 other events, 11.9 us)

commit v6 on v5

--- a/solution.py
+++ b/solution.py
@@ -76,62 +76,70 @@
 
 
 def cold_kernel(asked_ref, table_ref, out_ref):
-    out_ref[...] = pick(asked_ref[...], table_ref[...])
+    devices, slots = out_ref.shape[:2]
+    found = pick(asked_ref[...], table_ref[...])
+    for device in range(devices):
+        out_ref[device] = found[device * slots : (device + 1) * slots, :]
 
 
 def cold_look_up(asked, table):
-    count, width = asked.shape[1], table.shape[1]
+    count, width = asked.size, table.shape[1]
     return pl.pallas_call(
         cold_kernel,
-        out_shape=jax.ShapeDtypeStruct((count, width), jnp.float32),
+        out_shape=jax.ShapeDtypeStruct(asked.shape + (width,), jnp.float32),
         compiler_params=pltpu.CompilerParams(vmem_limit_bytes=60 * MIB),
         cost_estimate=pl.CostEstimate(
             flops=4 * count * table.size, bytes_accessed=4 * table.size, transcendentals=0
         ),
         name="cold_look_up",
-    )(asked, table)
-
-
-def hot_kernel(half, device_ref, asked_ref, own_ref, far_ref, *out_refs):
+    )(asked.reshape(1, -1), table)
+
+
+def hot_kernel(half, device_ref, asked_ref, own_ref, mine_ref, got_ref, *rest):
+    *out_refs, high, low = rest
     slots = asked_ref.shape[1] // 2
     rows = own_ref.shape[0]
     at = device_ref[1] % half
-    table = jnp.concatenate([own_ref[...], far_ref[...]], axis=0)
-    high, low = split(table)
+    share = rows // 2
+    first = device_ref[0] * share
+    for part, start in ((own_ref, 0), (mine_ref, rows + first), (got_ref, 2 * rows - share - first)):
+        here = pl.ds(pl.multiple_of(start, share), part.shape[0])
+        high[here, :], low[here, :] = split(part[...])
     lanes = lax.broadcasted_iota(jnp.int32, (1, 2 * slots), 1)
     ids = lax.broadcasted_iota(jnp.int32, (2 * rows, 2 * slots), 0)
     for away in range(half):
         asked = asked_ref[pl.ds(at ^ away, 1), :]
         asked = jnp.where((lanes >= slots) & (asked >= 0), asked + rows, asked)
         chosen = jnp.where(ids == asked, 1.0, 0.0).astype(jnp.bfloat16)
-        out_refs[away][...] = dot_rows(chosen, high) + dot_rows(chosen, low)
-
-
-def hot_look_up(half, device, asked, own, far):
+        out_refs[away][...] = dot_rows(chosen, high[...]) + dot_rows(chosen, low[...])
+
+
+def hot_look_up(half, device, asked, own, mine, got):
     slots, width = asked.shape[1], own.shape[1]
     vmem = pl.BlockSpec(memory_space=pltpu.VMEM)
     return pl.pallas_call(
         functools.partial(hot_kernel, half),
-        in_specs=[pl.BlockSpec(memory_space=pltpu.SMEM)] + [vmem] * 3,
+        in_specs=[pl.BlockSpec(memory_space=pltpu.SMEM)] + [vmem] * 4,
         out_specs=[vmem] * half,
         out_shape=[jax.ShapeDtypeStruct((slots, width), jnp.float32)] * half,
+        scratch_shapes=[pltpu.VMEM((2 * own.shape[0], width), jnp.bfloat16)] * 2,
         compiler_params=pltpu.CompilerParams(vmem_limit_bytes=60 * MIB),
         cost_estimate=pl.CostEstimate(
             flops=8 * half * slots * own.size, bytes_accessed=12 * own.size, transcendentals=0
         ),
         name="hot_look_up",
-    )(device, asked, own, far)
+    )(device, asked, own, mine, got)
 
 
 def layer_kernel(
     chunks, half, far_mask, device_ref, counts_ref, cold_ref, w_self_ref, w_neigh_ref, cot_ref, *rest
 ):
     hot_refs = rest[:half]
-    src, prod, back = rest[-3:]
-    grad_refs = rest[-3 - 2 * chunks : -3]
-    hidden_ref = rest[-4 - 2 * chunks]
+    src, cold, prod, back, grads, sems = rest[-6:]
+    grad_refs = rest[-6 - 2 * chunks : -6]
+    hidden_ref = rest[-7 - 2 * chunks]
     n_src = src.shape[1]
-    n_hot = n_src - cold_ref.shape[0]
+    n_hot = n_src - cold.shape[0]
     slots = hot_refs[0].shape[0] // 2
     step = pl.program_id(0)
 
@@ -144,7 +152,10 @@
                 rows = pl.ds(pl.multiple_of(peer * slots, slots), slots)
                 src[0, rows, :] = high[first : first + slots, :]
                 src[1, rows, :] = low[first : first + slots, :]
-        src[0, n_hot:, :], src[1, n_hot:, :] = split(cold_ref[...])
+        cold_slots = cold_ref.shape[1]
+        for peer in range(cold_ref.shape[0]):
+            cold[peer * cold_slots : (peer + 1) * cold_slots, :] = cold_ref[peer]
+        src[0, n_hot:, :], src[1, n_hot:, :] = split(cold[...])
         prod[:n_src, :] = dot(src[0], w_self_ref[...]).astype(jnp.bfloat16)
         both = dot(src[0], w_neigh_ref[...]) + dot(src[1], w_neigh_ref[...])
         prod[n_src:, :] = (both * (1.0 / FAN)).astype(jnp.bfloat16)
@@ -163,29 +174,33 @@
 
         half_rows = src.shape[2] // 2
 
-        def put(out_ref, part, neigh):
+        def put(at, part, neigh):
             first = n_src if neigh else 0
             term = back[first : first + n_src, pl.ds(part * cols, cols)]
-            high, low = split(term * (1.0 / FAN) if neigh else term)
+            term = (term * (1.0 / FAN) if neigh else term).astype(jnp.bfloat16)
             bit = device_ref[2 + part]
-            for k, at in enumerate((bit, 1 - bit)):
-                here = pl.ds(pl.multiple_of(at * half_rows, half_rows), half_rows)
-                total = dot_rows(src[0, :, here], high) + dot_rows(src[0, :, here], low)
+            for k, half_at in enumerate((bit, 1 - bit)):
+                here = pl.ds(pl.multiple_of(half_at * half_rows, half_rows), half_rows)
+                total = dot_rows(src[0, :, here], term)
                 if neigh:
-                    total += dot_rows(src[1, :, here], high)
-                out_ref[k * half_rows : (k + 1) * half_rows, :] = total
+                    total += dot_rows(src[1, :, here], term)
+                grads[at, k * half_rows : (k + 1) * half_rows, :] = total
+            pltpu.make_async_copy(grads.at[at], grad_refs[at], sems.at[at]).start()
 
         @pl.when(device_ref[0] == 0)
         def _():
             for part in range(chunks):
-                put(grad_refs[2 * part], part, False)
-                put(grad_refs[2 * part + 1], part, True)
+                put(2 * part, part, False)
+                put(2 * part + 1, part, True)
 
         @pl.when(device_ref[0] != 0)
         def _():
             for part in range(chunks):
-                put(grad_refs[2 * part], part, True)
-                put(grad_refs[2 * part + 1], part, False)
+                put(2 * part, part, True)
+                put(2 * part + 1, part, False)
+
+        for at in range(2 * chunks):
+            pltpu.make_async_copy(grads.at[at], grad_refs[at], sems.at[at]).wait()
 
 
 def layer(call, chunks, far_mask, device, counts, hot_rows, cold_rows, w_self, w_neigh, cotangent, hidden):
@@ -200,7 +215,7 @@
     tile = lambda i, c: (i, call)
     in_specs = [
         pl.BlockSpec((2 * n_src, block), lambda i, c: (0, i)),
-        pl.BlockSpec(cold_rows.shape, whole),
+        pl.BlockSpec(cold_rows.shape, lambda i, c: (0, 0, 0)),
         pl.BlockSpec((feat_width, wide), column),
         pl.BlockSpec((feat_width, wide), column),
         pl.BlockSpec((block, wide), tile),
@@ -218,11 +233,14 @@
             grid=(targets // block,),
             in_specs=in_specs,
             out_specs=[pl.BlockSpec((block, wide), tile)]
-            + [pl.BlockSpec((feat_width, cols), whole)] * (2 * chunks),
+            + [pl.BlockSpec(memory_space=pl.ANY)] * (2 * chunks),
             scratch_shapes=[
                 pltpu.VMEM((2, n_src, feat_width), jnp.bfloat16),
+                pltpu.VMEM((cold_rows.shape[0] * cold_rows.shape[1], feat_width), jnp.float32),
                 pltpu.VMEM((2 * n_src, wide), jnp.bfloat16),
                 pltpu.VMEM((2 * n_src, wide), jnp.float32),
+                pltpu.VMEM((2 * chunks, feat_width, cols), jnp.float32),
+                pltpu.SemaphoreType.DMA((2 * chunks,)),
             ],
         ),
         out_shape=[jax.ShapeDtypeStruct((targets, hidden_units), jnp.bfloat16)]
@@ -340,7 +358,8 @@
     me = lax.axis_index("dev")
     slots = hot_need.shape[1]
 
-    spread = along_x + core
+    (core,) = core
+    spread = along_x + [core]
     share = hot_table.shape[0] // lax.axis_size("grp")
     which = functools.reduce(jnp.add, [s.bit * (1 << k) for k, s in enumerate(spread)])
     far_table = far.send(lax.dynamic_slice_in_dim(hot_table, which * share, share, axis=0))
@@ -362,13 +381,12 @@
         ],
         axis=1,
     )
-    cold_served = cold_look_up(cold_asked.reshape(1, -1), cold_table)
-    for swap in spread[:-1]:
+    cold_served = cold_look_up(cold_asked, cold_table)
+    for swap in along_x:
         far_table = double(far_table, swap)
     far_table, cold_served = lax.optimization_barrier((far_table, cold_served))
-    far_table = double(far_table, spread[-1])
     cold_rows = exchange(cold_served)
-    served = hot_look_up(half, device, hot_asked, hot_table, far_table)
+    served = hot_look_up(half, device, hot_asked, hot_table, far_table, core.send(far_table))
     pairs = lambda away: [(i, i ^ away) for i in range(2 * half)]
     hot_rows = [served[0]] + [
         lax.ppermute(served[away], "dev", pairs(away)) for away in range(1, half)

time: 156 us -> 151 us (0.968)
  starting transfers between devices: 48.2 us -> 51.2 us
  Pallas kernels: 40.4 us -> 37.7 us
  waiting for transfers between devices: 43.2 us -> 41.2 us
  local copies, waits for them, and re-layouts: 7.47 us -> 5.62 us
    ppermute x43, starting transfers between devices: 42.1 us -> 45 us  [send(): return lax.ppermute(value, self.name, self.pairs)]
    pallas_call x1, Pallas kernels: 21.7 us -> 18.8 us  [layer(): pl.pallas_call(functools.partial(layer_kernel, chunks, len(hot_rows), far...]
    all_to_all x2 -> x0, local copies, waits for them, and re-layouts: 2.75 us -> none  [fetch_rows(): cold_rows = exchange(cold_served)]
    ppermute x43, waiting for transfers between devices: 40.2 us -> 38 us  [send(): return lax.ppermute(value, self.name, self.pairs)]
  transfers between devices with their start and end apart: 47 -> 47, of which waited for: 20 -> 21; matrix products, arithmetic and copies ran while one was open for 5% -> 5% of each run, Pallas kernels for 9% -> 10%
where the time goes in v6:
time: 151 us
  starting transfers between devices  51.2 us (34%)
  waiting for transfers between devices  41.2 us (27%)
  Pallas kernels  37.7 us (25%)
  blocking collectives  9.85 us (7%)
  local copies, waits for them, and re-layouts  5.62 us (4%)
  other arithmetic  4.28 us (3%)
    ppermute x43, starting transfers between devices, send(): return lax.ppermute(value, self.name, self.pairs)  45 us
    ppermute x43, waiting for transfers between devices, send(): return lax.ppermute(value, self.name, self.pairs)  38 us
    pallas_call x1, Pallas kernels, layer(): pl.pallas_call(functools.partial(layer_kernel, chunks, len(hot_rows), far...  18.8 us
    all_to_all x1, blocking collectives, fetch_rows(): asked = exchange(jnp.concatenate([cold_need, hot_list], axis=1))  9.85 us
    pallas_call x1, Pallas kernels, count_matrices(): pl.pallas_call(count_kernel, grid=(targets // block,), in_specs=[pl.Block...  7.39 us
    pallas_call x1, Pallas kernels, place(): pl.pallas_call(place_kernel, in_specs=[pl.BlockSpec(memory_space=pltpu.SM...  4.5 us
    pallas_call x1, Pallas kernels, hot_look_up(): pl.pallas_call(functools.partial(hot_kernel, half), in_specs=[pl.BlockSpe...  3.59 us
    ppermute x3, starting transfers between devices, fetch_rows(): lax.ppermute(served[away], 'dev', pairs(away))  3.49 us
  transfers between devices with their start and end apart: 47, of which 21 were waited for; matrix products, arithmetic and copies ran while one was open for 5% of the time, Pallas kernels for 10%

profile of v6, /device:TPU:0, one launch (start us, length us, event | category | flops | bytes accessed | tf_op | source)
XLA Modules:
  0.0 151.0 jit_solution(7270859856269521636)
XLA Ops:
  0.7 0.9 constant_dynamic-slice_fusion
  1.6 5.1 %collective-permute-start = (f32[64,768]{1,0:T(8,128)S(1)}, f32[64,768]{1,0:T(8,128)S(1)}, u32[]{:S(2)}, u32[]{:S(2)}) collective-permute-start(f32[64,768]{1,0:T(8,128)S(1)} %constant_dynamic-slice_fusion), channel_id=1, source_target_pairs={{0,6},{1,7},{2,4},{3,5},{4,2},{5,3},{6,0},{7,1},{8,14},{9,15},{10,... | collective-permute-start | bytes 589832 | tf_op jit(solution)/shard_map/ppermute | solution.py:312
  6.7 0.8 reshape.14
  7.6 0.8 copy.14
  8.4 9.9 %all_to_all.17 = s32[32,1,260]{2,1,0:T(1,128)S(1)} all-to-all(s32[32,1,260]{2,1,0:T(1,128)S(1)} %all_to_all.11), channel_id=1, replica_groups=mesh['grp'=4,'dev'=8] {'grp','dev'}, dimensions={0} | all-to-all | bytes 66560 | tf_op jit(solution)/shard_map/all_to_all | solution.py:373
  18.2 0.7 collective-permute-start.1
  19.6 3.4 %cold_look_up.1 = f32[32,4,768]{2,1,0:T(4,128)} custom-call(s32[1,128]{1,0:T(1,128)} %reshape.13.asked_ref, f32[1024,768]{1,0:T(8,128)} %table_ref.1), custom_call_target="tpu_custom_call" | custom-call | flops 402653184 | bytes 3145728 | tf_op jit(solution)/shard_map/cold_look_up/pallas_call | solution.py:87
  23.0 2.2 %collective-permute-done.1 = f32[64,768]{1,0:T(8,128)S(1)} collective-permute-done((f32[64,768]{1,0:T(8,128)S(1)}, f32[64,768]{1,0:T(8,128)S(1)}, u32[]{:S(2)}, u32[]{:S(2)}) %collective-permute-start.1) | collective-permute-done | bytes 196640 | tf_op jit(solution)/shard_map/ppermute | solution.py:312
  25.3 2.6 %all-to-all-start.1 = ((f32[32,4,768]{2,1,0:T(4,128)}), f32[32,4,768]{2,1,0:T(4,128)S(1)}, u32[]{:S(2)}, u32[]{:S(2)}) async-start(f32[32,4,768]{2,1,0:T(4,128)} %cold_look_up.1), calls=%async_computation.1 | async-start | bytes 786432 | tf_op jit(solution)/shard_map/all_to_all | solution.py:388
  29.7 0.7 copy-done.4
  30.5 3.6 %hot_look_up.1 = (f32[64,768]{1,0:T(8,128)}, f32[64,768]{1,0:T(8,128)}, f32[64,768]{1,0:T(8,128)}, f32[64,768]{1,0:T(8,128)}) custom-call(s32[6]{0:T(128)} %stack.32.device_ref, s32[4,64]{1,0:T(4,128)} %pad_add_fusion.1.asked_ref, f32[256,768]{1,0:T(8,128)} %own_ref.1, f32[128,768]{1,0:T(8,128)} %copy-done, f32[128,768]{1,0:T(8,128)} %copy-done.4), custom_call_target="tpu_custom_call" | custom-call | flops 402653184 | bytes 2359296 | tf_op jit(solution)/shard_map/hot_look_up/pallas_call | solution.py:120
  34.1 1.7 %collective-permute-start.3 = (f32[64,768]{1,0:T(8,128)}, f32[64,768]{1,0:T(8,128)S(1)}, u32[]{:S(2)}, u32[]{:S(2)}) collective-permute-start(f32[64,768]{1,0:T(8,128)} %get-tuple-element.27), channel_id=1, source_target_pairs={{0,1},{1,0},{2,3},{3,2},{4,5},{5,4},{6,7},{7,6},{8,9},{9,8},{10,11... | collective-permute-start | bytes 589832 | tf_op jit(solution)/shard_map/ppermute | solution.py:392
  35.7 1.5 %collective-permute-start.4 = (f32[64,768]{1,0:T(8,128)}, f32[64,768]{1,0:T(8,128)S(1)}, u32[]{:S(2)}, u32[]{:S(2)}) collective-permute-start(f32[64,768]{1,0:T(8,128)} %get-tuple-element.28), channel_id=1, source_target_pairs={{0,2},{1,3},{2,0},{3,1},{4,6},{5,7},{6,4},{7,5},{8,10},{9,11},{10,... | collective-permute-start | bytes 589832 | tf_op jit(solution)/shard_map/ppermute | solution.py:392
  37.5 7.4 %count_matrices.1.counts_ref = bf16[768,2048]{1,0:T(8,128)(2,1)} custom-call(s32[25,2048]{1,0:T(8,128)} %bitcast.10, s32[1,2048]{1,0:T(1,128)} %bitcast.13), custom_call_target="tpu_custom_call" | custom-call | flops 39321600 | bytes 3145728 | tf_op jit(solution)/shard_map/count_matrices/pallas_call | solution.py:54
  45.0 3.2 %collective-permute-done.5.rest_3_ = f32[64,768]{1,0:T(8,128)S(1)} collective-permute-done((f32[64,768]{1,0:T(8,128)}, f32[64,768]{1,0:T(8,128)S(1)}, u32[]{:S(2)}, u32[]{:S(2)}) %collective-permute-start.5) | collective-permute-done | bytes 196640 | tf_op jit(solution)/shard_map/ppermute | solution.py:392
  49.0 18.8 %layer_0.1 = (bf16[2048,1024]{1,0:T(8,128)(2,1)}, f32[768,256]{1,0:T(8,128)}, f32[768,256]{1,0:T(8,128)}, f32[768,256]{1,0:T(8,128)}, f32[768,256]{1,0:T(8,128)}...) custom-call(s32[6]{0:T(128)} %stack.32.device_ref, ...), custom_call_target="tpu_custom_call" | custom-call | flops 8858370048 | bytes 11534336 | tf_op jit(solution)/shard_map/layer_0/pallas_call | solution.py:229
  68.9 1.5 collective-permute-done.6
  70.4 1.3 slice_add_fusion.7
  71.7 1.6 %collective-permute-start.7 = (f32[384,256]{1,0:T(8,128)S(1)}, f32[384,256]{1,0:T(8,128)S(1)}, u32[]{:S(2)}, u32[]{:S(2)}) collective-permute-start(f32[384,256]{1,0:T(8,128)S(1)} %get-tuple-element.48), channel_id=1, source_target_pairs={{0,16},{8,24},{16,0},{24,8},{1,17},{9,25},{17,1},{25,9},{2,18},{10... | collective-permute-start | bytes 1179656 | tf_op jit(solution)/shard_map/ppermute | solution.py:312
  73.3 1.2 slice_add_fusion.5
  74.5 1.3 collective-permute-start.17
  77.1 6.6 %collective-permute-done.7 = f32[384,256]{1,0:T(8,128)S(1)} collective-permute-done((f32[384,256]{1,0:T(8,128)S(1)}, f32[384,256]{1,0:T(8,128)S(1)}, u32[]{:S(2)}, u32[]{:S(2)}) %collective-permute-start.7) | collective-permute-done | bytes 393248 | tf_op jit(solution)/shard_map/ppermute | solution.py:312
  83.7 1.3 collective-permute-start.8
  85.1 0.8 collective-permute-done.17
  86.6 2.4 %collective-permute-start.28 = (f32[192,256]{1,0:T(8,128)S(1)}, f32[192,256]{1,0:T(8,128)S(1)}, u32[]{:S(2)}, u32[]{:S(2)}) collective-permute-start(f32[192,256]{1,0:T(8,128)S(1)} %get-tuple-element.52), channel_id=1, source_target_pairs={{0,6},{1,7},{2,4},{3,5},{4,2},{5,3},{6,0},{7,1},{8,14},{9,15},{10,... | collective-permute-start | bytes 589832 | tf_op jit(solution)/shard_map/ppermute | solution.py:312
  89.0 2.3 %collective-permute-done.37 = f32[384,256]{1,0:T(8,128)S(1)} collective-permute-done((f32[384,256]{1,0:T(8,128)S(1)}, f32[384,256]{1,0:T(8,128)S(1)}, u32[]{:S(2)}, u32[]{:S(2)}) %collective-permute-start.37) | collective-permute-done | bytes 393248 | tf_op jit(solution)/shard_map/ppermute | solution.py:312
  91.4 1.3 collective-permute-start.38
  93.8 1.0 collective-permute-start.19
  94.8 2.1 %collective-permute-done.28 = f32[192,256]{1,0:T(8,128)S(1)} collective-permute-done((f32[192,256]{1,0:T(8,128)S(1)}, f32[192,256]{1,0:T(8,128)S(1)}, u32[]{:S(2)}, u32[]{:S(2)}) %collective-permute-start.28) | collective-permute-done | bytes 196640 | tf_op jit(solution)/shard_map/ppermute | solution.py:312
  98.3 2.3 %collective-permute-start.10 = (f32[96,256]{1,0:T(8,128)S(1)}, f32[96,256]{1,0:T(8,128)S(1)}, u32[]{:S(2)}, u32[]{:S(2)}) collective-permute-start(f32[96,256]{1,0:T(8,128)S(1)} %select_add_fusion.3), channel_id=1, source_target_pairs={{0,6},{1,7},{2,4},{3,5},{4,2},{5,3},{6,0},{7,1},{8,14},{9,15},{10,... | collective-permute-start | bytes 294920 | tf_op jit(solution)/shard_map/ppermute | solution.py:312
  100.7 2.0 %collective-permute-start.20 = (f32[96,256]{1,0:T(8,128)S(1)}, f32[96,256]{1,0:T(8,128)S(1)}, u32[]{:S(2)}, u32[]{:S(2)}) collective-permute-start(f32[96,256]{1,0:T(8,128)S(1)} %select_add_fusion.2), channel_id=1, source_target_pairs={{0,6},{1,7},{2,4},{3,5},{4,2},{5,3},{6,0},{7,1},{8,14},{9,15},{10,... | collective-permute-start | bytes 294920 | tf_op jit(solution)/shard_map/ppermute | solution.py:312
  102.7 0.8 collective-permute-start.30
  103.6 2.5 %collective-permute-start.40 = (f32[96,256]{1,0:T(8,128)S(1)}, f32[96,256]{1,0:T(8,128)S(1)}, u32[]{:S(2)}, u32[]{:S(2)}) collective-permute-start(f32[96,256]{1,0:T(8,128)S(1)} %select_add_fusion), channel_id=1, source_target_pairs={{0,6},{1,7},{2,4},{3,5},{4,2},{5,3},{6,0},{7,1},{8,14},{9,15},{10,... | collective-permute-start | bytes 294920 | tf_op jit(solution)/shard_map/ppermute | solution.py:312
  106.1 5.5 %collective-permute-start.11 = (f32[96,256]{1,0:T(8,128)S(1)}, f32[96,256]{1,0:T(8,128)S(1)}, u32[]{:S(2)}, u32[]{:S(2)}) collective-permute-start(f32[96,256]{1,0:T(8,128)S(1)} %add.140), channel_id=1, source_target_pairs={{0,2},{1,3},{2,0},{3,1},{4,6},{5,7},{6,4},{7,5},{8,10},{9,11},{10,... | collective-permute-start | bytes 294920 | tf_op jit(solution)/shard_map/ppermute | solution.py:312
  111.7 2.1 %collective-permute-start.31 = (f32[96,256]{1,0:T(8,128)S(1)}, f32[96,256]{1,0:T(8,128)S(1)}, u32[]{:S(2)}, u32[]{:S(2)}) collective-permute-start(f32[96,256]{1,0:T(8,128)S(1)} %add.156), channel_id=1, source_target_pairs={{0,16},{8,24},{16,0},{24,8},{1,17},{9,25},{17,1},{25,9},{2,18},{10... | collective-permute-start | bytes 294920 | tf_op jit(solution)/shard_map/ppermute | solution.py:312
  113.8 1.0 collective-permute-start.41
  116.3 1.6 %collective-permute-start.22 = (f32[192,256]{1,0:T(8,128)S(1)}, f32[192,256]{1,0:T(8,128)S(1)}, u32[]{:S(2)}, u32[]{:S(2)}) collective-permute-start(f32[192,256]{1,0:T(8,128)S(1)} %pad_maximum_fusion.6), channel_id=1, source_target_pairs={{0,2},{1,3},{2,0},{3,1},{4,6},{5,7},{6,4},{7,5},{8,10},{9,11},{10,... | collective-permute-start | bytes 589832 | tf_op jit(solution)/shard_map/ppermute | solution.py:312
  118.0 2.8 %collective-permute-start.32 = (f32[192,256]{1,0:T(8,128)S(1)}, f32[192,256]{1,0:T(8,128)S(1)}, u32[]{:S(2)}, u32[]{:S(2)}) collective-permute-start(f32[192,256]{1,0:T(8,128)S(1)} %pad_maximum_fusion.7), channel_id=1, source_target_pairs={{0,6},{1,7},{2,4},{3,5},{4,2},{5,3},{6,0},{7,1},{8,14},{9,15},{10,... | collective-permute-start | bytes 589832 | tf_op jit(solution)/shard_map/ppermute | solution.py:312
  120.8 0.9 collective-permute-start.42
  121.8 1.4 collective-permute-start.13
  123.6 2.8 %collective-permute-done.32 = f32[192,256]{1,0:T(8,128)S(1)} collective-permute-done((f32[192,256]{1,0:T(8,128)S(1)}, f32[192,256]{1,0:T(8,128)S(1)}, u32[]{:S(2)}, u32[]{:S(2)}) %collective-permute-start.32) | collective-permute-done | bytes 196640 | tf_op jit(solution)/shard_map/ppermute | solution.py:312
  126.4 0.8 collective-permute-start.23
  127.5 5.8 %collective-permute-done.13.rest_1_ = f32[384,256]{1,0:T(8,128)S(1)} collective-permute-done((f32[384,256]{1,0:T(8,128)S(1)}, f32[384,256]{1,0:T(8,128)S(1)}, u32[]{:S(2)}, u32[]{:S(2)}) %collective-permute-start.13) | collective-permute-done | bytes 393248 | tf_op jit(solution)/shard_map/ppermute | solution.py:312
  133.4 1.3 collective-permute-start.43
  135.6 3.5 %collective-permute-done.33.rest_9_ = f32[384,256]{1,0:T(8,128)} collective-permute-done((f32[384,256]{1,0:T(8,128)S(1)}, f32[384,256]{1,0:T(8,128)}, u32[]{:S(2)}, u32[]{:S(2)}) %collective-permute-start.33) | collective-permute-done | bytes 393248 | tf_op jit(solution)/shard_map/ppermute | solution.py:312
  139.1 5.1 %collective-permute-done.43.rest_13_ = f32[384,256]{1,0:T(8,128)} collective-permute-done((f32[384,256]{1,0:T(8,128)S(1)}, f32[384,256]{1,0:T(8,128)}, u32[]{:S(2)}, u32[]{:S(2)}) %collective-permute-start.43) | collective-permute-done | bytes 393248 | tf_op jit(solution)/shard_map/ppermute | solution.py:312
  144.4 2.0 %collective-permute-done.45.rest_15_ = f32[384,256]{1,0:T(8,128)} collective-permute-done((f32[384,256]{1,0:T(8,128)}, f32[384,256]{1,0:T(8,128)}, u32[]{:S(2)}, u32[]{:S(2)}) %collective-permute-start.45) | collective-permute-done | bytes 393248 | tf_op jit(solution)/shard_map/ppermute | solution.py:312
  146.3 4.5 %place.1 = (f32[768,1024]{1,0:T(8,128)}, f32[768,1024]{1,0:T(8,128)}) custom-call(s32[5]{0:T(128)S(1)} %stack.33.where_ref, f32[384,256]{1,0:T(8,128)S(1)} %pad_maximum_fusion.1.rest_0_, f32[384,256]{1,0:T(8,128)S(1)} %collective-permute-done.13.rest_1_, f32[384,256]{1,0:T(8,128)S(1)} %collective-permute-done.14.rest_2_, ...), custom_call_target="tpu_custom_call" | custom-call | bytes 12582912 | tf_op jit(solution)/shard_map/place/pallas_call | solution.py:291
  (119 shorter events, 13.0 us)
Async XLA Ops:
  1.6 16.6 %collective-permute-start = (f32[64,768]{1,0:T(8,128)S(1)}, f32[64,768]{1,0:T(8,128)S(1)}, u32[]{:S(2)}, u32[]{:S(2)}) collective-permute-start(f32[64,768]{1,0:T(8,128)S(1)} %constant_dynamic-slice_fusion), channel_id=1, source_target_pairs={{0,6},{1,7},{2,4},{3,5},{4,2},{5,3},{6,0},{7,1},{8,14},{9,15},{10,... | collective-permute-start | bytes 589832 | tf_op jit(solution)/shard_map/ppermute | solution.py:312
  18.2 7.0 %collective-permute-start.1 = (f32[64,768]{1,0:T(8,128)S(1)}, f32[64,768]{1,0:T(8,128)S(1)}, u32[]{:S(2)}, u32[]{:S(2)}) collective-permute-start(f32[64,768]{1,0:T(8,128)S(1)} %collective-permute-done), channel_id=1, source_target_pairs={{0,16},{8,24},{16,0},{24,8},{1,17},{9,25},{17,1},{25,9},{2,18},{10... | collective-permute-start | bytes 589832 | tf_op jit(solution)/shard_map/ppermute | solution.py:312
  25.3 22.8 %all-to-all-start.1 = ((f32[32,4,768]{2,1,0:T(4,128)}), f32[32,4,768]{2,1,0:T(4,128)S(1)}, u32[]{:S(2)}, u32[]{:S(2)}) async-start(f32[32,4,768]{2,1,0:T(4,128)} %cold_look_up.1), calls=%async_computation.1 | async-start | bytes 786432 | tf_op jit(solution)/shard_map/all_to_all | solution.py:388
  27.9 1.8 %collective-permute-start.2 = (f32[128,768]{1,0:T(8,128)S(1)}, f32[128,768]{1,0:T(8,128)S(1)}, u32[]{:S(2)}, u32[]{:S(2)}) collective-permute-start(f32[128,768]{1,0:T(8,128)S(1)} %pad_maximum_fusion.mine_ref), channel_id=1, source_target_pairs={{0,8},{8,0},{16,24},{24,16},{1,9},{9,1},{17,25},{25,17},{2,10},{10... | collective-permute-start | bytes 1179656 | tf_op jit(solution)/shard_map/ppermute | solution.py:312
  34.1 10.9 %collective-permute-start.3 = (f32[64,768]{1,0:T(8,128)}, f32[64,768]{1,0:T(8,128)S(1)}, u32[]{:S(2)}, u32[]{:S(2)}) collective-permute-start(f32[64,768]{1,0:T(8,128)} %get-tuple-element.27), channel_id=1, source_target_pairs={{0,1},{1,0},{2,3},{3,2},{4,5},{5,4},{6,7},{7,6},{8,9},{9,8},{10,11... | collective-permute-start | bytes 589832 | tf_op jit(solution)/shard_map/ppermute | solution.py:392
  35.7 9.2 %collective-permute-start.4 = (f32[64,768]{1,0:T(8,128)}, f32[64,768]{1,0:T(8,128)S(1)}, u32[]{:S(2)}, u32[]{:S(2)}) collective-permute-start(f32[64,768]{1,0:T(8,128)} %get-tuple-element.28), channel_id=1, source_target_pairs={{0,2},{1,3},{2,0},{3,1},{4,6},{5,7},{6,4},{7,5},{8,10},{9,11},{10,... | collective-permute-start | bytes 589832 | tf_op jit(solution)/shard_map/ppermute | solution.py:392
  37.2 10.9 %collective-permute-start.5 = (f32[64,768]{1,0:T(8,128)}, f32[64,768]{1,0:T(8,128)S(1)}, u32[]{:S(2)}, u32[]{:S(2)}) collective-permute-start(f32[64,768]{1,0:T(8,128)} %get-tuple-element.29), channel_id=1, source_target_pairs={{0,3},{1,2},{2,1},{3,0},{4,7},{5,6},{6,5},{7,4},{8,11},{9,10},{10,... | collective-permute-start | bytes 589832 | tf_op jit(solution)/shard_map/ppermute | solution.py:392
  67.8 8.0 %copy-start.2 = (f32[768,256]{1,0:T(8,128)S(1)}, f32[768,256]{1,0:T(8,128)}, u32[]{:S(2)}) copy-start(f32[768,256]{1,0:T(8,128)} %get-tuple-element.35) | copy-start | bytes 2359300
  67.8 2.6 %collective-permute-start.6 = (f32[768,256]{1,0:T(8,128)}, f32[768,256]{1,0:T(8,128)S(1)}, u32[]{:S(2)}, u32[]{:S(2)}) collective-permute-start(f32[768,256]{1,0:T(8,128)} %get-tuple-element.32), channel_id=1, source_target_pairs={{0,8},{8,0},{16,24},{24,16},{1,9},{9,1},{17,25},{25,17},{2,10},{10... | collective-permute-start | bytes 2359304 | tf_op jit(solution)/shard_map/ppermute | solution.py:312
  67.9 5.4 %collective-permute-start.16 = (f32[768,256]{1,0:T(8,128)}, f32[768,256]{1,0:T(8,128)S(1)}, u32[]{:S(2)}, u32[]{:S(2)}) collective-permute-start(f32[768,256]{1,0:T(8,128)} %get-tuple-element.34), channel_id=1, source_target_pairs={{0,8},{8,0},{16,24},{24,16},{1,9},{9,1},{17,25},{25,17},{2,10},{10... | collective-permute-start | bytes 2359304 | tf_op jit(solution)/shard_map/ppermute | solution.py:312
  68.4 7.4 %collective-permute-start.26 = (f32[768,256]{1,0:T(8,128)}, f32[768,256]{1,0:T(8,128)S(1)}, u32[]{:S(2)}, u32[]{:S(2)}) collective-permute-start(f32[768,256]{1,0:T(8,128)} %get-tuple-element.36), channel_id=1, source_target_pairs={{0,8},{8,0},{16,24},{24,16},{1,9},{9,1},{17,25},{25,17},{2,10},{10... | collective-permute-start | bytes 2359304 | tf_op jit(solution)/shard_map/ppermute | solution.py:312
  68.5 7.9 %collective-permute-start.36 = (f32[768,256]{1,0:T(8,128)}, f32[768,256]{1,0:T(8,128)S(1)}, u32[]{:S(2)}, u32[]{:S(2)}) collective-permute-start(f32[768,256]{1,0:T(8,128)} %get-tuple-element.38), channel_id=1, source_target_pairs={{0,8},{8,0},{16,24},{24,16},{1,9},{9,1},{17,25},{25,17},{2,10},{10... | collective-permute-start | bytes 2359304 | tf_op jit(solution)/shard_map/ppermute | solution.py:312
  71.7 12.0 %collective-permute-start.7 = (f32[384,256]{1,0:T(8,128)S(1)}, f32[384,256]{1,0:T(8,128)S(1)}, u32[]{:S(2)}, u32[]{:S(2)}) collective-permute-start(f32[384,256]{1,0:T(8,128)S(1)} %get-tuple-element.48), channel_id=1, source_target_pairs={{0,16},{8,24},{16,0},{24,8},{1,17},{9,25},{17,1},{25,9},{2,18},{10... | collective-permute-start | bytes 1179656 | tf_op jit(solution)/shard_map/ppermute | solution.py:312
  74.5 11.4 %collective-permute-start.17 = (f32[384,256]{1,0:T(8,128)S(1)}, f32[384,256]{1,0:T(8,128)S(1)}, u32[]{:S(2)}, u32[]{:S(2)}) collective-permute-start(f32[384,256]{1,0:T(8,128)S(1)} %get-tuple-element.46), channel_id=1, source_target_pairs={{0,1},{1,0},{2,3},{3,2},{4,5},{5,4},{6,7},{7,6},{8,9},{9,8},{10,11... | collective-permute-start | bytes 1179656 | tf_op jit(solution)/shard_map/ppermute | solution.py:312
  75.9 10.7 %collective-permute-start.27 = (f32[384,256]{1,0:T(8,128)S(1)}, f32[384,256]{1,0:T(8,128)S(1)}, u32[]{:S(2)}, u32[]{:S(2)}) collective-permute-start(f32[384,256]{1,0:T(8,128)S(1)} %get-tuple-element.44), channel_id=1, source_target_pairs={{0,2},{1,3},{2,0},{3,1},{4,6},{5,7},{6,4},{7,5},{8,10},{9,11},{10,... | collective-permute-start | bytes 1179656 | tf_op jit(solution)/shard_map/ppermute | solution.py:312
  76.5 14.8 %collective-permute-start.37 = (f32[384,256]{1,0:T(8,128)S(1)}, f32[384,256]{1,0:T(8,128)S(1)}, u32[]{:S(2)}, u32[]{:S(2)}) collective-permute-start(f32[384,256]{1,0:T(8,128)S(1)} %get-tuple-element.42), channel_id=1, source_target_pairs={{0,16},{8,24},{16,0},{24,8},{1,17},{9,25},{17,1},{25,9},{2,18},{10... | collective-permute-start | bytes 1179656 | tf_op jit(solution)/shard_map/ppermute | solution.py:312
  83.7 9.0 %collective-permute-start.8 = (f32[192,256]{1,0:T(8,128)S(1)}, f32[192,256]{1,0:T(8,128)S(1)}, u32[]{:S(2)}, u32[]{:S(2)}) collective-permute-start(f32[192,256]{1,0:T(8,128)S(1)} %get-tuple-element.56), channel_id=1, source_target_pairs={{0,1},{1,0},{2,3},{3,2},{4,5},{5,4},{6,7},{7,6},{8,9},{9,8},{10,11... | collective-permute-start | bytes 589832 | tf_op jit(solution)/shard_map/ppermute | solution.py:312
  86.0 7.8 %collective-permute-start.18 = (f32[192,256]{1,0:T(8,128)S(1)}, f32[192,256]{1,0:T(8,128)S(1)}, u32[]{:S(2)}, u32[]{:S(2)}) collective-permute-start(f32[192,256]{1,0:T(8,128)S(1)} %get-tuple-element.54), channel_id=1, source_target_pairs={{0,2},{1,3},{2,0},{3,1},{4,6},{5,7},{6,4},{7,5},{8,10},{9,11},{10,... | collective-permute-start | bytes 589832 | tf_op jit(solution)/shard_map/ppermute | solution.py:312
  86.6 10.4 %collective-permute-start.28 = (f32[192,256]{1,0:T(8,128)S(1)}, f32[192,256]{1,0:T(8,128)S(1)}, u32[]{:S(2)}, u32[]{:S(2)}) collective-permute-start(f32[192,256]{1,0:T(8,128)S(1)} %get-tuple-element.52), channel_id=1, source_target_pairs={{0,6},{1,7},{2,4},{3,5},{4,2},{5,3},{6,0},{7,1},{8,14},{9,15},{10,... | collective-permute-start | bytes 589832 | tf_op jit(solution)/shard_map/ppermute | solution.py:312
  91.4 6.2 %collective-permute-start.38 = (f32[192,256]{1,0:T(8,128)S(1)}, f32[192,256]{1,0:T(8,128)S(1)}, u32[]{:S(2)}, u32[]{:S(2)}) collective-permute-start(f32[192,256]{1,0:T(8,128)S(1)} %get-tuple-element.50), channel_id=1, source_target_pairs={{0,1},{1,0},{2,3},{3,2},{4,5},{5,4},{6,7},{7,6},{8,9},{9,8},{10,11... | collective-permute-start | bytes 589832 | tf_op jit(solution)/shard_map/ppermute | solution.py:312
  92.7 5.6 %collective-permute-start.9 = (f32[96,256]{1,0:T(8,128)S(1)}, f32[96,256]{1,0:T(8,128)S(1)}, u32[]{:S(2)}, u32[]{:S(2)}) collective-permute-start(f32[96,256]{1,0:T(8,128)S(1)} %broadcast_select_fusion.29), channel_id=1, source_target_pairs={{0,2},{1,3},{2,0},{3,1},{4,6},{5,7},{6,4},{7,5},{8,10},{9,11},{10,... | collective-permute-start | bytes 294920 | tf_op jit(solution)/shard_map/ppermute | solution.py:312
  93.8 6.8 %collective-permute-start.19 = (f32[96,256]{1,0:T(8,128)S(1)}, f32[96,256]{1,0:T(8,128)S(1)}, u32[]{:S(2)}, u32[]{:S(2)}) collective-permute-start(f32[96,256]{1,0:T(8,128)S(1)} %broadcast_select_fusion.23), channel_id=1, source_target_pairs={{0,16},{8,24},{16,0},{24,8},{1,17},{9,25},{17,1},{25,9},{2,18},{10... | collective-permute-start | bytes 294920 | tf_op jit(solution)/shard_map/ppermute | solution.py:312
  97.0 5.7 %collective-permute-start.29 = (f32[96,256]{1,0:T(8,128)S(1)}, f32[96,256]{1,0:T(8,128)S(1)}, u32[]{:S(2)}, u32[]{:S(2)}) collective-permute-start(f32[96,256]{1,0:T(8,128)S(1)} %broadcast_select_fusion.20), channel_id=1, source_target_pairs={{0,16},{8,24},{16,0},{24,8},{1,17},{9,25},{17,1},{25,9},{2,18},{10... | collective-permute-start | bytes 294920 | tf_op jit(solution)/shard_map/ppermute | solution.py:312
  97.6 6.0 %collective-permute-start.39 = (f32[96,256]{1,0:T(8,128)S(1)}, f32[96,256]{1,0:T(8,128)S(1)}, u32[]{:S(2)}, u32[]{:S(2)}) collective-permute-start(f32[96,256]{1,0:T(8,128)S(1)} %broadcast_select_fusion.26), channel_id=1, source_target_pairs={{0,2},{1,3},{2,0},{3,1},{4,6},{5,7},{6,4},{7,5},{8,10},{9,11},{10,... | collective-permute-start | bytes 294920 | tf_op jit(solution)/shard_map/ppermute | solution.py:312
  98.3 7.7 %collective-permute-start.10 = (f32[96,256]{1,0:T(8,128)S(1)}, f32[96,256]{1,0:T(8,128)S(1)}, u32[]{:S(2)}, u32[]{:S(2)}) collective-permute-start(f32[96,256]{1,0:T(8,128)S(1)} %select_add_fusion.3), channel_id=1, source_target_pairs={{0,6},{1,7},{2,4},{3,5},{4,2},{5,3},{6,0},{7,1},{8,14},{9,15},{10,... | collective-permute-start | bytes 294920 | tf_op jit(solution)/shard_map/ppermute | solution.py:312
  100.7 10.9 %collective-permute-start.20 = (f32[96,256]{1,0:T(8,128)S(1)}, f32[96,256]{1,0:T(8,128)S(1)}, u32[]{:S(2)}, u32[]{:S(2)}) collective-permute-start(f32[96,256]{1,0:T(8,128)S(1)} %select_add_fusion.2), channel_id=1, source_target_pairs={{0,6},{1,7},{2,4},{3,5},{4,2},{5,3},{6,0},{7,1},{8,14},{9,15},{10,... | collective-permute-start | bytes 294920 | tf_op jit(solution)/shard_map/ppermute | solution.py:312
  102.7 9.0 %collective-permute-start.30 = (f32[96,256]{1,0:T(8,128)S(1)}, f32[96,256]{1,0:T(8,128)S(1)}, u32[]{:S(2)}, u32[]{:S(2)}) collective-permute-start(f32[96,256]{1,0:T(8,128)S(1)} %select_add_fusion.1), channel_id=1, source_target_pairs={{0,1},{1,0},{2,3},{3,2},{4,5},{5,4},{6,7},{7,6},{8,9},{9,8},{10,11... | collective-permute-start | bytes 294920 | tf_op jit(solution)/shard_map/ppermute | solution.py:312
  103.6 10.2 %collective-permute-start.40 = (f32[96,256]{1,0:T(8,128)S(1)}, f32[96,256]{1,0:T(8,128)S(1)}, u32[]{:S(2)}, u32[]{:S(2)}) collective-permute-start(f32[96,256]{1,0:T(8,128)S(1)} %select_add_fusion), channel_id=1, source_target_pairs={{0,6},{1,7},{2,4},{3,5},{4,2},{5,3},{6,0},{7,1},{8,14},{9,15},{10,... | collective-permute-start | bytes 294920 | tf_op jit(solution)/shard_map/ppermute | solution.py:312
  106.1 8.9 %collective-permute-start.11 = (f32[96,256]{1,0:T(8,128)S(1)}, f32[96,256]{1,0:T(8,128)S(1)}, u32[]{:S(2)}, u32[]{:S(2)}) collective-permute-start(f32[96,256]{1,0:T(8,128)S(1)} %add.140), channel_id=1, source_target_pairs={{0,2},{1,3},{2,0},{3,1},{4,6},{5,7},{6,4},{7,5},{8,10},{9,11},{10,... | collective-permute-start | bytes 294920 | tf_op jit(solution)/shard_map/ppermute | solution.py:312
  111.6 4.7 %collective-permute-start.21 = (f32[96,256]{1,0:T(8,128)S(1)}, f32[96,256]{1,0:T(8,128)S(1)}, u32[]{:S(2)}, u32[]{:S(2)}) collective-permute-start(f32[96,256]{1,0:T(8,128)S(1)} %add.148), channel_id=1, source_target_pairs={{0,16},{8,24},{16,0},{24,8},{1,17},{9,25},{17,1},{25,9},{2,18},{10... | collective-permute-start | bytes 294920 | tf_op jit(solution)/shard_map/ppermute | solution.py:312
  111.7 6.2 %collective-permute-start.31 = (f32[96,256]{1,0:T(8,128)S(1)}, f32[96,256]{1,0:T(8,128)S(1)}, u32[]{:S(2)}, u32[]{:S(2)}) collective-permute-start(f32[96,256]{1,0:T(8,128)S(1)} %add.156), channel_id=1, source_target_pairs={{0,16},{8,24},{16,0},{24,8},{1,17},{9,25},{17,1},{25,9},{2,18},{10... | collective-permute-start | bytes 294920 | tf_op jit(solution)/shard_map/ppermute | solution.py:312
  113.8 6.9 %collective-permute-start.41 = (f32[96,256]{1,0:T(8,128)S(1)}, f32[96,256]{1,0:T(8,128)S(1)}, u32[]{:S(2)}, u32[]{:S(2)}) collective-permute-start(f32[96,256]{1,0:T(8,128)S(1)} %add.164), channel_id=1, source_target_pairs={{0,2},{1,3},{2,0},{3,1},{4,6},{5,7},{6,4},{7,5},{8,10},{9,11},{10,... | collective-permute-start | bytes 294920 | tf_op jit(solution)/shard_map/ppermute | solution.py:312
  115.0 6.6 %collective-permute-start.12 = (f32[192,256]{1,0:T(8,128)S(1)}, f32[192,256]{1,0:T(8,128)S(1)}, u32[]{:S(2)}, u32[]{:S(2)}) collective-permute-start(f32[192,256]{1,0:T(8,128)S(1)} %pad_maximum_fusion.5), channel_id=1, source_target_pairs={{0,1},{1,0},{2,3},{3,2},{4,5},{5,4},{6,7},{7,6},{8,9},{9,8},{10,11... | collective-permute-start | bytes 589832 | tf_op jit(solution)/shard_map/ppermute | solution.py:312
  116.3 7.1 %collective-permute-start.22 = (f32[192,256]{1,0:T(8,128)S(1)}, f32[192,256]{1,0:T(8,128)S(1)}, u32[]{:S(2)}, u32[]{:S(2)}) collective-permute-start(f32[192,256]{1,0:T(8,128)S(1)} %pad_maximum_fusion.6), channel_id=1, source_target_pairs={{0,2},{1,3},{2,0},{3,1},{4,6},{5,7},{6,4},{7,5},{8,10},{9,11},{10,... | collective-permute-start | bytes 589832 | tf_op jit(solution)/shard_map/ppermute | solution.py:312
  118.0 8.4 %collective-permute-start.32 = (f32[192,256]{1,0:T(8,128)S(1)}, f32[192,256]{1,0:T(8,128)S(1)}, u32[]{:S(2)}, u32[]{:S(2)}) collective-permute-start(f32[192,256]{1,0:T(8,128)S(1)} %pad_maximum_fusion.7), channel_id=1, source_target_pairs={{0,6},{1,7},{2,4},{3,5},{4,2},{5,3},{6,0},{7,1},{8,14},{9,15},{10,... | collective-permute-start | bytes 589832 | tf_op jit(solution)/shard_map/ppermute | solution.py:312
  120.8 6.5 %collective-permute-start.42 = (f32[192,256]{1,0:T(8,128)S(1)}, f32[192,256]{1,0:T(8,128)S(1)}, u32[]{:S(2)}, u32[]{:S(2)}) collective-permute-start(f32[192,256]{1,0:T(8,128)S(1)} %pad_maximum_fusion.8), channel_id=1, source_target_pairs={{0,1},{1,0},{2,3},{3,2},{4,5},{5,4},{6,7},{7,6},{8,9},{9,8},{10,11... | collective-permute-start | bytes 589832 | tf_op jit(solution)/shard_map/ppermute | solution.py:312
  121.8 5.7 %collective-permute-start.14 = (f32[384,256]{1,0:T(8,128)S(1)}, f32[384,256]{1,0:T(8,128)S(1)}, u32[]{:S(2)}, u32[]{:S(2)}) collective-permute-start(f32[384,256]{1,0:T(8,128)S(1)} %pad_maximum_fusion.1.rest_0_), channel_id=1, source_target_pairs={{0,8},{8,0},{16,24},{24,16},{1,9},{9,1},{17,25},{25,17},{2,10},{10... | collective-permute-start | bytes 1179656 | tf_op jit(solution)/shard_map/ppermute | solution.py:312
  121.8 11.5 %collective-permute-start.13 = (f32[384,256]{1,0:T(8,128)S(1)}, f32[384,256]{1,0:T(8,128)S(1)}, u32[]{:S(2)}, u32[]{:S(2)}) collective-permute-start(f32[384,256]{1,0:T(8,128)S(1)} %pad_maximum_fusion.1.rest_0_), channel_id=1, source_target_pairs={{0,16},{8,24},{16,0},{24,8},{1,17},{9,25},{17,1},{25,9},{2,18},{10... | collective-permute-start | bytes 1179656 | tf_op jit(solution)/shard_map/ppermute | solution.py:312
  123.5 11.2 %collective-permute-start.24 = (f32[384,256]{1,0:T(8,128)S(1)}, f32[384,256]{1,0:T(8,128)S(1)}, u32[]{:S(2)}, u32[]{:S(2)}) collective-permute-start(f32[384,256]{1,0:T(8,128)S(1)} %pad_maximum_fusion.2.rest_4_), channel_id=1, source_target_pairs={{0,8},{8,0},{16,24},{24,16},{1,9},{9,1},{17,25},{25,17},{2,10},{10... | collective-permute-start | bytes 1179656 | tf_op jit(solution)/shard_map/ppermute | solution.py:312
  126.4 8.7 %collective-permute-start.23 = (f32[384,256]{1,0:T(8,128)S(1)}, f32[384,256]{1,0:T(8,128)S(1)}, u32[]{:S(2)}, u32[]{:S(2)}) collective-permute-start(f32[384,256]{1,0:T(8,128)S(1)} %pad_maximum_fusion.2.rest_4_), channel_id=1, source_target_pairs={{0,1},{1,0},{2,3},{3,2},{4,5},{5,4},{6,7},{7,6},{8,9},{9,8},{10,11... | collective-permute-start | bytes 1179656 | tf_op jit(solution)/shard_map/ppermute | solution.py:312
  127.3 7.9 %collective-permute-start.34 = (f32[384,256]{1,0:T(8,128)S(1)}, f32[384,256]{1,0:T(8,128)S(1)}, u32[]{:S(2)}, u32[]{:S(2)}) collective-permute-start(f32[384,256]{1,0:T(8,128)S(1)} %pad_maximum_fusion.3.rest_8_), channel_id=1, source_target_pairs={{0,8},{8,0},{16,24},{24,16},{1,9},{9,1},{17,25},{25,17},{2,10},{10... | collective-permute-start | bytes 1179656 | tf_op jit(solution)/shard_map/ppermute | solution.py:312
  127.5 11.7 %collective-permute-start.33 = (f32[384,256]{1,0:T(8,128)S(1)}, f32[384,256]{1,0:T(8,128)}, u32[]{:S(2)}, u32[]{:S(2)}) collective-permute-start(f32[384,256]{1,0:T(8,128)S(1)} %pad_maximum_fusion.3.rest_8_), channel_id=1, source_target_pairs={{0,2},{1,3},{2,0},{3,1},{4,6},{5,7},{6,4},{7,5},{8,10},{9,11},{10,... | collective-permute-start | bytes 1179656 | tf_op jit(solution)/shard_map/ppermute | solution.py:312
  133.4 10.9 %collective-permute-start.43 = (f32[384,256]{1,0:T(8,128)S(1)}, f32[384,256]{1,0:T(8,128)}, u32[]{:S(2)}, u32[]{:S(2)}) collective-permute-start(f32[384,256]{1,0:T(8,128)S(1)} %pad_maximum_fusion.4.rest_12_), channel_id=1, source_target_pairs={{0,16},{8,24},{16,0},{24,8},{1,17},{9,25},{17,1},{25,9},{2,18},{10... | collective-permute-start | bytes 1179656 | tf_op jit(solution)/shard_map/ppermute | solution.py:312
  134.7 9.7 %collective-permute-start.44 = (f32[384,256]{1,0:T(8,128)S(1)}, f32[384,256]{1,0:T(8,128)}, u32[]{:S(2)}, u32[]{:S(2)}) collective-permute-start(f32[384,256]{1,0:T(8,128)S(1)} %pad_maximum_fusion.4.rest_12_), channel_id=1, source_target_pairs={{0,8},{8,0},{16,24},{24,16},{1,9},{9,1},{17,25},{25,17},{2,10},{10... | collective-permute-start | bytes 1179656 | tf_op jit(solution)/shard_map/ppermute | solution.py:312
  135.1 9.3 %collective-permute-start.15 = (f32[384,256]{1,0:T(8,128)S(1)}, f32[384,256]{1,0:T(8,128)}, u32[]{:S(2)}, u32[]{:S(2)}) collective-permute-start(f32[384,256]{1,0:T(8,128)S(1)} %collective-permute-done.13.rest_1_), channel_id=1, source_target_pairs={{0,8},{8,0},{16,24},{24,16},{1,9},{9,1},{17,25},{25,17},{2,10},{10... | collective-permute-start | bytes 1179656 | tf_op jit(solution)/shard_map/ppermute | solution.py:312
  135.2 9.2 %collective-permute-start.25 = (f32[384,256]{1,0:T(8,128)S(1)}, f32[384,256]{1,0:T(8,128)}, u32[]{:S(2)}, u32[]{:S(2)}) collective-permute-start(f32[384,256]{1,0:T(8,128)S(1)} %collective-permute-done.23.rest_5_), channel_id=1, source_target_pairs={{0,8},{8,0},{16,24},{24,16},{1,9},{9,1},{17,25},{25,17},{2,10},{10... | collective-permute-start | bytes 1179656 | tf_op jit(solution)/shard_map/ppermute | solution.py:312
  139.1 5.2 %collective-permute-start.35 = (f32[384,256]{1,0:T(8,128)}, f32[384,256]{1,0:T(8,128)}, u32[]{:S(2)}, u32[]{:S(2)}) collective-permute-start(f32[384,256]{1,0:T(8,128)} %collective-permute-done.33.rest_9_), channel_id=1, source_target_pairs={{0,8},{8,0},{16,24},{24,16},{1,9},{9,1},{17,25},{25,17},{2,10},{10... | collective-permute-start | bytes 1179656 | tf_op jit(solution)/shard_map/ppermute | solution.py:312
  144.3 2.1 %collective-permute-start.45 = (f32[384,256]{1,0:T(8,128)}, f32[384,256]{1,0:T(8,128)}, u32[]{:S(2)}, u32[]{:S(2)}) collective-permute-start(f32[384,256]{1,0:T(8,128)} %collective-permute-done.43.rest_13_), channel_id=1, source_target_pairs={{0,8},{8,0},{16,24},{24,16},{1,9},{9,1},{17,25},{25,17},{2,10},{10... | collective-permute-start | bytes 1179656 | tf_op jit(solution)/shard_map/ppermute | solution.py:312
  (7 other events, 19.1 us)

commit v7 on v6

--- a/solution.py
+++ b/solution.py
@@ -123,7 +123,7 @@
         out_specs=[vmem] * half,
         out_shape=[jax.ShapeDtypeStruct((slots, width), jnp.float32)] * half,
         scratch_shapes=[pltpu.VMEM((2 * own.shape[0], width), jnp.bfloat16)] * 2,
-        compiler_params=pltpu.CompilerParams(vmem_limit_bytes=60 * MIB),
+        compiler_params=pltpu.CompilerParams(vmem_limit_bytes=24 * MIB),
         cost_estimate=pl.CostEstimate(
             flops=8 * half * slots * own.size, bytes_accessed=12 * own.size, transcendentals=0
         ),
@@ -209,7 +209,7 @@
     n_src = counts.shape[0] // 2
     wide = hidden_units // CALLS
     cols = wide // chunks
-    block = 512
+    block = 1024
     whole = lambda i, c: (0, 0)
     column = lambda i, c: (0, call)
     tile = lambda i, c: (i, call)
@@ -295,7 +295,7 @@
         out_specs=[pl.BlockSpec(memory_space=pl.ANY)] * 2,
         out_shape=[shape, shape],
         scratch_shapes=[pltpu.SemaphoreType.DMA((len(pieces),))],
-        compiler_params=pltpu.CompilerParams(vmem_limit_bytes=16 * MIB),
+        compiler_params=pltpu.CompilerParams(vmem_limit_bytes=8 * MIB),
         cost_estimate=pl.CostEstimate(
             flops=0, bytes_accessed=8 * len(pieces) * rows * cols, transcendentals=0
         ),

time: 151 us -> 150 us (level)
  waiting for transfers between devices: 41.2 us -> 44.8 us
  starting transfers between devices: 51.2 us -> 49.1 us
  Pallas kernels: 37.7 us -> 35.9 us
    ppermute x43, waiting for transfers between devices: 38 us -> 40.9 us  [send(): return lax.ppermute(value, self.name, self.pairs)]
    ppermute x43, starting transfers between devices: 45 us -> 43 us  [send(): return lax.ppermute(value, self.name, self.pairs)]
  transfers between devices with their start and end apart: 47 -> 47, of which waited for: 21 -> 20; matrix products, arithmetic and copies ran while one was open for 5% -> 4% of each run, Pallas kernels for 10% -> 9%
where the time goes in v7:
time: 150 us
  starting transfers between devices  49.1 us (33%)
  waiting for transfers between devices  44.8 us (30%)
  Pallas kernels  35.9 us (24%)
  blocking collectives  9.85 us (7%)
  local copies, waits for them, and re-layouts  4.94 us (3%)
  other arithmetic  3.69 us (2%)
    ppermute x43, starting transfers between devices, send(): return lax.ppermute(value, self.name, self.pairs)  43 us
    ppermute x43, waiting for transfers between devices, send(): return lax.ppermute(value, self.name, self.pairs)  40.9 us
    pallas_call x1, Pallas kernels, layer(): pl.pallas_call(functools.partial(layer_kernel, chunks, len(hot_rows), far...  18.5 us
    all_to_all x1, blocking collectives, fetch_rows(): asked = exchange(jnp.concatenate([cold_need, hot_list], axis=1))  9.85 us
    pallas_call x1, Pallas kernels, count_matrices(): pl.pallas_call(count_kernel, grid=(targets // block,), in_specs=[pl.Block...  7.39 us
    pallas_call x1, Pallas kernels, place(): pl.pallas_call(place_kernel, in_specs=[pl.BlockSpec(memory_space=pltpu.SM...  4.5 us
    ppermute x3, waiting for transfers between devices, fetch_rows(): lax.ppermute(served[away], 'dev', pairs(away))  3.95 us
    ppermute x3, starting transfers between devices, fetch_rows(): lax.ppermute(served[away], 'dev', pairs(away))  3.49 us
  transfers between devices with their start and end apart: 47, of which 20 were waited for; matrix products, arithmetic and copies ran while one was open for 4% of the time, Pallas kernels for 9%

profile of v7, /device:TPU:0, one launch (start us, length us, event | category | flops | bytes accessed | tf_op | source)
XLA Modules:
  0.0 149.5 jit_solution(13021100400923844307)
XLA Ops:
  0.7 0.9 constant_dynamic-slice_fusion
  1.6 5.1 %collective-permute-start = (f32[64,768]{1,0:T(8,128)S(1)}, f32[64,768]{1,0:T(8,128)S(1)}, u32[]{:S(2)}, u32[]{:S(2)}) collective-permute-start(f32[64,768]{1,0:T(8,128)S(1)} %constant_dynamic-slice_fusion), channel_id=1, source_target_pairs={{0,6},{1,7},{2,4},{3,5},{4,2},{5,3},{6,0},{7,1},{8,14},{9,15},{10,... | collective-permute-start | bytes 589832 | tf_op jit(solution)/shard_map/ppermute | solution.py:312
  7.6 0.8 copy.14
  8.4 9.9 %all_to_all.17 = s32[32,1,260]{2,1,0:T(1,128)S(1)} all-to-all(s32[32,1,260]{2,1,0:T(1,128)S(1)} %all_to_all.11), channel_id=1, replica_groups=mesh['grp'=4,'dev'=8] {'grp','dev'}, dimensions={0} | all-to-all | bytes 66560 | tf_op jit(solution)/shard_map/all_to_all | solution.py:373
  19.6 3.4 %cold_look_up.1 = f32[32,4,768]{2,1,0:T(4,128)} custom-call(s32[1,128]{1,0:T(1,128)} %reshape.13.asked_ref, f32[1024,768]{1,0:T(8,128)} %table_ref.1), custom_call_target="tpu_custom_call" | custom-call | flops 402653184 | bytes 3145728 | tf_op jit(solution)/shard_map/cold_look_up/pallas_call | solution.py:87
  23.0 2.2 %collective-permute-done.1 = f32[64,768]{1,0:T(8,128)S(1)} collective-permute-done((f32[64,768]{1,0:T(8,128)S(1)}, f32[64,768]{1,0:T(8,128)S(1)}, u32[]{:S(2)}, u32[]{:S(2)}) %collective-permute-start.1) | collective-permute-done | bytes 196640 | tf_op jit(solution)/shard_map/ppermute | solution.py:312
  25.3 2.6 %all-to-all-start.1 = ((f32[32,4,768]{2,1,0:T(4,128)}), f32[32,4,768]{2,1,0:T(4,128)S(1)}, u32[]{:S(2)}, u32[]{:S(2)}) async-start(f32[32,4,768]{2,1,0:T(4,128)} %cold_look_up.1), calls=%async_computation.1 | async-start | bytes 786432 | tf_op jit(solution)/shard_map/all_to_all | solution.py:388
  28.3 1.4 collective-permute-done.2.got_ref
  29.7 2.1 %hot_look_up.1 = (f32[64,768]{1,0:T(8,128)S(1)}, f32[64,768]{1,0:T(8,128)S(1)}, f32[64,768]{1,0:T(8,128)S(1)}, f32[64,768]{1,0:T(8,128)S(1)}) custom-call(s32[6]{0:T(128)S(1)} %stack.32.device_ref, s32[4,64]{1,0:T(4,128)S(1)} %pad_add_fusion.1.asked_ref, f32[256,768]{1,0:T(8,128)S(1)} %copy-done, f32[128,768]{1,0:T(8,128)S(1)} %pad_maximum_fusion.mine_ref, ...), custom_call_target="tpu_custom_call" | custom-call | flops 402653184 | bytes 2359296 | tf_op jit(solution)/shard_map/hot_look_up/pallas_call | solution.py:120
  32.5 1.7 %collective-permute-start.3 = (f32[64,768]{1,0:T(8,128)S(1)}, f32[64,768]{1,0:T(8,128)S(1)}, u32[]{:S(2)}, u32[]{:S(2)}) collective-permute-start(f32[64,768]{1,0:T(8,128)S(1)} %get-tuple-element.27), channel_id=1, source_target_pairs={{0,1},{1,0},{2,3},{3,2},{4,5},{5,4},{6,7},{7,6},{8,9},{9,8},{10,11... | collective-permute-start | bytes 589832 | tf_op jit(solution)/shard_map/ppermute | solution.py:392
  34.1 1.5 %collective-permute-start.4 = (f32[64,768]{1,0:T(8,128)S(1)}, f32[64,768]{1,0:T(8,128)S(1)}, u32[]{:S(2)}, u32[]{:S(2)}) collective-permute-start(f32[64,768]{1,0:T(8,128)S(1)} %get-tuple-element.28), channel_id=1, source_target_pairs={{0,2},{1,3},{2,0},{3,1},{4,6},{5,7},{6,4},{7,5},{8,10},{9,11},{10,... | collective-permute-start | bytes 589832 | tf_op jit(solution)/shard_map/ppermute | solution.py:392
  36.0 7.4 %count_matrices.1.counts_ref = bf16[768,2048]{1,0:T(8,128)(2,1)} custom-call(s32[25,2048]{1,0:T(8,128)} %bitcast.10, s32[1,2048]{1,0:T(1,128)} %bitcast.13), custom_call_target="tpu_custom_call" | custom-call | flops 39321600 | bytes 3145728 | tf_op jit(solution)/shard_map/count_matrices/pallas_call | solution.py:54
  43.4 3.9 %collective-permute-done.5.rest_3_ = f32[64,768]{1,0:T(8,128)S(1)} collective-permute-done((f32[64,768]{1,0:T(8,128)S(1)}, f32[64,768]{1,0:T(8,128)S(1)}, u32[]{:S(2)}, u32[]{:S(2)}) %collective-permute-start.5) | collective-permute-done | bytes 196640 | tf_op jit(solution)/shard_map/ppermute | solution.py:392
  48.1 18.5 %layer_0.1 = (bf16[2048,1024]{1,0:T(8,128)(2,1)}, f32[768,256]{1,0:T(8,128)}, f32[768,256]{1,0:T(8,128)}, f32[768,256]{1,0:T(8,128)}, f32[768,256]{1,0:T(8,128)}...) custom-call(s32[6]{0:T(128)} %copy-done.1, ...), custom_call_target="tpu_custom_call" | custom-call | flops 8858370048 | bytes 11534336 | tf_op jit(solution)/shard_map/layer_0/pallas_call | solution.py:229
  67.7 1.5 collective-permute-done.6
  69.2 1.3 slice_add_fusion.7
  70.5 1.7 %collective-permute-start.7 = (f32[384,256]{1,0:T(8,128)S(1)}, f32[384,256]{1,0:T(8,128)S(1)}, u32[]{:S(2)}, u32[]{:S(2)}) collective-permute-start(f32[384,256]{1,0:T(8,128)S(1)} %get-tuple-element.48), channel_id=1, source_target_pairs={{0,16},{8,24},{16,0},{24,8},{1,17},{9,25},{17,1},{25,9},{2,18},{10... | collective-permute-start | bytes 1179656 | tf_op jit(solution)/shard_map/ppermute | solution.py:312
  72.2 1.2 slice_add_fusion.5
  73.4 1.1 collective-permute-start.17
  75.5 7.0 %collective-permute-done.7 = f32[384,256]{1,0:T(8,128)S(1)} collective-permute-done((f32[384,256]{1,0:T(8,128)S(1)}, f32[384,256]{1,0:T(8,128)S(1)}, u32[]{:S(2)}, u32[]{:S(2)}) %collective-permute-start.7) | collective-permute-done | bytes 393248 | tf_op jit(solution)/shard_map/ppermute | solution.py:312
  82.6 1.2 collective-permute-start.8
  83.8 1.1 collective-permute-done.17
  85.3 2.6 %collective-permute-start.28 = (f32[192,256]{1,0:T(8,128)S(1)}, f32[192,256]{1,0:T(8,128)S(1)}, u32[]{:S(2)}, u32[]{:S(2)}) collective-permute-start(f32[192,256]{1,0:T(8,128)S(1)} %get-tuple-element.52), channel_id=1, source_target_pairs={{0,6},{1,7},{2,4},{3,5},{4,2},{5,3},{6,0},{7,1},{8,14},{9,15},{10,... | collective-permute-start | bytes 589832 | tf_op jit(solution)/shard_map/ppermute | solution.py:312
  87.9 2.3 %collective-permute-done.37 = f32[384,256]{1,0:T(8,128)S(1)} collective-permute-done((f32[384,256]{1,0:T(8,128)S(1)}, f32[384,256]{1,0:T(8,128)S(1)}, u32[]{:S(2)}, u32[]{:S(2)}) %collective-permute-start.37) | collective-permute-done | bytes 393248 | tf_op jit(solution)/shard_map/ppermute | solution.py:312
  90.2 1.2 collective-permute-start.38
  91.7 1.0 collective-permute-done.18
  93.3 3.1 %collective-permute-done.28 = f32[192,256]{1,0:T(8,128)S(1)} collective-permute-done((f32[192,256]{1,0:T(8,128)S(1)}, f32[192,256]{1,0:T(8,128)S(1)}, u32[]{:S(2)}, u32[]{:S(2)}) %collective-permute-start.28) | collective-permute-done | bytes 196640 | tf_op jit(solution)/shard_map/ppermute | solution.py:312
  97.4 2.2 %collective-permute-start.10 = (f32[96,256]{1,0:T(8,128)S(1)}, f32[96,256]{1,0:T(8,128)S(1)}, u32[]{:S(2)}, u32[]{:S(2)}) collective-permute-start(f32[96,256]{1,0:T(8,128)S(1)} %select_add_fusion.3), channel_id=1, source_target_pairs={{0,6},{1,7},{2,4},{3,5},{4,2},{5,3},{6,0},{7,1},{8,14},{9,15},{10,... | collective-permute-start | bytes 294920 | tf_op jit(solution)/shard_map/ppermute | solution.py:312
  99.6 1.7 %collective-permute-start.20 = (f32[96,256]{1,0:T(8,128)S(1)}, f32[96,256]{1,0:T(8,128)S(1)}, u32[]{:S(2)}, u32[]{:S(2)}) collective-permute-start(f32[96,256]{1,0:T(8,128)S(1)} %select_add_fusion.2), channel_id=1, source_target_pairs={{0,6},{1,7},{2,4},{3,5},{4,2},{5,3},{6,0},{7,1},{8,14},{9,15},{10,... | collective-permute-start | bytes 294920 | tf_op jit(solution)/shard_map/ppermute | solution.py:312
  101.4 0.8 collective-permute-start.30
  102.2 2.2 %collective-permute-start.40 = (f32[96,256]{1,0:T(8,128)S(1)}, f32[96,256]{1,0:T(8,128)S(1)}, u32[]{:S(2)}, u32[]{:S(2)}) collective-permute-start(f32[96,256]{1,0:T(8,128)S(1)} %select_add_fusion), channel_id=1, source_target_pairs={{0,6},{1,7},{2,4},{3,5},{4,2},{5,3},{6,0},{7,1},{8,14},{9,15},{10,... | collective-permute-start | bytes 294920 | tf_op jit(solution)/shard_map/ppermute | solution.py:312
  104.4 0.9 collective-permute-done.10
  105.3 5.0 %collective-permute-start.11 = (f32[96,256]{1,0:T(8,128)S(1)}, f32[96,256]{1,0:T(8,128)S(1)}, u32[]{:S(2)}, u32[]{:S(2)}) collective-permute-start(f32[96,256]{1,0:T(8,128)S(1)} %add.140), channel_id=1, source_target_pairs={{0,2},{1,3},{2,0},{3,1},{4,6},{5,7},{6,4},{7,5},{8,10},{9,11},{10,... | collective-permute-start | bytes 294920 | tf_op jit(solution)/shard_map/ppermute | solution.py:312
  110.6 1.9 %collective-permute-start.31 = (f32[96,256]{1,0:T(8,128)S(1)}, f32[96,256]{1,0:T(8,128)S(1)}, u32[]{:S(2)}, u32[]{:S(2)}) collective-permute-start(f32[96,256]{1,0:T(8,128)S(1)} %add.156), channel_id=1, source_target_pairs={{0,16},{8,24},{16,0},{24,8},{1,17},{9,25},{17,1},{25,9},{2,18},{10... | collective-permute-start | bytes 294920 | tf_op jit(solution)/shard_map/ppermute | solution.py:312
  112.5 1.0 collective-permute-start.41
  113.6 1.0 collective-permute-start.12
  115.0 2.1 %collective-permute-start.22 = (f32[192,256]{1,0:T(8,128)S(1)}, f32[192,256]{1,0:T(8,128)S(1)}, u32[]{:S(2)}, u32[]{:S(2)}) collective-permute-start(f32[192,256]{1,0:T(8,128)S(1)} %pad_maximum_fusion.6), channel_id=1, source_target_pairs={{0,2},{1,3},{2,0},{3,1},{4,6},{5,7},{6,4},{7,5},{8,10},{9,11},{10,... | collective-permute-start | bytes 589832 | tf_op jit(solution)/shard_map/ppermute | solution.py:312
  117.2 1.8 %collective-permute-start.32 = (f32[192,256]{1,0:T(8,128)S(1)}, f32[192,256]{1,0:T(8,128)S(1)}, u32[]{:S(2)}, u32[]{:S(2)}) collective-permute-start(f32[192,256]{1,0:T(8,128)S(1)} %pad_maximum_fusion.7), channel_id=1, source_target_pairs={{0,6},{1,7},{2,4},{3,5},{4,2},{5,3},{6,0},{7,1},{8,14},{9,15},{10,... | collective-permute-start | bytes 589832 | tf_op jit(solution)/shard_map/ppermute | solution.py:312
  119.0 1.2 collective-permute-start.42
  120.4 1.5 %collective-permute-start.13 = (f32[384,256]{1,0:T(8,128)S(1)}, f32[384,256]{1,0:T(8,128)S(1)}, u32[]{:S(2)}, u32[]{:S(2)}) collective-permute-start(f32[384,256]{1,0:T(8,128)S(1)} %pad_maximum_fusion.1.rest_0_), channel_id=1, source_target_pairs={{0,16},{8,24},{16,0},{24,8},{1,17},{9,25},{17,1},{25,9},{2,18},{10... | collective-permute-start | bytes 1179656 | tf_op jit(solution)/shard_map/ppermute | solution.py:312
  122.3 2.4 %collective-permute-done.32 = f32[192,256]{1,0:T(8,128)S(1)} collective-permute-done((f32[192,256]{1,0:T(8,128)S(1)}, f32[192,256]{1,0:T(8,128)S(1)}, u32[]{:S(2)}, u32[]{:S(2)}) %collective-permute-start.32) | collective-permute-done | bytes 196640 | tf_op jit(solution)/shard_map/ppermute | solution.py:312
  124.7 1.1 collective-permute-start.23
  126.1 5.8 %collective-permute-done.13.rest_1_ = f32[384,256]{1,0:T(8,128)S(1)} collective-permute-done((f32[384,256]{1,0:T(8,128)S(1)}, f32[384,256]{1,0:T(8,128)S(1)}, u32[]{:S(2)}, u32[]{:S(2)}) %collective-permute-start.13) | collective-permute-done | bytes 393248 | tf_op jit(solution)/shard_map/ppermute | solution.py:312
  131.9 1.5 collective-permute-start.43
  134.3 3.4 %collective-permute-done.33.rest_9_ = f32[384,256]{1,0:T(8,128)} collective-permute-done((f32[384,256]{1,0:T(8,128)S(1)}, f32[384,256]{1,0:T(8,128)}, u32[]{:S(2)}, u32[]{:S(2)}) %collective-permute-start.33) | collective-permute-done | bytes 393248 | tf_op jit(solution)/shard_map/ppermute | solution.py:312
  137.7 5.1 %collective-permute-done.43.rest_13_ = f32[384,256]{1,0:T(8,128)} collective-permute-done((f32[384,256]{1,0:T(8,128)S(1)}, f32[384,256]{1,0:T(8,128)}, u32[]{:S(2)}, u32[]{:S(2)}) %collective-permute-start.43) | collective-permute-done | bytes 393248 | tf_op jit(solution)/shard_map/ppermute | solution.py:312
  142.9 2.0 %collective-permute-done.45.rest_15_ = f32[384,256]{1,0:T(8,128)} collective-permute-done((f32[384,256]{1,0:T(8,128)}, f32[384,256]{1,0:T(8,128)}, u32[]{:S(2)}, u32[]{:S(2)}) %collective-permute-start.45) | collective-permute-done | bytes 393248 | tf_op jit(solution)/shard_map/ppermute | solution.py:312
  144.9 4.5 %place.1 = (f32[768,1024]{1,0:T(8,128)}, f32[768,1024]{1,0:T(8,128)}) custom-call(s32[5]{0:T(128)S(1)} %stack.33.where_ref, f32[384,256]{1,0:T(8,128)S(1)} %pad_maximum_fusion.1.rest_0_, f32[384,256]{1,0:T(8,128)S(1)} %collective-permute-done.13.rest_1_, f32[384,256]{1,0:T(8,128)S(1)} %collective-permute-done.14.rest_2_, ...), custom_call_target="tpu_custom_call" | custom-call | bytes 12582912 | tf_op jit(solution)/shard_map/place/pallas_call | solution.py:291
  (121 shorter events, 11.8 us)
Async XLA Ops:
  1.6 16.6 %collective-permute-start = (f32[64,768]{1,0:T(8,128)S(1)}, f32[64,768]{1,0:T(8,128)S(1)}, u32[]{:S(2)}, u32[]{:S(2)}) collective-permute-start(f32[64,768]{1,0:T(8,128)S(1)} %constant_dynamic-slice_fusion), channel_id=1, source_target_pairs={{0,6},{1,7},{2,4},{3,5},{4,2},{5,3},{6,0},{7,1},{8,14},{9,15},{10,... | collective-permute-start | bytes 589832 | tf_op jit(solution)/shard_map/ppermute | solution.py:312
  8.4 21.3 %copy-start = (f32[256,768]{1,0:T(8,128)S(1)}, f32[256,768]{1,0:T(8,128)}, u32[]{:S(2)}) copy-start(f32[256,768]{1,0:T(8,128)} %own_ref.1) | copy-start | bytes 2359300
  18.2 7.0 %collective-permute-start.1 = (f32[64,768]{1,0:T(8,128)S(1)}, f32[64,768]{1,0:T(8,128)S(1)}, u32[]{:S(2)}, u32[]{:S(2)}) collective-permute-start(f32[64,768]{1,0:T(8,128)S(1)} %collective-permute-done), channel_id=1, source_target_pairs={{0,16},{8,24},{16,0},{24,8},{1,17},{9,25},{17,1},{25,9},{2,18},{10... | collective-permute-start | bytes 589832 | tf_op jit(solution)/shard_map/ppermute | solution.py:312
  25.3 22.0 %all-to-all-start.1 = ((f32[32,4,768]{2,1,0:T(4,128)}), f32[32,4,768]{2,1,0:T(4,128)S(1)}, u32[]{:S(2)}, u32[]{:S(2)}) async-start(f32[32,4,768]{2,1,0:T(4,128)} %cold_look_up.1), calls=%async_computation.1 | async-start | bytes 786432 | tf_op jit(solution)/shard_map/all_to_all | solution.py:388
  27.9 1.8 %collective-permute-start.2 = (f32[128,768]{1,0:T(8,128)S(1)}, f32[128,768]{1,0:T(8,128)S(1)}, u32[]{:S(2)}, u32[]{:S(2)}) collective-permute-start(f32[128,768]{1,0:T(8,128)S(1)} %pad_maximum_fusion.mine_ref), channel_id=1, source_target_pairs={{0,8},{8,0},{16,24},{24,16},{1,9},{9,1},{17,25},{25,17},{2,10},{10... | collective-permute-start | bytes 1179656 | tf_op jit(solution)/shard_map/ppermute | solution.py:312
  32.5 10.9 %collective-permute-start.3 = (f32[64,768]{1,0:T(8,128)S(1)}, f32[64,768]{1,0:T(8,128)S(1)}, u32[]{:S(2)}, u32[]{:S(2)}) collective-permute-start(f32[64,768]{1,0:T(8,128)S(1)} %get-tuple-element.27), channel_id=1, source_target_pairs={{0,1},{1,0},{2,3},{3,2},{4,5},{5,4},{6,7},{7,6},{8,9},{9,8},{10,11... | collective-permute-start | bytes 589832 | tf_op jit(solution)/shard_map/ppermute | solution.py:392
  34.1 9.2 %collective-permute-start.4 = (f32[64,768]{1,0:T(8,128)S(1)}, f32[64,768]{1,0:T(8,128)S(1)}, u32[]{:S(2)}, u32[]{:S(2)}) collective-permute-start(f32[64,768]{1,0:T(8,128)S(1)} %get-tuple-element.28), channel_id=1, source_target_pairs={{0,2},{1,3},{2,0},{3,1},{4,6},{5,7},{6,4},{7,5},{8,10},{9,11},{10,... | collective-permute-start | bytes 589832 | tf_op jit(solution)/shard_map/ppermute | solution.py:392
  35.7 11.7 %collective-permute-start.5 = (f32[64,768]{1,0:T(8,128)S(1)}, f32[64,768]{1,0:T(8,128)S(1)}, u32[]{:S(2)}, u32[]{:S(2)}) collective-permute-start(f32[64,768]{1,0:T(8,128)S(1)} %get-tuple-element.29), channel_id=1, source_target_pairs={{0,3},{1,2},{2,1},{3,0},{4,7},{5,6},{6,5},{7,4},{8,11},{9,10},{10,... | collective-permute-start | bytes 589832 | tf_op jit(solution)/shard_map/ppermute | solution.py:392
  66.6 2.6 %collective-permute-start.6 = (f32[768,256]{1,0:T(8,128)}, f32[768,256]{1,0:T(8,128)S(1)}, u32[]{:S(2)}, u32[]{:S(2)}) collective-permute-start(f32[768,256]{1,0:T(8,128)} %get-tuple-element.32), channel_id=1, source_target_pairs={{0,8},{8,0},{16,24},{24,16},{1,9},{9,1},{17,25},{25,17},{2,10},{10... | collective-permute-start | bytes 2359304 | tf_op jit(solution)/shard_map/ppermute | solution.py:312
  66.7 5.5 %collective-permute-start.16 = (f32[768,256]{1,0:T(8,128)}, f32[768,256]{1,0:T(8,128)S(1)}, u32[]{:S(2)}, u32[]{:S(2)}) collective-permute-start(f32[768,256]{1,0:T(8,128)} %get-tuple-element.34), channel_id=1, source_target_pairs={{0,8},{8,0},{16,24},{24,16},{1,9},{9,1},{17,25},{25,17},{2,10},{10... | collective-permute-start | bytes 2359304 | tf_op jit(solution)/shard_map/ppermute | solution.py:312
  67.2 7.3 %collective-permute-start.26 = (f32[768,256]{1,0:T(8,128)}, f32[768,256]{1,0:T(8,128)S(1)}, u32[]{:S(2)}, u32[]{:S(2)}) collective-permute-start(f32[768,256]{1,0:T(8,128)} %get-tuple-element.36), channel_id=1, source_target_pairs={{0,8},{8,0},{16,24},{24,16},{1,9},{9,1},{17,25},{25,17},{2,10},{10... | collective-permute-start | bytes 2359304 | tf_op jit(solution)/shard_map/ppermute | solution.py:312
  67.3 7.6 %collective-permute-start.36 = (f32[768,256]{1,0:T(8,128)}, f32[768,256]{1,0:T(8,128)S(1)}, u32[]{:S(2)}, u32[]{:S(2)}) collective-permute-start(f32[768,256]{1,0:T(8,128)} %get-tuple-element.38), channel_id=1, source_target_pairs={{0,8},{8,0},{16,24},{24,16},{1,9},{9,1},{17,25},{25,17},{2,10},{10... | collective-permute-start | bytes 2359304 | tf_op jit(solution)/shard_map/ppermute | solution.py:312
  70.5 12.0 %collective-permute-start.7 = (f32[384,256]{1,0:T(8,128)S(1)}, f32[384,256]{1,0:T(8,128)S(1)}, u32[]{:S(2)}, u32[]{:S(2)}) collective-permute-start(f32[384,256]{1,0:T(8,128)S(1)} %get-tuple-element.48), channel_id=1, source_target_pairs={{0,16},{8,24},{16,0},{24,8},{1,17},{9,25},{17,1},{25,9},{2,18},{10... | collective-permute-start | bytes 1179656 | tf_op jit(solution)/shard_map/ppermute | solution.py:312
  73.4 11.5 %collective-permute-start.17 = (f32[384,256]{1,0:T(8,128)S(1)}, f32[384,256]{1,0:T(8,128)S(1)}, u32[]{:S(2)}, u32[]{:S(2)}) collective-permute-start(f32[384,256]{1,0:T(8,128)S(1)} %get-tuple-element.46), channel_id=1, source_target_pairs={{0,1},{1,0},{2,3},{3,2},{4,5},{5,4},{6,7},{7,6},{8,9},{9,8},{10,11... | collective-permute-start | bytes 1179656 | tf_op jit(solution)/shard_map/ppermute | solution.py:312
  74.6 10.7 %collective-permute-start.27 = (f32[384,256]{1,0:T(8,128)S(1)}, f32[384,256]{1,0:T(8,128)S(1)}, u32[]{:S(2)}, u32[]{:S(2)}) collective-permute-start(f32[384,256]{1,0:T(8,128)S(1)} %get-tuple-element.44), channel_id=1, source_target_pairs={{0,2},{1,3},{2,0},{3,1},{4,6},{5,7},{6,4},{7,5},{8,10},{9,11},{10,... | collective-permute-start | bytes 1179656 | tf_op jit(solution)/shard_map/ppermute | solution.py:312
  75.0 15.2 %collective-permute-start.37 = (f32[384,256]{1,0:T(8,128)S(1)}, f32[384,256]{1,0:T(8,128)S(1)}, u32[]{:S(2)}, u32[]{:S(2)}) collective-permute-start(f32[384,256]{1,0:T(8,128)S(1)} %get-tuple-element.42), channel_id=1, source_target_pairs={{0,16},{8,24},{16,0},{24,8},{1,17},{9,25},{17,1},{25,9},{2,18},{10... | collective-permute-start | bytes 1179656 | tf_op jit(solution)/shard_map/ppermute | solution.py:312
  82.6 8.8 %collective-permute-start.8 = (f32[192,256]{1,0:T(8,128)S(1)}, f32[192,256]{1,0:T(8,128)S(1)}, u32[]{:S(2)}, u32[]{:S(2)}) collective-permute-start(f32[192,256]{1,0:T(8,128)S(1)} %get-tuple-element.56), channel_id=1, source_target_pairs={{0,1},{1,0},{2,3},{3,2},{4,5},{5,4},{6,7},{7,6},{8,9},{9,8},{10,11... | collective-permute-start | bytes 589832 | tf_op jit(solution)/shard_map/ppermute | solution.py:312
  84.9 7.8 %collective-permute-start.18 = (f32[192,256]{1,0:T(8,128)S(1)}, f32[192,256]{1,0:T(8,128)S(1)}, u32[]{:S(2)}, u32[]{:S(2)}) collective-permute-start(f32[192,256]{1,0:T(8,128)S(1)} %get-tuple-element.54), channel_id=1, source_target_pairs={{0,2},{1,3},{2,0},{3,1},{4,6},{5,7},{6,4},{7,5},{8,10},{9,11},{10,... | collective-permute-start | bytes 589832 | tf_op jit(solution)/shard_map/ppermute | solution.py:312
  85.3 11.1 %collective-permute-start.28 = (f32[192,256]{1,0:T(8,128)S(1)}, f32[192,256]{1,0:T(8,128)S(1)}, u32[]{:S(2)}, u32[]{:S(2)}) collective-permute-start(f32[192,256]{1,0:T(8,128)S(1)} %get-tuple-element.52), channel_id=1, source_target_pairs={{0,6},{1,7},{2,4},{3,5},{4,2},{5,3},{6,0},{7,1},{8,14},{9,15},{10,... | collective-permute-start | bytes 589832 | tf_op jit(solution)/shard_map/ppermute | solution.py:312
  90.2 6.6 %collective-permute-start.38 = (f32[192,256]{1,0:T(8,128)S(1)}, f32[192,256]{1,0:T(8,128)S(1)}, u32[]{:S(2)}, u32[]{:S(2)}) collective-permute-start(f32[192,256]{1,0:T(8,128)S(1)} %get-tuple-element.50), channel_id=1, source_target_pairs={{0,1},{1,0},{2,3},{3,2},{4,5},{5,4},{6,7},{7,6},{8,9},{9,8},{10,11... | collective-permute-start | bytes 589832 | tf_op jit(solution)/shard_map/ppermute | solution.py:312
  91.4 5.9 %collective-permute-start.9 = (f32[96,256]{1,0:T(8,128)S(1)}, f32[96,256]{1,0:T(8,128)S(1)}, u32[]{:S(2)}, u32[]{:S(2)}) collective-permute-start(f32[96,256]{1,0:T(8,128)S(1)} %broadcast_select_fusion.29), channel_id=1, source_target_pairs={{0,2},{1,3},{2,0},{3,1},{4,6},{5,7},{6,4},{7,5},{8,10},{9,11},{10,... | collective-permute-start | bytes 294920 | tf_op jit(solution)/shard_map/ppermute | solution.py:312
  92.7 6.8 %collective-permute-start.19 = (f32[96,256]{1,0:T(8,128)S(1)}, f32[96,256]{1,0:T(8,128)S(1)}, u32[]{:S(2)}, u32[]{:S(2)}) collective-permute-start(f32[96,256]{1,0:T(8,128)S(1)} %broadcast_select_fusion.23), channel_id=1, source_target_pairs={{0,16},{8,24},{16,0},{24,8},{1,17},{9,25},{17,1},{25,9},{2,18},{10... | collective-permute-start | bytes 294920 | tf_op jit(solution)/shard_map/ppermute | solution.py:312
  96.4 4.9 %collective-permute-start.29 = (f32[96,256]{1,0:T(8,128)S(1)}, f32[96,256]{1,0:T(8,128)S(1)}, u32[]{:S(2)}, u32[]{:S(2)}) collective-permute-start(f32[96,256]{1,0:T(8,128)S(1)} %broadcast_select_fusion.20), channel_id=1, source_target_pairs={{0,16},{8,24},{16,0},{24,8},{1,17},{9,25},{17,1},{25,9},{2,18},{10... | collective-permute-start | bytes 294920 | tf_op jit(solution)/shard_map/ppermute | solution.py:312
  96.8 5.4 %collective-permute-start.39 = (f32[96,256]{1,0:T(8,128)S(1)}, f32[96,256]{1,0:T(8,128)S(1)}, u32[]{:S(2)}, u32[]{:S(2)}) collective-permute-start(f32[96,256]{1,0:T(8,128)S(1)} %broadcast_select_fusion.26), channel_id=1, source_target_pairs={{0,2},{1,3},{2,0},{3,1},{4,6},{5,7},{6,4},{7,5},{8,10},{9,11},{10,... | collective-permute-start | bytes 294920 | tf_op jit(solution)/shard_map/ppermute | solution.py:312
  97.4 7.9 %collective-permute-start.10 = (f32[96,256]{1,0:T(8,128)S(1)}, f32[96,256]{1,0:T(8,128)S(1)}, u32[]{:S(2)}, u32[]{:S(2)}) collective-permute-start(f32[96,256]{1,0:T(8,128)S(1)} %select_add_fusion.3), channel_id=1, source_target_pairs={{0,6},{1,7},{2,4},{3,5},{4,2},{5,3},{6,0},{7,1},{8,14},{9,15},{10,... | collective-permute-start | bytes 294920 | tf_op jit(solution)/shard_map/ppermute | solution.py:312
  99.6 10.7 %collective-permute-start.20 = (f32[96,256]{1,0:T(8,128)S(1)}, f32[96,256]{1,0:T(8,128)S(1)}, u32[]{:S(2)}, u32[]{:S(2)}) collective-permute-start(f32[96,256]{1,0:T(8,128)S(1)} %select_add_fusion.2), channel_id=1, source_target_pairs={{0,6},{1,7},{2,4},{3,5},{4,2},{5,3},{6,0},{7,1},{8,14},{9,15},{10,... | collective-permute-start | bytes 294920 | tf_op jit(solution)/shard_map/ppermute | solution.py:312
  101.4 9.2 %collective-permute-start.30 = (f32[96,256]{1,0:T(8,128)S(1)}, f32[96,256]{1,0:T(8,128)S(1)}, u32[]{:S(2)}, u32[]{:S(2)}) collective-permute-start(f32[96,256]{1,0:T(8,128)S(1)} %select_add_fusion.1), channel_id=1, source_target_pairs={{0,1},{1,0},{2,3},{3,2},{4,5},{5,4},{6,7},{7,6},{8,9},{9,8},{10,11... | collective-permute-start | bytes 294920 | tf_op jit(solution)/shard_map/ppermute | solution.py:312
  102.2 10.2 %collective-permute-start.40 = (f32[96,256]{1,0:T(8,128)S(1)}, f32[96,256]{1,0:T(8,128)S(1)}, u32[]{:S(2)}, u32[]{:S(2)}) collective-permute-start(f32[96,256]{1,0:T(8,128)S(1)} %select_add_fusion), channel_id=1, source_target_pairs={{0,6},{1,7},{2,4},{3,5},{4,2},{5,3},{6,0},{7,1},{8,14},{9,15},{10,... | collective-permute-start | bytes 294920 | tf_op jit(solution)/shard_map/ppermute | solution.py:312
  105.3 8.2 %collective-permute-start.11 = (f32[96,256]{1,0:T(8,128)S(1)}, f32[96,256]{1,0:T(8,128)S(1)}, u32[]{:S(2)}, u32[]{:S(2)}) collective-permute-start(f32[96,256]{1,0:T(8,128)S(1)} %add.140), channel_id=1, source_target_pairs={{0,2},{1,3},{2,0},{3,1},{4,6},{5,7},{6,4},{7,5},{8,10},{9,11},{10,... | collective-permute-start | bytes 294920 | tf_op jit(solution)/shard_map/ppermute | solution.py:312
  110.3 4.7 %collective-permute-start.21 = (f32[96,256]{1,0:T(8,128)S(1)}, f32[96,256]{1,0:T(8,128)S(1)}, u32[]{:S(2)}, u32[]{:S(2)}) collective-permute-start(f32[96,256]{1,0:T(8,128)S(1)} %add.148), channel_id=1, source_target_pairs={{0,16},{8,24},{16,0},{24,8},{1,17},{9,25},{17,1},{25,9},{2,18},{10... | collective-permute-start | bytes 294920 | tf_op jit(solution)/shard_map/ppermute | solution.py:312
  110.6 6.5 %collective-permute-start.31 = (f32[96,256]{1,0:T(8,128)S(1)}, f32[96,256]{1,0:T(8,128)S(1)}, u32[]{:S(2)}, u32[]{:S(2)}) collective-permute-start(f32[96,256]{1,0:T(8,128)S(1)} %add.156), channel_id=1, source_target_pairs={{0,16},{8,24},{16,0},{24,8},{1,17},{9,25},{17,1},{25,9},{2,18},{10... | collective-permute-start | bytes 294920 | tf_op jit(solution)/shard_map/ppermute | solution.py:312
  112.5 6.4 %collective-permute-start.41 = (f32[96,256]{1,0:T(8,128)S(1)}, f32[96,256]{1,0:T(8,128)S(1)}, u32[]{:S(2)}, u32[]{:S(2)}) collective-permute-start(f32[96,256]{1,0:T(8,128)S(1)} %add.164), channel_id=1, source_target_pairs={{0,2},{1,3},{2,0},{3,1},{4,6},{5,7},{6,4},{7,5},{8,10},{9,11},{10,... | collective-permute-start | bytes 294920 | tf_op jit(solution)/shard_map/ppermute | solution.py:312
  113.6 6.6 %collective-permute-start.12 = (f32[192,256]{1,0:T(8,128)S(1)}, f32[192,256]{1,0:T(8,128)S(1)}, u32[]{:S(2)}, u32[]{:S(2)}) collective-permute-start(f32[192,256]{1,0:T(8,128)S(1)} %pad_maximum_fusion.5), channel_id=1, source_target_pairs={{0,1},{1,0},{2,3},{3,2},{4,5},{5,4},{6,7},{7,6},{8,9},{9,8},{10,11... | collective-permute-start | bytes 589832 | tf_op jit(solution)/shard_map/ppermute | solution.py:312
  115.0 7.1 %collective-permute-start.22 = (f32[192,256]{1,0:T(8,128)S(1)}, f32[192,256]{1,0:T(8,128)S(1)}, u32[]{:S(2)}, u32[]{:S(2)}) collective-permute-start(f32[192,256]{1,0:T(8,128)S(1)} %pad_maximum_fusion.6), channel_id=1, source_target_pairs={{0,2},{1,3},{2,0},{3,1},{4,6},{5,7},{6,4},{7,5},{8,10},{9,11},{10,... | collective-permute-start | bytes 589832 | tf_op jit(solution)/shard_map/ppermute | solution.py:312
  117.2 7.5 %collective-permute-start.32 = (f32[192,256]{1,0:T(8,128)S(1)}, f32[192,256]{1,0:T(8,128)S(1)}, u32[]{:S(2)}, u32[]{:S(2)}) collective-permute-start(f32[192,256]{1,0:T(8,128)S(1)} %pad_maximum_fusion.7), channel_id=1, source_target_pairs={{0,6},{1,7},{2,4},{3,5},{4,2},{5,3},{6,0},{7,1},{8,14},{9,15},{10,... | collective-permute-start | bytes 589832 | tf_op jit(solution)/shard_map/ppermute | solution.py:312
  119.0 6.9 %collective-permute-start.42 = (f32[192,256]{1,0:T(8,128)S(1)}, f32[192,256]{1,0:T(8,128)S(1)}, u32[]{:S(2)}, u32[]{:S(2)}) collective-permute-start(f32[192,256]{1,0:T(8,128)S(1)} %pad_maximum_fusion.8), channel_id=1, source_target_pairs={{0,1},{1,0},{2,3},{3,2},{4,5},{5,4},{6,7},{7,6},{8,9},{9,8},{10,11... | collective-permute-start | bytes 589832 | tf_op jit(solution)/shard_map/ppermute | solution.py:312
  120.3 5.7 %collective-permute-start.14 = (f32[384,256]{1,0:T(8,128)S(1)}, f32[384,256]{1,0:T(8,128)S(1)}, u32[]{:S(2)}, u32[]{:S(2)}) collective-permute-start(f32[384,256]{1,0:T(8,128)S(1)} %pad_maximum_fusion.1.rest_0_), channel_id=1, source_target_pairs={{0,8},{8,0},{16,24},{24,16},{1,9},{9,1},{17,25},{25,17},{2,10},{10... | collective-permute-start | bytes 1179656 | tf_op jit(solution)/shard_map/ppermute | solution.py:312
  120.4 11.5 %collective-permute-start.13 = (f32[384,256]{1,0:T(8,128)S(1)}, f32[384,256]{1,0:T(8,128)S(1)}, u32[]{:S(2)}, u32[]{:S(2)}) collective-permute-start(f32[384,256]{1,0:T(8,128)S(1)} %pad_maximum_fusion.1.rest_0_), channel_id=1, source_target_pairs={{0,16},{8,24},{16,0},{24,8},{1,17},{9,25},{17,1},{25,9},{2,18},{10... | collective-permute-start | bytes 1179656 | tf_op jit(solution)/shard_map/ppermute | solution.py:312
  122.2 11.1 %collective-permute-start.24 = (f32[384,256]{1,0:T(8,128)S(1)}, f32[384,256]{1,0:T(8,128)S(1)}, u32[]{:S(2)}, u32[]{:S(2)}) collective-permute-start(f32[384,256]{1,0:T(8,128)S(1)} %pad_maximum_fusion.2.rest_4_), channel_id=1, source_target_pairs={{0,8},{8,0},{16,24},{24,16},{1,9},{9,1},{17,25},{25,17},{2,10},{10... | collective-permute-start | bytes 1179656 | tf_op jit(solution)/shard_map/ppermute | solution.py:312
  124.7 9.1 %collective-permute-start.23 = (f32[384,256]{1,0:T(8,128)S(1)}, f32[384,256]{1,0:T(8,128)S(1)}, u32[]{:S(2)}, u32[]{:S(2)}) collective-permute-start(f32[384,256]{1,0:T(8,128)S(1)} %pad_maximum_fusion.2.rest_4_), channel_id=1, source_target_pairs={{0,1},{1,0},{2,3},{3,2},{4,5},{5,4},{6,7},{7,6},{8,9},{9,8},{10,11... | collective-permute-start | bytes 1179656 | tf_op jit(solution)/shard_map/ppermute | solution.py:312
  125.9 8.0 %collective-permute-start.34 = (f32[384,256]{1,0:T(8,128)S(1)}, f32[384,256]{1,0:T(8,128)S(1)}, u32[]{:S(2)}, u32[]{:S(2)}) collective-permute-start(f32[384,256]{1,0:T(8,128)S(1)} %pad_maximum_fusion.3.rest_8_), channel_id=1, source_target_pairs={{0,8},{8,0},{16,24},{24,16},{1,9},{9,1},{17,25},{25,17},{2,10},{10... | collective-permute-start | bytes 1179656 | tf_op jit(solution)/shard_map/ppermute | solution.py:312
  126.0 11.7 %collective-permute-start.33 = (f32[384,256]{1,0:T(8,128)S(1)}, f32[384,256]{1,0:T(8,128)}, u32[]{:S(2)}, u32[]{:S(2)}) collective-permute-start(f32[384,256]{1,0:T(8,128)S(1)} %pad_maximum_fusion.3.rest_8_), channel_id=1, source_target_pairs={{0,2},{1,3},{2,0},{3,1},{4,6},{5,7},{6,4},{7,5},{8,10},{9,11},{10,... | collective-permute-start | bytes 1179656 | tf_op jit(solution)/shard_map/ppermute | solution.py:312
  131.9 10.9 %collective-permute-start.43 = (f32[384,256]{1,0:T(8,128)S(1)}, f32[384,256]{1,0:T(8,128)}, u32[]{:S(2)}, u32[]{:S(2)}) collective-permute-start(f32[384,256]{1,0:T(8,128)S(1)} %pad_maximum_fusion.4.rest_12_), channel_id=1, source_target_pairs={{0,16},{8,24},{16,0},{24,8},{1,17},{9,25},{17,1},{25,9},{2,18},{10... | collective-permute-start | bytes 1179656 | tf_op jit(solution)/shard_map/ppermute | solution.py:312
  133.4 9.5 %collective-permute-start.44 = (f32[384,256]{1,0:T(8,128)S(1)}, f32[384,256]{1,0:T(8,128)}, u32[]{:S(2)}, u32[]{:S(2)}) collective-permute-start(f32[384,256]{1,0:T(8,128)S(1)} %pad_maximum_fusion.4.rest_12_), channel_id=1, source_target_pairs={{0,8},{8,0},{16,24},{24,16},{1,9},{9,1},{17,25},{25,17},{2,10},{10... | collective-permute-start | bytes 1179656 | tf_op jit(solution)/shard_map/ppermute | solution.py:312
  133.8 9.1 %collective-permute-start.15 = (f32[384,256]{1,0:T(8,128)S(1)}, f32[384,256]{1,0:T(8,128)}, u32[]{:S(2)}, u32[]{:S(2)}) collective-permute-start(f32[384,256]{1,0:T(8,128)S(1)} %collective-permute-done.13.rest_1_), channel_id=1, source_target_pairs={{0,8},{8,0},{16,24},{24,16},{1,9},{9,1},{17,25},{25,17},{2,10},{10... | collective-permute-start | bytes 1179656 | tf_op jit(solution)/shard_map/ppermute | solution.py:312
  133.9 9.0 %collective-permute-start.25 = (f32[384,256]{1,0:T(8,128)S(1)}, f32[384,256]{1,0:T(8,128)}, u32[]{:S(2)}, u32[]{:S(2)}) collective-permute-start(f32[384,256]{1,0:T(8,128)S(1)} %collective-permute-done.23.rest_5_), channel_id=1, source_target_pairs={{0,8},{8,0},{16,24},{24,16},{1,9},{9,1},{17,25},{25,17},{2,10},{10... | collective-permute-start | bytes 1179656 | tf_op jit(solution)/shard_map/ppermute | solution.py:312
  137.7 5.2 %collective-permute-start.35 = (f32[384,256]{1,0:T(8,128)}, f32[384,256]{1,0:T(8,128)}, u32[]{:S(2)}, u32[]{:S(2)}) collective-permute-start(f32[384,256]{1,0:T(8,128)} %collective-permute-done.33.rest_9_), channel_id=1, source_target_pairs={{0,8},{8,0},{16,24},{24,16},{1,9},{9,1},{17,25},{25,17},{2,10},{10... | collective-permute-start | bytes 1179656 | tf_op jit(solution)/shard_map/ppermute | solution.py:312
  142.8 2.1 %collective-permute-start.45 = (f32[384,256]{1,0:T(8,128)}, f32[384,256]{1,0:T(8,128)}, u32[]{:S(2)}, u32[]{:S(2)}) collective-permute-start(f32[384,256]{1,0:T(8,128)} %collective-permute-done.43.rest_13_), channel_id=1, source_target_pairs={{0,8},{8,0},{16,24},{24,16},{1,9},{9,1},{17,25},{25,17},{2,10},{10... | collective-permute-start | bytes 1179656 | tf_op jit(solution)/shard_map/ppermute | solution.py:312
  (8 other events, 42.8 us)
